TPU v7x, 32 devices: a whole 2x2x4 slice. The times are simulated.
32 devices in a mesh: dp: 4 (over x, core), row: 2 (over y), col: 4 (over z).
Axes of the slice: x: 2, y: 2, z: 4, core: 2. Of those that a mesh axis runs over, the one named last changes fastest.
Arguments:
- tokens_in: bfloat16 [8192, 1536], P(('dp', 'row')), may hold values from -6 to 6
- segment_ids: int32 [4, 2048], P('dp'), may hold values from 0 to 3, never falling along the last dimension, each value on 1 to 1024 neighbouring positions
- norm_gain: float32 [1536], replicated, may hold values from 0.5 to 1.5
- proj_gate: bfloat16 [1536, 3072], P('col', 'row'), may hold values from -0.15625 to 0.15625
- proj_inner: bfloat16 [1536, 3072], P('col', 'row'), may hold values from -0.15625 to 0.15625
- proj_step: bfloat16 [1536, 48], P('col', 'row'), may hold values from -0.15625 to 0.15625
- proj_states: bfloat16 [1536, 256], replicated, may hold values from -0.15625 to 0.15625
- conv_inner: float32 [4, 3072], P(None, ('row', 'col')), may hold values from -3 to 3
- conv_inner_bias: float32 [3072], P(('row', 'col')), may hold values from -1.5 to 1.5
- conv_states: float32 [4, 256], replicated, may hold values from -3 to 3
- conv_states_bias: float32 [256], replicated, may hold values from -1.5 to 1.5
- step_bias: float32 [48], P(('row', 'col')), may hold values from -6 to -1
- decay_log: float32 [48], P(('row', 'col')), may hold values from 0 to 2.77
- skip_gain: float32 [48], P(('row', 'col')), may hold values from 0.5 to 1.5
- gate_gain: float32 [3072], P(('row', 'col')), may hold values from 0.5 to 1.5
- proj_out: bfloat16 [3072, 1536], P('row', 'col'), may hold values from -0.109375 to 0.109375
- cotangent: bfloat16 [8192, 1536], P(('dp', 'row'), 'col'), may hold values from -6 to 6
Outputs:
- mixed_out: bfloat16 [8192, 1536], P(('dp', 'row'), 'col')
- grad_tokens: bfloat16 [8192, 1536], P(('dp', 'row'), 'col')
- grad_norm_gain: float32 [1536], P('col')
- grad_proj_gate: float32 [1536, 3072], P('col', 'row')
- grad_proj_inner: float32 [1536, 3072], P('col', 'row')
- grad_proj_step: float32 [1536, 48], P('col', 'row')
- grad_proj_states: float32 [1536, 256], replicated
- grad_conv_inner: float32 [4, 3072], P(None, ('row', 'col'))
- grad_conv_inner_bias: float32 [3072], P(('row', 'col'))
- grad_conv_states: float32 [4, 256], replicated
- grad_conv_states_bias: float32 [256], replicated
- grad_step_bias: float32 [48], P(('row', 'col'))
- grad_decay_log: float32 [48], P(('row', 'col'))
- grad_skip_gain: float32 [48], P(('row', 'col'))
- grad_gate_gain: float32 [3072], P(('row', 'col'))
- grad_proj_out: float32 [3072, 1536], P('row', 'col')
Inputs may be any that keep to these rules, and one draw needn't show every extreme that they name: `segment_ids`: in each sequence the numbers never fall; each number covers 1 to 1024 consecutive positions, and some number covers exactly 1024.
All inputs are finite; a program needn't handle non-finite values.
Results may differ from a plain program's by a relative error of at most 0.01.
Values may be sent and summed in bfloat16 or wider, within the bound.
A program may use at most 256 MiB of HBM per device.

v0:
```python
import jax
import jax.numpy as jnp
from jax import lax
from jax.sharding import PartitionSpec as P

D = 1536
SPAN = 256
INNER = 3072


epsilon = 1e-05


def rounded(values):
    return lax.optimization_barrier(values.astype(jnp.bfloat16)).astype(jnp.float32)


def product(left, right):
    return jnp.dot(left, right, preferred_element_type=jnp.float32)


def causal_conv(signal, kernel, offset, segments):
    length = signal.shape[1]
    running = offset + kernel[0] * signal
    for back_step in range(1, kernel.shape[0]):
        shifted = jnp.pad(signal, ((0, 0), (back_step, 0), (0, 0)))[:, :length]
        earlier = jnp.pad(segments, ((0, 0), (back_step, 0)), constant_values=-1)[:, :length]
        same_doc = (earlier == segments)[:, :, None]
        running = running + jnp.where(same_doc, kernel[back_step] * shifted, 0.0)
    return running


def span_scan(inner_seq, write_seq, read_seq, step_seq, decay_rate, skip_gain, doc_seq):
    length, heads, width = inner_seq.shape
    blocks = length // SPAN
    pieces = (
        inner_seq.reshape(blocks, SPAN, heads, width),
        write_seq.reshape(blocks, SPAN, -1),
        read_seq.reshape(blocks, SPAN, -1),
        step_seq.reshape(blocks, SPAN, heads),
        doc_seq.reshape(blocks, SPAN),
    )
    positions = jnp.arange(SPAN)
    causal = positions[:, None] >= positions[None, :]

    def advance(carry, block):
        memory, previous = carry
        inner_part, write_part, read_part, step_part, doc_part = block
        log_decay = step_part * decay_rate[None, :]
        running = jnp.cumsum(log_decay, axis=0)
        allowed = (causal & (doc_part[:, None] == doc_part[None, :]))[:, :, None]
        differ = running[:, None, :] - running[None, :, :]
        weights_in = jnp.where(allowed, jnp.exp(jnp.where(allowed, differ, 0.0)), 0.0)
        scores = jnp.dot(read_part, write_part.T, precision=lax.Precision.HIGHEST)
        mixing = scores[:, :, None] * weights_in * step_part[None, :, :]
        within = jnp.einsum("tsh,shp->thp", mixing, inner_part, precision=lax.Precision.HIGHEST)
        linked = jnp.where((doc_part == previous)[:, None], jnp.exp(running), 0.0)
        carried = (
            jnp.einsum("tn,hnp->thp", read_part, memory, precision=lax.Precision.HIGHEST)
            * linked[:, :, None]
        )
        output = within + carried + skip_gain[None, :, None] * inner_part
        last_doc = doc_part[-1]
        to_end = (
            jnp.where((doc_part == last_doc)[:, None], jnp.exp(running[-1][None, :] - running), 0.0)
            * step_part
        )
        fresh = jnp.einsum(
            "sh,sn,shp->hnp", to_end, write_part, inner_part, precision=lax.Precision.HIGHEST
        )
        retained = jnp.where(
            last_doc == previous, jnp.exp(running[-1])[:, None, None] * memory, 0.0
        )
        return ((fresh + retained, last_doc), output)

    start = (jnp.zeros((heads, write_seq.shape[1], width), jnp.float32), jnp.array(-1, jnp.int32))
    _, outputs = lax.scan(jax.checkpoint(advance), start, pieces)
    return outputs.reshape(length, heads, width)


def per_device(
    tokens_in,
    segment_ids,
    norm_gain,
    proj_gate,
    proj_inner,
    proj_step,
    proj_states,
    conv_inner,
    conv_inner_bias,
    conv_states,
    conv_states_bias,
    step_bias,
    decay_log,
    skip_gain,
    gate_gain,
    proj_out,
    cotangent,
):
    seqs, length = segment_ids.shape
    gathered = lax.all_gather(tokens_in, "row", axis=0, tiled=True)
    wide = gathered.astype(jnp.float32)
    inverse = lax.rsqrt(jnp.mean(wide * wide, -1, keepdims=True) + epsilon)
    raw_normed = wide * inverse
    normed = (raw_normed * norm_gain).astype(jnp.bfloat16)
    col_width = normed.shape[1] // lax.axis_size("col")
    col_start = lax.axis_index("col") * col_width
    normed_cols = lax.dynamic_slice_in_dim(normed, col_start, col_width, 1)
    parts = (
        product(normed_cols, proj_gate),
        product(normed_cols, proj_inner),
        product(normed_cols, proj_step),
    )
    gate_pre, inner_pre, step_raw = (
        lax.psum_scatter(parts[0], "col", scatter_dimension=1, tiled=True),
        lax.psum_scatter(parts[1], "col", scatter_dimension=1, tiled=True),
        lax.psum_scatter(parts[2], "col", scatter_dimension=1, tiled=True),
    )
    states_pre = product(normed, proj_states)

    def convolve(inner_in, states_in, taps_inner, bias_inner, taps_states, bias_states):
        inner_out = jax.nn.silu(
            causal_conv(inner_in.reshape(seqs, length, -1), taps_inner, bias_inner, segment_ids)
        )
        states_out = jax.nn.silu(
            causal_conv(states_in.reshape(seqs, length, -1), taps_states, bias_states, segment_ids)
        )
        return (inner_out.reshape(seqs * length, -1), states_out.reshape(seqs * length, -1))

    (inner_act, states_act), conv_back = jax.vjp(
        convolve, inner_pre, states_pre, conv_inner, conv_inner_bias, conv_states, conv_states_bias
    )
    half = states_act.shape[1] // 2
    inner_low = rounded(inner_act)
    write_low = rounded(states_act[:, :half])
    read_low = rounded(states_act[:, half:])

    def mixer(inner_in, write_in, read_in, step_in, gate_in, bias_in, decay_in, skip_in):
        heads = step_in.shape[1]
        width = inner_in.shape[1] // heads
        step = jax.nn.softplus(step_in + bias_in)
        decay_rate = -jnp.exp(decay_in)

        def one_sequence(inner_seq, write_seq, read_seq, step_seq, doc_seq):
            return span_scan(inner_seq, write_seq, read_seq, step_seq, decay_rate, skip_in, doc_seq)

        outputs = jax.vmap(one_sequence)(
            inner_in.reshape(seqs, length, heads, width),
            write_in.reshape(seqs, length, -1),
            read_in.reshape(seqs, length, -1),
            step.reshape(seqs, length, heads),
            segment_ids,
        )
        return outputs.reshape(seqs * length, heads * width) * jax.nn.silu(gate_in)

    mixed, mix_back = jax.vjp(
        mixer, inner_low, write_low, read_low, step_raw, gate_pre, step_bias, decay_log, skip_gain
    )
    square_total = lax.psum(jnp.sum(mixed * mixed, -1), ("row", "col"))
    gate_scale = lax.rsqrt(square_total / INNER + epsilon)[:, None]
    gated = (mixed * gate_scale * gate_gain).astype(jnp.bfloat16)
    gate_cols = lax.all_gather(gated, "col", axis=1, tiled=True)
    out_rows = lax.psum_scatter(
        product(gate_cols, proj_out), "row", scatter_dimension=0, tiled=True
    )
    own_tokens = lax.dynamic_slice_in_dim(tokens_in, col_start, col_width, 1).astype(jnp.float32)
    mixed_out = (own_tokens + out_rows).astype(jnp.bfloat16)
    cot_all = lax.all_gather(cotangent, "row", axis=0, tiled=True)
    grad_proj_out = jnp.einsum("tk,td->kd", gate_cols, cot_all, preferred_element_type=jnp.float32)
    back_parts = jnp.einsum("td,kd->tk", cot_all, proj_out, preferred_element_type=jnp.float32)
    grad_gated = lax.psum_scatter(back_parts, "col", scatter_dimension=1, tiled=True)
    grad_gate_gain = jnp.sum(grad_gated * mixed * gate_scale, 0)
    scaled = grad_gated * gate_gain
    inner_total = lax.psum(jnp.sum(scaled * mixed, -1), ("row", "col"))
    grad_mixed = gate_scale * scaled - mixed * gate_scale**3 * (inner_total / INNER)[:, None]
    (
        grad_inner_low,
        grad_write,
        grad_read,
        grad_step_raw,
        grad_gate_pre,
        grad_step_bias,
        grad_decay_log,
        grad_skip_gain,
    ) = mix_back(grad_mixed)
    grad_inner_pre, states_share, grad_conv_inner, grad_conv_inner_bias, taps_share, bias_share = (
        conv_back((grad_inner_low, jnp.concatenate([grad_write, grad_read], -1)))
    )
    grad_states_pre, grad_conv_states, grad_conv_states_bias = lax.psum(
        (states_share, taps_share, bias_share), ("row", "col")
    )
    states_back = grad_states_pre.astype(jnp.bfloat16)
    gate_back, inner_back, step_back = (
        lax.all_gather(grad_gate_pre.astype(jnp.bfloat16), "col", axis=1, tiled=True),
        lax.all_gather(grad_inner_pre.astype(jnp.bfloat16), "col", axis=1, tiled=True),
        lax.all_gather(grad_step_raw.astype(jnp.bfloat16), "col", axis=1, tiled=True),
    )
    grad_proj_gate = jnp.einsum(
        "tk,tj->kj", normed_cols, gate_back, preferred_element_type=jnp.float32
    )
    grad_proj_inner = jnp.einsum(
        "tk,tj->kj", normed_cols, inner_back, preferred_element_type=jnp.float32
    )
    grad_proj_step = jnp.einsum(
        "tk,tj->kj", normed_cols, step_back, preferred_element_type=jnp.float32
    )
    grad_proj_states = jnp.einsum(
        "tk,tj->kj", normed, states_back, preferred_element_type=jnp.float32
    )
    normed_grad = (
        jnp.einsum("tj,kj->tk", gate_back, proj_gate, preferred_element_type=jnp.float32)
        + jnp.einsum("tj,kj->tk", inner_back, proj_inner, preferred_element_type=jnp.float32)
        + jnp.einsum("tj,kj->tk", step_back, proj_step, preferred_element_type=jnp.float32)
    )
    states_cols = lax.dynamic_slice_in_dim(proj_states, col_start, col_width, 0)
    states_term = jnp.einsum(
        "tj,kj->tk", states_back, states_cols, preferred_element_type=jnp.float32
    )
    normed_grad = normed_grad + jnp.where(lax.axis_index("row") == 0, states_term, 0.0)
    raw_cols = lax.dynamic_slice_in_dim(raw_normed, col_start, col_width, 1)
    gain_share = jnp.sum(normed_grad * raw_cols, 0)
    gain_tiles = jnp.broadcast_to(gain_share[None, :], (lax.axis_size("row"), col_width))
    own_grad, gain_rows = (
        lax.psum_scatter(normed_grad, "row", scatter_dimension=0, tiled=True),
        lax.psum_scatter(gain_tiles, "row", scatter_dimension=0, tiled=True),
    )
    own_wide = tokens_in.astype(jnp.float32)
    own_inverse = lax.rsqrt(jnp.mean(own_wide * own_wide, -1, keepdims=True) + epsilon)
    gain_cols = lax.dynamic_slice_in_dim(norm_gain, col_start, col_width, 0)
    scaled_in = own_grad * gain_cols
    input_total = lax.psum(jnp.sum(scaled_in * own_tokens, -1), "col")
    grad_input = own_inverse * scaled_in - own_tokens * own_inverse**3 * (input_total / D)[:, None]
    grad_tokens = (grad_input + cotangent.astype(jnp.float32)).astype(jnp.bfloat16)
    summed = lax.psum(
        (
            gain_rows[0],
            grad_proj_gate,
            grad_proj_inner,
            grad_proj_step,
            grad_proj_states,
            grad_conv_inner,
            grad_conv_inner_bias,
            grad_conv_states,
            grad_conv_states_bias,
            grad_step_bias,
            grad_decay_log,
            grad_skip_gain,
            grad_gate_gain,
            grad_proj_out,
        ),
        "dp",
    )
    return (
        mixed_out,
        grad_tokens,
        summed[0],
        summed[1],
        summed[2],
        summed[3],
        summed[4],
        summed[5],
        summed[6],
        summed[7],
        summed[8],
        summed[9],
        summed[10],
        summed[11],
        summed[12],
        summed[13],
    )


def solution(mesh):
    in_specs = (
        P(("dp", "row"), None),
        P("dp", None),
        P(),
        P("col", "row"),
        P("col", "row"),
        P("col", "row"),
        P(),
        P(None, ("row", "col")),
        P(("row", "col")),
        P(),
        P(),
        P(("row", "col")),
        P(("row", "col")),
        P(("row", "col")),
        P(("row", "col")),
        P("row", "col"),
        P(("dp", "row"), "col"),
    )
    out_specs = (
        P(("dp", "row"), "col"),
        P(("dp", "row"), "col"),
        P("col"),
        P("col", "row"),
        P("col", "row"),
        P("col", "row"),
        P(),
        P(None, ("row", "col")),
        P(("row", "col")),
        P(),
        P(),
        P(("row", "col")),
        P(("row", "col")),
        P(("row", "col")),
        P(("row", "col")),
        P("row", "col"),
    )
    return jax.shard_map(
        per_device, mesh=mesh, in_specs=in_specs, out_specs=out_specs, check_vma=False
    )
```

profile of v0, /device:TPU:0, one launch (start us, length us, event | category | flops | bytes accessed | tf_op | source)
XLA Modules:
  0.0 2026.6 jit_solution(3465535056510787566)
XLA Ops:
  8.7 83.9 %all-gather.8.cloned.1.call-done = bf16[2048,1536]{1,0:T(8,128)(2,1)} async-done(((bf16[1024,1536]{1,0:T(8,128)(2,1)}), bf16[2048,1536]{1,0:T(8,128)(2,1)}) %all-gather.8.cloned.1.call-update) | async-done | bytes 6291472 | tf_op jit(solution)/shard_map/all_gather | solution.py:101
  96.8 11.0 convert_multiply_fusion
  107.8 7.8 fusion.163
  116.9 7.8 fusion.161
  129.4 8.3 fusion.196
  137.8 4.7 fusion.194
  146.0 21.0 %fusion.4 = f32[2048,8]{0,1:T(8,128)S(1)} fusion(f32[2048,24]{0,1:T(8,128)} %fusion.165), kind=kCustom, calls=%all-reduce-scatter | all-reduce-scatter fusion | flops 65537 | bytes 262656
  169.2 4.1 fusion.155
  177.3 162.9 %reduce-scatter.8.cloned.1.call-done = f32[2048,384]{1,0:T(8,128)} async-done(((f32[2048,1536]{1,0:T(8,128)}), f32[2048,384]{1,0:T(8,128)}) %reduce-scatter.8.cloned.1.call-update) | async-done | bytes 3145744 | tf_op jit(solution)/shard_map/reduce_scatter | solution.py:116
  340.3 10.0 fusion.154
  360.3 222.5 %while.48 = (s32[]{:T(128)}, f32[1,6,128,64]{2,3,1,0:T(8,128)S(1)}, s32[1]{0:T(128)}, f32[8,1,256,6,64]{2,0,4,3,1:T(8,128)}, f32[8,1,6,128,64]{3,4,2,1,0:T(8,128...) while((s32[]{:T(128)}, f32[1,6,128,64]{2,3,1,0:T(8,128)S(1)}, ...), condition=%wide.region_6.7_spmd.clone, body=%wide.region_3.6_spmd.clone.sunk | while | flops 707698688 | bytes 6478776 | solution.py:77
  373.8 9.9 dynamic_update_slice.78
  401.5 9.9 dynamic_update_slice.78
  429.4 9.9 dynamic_update_slice.78
  457.1 9.9 dynamic_update_slice.78
  485.0 9.8 dynamic_update_slice.78
  512.8 9.9 dynamic_update_slice.78
  540.5 9.8 dynamic_update_slice.78
  568.5 9.8 dynamic_update_slice.78
  582.8 5.0 copy.259
  591.3 5.6 multiply_reduce_fusion.12
  596.9 24.9 %psum.140 = f32[2048]{0:T(1024)S(1)} all-reduce(f32[2048]{0:T(1024)S(1)} %get-tuple-element.971), channel_id=1, replica_groups=mesh['dp'=4,'row'=2,'col'=4] {'row','col'}, use_global_device_ids=true, to_apply=%region_9.10 | all-reduce | flops 2048 | bytes 16384 | tf_op jit(solution)/shard_map/psum | solution.py:159
  621.8 150.9 %reduce-scatter.14.cloned.1.call-done = f32[2048,384]{1,0:T(8,128)} async-done(((f32[2048,1536]{1,0:T(8,128)}), f32[2048,384]{1,0:T(8,128)}) %reduce-scatter.14.cloned.1.call-update) | async-done | bytes 3145744 | tf_op jit(solution)/shard_map/reduce_scatter | solution.py:171
  772.7 4.3 multiply_reduce_fusion.5
  776.9 21.7 %psum.141 = f32[2048]{0:T(1024)S(1)} all-reduce(f32[2048]{0:T(1024)S(1)} %get-tuple-element.864), channel_id=1, replica_groups=mesh['dp'=4,'row'=2,'col'=4] {'row','col'}, use_global_device_ids=true, to_apply=%region_14.15 | all-reduce | flops 2048 | bytes 16384 | tf_op jit(solution)/shard_map/psum | solution.py:174
  798.6 7.4 fusion.133
  809.6 5.0 copy.260
  819.3 491.8 %while.49 = (s32[]{:T(128)}, f32[6]{0:T(128)}, f32[6]{0:T(128)}, f32[1,6,128,64]{2,3,1,0:T(8,128)S(1)}, f32[8,1,256,6,64]{2,0,4,3,1:T(8,128)}, /*index=5*/f32[8,...) while((s32[]{:T(128)}, f32[6]{0:T(128)}, f32[6]{0:T(128)}, ...), condition=%wide.region_29.30_spmd.clone, body=%wide.region_15.29_spmd.clone.sunk | while | flops 1671062528 | bytes 17263068 | solution.py:77
  844.2 8.8 reduce-window.74
  870.1 9.8 dynamic_update_slice.83
  905.6 8.8 reduce-window.74
  931.6 9.8 dynamic_update_slice.83
  967.1 8.8 reduce-window.74
  993.0 9.8 dynamic_update_slice.83
  1028.5 8.8 reduce-window.74
  1054.4 9.8 dynamic_update_slice.83
  1089.9 8.8 reduce-window.74
  1115.8 9.8 dynamic_update_slice.83
  1151.3 8.8 reduce-window.74
  1177.3 9.8 dynamic_update_slice.83
  1212.8 8.8 reduce-window.74
  1238.7 9.8 dynamic_update_slice.83
  1274.2 8.8 reduce-window.74
  1300.1 9.8 dynamic_update_slice.83
  1311.2 4.6 transpose.199
  1319.4 10.8 multiply_reduce_fusion.9
  1335.7 5.5 multiply_reduce_fusion.16
  1344.6 15.9 all-gather.1
  1360.5 170.3 %all-reduce.35 = (bf16[2048,256]{1,0:T(8,128)(2,1)}, f32[4,256]{1,0:T(4,128)}, f32[256]{0:T(256)}) all-reduce(f32[2048,256]{1,0:T(8,128)S(1)} %fusion.142, f32[4,256]{1,0:T(4,128)S(1)} %pad_add_fusion.1, f32[256]{0:T(256)S(1)} %get-tuple-element.873), channel_id=1, replica_groups=mesh['dp'=4,'row'=2,'col'=4] {'row','col'}, use_global_device_ids=true, to_apply=%region_30.31 | all-reduce | flops 525568 | bytes 3155968 | tf_op jit(solution)/shard_map/psum | solution.py:189
  1534.4 8.6 fusion.125
  1543.0 101.9 %all-gather.14.cloned.1.call-done = bf16[2048,1536]{1,0:T(8,128)(2,1)} async-done(((bf16[2048,384]{1,0:T(8,128)(2,1)}), bf16[2048,1536]{1,0:T(8,128)(2,1)}) %all-gather.14.cloned.1.call-update) | async-done | bytes 6291472 | tf_op jit(solution)/shard_map/all_gather | solution.py:194
  1644.9 5.7 fusion.197
  1650.6 4.8 multiply_reduce_fusion.10
  1655.7 104.4 %all-gather.10.cloned.1.call-done = bf16[2048,1536]{1,0:T(8,128)(2,1)} async-done(((bf16[2048,384]{1,0:T(8,128)(2,1)}), bf16[2048,1536]{1,0:T(8,128)(2,1)}) %all-gather.10.cloned.1.call-update) | async-done | bytes 6291472 | tf_op jit(solution)/shard_map/all_gather | solution.py:162
  1760.1 7.9 fusion.195
  1769.2 5.9 fusion.199
  1775.1 7.5 fusion.123
  1782.6 5.6 fusion.159
  1788.2 4.9 fusion.198
  1800.0 4.9 all-reduce.26
  1805.7 11.5 all-reduce.29
  1819.2 9.7 psum.143
  1828.9 20.6 %reduce-scatter.12.cloned.1.call-done = f32[1024,384]{1,0:T(8,128)} async-done(((f32[2048,384]{1,0:T(8,128)}), f32[1024,384]{1,0:T(8,128)}) %reduce-scatter.12.cloned.1.call-update) | async-done | bytes 1572880 | tf_op jit(solution)/shard_map/reduce_scatter | solution.py:163
  1852.9 158.8 %all-reduce.34.cloned.1.call-done = (f32[384,1536]{1,0:T(8,128)}, f32[384,1536]{1,0:T(8,128)}, f32[1536,256]{1,0:T(8,128)}, f32[1536,384]{1,0:T(8,128)}) async-done(((f32[384,1536]{1,0:T(8,128)}, f32[384,1536]{1,0:T(8,128)}, f32[1536,256]{1,0:T(8,128)}, f32[1536,384]{1,0:T(8,128)}), (f32[384,1536]{1,0:T(8,128)}, f32[384,1536]{1,0:T(8,128)}, f32[1536,256]{1,0:T(8,128)}, ...) | async-done | bytes 8650768 | tf_op jit(solution)/shard_map/psum | solution.py:234
  (1253 shorter events, 542.3 us)
Async XLA Ops:
  7.2 100.6 %copy-start = (bf16[384,1536]{1,0:T(8,128)(2,1)S(1)}, bf16[384,1536]{1,0:T(8,128)(2,1)}, u32[]{:S(2)}) copy-start(bf16[384,1536]{1,0:T(8,128)(2,1)} %param.25) | copy-start | bytes 3538948
  7.2 85.5 %all-gather.8.cloned.1.call-start = ((), (), s32[]{:S(2)}) async-start(), calls=%async_computation.5 | async-start | bytes 9437184 | tf_op jit(solution)/shard_map/all_gather | solution.py:101
  7.9 121.4 %all-gather.12.cloned.1.call-start = ((), (), s32[]{:S(2)}) async-start(), calls=%async_computation.10 | async-start | bytes 2359296 | tf_op jit(solution)/shard_map/all_gather | solution.py:168
  8.7 331.5 %reduce-scatter.8.cloned.1.call-start = ((), (), s32[]{:S(2)}) async-start(), calls=%async_computation.6 | async-start | bytes 15728640 | tf_op jit(solution)/shard_map/reduce_scatter | solution.py:116
  8.7 88.0 %copy-start.59 = (f32[1536]{0:T(1024)S(1)}, f32[1536]{0:T(1024)}, u32[]{:S(2)}) copy-start(f32[1536]{0:T(1024)} %param.23) | copy-start | bytes 18436
  115.6 475.7 %reduce-scatter.10.cloned.1.call-start = ((), (), s32[]{:S(2)}) async-start(), calls=%async_computation.7 | async-start | bytes 15728640 | tf_op jit(solution)/shard_map/reduce_scatter | solution.py:115
  124.7 648.0 %reduce-scatter.14.cloned.1.call-start = ((), (), s32[]{:S(2)}) async-start(), calls=%async_computation.11 | async-start | bytes 15728640 | tf_op jit(solution)/shard_map/reduce_scatter | solution.py:171
  127.2 213.0 %copy-start.51 = (f32[384]{0:T(512)}, f32[384]{0:T(512)S(1)}, u32[]{:S(2)}) copy-start(f32[384]{0:T(512)S(1)} %get-tuple-element.879) | copy-start | bytes 4612
  128.2 212.0 %copy-start.39 = (pred[2048]{0:T(1024)(128)(4,1)}, pred[2048]{0:T(1024)(128)(4,1)S(1)}, u32[]{:S(2)}) copy-start(pred[2048]{0:T(1024)(128)(4,1)S(1)} %get-tuple-element.875) | copy-start | bytes 6148
  128.2 212.0 %copy-start.41 = (pred[2048]{0:T(1024)(128)(4,1)}, pred[2048]{0:T(1024)(128)(4,1)S(1)}, u32[]{:S(2)}) copy-start(pred[2048]{0:T(1024)(128)(4,1)S(1)} %get-tuple-element.876) | copy-start | bytes 6148
  128.2 212.0 %copy-start.43 = (pred[2048]{0:T(1024)(128)(4,1)}, pred[2048]{0:T(1024)(128)(4,1)S(1)}, u32[]{:S(2)}) copy-start(pred[2048]{0:T(1024)(128)(4,1)S(1)} %get-tuple-element.877) | copy-start | bytes 6148
  137.7 1396.7 %all-gather.16.cloned.1.call-start = ((), (), s32[]{:S(2)}) async-start(), calls=%async_computation.14 | async-start | bytes 7864320 | tf_op jit(solution)/shard_map/all_gather | solution.py:195
  142.5 30.8 %copy-start.1 = (f32[2048,256]{1,0:T(8,128)}, f32[2048,256]{1,0:T(8,128)S(1)}, u32[]{:S(2)}) copy-start(f32[2048,256]{1,0:T(8,128)S(1)} %fusion.194) | copy-start | bytes 6291460
  167.1 8.4 collective-permute-start
  173.3 166.9 %copy-start.53 = (f32[384]{0:T(512)S(1)}, f32[384]{0:T(512)}, u32[]{:S(2)}) copy-start(f32[384]{0:T(512)} %get-tuple-element.880) | copy-start | bytes 4612
  173.3 166.9 %copy-start.55 = (f32[384]{0:T(512)S(1)}, f32[384]{0:T(512)}, u32[]{:S(2)}) copy-start(f32[384]{0:T(512)} %get-tuple-element.881) | copy-start | bytes 4612
  173.3 166.9 %copy-start.57 = (f32[384]{0:T(512)S(1)}, f32[384]{0:T(512)}, u32[]{:S(2)}) copy-start(f32[384]{0:T(512)} %get-tuple-element.878) | copy-start | bytes 4612
  173.3 166.9 %copy-start.81 = (f32[384]{0:T(512)S(1)}, f32[384]{0:T(512)}, u32[]{:S(2)}) copy-start(f32[384]{0:T(512)} %param.29) | copy-start | bytes 4612
  176.5 163.7 %copy-start.26 = (f32[2048,14]{0,1:T(8,128)}, f32[2048,14]{0,1:T(8,128)S(1)}, u32[]{:S(2)}) copy-start(f32[2048,14]{0,1:T(8,128)S(1)} %concatenate.4) | copy-start | bytes 344068
  591.3 181.4 %copy-start.74 = (f32[384]{0:T(512)S(1)}, f32[384]{0:T(512)}, u32[]{:S(2)}) copy-start(f32[384]{0:T(512)} %param.35) | copy-start | bytes 4612
  865.2 14.7 copy-start.33
  865.3 14.7 copy-start.14
  867.2 13.4 copy-start.47
  867.2 13.4 copy-start.48
  926.7 14.7 copy-start.33
  926.7 14.7 copy-start.14
  928.7 13.4 copy-start.47
  928.7 13.4 copy-start.48
  988.1 14.7 copy-start.33
  988.1 14.7 copy-start.14
  990.1 13.4 copy-start.47
  990.1 13.4 copy-start.48
  1049.5 14.7 copy-start.33
  1049.5 14.7 copy-start.14
  1051.5 13.4 copy-start.47
  1051.5 13.4 copy-start.48
  1111.0 14.7 copy-start.33
  1111.0 14.7 copy-start.14
  1113.0 13.4 copy-start.47
  1113.0 13.4 copy-start.48
  1172.4 14.7 copy-start.33
  1172.4 14.7 copy-start.14
  1174.4 13.4 copy-start.47
  1174.4 13.4 copy-start.48
  1233.8 14.7 copy-start.33
  1233.8 14.7 copy-start.14
  1235.8 13.4 copy-start.47
  1235.8 13.4 copy-start.48
  1295.2 14.7 copy-start.33
  1295.2 14.7 copy-start.14
  1297.2 13.4 copy-start.47
  1297.2 13.4 copy-start.48
  1334.1 310.7 %all-gather.14.cloned.1.call-start = ((), (), s32[]{:S(2)}) async-start(), calls=%async_computation.12 | async-start | bytes 7864320 | tf_op jit(solution)/shard_map/all_gather | solution.py:194
  1334.9 425.2 %all-gather.10.cloned.1.call-start = ((), (), s32[]{:S(2)}) async-start(), calls=%async_computation.8 | async-start | bytes 7864320 | tf_op jit(solution)/shard_map/all_gather | solution.py:162
  1335.6 481.5 %reduce-scatter.16.cloned.1.call-start = ((), (), s32[]{:S(2)}) async-start(), calls=%async_computation.13 | async-start | bytes 4718592 | tf_op jit(solution)/shard_map/reduce_scatter | solution.py:224
  1360.5 290.1 %copy-start.23 = (bf16[24,2048]{1,0:T(8,128)(2,1)}, bf16[24,2048]{1,0:T(8,128)(2,1)S(1)}, u32[]{:S(2)}) copy-start(bf16[24,2048]{1,0:T(8,128)(2,1)S(1)} %reshape.1164) | copy-start | bytes 294916
  1534.4 110.5 %copy-start.19 = (bf16[384,1536]{1,0:T(8,128)(2,1)S(1)}, bf16[384,1536]{1,0:T(8,128)(2,1)}, u32[]{:S(2)}) copy-start(bf16[384,1536]{1,0:T(8,128)(2,1)} %param.24) | copy-start | bytes 3538948
  1543.0 107.6 %copy-start.46 = (bf16[384,24]{0,1:T(8,128)(2,1)S(1)}, bf16[384,24]{0,1:T(8,128)(2,1)}, u32[]{:S(2)}) copy-start(bf16[384,24]{0,1:T(8,128)(2,1)} %param.26) | copy-start | bytes 55300
  1655.4 104.7 %copy-start.21 = (bf16[1536,384]{1,0:T(8,128)(2,1)S(1)}, bf16[1536,384]{1,0:T(8,128)(2,1)}, u32[]{:S(2)}) copy-start(bf16[1536,384]{1,0:T(8,128)(2,1)} %param.36) | copy-start | bytes 3538948
  1655.4 194.1 %reduce-scatter.12.cloned.1.call-start = ((), (), s32[]{:S(2)}) async-start(), calls=%async_computation.9 | async-start | bytes 4718592 | tf_op jit(solution)/shard_map/reduce_scatter | solution.py:163
  1768.0 243.7 %all-reduce.34.cloned.1.call-start = ((), (), s32[]{:S(2)}) async-start(), calls=%async_computation.15 | async-start | bytes 17301504 | tf_op jit(solution)/shard_map/psum | solution.py:234
  1769.2 13.4 slice-start
  1794.8 54.7 %copy-start.8 = (bf16[1024,384]{1,0:T(8,128)(2,1)S(1)}, bf16[1024,384]{1,0:T(8,128)(2,1)}, u32[]{:S(2)}) copy-start(bf16[1024,384]{1,0:T(8,128)(2,1)} %param.37) | copy-start | bytes 2359300
  1817.2 32.3 %copy-start.4 = (f32[1024,384]{1,0:T(8,128)S(1)}, f32[1024,384]{1,0:T(8,128)}, u32[]{:S(2)}) copy-start(f32[1024,384]{1,0:T(8,128)} %reduce-scatter.16.cloned.1.call-done) | copy-start | bytes 4718596
  (193 other events, 1018.5 us)
Sparse Core Ops, SparseCore 0:
  9.6 83.0 all-gather.7
  94.2 27.2 all-gather.11
  123.8 216.3 reduce-scatter.7
  342.4 213.8 reduce-scatter.9
  558.5 214.1 reduce-scatter.13
  1334.2 194.9 all-gather.15
  1531.3 113.4 all-gather.13
  1646.4 113.5 all-gather.9
  1762.3 41.5 reduce-scatter.15
  1806.1 43.3 reduce-scatter.11
  1853.4 158.1 all-reduce.33
where the time goes:
time: 2050 us; the launch traced here: 2030 us
  waiting for transfers between devices  786 us (38%)
  local copies, waits for them, and re-layouts  413 us (20%)
  blocking collectives  280 us (14%)
  other arithmetic  266 us (13%)
  matrix products  239 us (12%)
  loops' own time  25 us (1%)
    dynamic_update_slice x56, local copies, waits for them, and re-layouts, span_scan(): _, outputs = lax.scan(jax.checkpoint(advance), start, pieces)  181 us
    psum x1, blocking collectives, per_device(): lax.psum((states_share, taps_share, bias_share), ('row', 'col'))  170 us
    reduce_scatter x1, waiting for transfers between devices, per_device(): lax.psum_scatter(parts[1], 'col', scatter_dimension=1, tiled=True)  163 us
    psum x1, waiting for transfers between devices, per_device(): lax.psum((gain_rows[0], grad_proj_gate, grad_proj_inner, grad_proj_step,...  159 us
    reduce_scatter x1, waiting for transfers between devices, per_device(): lax.psum_scatter(back_parts, 'col', scatter_dimension=1, tiled=True)  151 us
    another operation x74, other arithmetic  131 us
    all_gather x1, waiting for transfers between devices, per_device(): gate_cols = lax.all_gather(gated, 'col', axis=1, tiled=True)  104 us
    all_gather x1, waiting for transfers between devices, per_device(): lax.all_gather(grad_gate_pre.astype(jnp.bfloat16), 'col', axis=1, tiled=T...  102 us
  transfers between devices with their start and end apart: 12, of which 7 were waited for; matrix products, arithmetic and copies ran while one was open for 20% of the time, Pallas kernels for 0%

commit v1 on v0

v1 whole, which is shorter than its diff:
```python
import functools

import jax
import jax.numpy as jnp
from jax import lax
from jax.experimental import pallas as pl
from jax.experimental.pallas import tpu as pltpu
from jax.sharding import PartitionSpec as P

SPAN = 256
HEAD = 64
epsilon = 1e-05
LOG2E = 1.4426950408889634
f32 = jnp.float32
bf16 = jnp.bfloat16
ANY = pl.ANY


def mm(a, b):
    return lax.dot_general(a, b, (((1,), (0,)), ((), ())), preferred_element_type=f32)


def mm_nt(a, b):
    return lax.dot_general(a, b, (((1,), (1,)), ((), ())), preferred_element_type=f32)


def split(v, terms):
    parts = []
    for _ in range(terms):
        part = v.astype(bf16)
        parts.append(part)
        v = v - part.astype(f32)
    return parts


def mm_split(a, exact, terms=2):
    return sum(mm(part, exact) for part in split(a, terms))


def split_mm(exact, b, terms=3):
    return sum(mm(exact, part) for part in split(b, terms))


def spread_matrix(channels):
    heads = lax.broadcasted_iota(jnp.int32, (128, channels), 0)
    cols = lax.broadcasted_iota(jnp.int32, (128, channels), 1)
    low = heads * HEAD
    return jnp.where((cols >= low) & (cols < low + HEAD), 1.0, 0.0).astype(bf16)


def gather_matrix(channels):
    heads = lax.broadcasted_iota(jnp.int32, (channels, 128), 1)
    rows = lax.broadcasted_iota(jnp.int32, (channels, 128), 0)
    low = heads * HEAD
    return jnp.where((rows >= low) & (rows < low + HEAD), 1.0, 0.0).astype(bf16)


def lower_ones():
    rows = lax.broadcasted_iota(jnp.int32, (SPAN, SPAN), 0)
    cols = lax.broadcasted_iota(jnp.int32, (SPAN, SPAN), 1)
    return jnp.where(rows >= cols, 1.0, 0.0).astype(bf16)


def upper_ones():
    rows = lax.broadcasted_iota(jnp.int32, (SPAN, SPAN), 0)
    cols = lax.broadcasted_iota(jnp.int32, (SPAN, SPAN), 1)
    return jnp.where(rows <= cols, 1.0, 0.0).astype(bf16)


def sigmoid(v):
    return 1.0 / (1.0 + jnp.exp(-v))


def half_masks():
    lane = lax.broadcasted_iota(jnp.int32, (SPAN, 128), 1)
    return lane < HEAD


def rms_rows(tok, gain):
    wide = tok.astype(f32)
    inverse = lax.rsqrt(jnp.mean(wide * wide, -1, keepdims=True) + epsilon)
    return (wide * inverse * gain).astype(bf16)


def entry_kernel(
    tok, halo, ngain, w_inner, w_states, w_step, par, spar, head, meta,
    normed_o, pre_o, spre_o, sd_o, ssd_o, x_o, wr_o, step_o, r_o, sig_o, fresh_o, end_o,
    hpre_o, hspre_o,
    xbuf, sbuf, mem,
):
    at = pl.program_id(0)
    channels = w_inner.shape[1]
    gain = ngain[...]

    @pl.when(at == 0)
    def _():
        hn = rms_rows(halo[...], gain)
        hp = mm(hn, w_inner[...])[8:16]
        hs = mm(hn, w_states[...])[8:16]
        xbuf[0:8, :] = hp
        sbuf[0:8, :] = hs
        hpre_o[...] = hp
        hspre_o[...] = hs
        mem[...] = jnp.zeros_like(mem)

    @pl.when(at > 0)
    def _():
        xbuf[0:8, :] = xbuf[SPAN:SPAN + 8, :]
        sbuf[0:8, :] = sbuf[SPAN:SPAN + 8, :]

    normed = rms_rows(tok[...], gain)
    normed_o[...] = normed
    x_pre = mm(normed, w_inner[...])
    s_pre = mm(normed, w_states[...])
    xbuf[8:SPAN + 8, :] = x_pre
    sbuf[8:SPAN + 8, :] = s_pre
    pre_o[...] = x_pre.astype(bf16)
    spre_o[...] = s_pre.astype(bf16)

    def conv_silu(buf, here, taps):
        v = taps[4:5, :] + taps[0:1, :] * here
        for k in range(1, 4):
            v = v + meta[:, k:k + 1] * (taps[k:k + 1, :] * buf[8 - k:8 - k + SPAN, :])
        sg = sigmoid(v)
        return v * sg, sg * (1.0 + v * (1.0 - sg))

    act, slope = conv_silu(xbuf, x_pre, par)
    x_low = act.astype(bf16)
    x_o[...] = x_low
    sd_o[...] = slope.astype(bf16)
    sact, sslope = conv_silu(sbuf, s_pre, spar)
    wr = sact.astype(bf16)
    wr_o[...] = wr
    ssd_o[...] = sslope.astype(bf16)

    raw = mm(normed, w_step[...]) + head[0:1, :]
    step = jnp.maximum(raw, 0.0) + jnp.log1p(jnp.exp(-jnp.abs(raw)))
    sig_o[...] = sigmoid(raw)
    step_o[...] = step
    r = split_mm(lower_ones(), step * head[1:2, :])
    r_o[...] = r
    last = r[SPAN - 1:SPAN, :]
    to_end = jnp.exp2(jnp.minimum(last - r, 0.0)) * meta[:, 5:6]
    spread = spread_matrix(channels)
    coef = mm_split(to_end * step, spread)
    w_t = jnp.transpose(wr[:, 0:128].astype(f32)).astype(bf16)
    fresh = mm(w_t, (coef * x_low.astype(f32)).astype(bf16))
    fresh_o[...] = fresh[None]
    keep = mm_split(jnp.broadcast_to(jnp.exp2(last) * meta[0:1, 6:7], (8, 128)), spread)[0:1]
    mem[...] = keep * mem[...] + fresh
    end_o[...] = mem[...]


def scan_kernel(
    x, wr, r_ref, step_ref, meta, docrow, fresh, state_in, head, par, gate, ggated,
    y_o, sums_o, sprev_o,
    mem, ybuf,
):
    at = pl.program_id(0)
    channels = x.shape[1]

    @pl.when(at == 0)
    def _():
        mem[...] = state_in[...]

    spread = spread_matrix(channels)
    w_low = wr[:, 0:128]
    r_low = wr[:, 128:256]
    r = r_ref[...]
    r_t = jnp.transpose(r)
    rows = lax.broadcasted_iota(jnp.int32, (SPAN, SPAN), 0)
    cols = lax.broadcasted_iota(jnp.int32, (SPAN, SPAN), 1)
    allowed = (rows >= cols) & (meta[:, 0:1] == docrow[...])
    scores = jnp.where(allowed, mm_nt(r_low, w_low), 0.0)
    wide = x[...].astype(f32)
    xd = (mm_split(step_ref[...], spread) * wide).astype(bf16)
    sprev = mem[...].astype(bf16)
    sprev_o[...] = sprev[None]
    linked = jnp.exp2(r) * meta[:, 4:5]
    carried = mm(r_low, sprev) * mm_split(linked, spread)
    skip = mm_split(jnp.broadcast_to(head[2:3, :], (8, 128)), spread)[0:1]
    ybuf[...] = carried + skip * wide
    first = half_masks()
    for pair in range(channels // 128):
        lanes = slice(pair * 128, pair * 128 + 128)
        xp = xd[:, lanes]
        total = ybuf[:, lanes]
        for half in range(2):
            h = 2 * pair + half
            decay = jnp.exp2(jnp.minimum(r[:, h:h + 1] - r_t[h:h + 1, :], 0.0))
            mixing = (scores * decay).astype(bf16)
            own = jnp.where(first if half == 0 else ~first, xp, jnp.zeros_like(xp))
            total = total + mm(mixing, own)
        ybuf[:, lanes] = total
    last = r[SPAN - 1:SPAN, :]
    keep = mm_split(jnp.broadcast_to(jnp.exp2(last) * meta[0:1, 6:7], (8, 128)), spread)[0:1]
    mem[...] = keep * mem[...] + fresh[0]
    y = ybuf[...]
    y_o[...] = y
    g = gate[...]
    mixed = y * (g * sigmoid(g))
    ones = jnp.ones((8, channels), bf16)
    sq = sum(mm_nt(ones, part) for part in split(mixed * mixed, 2))
    pr = sum(mm_nt(ones, part) for part in split(mixed * (par[5:6, :] * ggated[...]), 2))
    row = lax.broadcasted_iota(jnp.int32, (8, SPAN), 0)
    sums_o[...] = jnp.where(row == 0, sq, jnp.where(row == 1, pr, 0.0))


def turn_kernel(
    inner, y_ref, gate, ggated, sums, x, wr, r_ref, meta, head, par,
    gated_o, ggate_o, gy_o, dr_o, dsf_o, dsout_o, acc_o,
    dmem,
):
    at = pl.program_id(0)
    channels = x.shape[1]

    @pl.when(at == 0)
    def _():
        dmem[...] = jnp.zeros_like(dmem)
        acc_o[...] = jnp.zeros_like(acc_o)

    spread = spread_matrix(channels)
    totals = jnp.transpose(sums[...])
    scale = lax.rsqrt(totals[:, 0:1] / inner + epsilon)
    cross = totals[:, 1:2] / inner
    y = y_ref[...]
    g = gate[...]
    sg = sigmoid(g)
    sl = g * sg
    mixed = y * sl
    gg = ggated[...]
    gain = par[5:6, :]
    normal = mixed * scale
    gated_o[...] = (normal * gain).astype(bf16)
    g_mixed = scale * (gain * gg - normal * (scale * cross))
    ggate_o[...] = (g_mixed * y * (sg * (1.0 + g * (1.0 - sg)))).astype(bf16)
    gy = (g_mixed * sl).astype(bf16)
    gy_o[...] = gy
    gyw = gy.astype(f32)
    wide = x[...].astype(f32)
    skip = mm_split(jnp.broadcast_to(head[2:3, :], (8, 128)), spread)[0:1]
    dr_o[...] = mm_split(gyw * (y - skip * wide), gather_matrix(channels))
    row = lax.broadcasted_iota(jnp.int32, (8, channels), 0)
    ggain = jnp.sum(gg * normal, 0, keepdims=True)
    gskip = jnp.sum(gyw * wide, 0, keepdims=True)
    acc_o[...] += jnp.where(row == 0, ggain, jnp.where(row == 1, gskip, 0.0))
    r = r_ref[...]
    linked = mm_split(jnp.exp2(r) * meta[:, 4:5], spread)
    r_t = jnp.transpose(wr[:, 128:256].astype(f32)).astype(bf16)
    dfresh = mm(r_t, (linked * gyw).astype(bf16))
    dsf_o[...] = dfresh[None]
    last = r[SPAN - 1:SPAN, :]
    keep = mm_split(jnp.broadcast_to(jnp.exp2(last) * meta[0:1, 6:7], (8, 128)), spread)[0:1]
    dmem[...] = keep * dmem[...] + dfresh
    dsout_o[...] = dmem[...]


def back_kernel(
    x, wr, gy_ref, r_ref, step_ref, sig_ref, meta, docrow, dr_ref, sprev, dsf, ds_in,
    pre, spre, sd, ssd, hpre, hspre, hmeta, head, par, spar,
    gx_o, gs_o, gz_o, hx_o, hs_o, accx_o, accs_o, acch_o,
    dmem, gbuf, hbuf, dxd,
):
    at = pl.program_id(0)
    channels = x.shape[1]

    @pl.when(at == 0)
    def _():
        dmem[...] = ds_in[...]
        accx_o[...] = jnp.zeros_like(accx_o)
        accs_o[...] = jnp.zeros_like(accs_o)
        acch_o[...] = jnp.zeros_like(acch_o)
        gbuf[...] = jnp.zeros_like(gbuf)
        hbuf[...] = jnp.zeros_like(hbuf)

    @pl.when(at > 0)
    def _():
        gbuf[SPAN + 8:SPAN + 16, :] = gbuf[8:16, :]
        hbuf[SPAN + 8:SPAN + 16, :] = hbuf[8:16, :]

    spread = spread_matrix(channels)
    gather = gather_matrix(channels)
    w_low = wr[:, 0:128]
    r_low = wr[:, 128:256]
    r = r_ref[...]
    r_t = jnp.transpose(r)
    step = step_ref[...]
    last = r[SPAN - 1:SPAN, :]
    rows = lax.broadcasted_iota(jnp.int32, (SPAN, SPAN), 0)
    cols = lax.broadcasted_iota(jnp.int32, (SPAN, SPAN), 1)
    allowed = (rows <= cols) & (meta[:, 0:1] == docrow[...])
    scores = jnp.where(allowed, mm_nt(w_low, r_low), 0.0)
    wide = x[...].astype(f32)
    step_wide = mm_split(step, spread)
    xd = (step_wide * wide).astype(bf16)
    gy = gy_ref[...]
    gyw = gy.astype(f32)
    ds = dmem[...]
    ds_low = ds.astype(bf16)
    te = mm_split(jnp.exp2(jnp.minimum(last - r, 0.0)) * meta[:, 5:6], spread)
    linked = mm_split(jnp.exp2(r) * meta[:, 4:5], spread)
    from_end = te * mm(w_low, ds_low)
    dxd[...] = from_end
    keep = mm_split(jnp.broadcast_to(jnp.exp2(last) * meta[0:1, 6:7], (8, 128)), spread)[0:1]
    ending = jnp.sum(xd.astype(f32) * from_end, 0, keepdims=True) + keep * jnp.sum(
        sprev[0].astype(f32) * ds, 0, keepdims=True
    )
    first = half_masks()
    dscores = jnp.zeros((SPAN, SPAN), f32)
    for pair in range(channels // 128):
        lanes = slice(pair * 128, pair * 128 + 128)
        xp = xd[:, lanes]
        gp = gy[:, lanes]
        total = dxd[:, lanes]
        for half in range(2):
            h = 2 * pair + half
            own = first if half == 0 else ~first
            decay = jnp.exp2(jnp.minimum(r_t[h:h + 1, :] - r[:, h:h + 1], 0.0))
            mixing = (scores * decay).astype(bf16)
            gown = jnp.where(own, gp, jnp.zeros_like(gp))
            total = total + mm(mixing, gown)
            dscores = dscores + mm_nt(xp, gown) * decay
        dxd[:, lanes] = total
    dscores = jnp.where(allowed, dscores, 0.0)
    dlow = dscores.astype(bf16)
    xdw = xd.astype(f32)
    g_write = mm(dlow, r_low) + mm_nt((te * xdw).astype(bf16), ds_low)
    g_read = mm(jnp.transpose(dscores).astype(bf16), w_low) + mm_nt(
        (linked * gyw).astype(bf16), sprev[0]
    )
    skip = mm_split(jnp.broadcast_to(head[2:3, :], (8, 128)), spread)[0:1]
    full = dxd[...]
    g_x = step_wide * full + skip * gyw
    dr = dr_ref[...] - mm_split(xdw * full, gather)
    at_end = mm_split(jnp.broadcast_to(ending, (8, channels)), gather, 3)[0:1]
    tail = lax.broadcasted_iota(jnp.int32, (SPAN, 128), 0) == SPAN - 1
    dr = dr + jnp.where(tail, at_end, 0.0)
    da = split_mm(upper_ones(), dr)
    dstep = mm_split(wide * full, gather) + head[3:4, :] * da
    gz = dstep * sig_ref[...]
    gz_o[...] = gz.astype(bf16)
    row = lax.broadcasted_iota(jnp.int32, (8, 128), 0)
    gbias = jnp.sum(gz, 0, keepdims=True)
    grate = jnp.sum(da * step, 0, keepdims=True)
    acch_o[...] += jnp.where(row == 0, gbias, jnp.where(row == 1, grate, 0.0))
    dmem[...] = keep * ds + dsf[0]

    def conv_back(buf, gv, base, taps, acc, halo_pre, out, halo_out):
        buf[8:SPAN + 8, :] = gv
        width = gv.shape[1]
        total = taps[0:1, :] * gv
        sums = [jnp.sum(gv * base, 0, keepdims=True)]
        halo = jnp.zeros((8, width), f32)
        hsum = []
        for k in range(1, 4):
            moved = meta[:, 7 + k:8 + k] * buf[8 + k:8 + k + SPAN, :]
            total = total + taps[k:k + 1, :] * moved
            sums.append(jnp.sum(moved * base, 0, keepdims=True))
            hmoved = hmeta[:, 7 + k:8 + k] * buf[k:8 + k, :]
            halo = halo + taps[k:k + 1, :] * hmoved
            hsum.append(jnp.sum(hmoved * halo_pre, 0, keepdims=True))
        sums.append(jnp.sum(gv, 0, keepdims=True))
        out[...] = total.astype(bf16)
        halo_out[...] = halo
        rows8 = lax.broadcasted_iota(jnp.int32, (8, width), 0)
        final = jnp.where(at == pl.num_programs(0) - 1, 1.0, 0.0)
        add = jnp.zeros((8, width), f32)
        for i, s in enumerate(sums):
            if 1 <= i <= 3:
                s = s + final * hsum[i - 1]
            add = add + jnp.where(rows8 == i, s, 0.0)
        acc[...] += add

    conv_back(gbuf, g_x * sd[...].astype(f32), pre[...].astype(f32), par, accx_o,
              hpre[...], gx_o, hx_o)
    g_wr = jnp.concatenate([g_write, g_read], 1)
    conv_back(hbuf, g_wr * ssd[...].astype(f32), spre[...].astype(f32), spar, accs_o,
              hspre[...], gs_o, hs_o)


PARAMS = dict(vmem_limit_bytes=56 * 1024 * 1024)


def whole(shape):
    return pl.BlockSpec(shape, lambda i: (0,) * len(shape))


def by_rows(cols, count=None):
    if count is None:
        return pl.BlockSpec((SPAN, cols), lambda i: (i, 0))
    return pl.BlockSpec((SPAN, cols), lambda i: (count - 1 - i, 0))


def swap(values, axis):
    return lax.ppermute(values, axis, [(0, 1), (1, 0)])


def per_device(
    tokens_in, segment_ids, norm_gain, proj_gate, proj_inner, proj_step, proj_states,
    conv_inner, conv_inner_bias, conv_states, conv_states_bias, step_bias, decay_log,
    skip_gain, gate_gain, proj_out, cotangent,
):
    tokens, width = tokens_in.shape
    blocks = tokens // SPAN
    row = lax.axis_index("row")
    col = lax.axis_index("col")
    cols = lax.axis_size("col")
    own_ch = conv_inner.shape[1]
    own_heads = step_bias.shape[0]
    channels = 2 * own_ch
    inner_all = channels * cols
    col_width = width // cols

    def fetch_columns(weight):
        moved = lax.all_to_all(weight, "col", 1, 0, tiled=True)
        return lax.all_gather(moved, "row", axis=1, tiled=True)

    halo = lax.ppermute(tokens_in[-16:], "row", [(0, 1)])
    w_inner = fetch_columns(proj_inner)
    step_all = lax.all_gather(
        lax.all_gather(proj_step, "col", axis=0, tiled=True), "row", axis=1, tiled=True
    )
    w_step = step_all.reshape(width, 2, cols, own_heads)
    w_step = lax.dynamic_index_in_dim(w_step, col, 2, keepdims=False).reshape(width, 2 * own_heads)
    w_step = jnp.pad(w_step, ((0, 0), (0, 128 - 2 * own_heads)))
    w_gate = fetch_columns(proj_gate)
    w_out = lax.all_gather(
        lax.all_to_all(proj_out, "col", 0, 1, tiled=True), "row", axis=0, tiled=True
    )
    cot_all = lax.all_gather(cotangent, "col", axis=1, tiled=True)

    heads_own = jnp.stack([step_bias, decay_log, skip_gain])
    own = jnp.concatenate(
        [
            conv_inner,
            conv_inner_bias[None],
            gate_gain[None],
            jnp.pad(heads_own.reshape(1, -1), ((0, 0), (0, own_ch - 3 * own_heads))),
            jnp.zeros((1, own_ch), f32),
        ],
        0,
    )
    both = lax.all_gather(own, "row", axis=0)
    par = jnp.concatenate([both[0], both[1]], 1)
    hp = jnp.concatenate(
        [both[i, 6, : 3 * own_heads].reshape(3, own_heads) for i in range(2)], 1
    )
    rate = -jnp.exp(hp[1])
    head = jnp.pad(
        jnp.stack([hp[0], rate * LOG2E, hp[2], rate]), ((0, 4), (0, 128 - 2 * own_heads))
    )
    spar = jnp.concatenate([conv_states, conv_states_bias[None], jnp.zeros((3, 256), f32)], 0)

    docs = jnp.pad(segment_ids[0].astype(f32), (8, 8), constant_values=-1.0)
    docs = lax.dynamic_slice_in_dim(docs, row * tokens, tokens + 16, 0)
    here = docs[8:8 + tokens]
    spans = here.reshape(blocks, SPAN)
    before = jnp.concatenate([docs[7:8], spans[:-1, -1]])
    after = spans[:, -1]

    def flat(cond):
        return jnp.broadcast_to(cond, (blocks, SPAN)).reshape(tokens)

    def forward_same(start, count):
        own_docs = docs[start:start + count]
        return [own_docs == docs[start + k:start + k + count] for k in range(1, 4)]

    meta = jnp.stack(
        [here]
        + [(here == docs[8 - k:8 - k + tokens]) for k in range(1, 4)]
        + [
            flat(spans == before[:, None]),
            flat(spans == after[:, None]),
            flat((before == after)[:, None]),
            jnp.zeros_like(here),
        ]
        + forward_same(8, tokens)
        + [jnp.zeros_like(here)] * 5,
        1,
    ).astype(f32)
    hmeta = jnp.stack(
        [jnp.zeros((8,), f32)] * 8
        + forward_same(0, 8)
        + [jnp.zeros((8,), f32)] * 5,
        1,
    ).astype(f32)
    docrow = here[None, :]

    sds = jax.ShapeDtypeStruct
    (
        normed, pre, spre, sd, ssd, x_low, wr, step, r, sig, fresh, end, hpre, hspre,
    ) = pl.pallas_call(
        entry_kernel,
        grid=(blocks,),
        in_specs=[
            by_rows(width), whole((16, width)), whole((1, width)), whole((width, channels)),
            whole((width, 256)), whole((width, 128)), whole((8, channels)), whole((8, 256)),
            whole((8, 128)), by_rows(16),
        ],
        out_specs=[
            by_rows(width), by_rows(channels), by_rows(256), by_rows(channels), by_rows(256),
            by_rows(channels), by_rows(256), by_rows(128), by_rows(128), by_rows(128),
            pl.BlockSpec((1, 128, channels), lambda i: (i, 0, 0)), whole((128, channels)),
            whole((8, channels)), whole((8, 256)),
        ],
        out_shape=[
            sds((tokens, width), bf16), sds((tokens, channels), bf16), sds((tokens, 256), bf16),
            sds((tokens, channels), bf16), sds((tokens, 256), bf16),
            sds((tokens, channels), bf16), sds((tokens, 256), bf16),
            sds((tokens, 128), f32), sds((tokens, 128), f32), sds((tokens, 128), f32),
            sds((blocks, 128, channels), f32), sds((128, channels), f32),
            sds((8, channels), f32), sds((8, 256), f32),
        ],
        scratch_shapes=[
            pltpu.VMEM((SPAN + 8, channels), f32),
            pltpu.VMEM((SPAN + 8, 256), f32),
            pltpu.VMEM((128, channels), f32),
        ],
        compiler_params=pltpu.CompilerParams(**PARAMS),
        name="entry",
    )(tokens_in, halo, norm_gain[None], w_inner, proj_states, w_step, par, spar, head, meta)

    state_in = lax.ppermute(end, "row", [(0, 1)])
    gate = mm(normed, w_gate)
    ggated = mm_nt(cot_all, w_out)

    y, sums, sprev = pl.pallas_call(
        scan_kernel,
        grid=(blocks,),
        in_specs=[
            by_rows(channels), by_rows(256), by_rows(128), by_rows(128), by_rows(16),
            pl.BlockSpec((1, SPAN), lambda i: (0, i)),
            pl.BlockSpec((1, 128, channels), lambda i: (i, 0, 0)), whole((128, channels)),
            whole((8, 128)), whole((8, channels)), by_rows(channels), by_rows(channels),
        ],
        out_specs=[
            by_rows(channels), pl.BlockSpec((8, SPAN), lambda i: (0, i)),
            pl.BlockSpec((1, 128, channels), lambda i: (i, 0, 0)),
        ],
        out_shape=[
            sds((tokens, channels), f32), sds((8, tokens), f32),
            sds((blocks, 128, channels), bf16),
        ],
        scratch_shapes=[pltpu.VMEM((128, channels), f32), pltpu.VMEM((SPAN, channels), f32)],
        compiler_params=pltpu.CompilerParams(**PARAMS),
        name="scan",
    )(x_low, wr, r, step, meta, docrow, fresh, state_in, head, par, gate, ggated)

    sums = lax.psum(sums, "col")

    back3 = pl.BlockSpec((1, 128, channels), lambda i: (blocks - 1 - i, 0, 0))
    gated, g_gate, gy, dr, dsf, dsout, acc1 = pl.pallas_call(
        functools.partial(turn_kernel, float(inner_all)),
        grid=(blocks,),
        in_specs=[
            by_rows(channels, blocks), by_rows(channels, blocks), by_rows(channels, blocks),
            pl.BlockSpec((8, SPAN), lambda i: (0, blocks - 1 - i)),
            by_rows(channels, blocks), by_rows(256, blocks), by_rows(128, blocks),
            by_rows(16, blocks), whole((8, 128)), whole((8, channels)),
        ],
        out_specs=[
            by_rows(channels, blocks), by_rows(channels, blocks), by_rows(channels, blocks),
            by_rows(128, blocks), back3, whole((128, channels)), whole((8, channels)),
        ],
        out_shape=[
            sds((tokens, channels), bf16), sds((tokens, channels), bf16),
            sds((tokens, channels), bf16), sds((tokens, 128), f32),
            sds((blocks, 128, channels), f32), sds((128, channels), f32),
            sds((8, channels), f32),
        ],
        scratch_shapes=[pltpu.VMEM((128, channels), f32)],
        compiler_params=pltpu.CompilerParams(**PARAMS),
        name="turn",
    )(y, gate, ggated, sums, x_low, wr, r, meta, head, par)

    ds_in = lax.ppermute(dsout, "row", [(1, 0)])
    out_part = mm(gated, w_out).astype(bf16)
    out_cols = lax.psum_scatter(out_part, "col", scatter_dimension=1, tiled=True)
    own_tokens = lax.dynamic_slice_in_dim(tokens_in, col * col_width, col_width, 1).astype(f32)
    mixed_out = (own_tokens + out_cols.astype(f32)).astype(bf16)
    grad_out_part = lax.dot_general(
        gated, cot_all, (((0,), (0,)), ((), ())), preferred_element_type=f32
    )

    gx, gs, gz, hx, hs, accx, accs, acch = pl.pallas_call(
        back_kernel,
        grid=(blocks,),
        in_specs=[
            by_rows(channels, blocks), by_rows(256, blocks), by_rows(channels, blocks),
            by_rows(128, blocks), by_rows(128, blocks), by_rows(128, blocks),
            by_rows(16, blocks), pl.BlockSpec((1, SPAN), lambda i: (0, blocks - 1 - i)),
            by_rows(128, blocks), back3, back3, whole((128, channels)),
            by_rows(channels, blocks), by_rows(256, blocks), by_rows(channels, blocks),
            by_rows(256, blocks), whole((8, channels)), whole((8, 256)), whole((8, 16)),
            whole((8, 128)), whole((8, channels)), whole((8, 256)),
        ],
        out_specs=[
            by_rows(channels, blocks), by_rows(256, blocks), by_rows(128, blocks),
            whole((8, channels)), whole((8, 256)), whole((8, channels)), whole((8, 256)),
            whole((8, 128)),
        ],
        out_shape=[
            sds((tokens, channels), bf16), sds((tokens, 256), bf16), sds((tokens, 128), bf16),
            sds((8, channels), f32), sds((8, 256), f32), sds((8, channels), f32),
            sds((8, 256), f32), sds((8, 128), f32),
        ],
        scratch_shapes=[
            pltpu.VMEM((128, channels), f32),
            pltpu.VMEM((SPAN + 16, channels), f32),
            pltpu.VMEM((SPAN + 16, 256), f32),
            pltpu.VMEM((SPAN, channels), f32),
        ],
        compiler_params=pltpu.CompilerParams(**PARAMS),
        name="back",
    )(
        x_low, wr, gy, r, step, sig, meta, docrow, dr, sprev, dsf, ds_in,
        pre, spre, sd, ssd, hpre, hspre, hmeta, head, par, spar,
    )

    hx_in, hs_in = lax.ppermute((hx, hs), "row", [(1, 0)])
    gx = gx.at[-8:].add(hx_in.astype(bf16))
    gs = gs.at[-8:].add(hs_in.astype(bf16))

    normed_grad = (
        mm_nt(g_gate, w_gate) + mm_nt(gx, w_inner) + mm_nt(gz, w_step) + mm_nt(gs, proj_states)
    )
    wide = tokens_in.astype(f32)
    inverse = lax.rsqrt(jnp.mean(wide * wide, -1, keepdims=True) + epsilon)
    input_share = jnp.sum(normed_grad * norm_gain * wide, -1)
    gain_share = jnp.sum(normed_grad * (wide * inverse), 0)
    own_grad = lax.psum_scatter(
        normed_grad.astype(bf16), "col", scatter_dimension=1, tiled=True
    ).astype(f32)
    input_total = lax.psum(input_share, "col")[:, None]
    gain_cols = lax.dynamic_slice_in_dim(norm_gain, col * col_width, col_width, 0)
    grad_input = inverse * (own_grad * gain_cols) - own_tokens * inverse**3 * (input_total / width)
    grad_tokens = (grad_input + cotangent.astype(f32)).astype(bf16)

    def weight_grad(left, right):
        return lax.dot_general(
            left, right, (((0,), (0,)), ((), ())), preferred_element_type=f32
        )

    def reduce_columns(part):
        part = part.reshape(width, 2, own_ch).astype(bf16)
        part = lax.psum_scatter(part, "row", scatter_dimension=1)
        part = lax.psum(part, "dp")
        return lax.all_to_all(part, "col", 0, 1, tiled=True).astype(f32)

    grad_gate = reduce_columns(weight_grad(normed, g_gate))
    grad_inner = reduce_columns(weight_grad(normed, gx))
    go = lax.psum_scatter(
        grad_out_part.astype(bf16), "row", scatter_dimension=0, tiled=True
    )
    go = lax.psum(go, "dp")
    grad_out = lax.all_to_all(go, "col", 1, 0, tiled=True).astype(f32)

    g_rest = weight_grad(normed, jnp.concatenate([gs, gz], 1))
    grad_states = lax.psum(g_rest[:, :256], ("dp", "row", "col"))
    gz_part = g_rest[:, 256:256 + 2 * own_heads].reshape(width, 2, own_heads)
    gz_own = lax.psum(gz_part, ("dp", "row"))
    gz_all = lax.all_gather(gz_own, "col", axis=0)
    gz_all = lax.dynamic_index_in_dim(gz_all, row, 2, keepdims=False)
    gz_all = lax.dynamic_slice_in_dim(gz_all, col * col_width, col_width, 1)
    grad_step = jnp.moveaxis(gz_all, 0, 1).reshape(col_width, cols * own_heads)

    def head_sum(values):
        return values.reshape(2 * own_heads, HEAD).sum(-1)

    small = jnp.concatenate(
        [
            accx[0:5].reshape(5, 2, own_ch).transpose(1, 0, 2).reshape(2, -1),
            acc1[0].reshape(2, own_ch),
            acch[0, : 2 * own_heads].reshape(2, own_heads),
            (acch[1] * head[3])[: 2 * own_heads].reshape(2, own_heads),
            head_sum(acc1[1]).reshape(2, own_heads),
        ],
        1,
    )
    small = lax.psum(small, ("dp", "row"))
    small = lax.dynamic_index_in_dim(small, row, 0, keepdims=False)
    grad_conv_inner = small[: 4 * own_ch].reshape(4, own_ch)
    grad_conv_inner_bias = small[4 * own_ch:5 * own_ch]
    grad_gate_gain = small[5 * own_ch:6 * own_ch]
    rest = small[6 * own_ch:].reshape(3, own_heads)
    accs = lax.psum(accs, ("dp", "row", "col"))
    gain_all = lax.psum(gain_share, ("dp", "row", "col"))
    grad_norm_gain = lax.dynamic_slice_in_dim(gain_all, col * col_width, col_width, 0)

    return (
        mixed_out,
        grad_tokens,
        grad_norm_gain,
        grad_gate,
        grad_inner,
        grad_step,
        grad_states,
        grad_conv_inner,
        grad_conv_inner_bias,
        accs[0:4],
        accs[4],
        rest[0],
        rest[1],
        rest[2],
        grad_gate_gain,
        grad_out,
    )


def solution(mesh):
    in_specs = (
        P(("dp", "row"), None),
        P("dp", None),
        P(),
        P("col", "row"),
        P("col", "row"),
        P("col", "row"),
        P(),
        P(None, ("row", "col")),
        P(("row", "col")),
        P(),
        P(),
        P(("row", "col")),
        P(("row", "col")),
        P(("row", "col")),
        P(("row", "col")),
        P("row", "col"),
        P(("dp", "row"), "col"),
    )
    out_specs = (
        P(("dp", "row"), "col"),
        P(("dp", "row"), "col"),
        P("col"),
        P("col", "row"),
        P("col", "row"),
        P("col", "row"),
        P(),
        P(None, ("row", "col")),
        P(("row", "col")),
        P(),
        P(),
        P(("row", "col")),
        P(("row", "col")),
        P(("row", "col")),
        P(("row", "col")),
        P("row", "col"),
    )
    return jax.shard_map(
        per_device, mesh=mesh, in_specs=in_specs, out_specs=out_specs, check_vma=False
    )
```

time: 2050 us -> 834 us (0.41)
  waiting for transfers between devices: 786 us -> 317 us
  local copies, waits for them, and re-layouts: 413 us -> 58.9 us
  other arithmetic: 266 us -> 13.9 us
  matrix products: 239 us -> 55.5 us
  Pallas kernels: 0 us -> 60.8 us
  loops' own time: 25 us -> 0 us
    reduce_scatter x5 -> x3, waiting for transfers between devices: 334 us -> 46.6 us  [the longest x2 46.6 us: reduce_columns(): part = lax.psum_scatter(part, 'row', scatter_dimension=1)]
    all_gather x5 -> x4, waiting for transfers between devices: 290 us -> 50.5 us  [the longest x1 50.5 us: per_device(): cot_all = lax.all_gather(cotangent, 'col', axis=1, tiled=True)]
    dynamic_update_slice x56 -> x0, local copies, waits for them, and re-layouts: 181 us -> none  [span_scan(): _, outputs = lax.scan(jax.checkpoint(advance), start, pieces)]
    dot_general x111 -> x11, matrix products: 224 us -> 55.5 us  [the longest x5 22.9 us: mm_nt(): lax.dot_general(a, b, (((1,), (1,)), ((), ())), preferred_element_type=f32)]
    all_to_all x0 -> x5, blocking collectives: none -> 160 us  [the longest x2 65.5 us: fetch_columns(): moved = lax.all_to_all(weight, 'col', 1, 0, tiled=True)]
    psum x5 -> x4, blocking collectives: 238 us -> 93.1 us  [the longest x1 39.7 us: per_device(): gain_all = lax.psum(gain_share, ('dp', 'row', 'col'))]
    another operation x82 -> x5, other arithmetic: 131 us -> 0.91 us  [the longest x1 0.6 us: per_device(): jnp.stack([hp[0], rate * LOG2E, hp[2], rate])]
    unnamed x12 -> x14, waiting for transfers between devices: 2.89 us -> 119 us
  transfers between devices with their start and end apart: 12 -> 18, of which waited for: 7 -> 10; matrix products, arithmetic and copies ran while one was open for 20% -> 13% of each run, Pallas kernels for 0% -> 5%
where the time goes in v1:
time: 834 us; the launch traced here: 827 us
  waiting for transfers between devices  317 us (38%)
  blocking collectives  291 us (35%)
  Pallas kernels  60.8 us (7%)
  local copies, waits for them, and re-layouts  58.9 us (7%)
  matrix products  55.5 us (7%)
  between operations  15.2 us (2%)
  starting transfers between devices  14.7 us (2%)
  other arithmetic  13.9 us (2%)
    unnamed x14, waiting for transfers between devices  119 us
    all_to_all x2, blocking collectives, fetch_columns(): moved = lax.all_to_all(weight, 'col', 1, 0, tiled=True)  65.5 us
    all_to_all x2, blocking collectives, reduce_columns(): return lax.all_to_all(part, 'col', 0, 1, tiled=True).astype(f32)  64.1 us
    all_gather x1, waiting for transfers between devices, per_device(): cot_all = lax.all_gather(cotangent, 'col', axis=1, tiled=True)  50.5 us
    reduce_scatter x2, waiting for transfers between devices, reduce_columns(): part = lax.psum_scatter(part, 'row', scatter_dimension=1)  46.6 us
    psum x1, waiting for transfers between devices, per_device(): grad_states = lax.psum(g_rest[:, :256], ('dp', 'row', 'col'))  42.3 us
    psum x1, blocking collectives, per_device(): gain_all = lax.psum(gain_share, ('dp', 'row', 'col'))  39.7 us
    psum x1, waiting for transfers between devices, reduce_columns(): part = lax.psum(part, 'dp')  31.2 us
  transfers between devices with their start and end apart: 18, of which 10 were waited for; matrix products, arithmetic and copies ran while one was open for 13% of the time, Pallas kernels for 5%

profile of v1, /device:TPU:0, one launch (start us, length us, event | category | flops | bytes accessed | tf_op | source)
XLA Modules:
  0.0 827.3 jit_solution(10614199868235940283)
XLA Ops:
  7.2 1.4 copy.163
  8.6 34.9 %all_to_all.96 = bf16[384,4,384]{2,0,1:T(8,128)(2,1)} all-to-all(bf16[384,4,384]{2,0,1:T(8,128)(2,1)S(1)} %bitcast.123), channel_id=1, replica_groups=mesh['dp'=4,'row'=2,'col'=4] {'col'}, dimensions={1} | all-to-all | bytes 2359296 | tf_op jit(solution)/shard_map/all_to_all | solution.py:415
  44.4 30.6 %all_to_all.97 = bf16[384,4,384]{0,2,1:T(8,128)(2,1)S(1)} all-to-all(bf16[384,4,384]{0,2,1:T(8,128)(2,1)S(1)} %bitcast.124), channel_id=1, replica_groups=mesh['dp'=4,'row'=2,'col'=4] {'col'}, dimensions={1} | all-to-all | bytes 2359296 | tf_op jit(solution)/shard_map/all_to_all | solution.py:415
  74.9 1.4 copy.131
  76.5 30.6 %all_to_all.98 = bf16[4,384,384]{2,1,0:T(8,128)(2,1)S(1)} all-to-all(bf16[4,384,384]{2,1,0:T(8,128)(2,1)S(1)} %bitcast.130), channel_id=1, replica_groups=mesh['dp'=4,'row'=2,'col'=4] {'col'}, dimensions={0} | all-to-all | bytes 2359296 | tf_op jit(solution)/shard_map/all_to_all | solution.py:428
  107.2 1.5 copy.132
  110.1 3.4 collective-permute-start
  116.3 4.4 all-gather
  120.9 13.2 %all_gather.31 = bf16[1536,24]{0,1:T(8,128)(2,1)S(1)} all-gather(bf16[384,24]{0,1:T(8,128)(2,1)S(1)} %copy-done.17), channel_id=1, replica_groups=mesh['dp'=4,'row'=2,'col'=4] {'col'}, dimensions={0}, use_global_device_ids=true | all-gather | bytes 92160 | tf_op jit(solution)/shard_map/all_gather | solution.py:421
  134.1 6.6 all_gather.32
  146.4 15.8 %entry.1 = (bf16[1024,1536]{1,0:T(8,128)(2,1)}, bf16[1024,768]{1,0:T(8,128)(2,1)}, bf16[1024,256]{1,0:T(8,128)(2,1)}, bf16[1024,768]{1,0:T(8,128)(2,1)}, bf16[10...) custom-call(bf16[1024,1536]{1,0:T(8,128)(2,1)} %tok.1, ...), custom_call_target="tpu_custom_call" | custom-call | tf_op jit(solution)/shard_map/entry/pallas_call | solution.py:492
  162.2 2.2 collective-permute-start.1
  164.5 7.4 fusion.35.gate
  171.8 50.5 %all-gather.10.cloned.1.call-done = bf16[1024,1536]{1,0:T(8,128)(2,1)} async-done(((bf16[1024,384]{1,0:T(8,128)(2,1)}), bf16[1024,1536]{1,0:T(8,128)(2,1)}) %all-gather.10.cloned.1.call-update) | async-done | bytes 3145744 | tf_op jit(solution)/shard_map/all_gather | solution.py:430
  222.3 6.9 fusion.36.ggated
  229.9 11.4 %scan.1 = (f32[1024,768]{1,0:T(8,128)}, f32[8,1024]{1,0:T(8,128)}, bf16[4,128,768]{2,1,0:T(8,128)(2,1)}) custom-call(bf16[1024,768]{1,0:T(8,128)(2,1)} %get-tuple-element.72.x, bf16[1024,256]{1,0:T(8,128)(2,1)} %get-tuple-element.73.wr, f32[1024,128]{1,0:T(8,128)} %get-tuple-element.74.r_ref, f32[1024,128]{1,0:T(8,128)} %get-tuple-element.75.step_ref, ...), custom_call_target="tpu_custom_call" | custom-call | tf_op jit(solution)/shard_map/scan/pallas_call | solution.py:527
  241.4 17.8 %psum.70.sums = f32[8,1024]{1,0:T(8,128)} all-reduce(f32[8,1024]{1,0:T(8,128)} %get-tuple-element.80), channel_id=1, replica_groups=mesh['dp'=4,'row'=2,'col'=4] {'col'}, use_global_device_ids=true, to_apply=%region_0.1 | all-reduce | flops 8192 | bytes 65536 | tf_op jit(solution)/shard_map/psum | solution.py:549
  259.2 10.9 %turn.1 = (bf16[1024,768]{1,0:T(8,128)(2,1)}, bf16[1024,768]{1,0:T(8,128)(2,1)}, bf16[1024,768]{1,0:T(8,128)(2,1)}, f32[1024,128]{1,0:T(8,128)}, f32[4,128,768]{...) custom-call(f32[1024,768]{1,0:T(8,128)} %get-tuple-element.79.y_ref, f32[1024,768]{1,0:T(8,128)} %fusion.35.gate, ...), custom_call_target="tpu_custom_call" | custom-call | tf_op jit(solution)/shard_map/turn/pallas_call | solution.py:552
  270.1 5.3 convolution_convert_fusion.1
  275.6 1.3 copy-done.33
  276.9 5.8 convolution_convert_fusion.3
  283.7 1.5 collective-permute-start.2
  286.2 18.2 %collective-permute-done.2.ds_in = f32[128,768]{1,0:T(8,128)S(1)} collective-permute-done((f32[128,768]{1,0:T(8,128)S(1)}, f32[128,768]{1,0:T(8,128)S(1)}, u32[]{:S(2)}, u32[]{:S(2)}) %collective-permute-start.2) | collective-permute-done | bytes 393248 | tf_op jit(solution)/shard_map/ppermute | solution.py:576
  305.1 22.7 %back.1 = (bf16[1024,768]{1,0:T(8,128)(2,1)}, bf16[1024,256]{1,0:T(8,128)(2,1)}, bf16[1024,128]{1,0:T(8,128)(2,1)}, f32[8,768]{1,0:T(8,128)}, f32[8,256]{1,0:T(8...) custom-call(bf16[1024,768]{1,0:T(8,128)(2,1)} %get-tuple-element.72.x, ...), custom_call_target="tpu_custom_call" | custom-call | tf_op jit(solution)/shard_map/back/pallas_call | solution.py:585
  328.5 1.3 collective-permute-start.3
  329.8 4.5 collective-permute-done.3
  334.3 1.3 add_dynamic-update-slice_fusion
  335.7 5.4 convolution_convert_fusion.2
  341.2 2.4 copy.162
  343.6 11.5 %reduce-scatter.10.cloned.1.call-done = bf16[1536,1,384]{0,2,1:T(8,128)(2,1)} async-done(((bf16[1536,2,384]{0,2,1:T(8,128)(2,1)}), bf16[1536,1,384]{0,2,1:T(8,128)(2,1)}) %reduce-scatter.10.cloned.1.call-update) | async-done | bytes 1179664 | tf_op jit(solution)/shard_map/reduce_scatter | solution.py:646
  355.1 2.4 copy.139
  357.5 35.1 %reduce-scatter.12.cloned.1.call-done = bf16[1536,1,384]{0,2,1:T(8,128)(2,1)} async-done(((bf16[1536,2,384]{0,2,1:T(8,128)(2,1)}), bf16[1536,1,384]{0,2,1:T(8,128)(2,1)}) %reduce-scatter.12.cloned.1.call-update) | async-done | bytes 1179664 | tf_op jit(solution)/shard_map/reduce_scatter | solution.py:646
  392.5 2.4 copy.141
  395.6 1.3 collective-permute-start.4
  396.9 4.2 collective-permute-done.4
  401.1 3.9 fusion.9
  405.7 1.3 slice.224
  407.1 4.8 convolution_convert_fusion
  411.9 3.0 copy.150
  415.2 1.6 copy-done
  418.5 4.1 fusion.37
  424.7 4.7 fusion.38
  429.4 6.2 fusion.3
  435.7 4.7 copy.152
  440.4 31.2 %all-reduce.14.cloned.1.call-done = (bf16[4,384,384]{2,1,0:T(8,128)(2,1)}, bf16[4,384,384]{2,1,0:T(8,128)(2,1)}, bf16[384,4,384]{2,0,1:T(8,128)(2,1)}) async-done(((bf16[4,384,384]{2,1,0:T(8,128)(2,1)}, bf16[4,384,384]{2,1,0:T(8,128)(2,1)}, bf16[384,4,384]{2,0,1:T(8,128)(2,1)}), (bf16[4,384,384]{2,1,0:T(8,128)(2,1)}, bf16[4,384,384]{2,1,0:T(8,128)(2,1)}, ...) | async-done | bytes 3538960 | tf_op jit(solution)/shard_map/psum | solution.py:647
  471.6 33.2 %all_to_all.99 = bf16[4,384,384]{2,1,0:T(8,128)(2,1)} all-to-all(bf16[4,384,384]{2,1,0:T(8,128)(2,1)} %get-tuple-element.212), channel_id=1, replica_groups=mesh['dp'=4,'row'=2,'col'=4] {'col'}, dimensions={0} | all-to-all | bytes 2359296 | tf_op jit(solution)/shard_map/all_to_all | solution.py:648
  504.9 30.8 %all_to_all.100 = bf16[4,384,384]{2,1,0:T(8,128)(2,1)} all-to-all(bf16[4,384,384]{2,1,0:T(8,128)(2,1)S(1)} %copy-done.5), channel_id=1, replica_groups=mesh['dp'=4,'row'=2,'col'=4] {'col'}, dimensions={0} | all-to-all | bytes 2359296 | tf_op jit(solution)/shard_map/all_to_all | solution.py:648
  535.7 4.3 all-to-all-start.5
  542.9 24.9 %psum.77 = f32[2,2322]{1,0:T(2,128)S(1)} all-reduce(f32[2,2322]{1,0:T(2,128)S(1)} %concatenate.38), channel_id=1, replica_groups=mesh['dp'=4,'row'=2,'col'=4] {'dp','row'}, use_global_device_ids=true, to_apply=%region_15.16 | all-reduce | flops 4644 | bytes 37152 | tf_op jit(solution)/shard_map/psum | solution.py:680
  569.7 39.7 %all-reduce.4 = (f32[1536]{0:T(1024)S(1)}, f32[8,256]{1,0:T(8,128)S(1)}) all-reduce(f32[1536]{0:T(1024)S(1)} %get-tuple-element.200, f32[8,256]{1,0:T(8,128)S(1)} %copy-done.20), channel_id=1, replica_groups=mesh['dp'=4,'row'=2,'col'=4] {'dp','row','col'}, use_global_device_ids=true, to_apply=%region_7.8 | all-reduce | flops 3584 | bytes 28672 | tf_op jit(solution)/shard_map/psum | solution.py:687
  611.3 10.6 %psum.71 = f32[1024]{0:T(1024)S(1)} all-reduce(f32[1024]{0:T(1024)S(1)} %get-tuple-element.201), channel_id=1, replica_groups=mesh['dp'=4,'row'=2,'col'=4] {'col'}, use_global_device_ids=true, to_apply=%region_5.6 | all-reduce | flops 1024 | bytes 8192 | tf_op jit(solution)/shard_map/psum | solution.py:634
  622.9 14.0 %all_gather.39 = f32[4,1536,2,6]{1,2,3,0:T(2,128)S(1)} all-gather(f32[1,1536,2,6]{1,2,3,0:T(2,128)S(1)} %copy.143), channel_id=1, replica_groups=mesh['dp'=4,'row'=2,'col'=4] {'col'}, dimensions={0}, use_global_device_ids=true | all-gather | bytes 368640 | tf_op jit(solution)/shard_map/all_gather | solution.py:662
  637.6 42.3 %all-reduce.12.cloned.1.call-done = f32[1536,256]{0,1:T(8,128)} async-done(((f32[1536,256]{0,1:T(8,128)}), f32[1536,256]{0,1:T(8,128)}) %all-reduce.12.cloned.1.call-update) | async-done | bytes 1572880 | tf_op jit(solution)/shard_map/psum | solution.py:659
  680.0 3.0 copy.149
  683.0 58.5 %reduce-scatter.16.cloned.1.call-done = bf16[384,1024]{1,0:T(8,128)(2,1)} async-done(((bf16[1536,1024]{1,0:T(8,128)(2,1)}), bf16[384,1024]{1,0:T(8,128)(2,1)}) %reduce-scatter.16.cloned.1.call-update) | async-done | bytes 786448
  741.4 2.3 copy.151
  743.7 60.2 %reduce-scatter.18.cloned.1.call-done = bf16[384,1024]{1,0:T(8,128)(2,1)} async-done(((bf16[1536,1024]{1,0:T(8,128)(2,1)}), bf16[384,1024]{1,0:T(8,128)(2,1)}) %reduce-scatter.18.cloned.1.call-update) | async-done | bytes 786448
  803.9 2.3 copy.153
  806.2 3.4 fusion.8
  809.6 1.7 copy.140
  811.4 2.0 copy.147
  813.4 1.7 copy.142
  815.3 2.0 copy.148
  817.2 2.8 convert_element_type.151
  (188 shorter events, 29.7 us)
Async XLA Ops:
  7.2 138.6 %all-gather.6.cloned.1.call-start = ((), (), s32[]{:S(2)}) async-start(), calls=%async_computation.11 | async-start | bytes 3538944 | tf_op jit(solution)/shard_map/all_gather | solution.py:416
  8.6 35.0 %copy-start.3 = (bf16[384,1536]{1,0:T(8,128)(2,1)S(1)}, bf16[384,1536]{1,0:T(8,128)(2,1)}, u32[]{:S(2)}) copy-start(bf16[384,1536]{1,0:T(8,128)(2,1)} %param.24) | copy-start | bytes 3538948
  43.5 120.9 %all-gather.8.cloned.1.call-start = ((), (), s32[]{:S(2)}) async-start(), calls=%async_computation.12 | async-start | bytes 3538944 | tf_op jit(solution)/shard_map/all_gather | solution.py:416
  74.9 1.5 copy-start.4
  76.4 95.4 %all-gather.12.cloned.1.call-start = ((), (), s32[]{:S(2)}) async-start(), calls=%async_computation.14 | async-start | bytes 3538944 | tf_op jit(solution)/shard_map/all_gather | solution.py:427
  107.1 6.4 copy-start.19
  107.1 9.0 %copy-start.26 = (f32[6]{0:T(128)S(1)}, f32[6]{0:T(128)}, u32[]{:S(2)}) copy-start(f32[6]{0:T(128)} %param.34) | copy-start | bytes 76
  107.1 9.0 %copy-start.27 = (f32[6]{0:T(128)S(1)}, f32[6]{0:T(128)}, u32[]{:S(2)}) copy-start(f32[6]{0:T(128)} %param.33) | copy-start | bytes 76
  107.1 9.0 %copy-start.28 = (f32[6]{0:T(128)S(1)}, f32[6]{0:T(128)}, u32[]{:S(2)}) copy-start(f32[6]{0:T(128)} %param.32) | copy-start | bytes 76
  107.1 9.1 %copy-start.23 = (f32[384]{0:T(512)S(1)}, f32[384]{0:T(512)}, u32[]{:S(2)}) copy-start(f32[384]{0:T(512)} %param.29) | copy-start | bytes 4612
  107.1 9.1 %copy-start.24 = (f32[384]{0:T(512)S(1)}, f32[384]{0:T(512)}, u32[]{:S(2)}) copy-start(f32[384]{0:T(512)} %param.35) | copy-start | bytes 4612
  107.1 9.2 %copy-start.21 = (f32[4,384]{1,0:T(4,128)S(1)}, f32[4,384]{1,0:T(4,128)}, u32[]{:S(2)}) copy-start(f32[4,384]{1,0:T(4,128)} %param.28) | copy-start | bytes 18436
  107.1 13.8 %copy-start.17 = (bf16[384,24]{0,1:T(8,128)(2,1)S(1)}, bf16[384,24]{0,1:T(8,128)(2,1)}, u32[]{:S(2)}) copy-start(bf16[384,24]{0,1:T(8,128)(2,1)} %param.26) | copy-start | bytes 55300
  107.1 34.4 %copy-start.22 = (f32[4,256]{1,0:T(4,128)S(1)}, f32[4,256]{1,0:T(4,128)}, u32[]{:S(2)}) copy-start(f32[4,256]{1,0:T(4,128)} %param.30) | copy-start | bytes 12292
  107.2 34.4 %copy-start.25 = (f32[256]{0:T(256)S(1)}, f32[256]{0:T(256)}, u32[]{:S(2)}) copy-start(f32[256]{0:T(256)} %param.31) | copy-start | bytes 3076
  108.6 35.7 %copy-start.15 = (f32[1536]{0:T(1024)S(1)}, f32[1536]{0:T(1024)}, u32[]{:S(2)}) copy-start(f32[1536]{0:T(1024)} %param.23) | copy-start | bytes 18436
  108.7 113.7 %all-gather.10.cloned.1.call-start = ((), (), s32[]{:S(2)}) async-start(), calls=%async_computation.13 | async-start | bytes 3932160 | tf_op jit(solution)/shard_map/all_gather | solution.py:430
  109.2 231.9 %reduce-scatter.14.cloned.1.call-start = ((), (), s32[]{:S(2)}) async-start(), calls=%async_computation.19 | async-start | bytes 3538944 | tf_op jit(solution)/shard_map/reduce_scatter | solution.py:652
  110.1 35.7 %collective-permute-start = (bf16[16,1536]{1,0:T(8,128)(2,1)S(1)}, bf16[16,1536]{1,0:T(8,128)(2,1)S(1)}, u32[]{:S(2)}, u32[]{:S(2)}) collective-permute-start(bf16[16,1536]{1,0:T(8,128)(2,1)S(1)} %slice.172), channel_id=1, source_target_pairs={{0,4},{1,5},{2,6},{3,7},{8,12},{9,13},{10,14},{11,15},{16,20},{17,... | collective-permute-start | bytes 147464 | tf_op jit(solution)/shard_map/ppermute | solution.py:418
  113.6 48.6 %copy-start.13 = (f32[1024]{0:T(1024)}, f32[1024]{0:T(1024)S(1)}, u32[]{:S(2)}) copy-start(f32[1024]{0:T(1024)S(1)} %get-tuple-element.217) | copy-start | bytes 12292
  145.8 0.6 copy-start.14
  162.2 67.0 %collective-permute-start.1 = (f32[128,768]{1,0:T(8,128)}, f32[128,768]{1,0:T(8,128)S(1)}, u32[]{:S(2)}, u32[]{:S(2)}) collective-permute-start(f32[128,768]{1,0:T(8,128)} %get-tuple-element.77), channel_id=1, source_target_pairs={{0,4},{1,5},{2,6},{3,7},{8,12},{9,13},{10,14},{11,15},{16,20},{17,... | collective-permute-start | bytes 1179656 | tf_op jit(solution)/shard_map/ppermute | solution.py:523
  229.2 0.7 copy-start.12
  259.2 10.9 %copy-start.30 = (bf16[1024,1536]{1,0:T(8,128)(2,1)S(1)}, bf16[1024,1536]{1,0:T(8,128)(2,1)}, u32[]{:S(2)}) copy-start(bf16[1024,1536]{1,0:T(8,128)(2,1)} %all-gather.10.cloned.1.call-done) | copy-start | bytes 9437188
  275.5 1.4 copy-start.33
  275.5 79.6 %reduce-scatter.10.cloned.1.call-start = ((), (), s32[]{:S(2)}) async-start(), calls=%async_computation.15 | async-start | bytes 3538944 | tf_op jit(solution)/shard_map/reduce_scatter | solution.py:646
  282.7 1.0 copy-start.34
  282.7 109.8 %reduce-scatter.12.cloned.1.call-start = ((), (), s32[]{:S(2)}) async-start(), calls=%async_computation.16 | async-start | bytes 3538944 | tf_op jit(solution)/shard_map/reduce_scatter | solution.py:646
  283.7 20.7 %collective-permute-start.2 = (f32[128,768]{1,0:T(8,128)S(1)}, f32[128,768]{1,0:T(8,128)S(1)}, u32[]{:S(2)}, u32[]{:S(2)}) collective-permute-start(f32[128,768]{1,0:T(8,128)S(1)} %copy-done.34), channel_id=1, source_target_pairs={{4,0},{5,1},{6,2},{7,3},{12,8},{13,9},{14,10},{15,11},{20,16},{21,... | collective-permute-start | bytes 1179656 | tf_op jit(solution)/shard_map/ppermute | solution.py:576
  304.4 0.7 copy-start.11
  305.1 30.5 %copy-start.31 = (bf16[1024,1536]{1,0:T(8,128)(2,1)S(1)}, bf16[1024,1536]{1,0:T(8,128)(2,1)}, u32[]{:S(2)}) copy-start(bf16[1024,1536]{1,0:T(8,128)(2,1)} %get-tuple-element.78) | copy-start | bytes 9437188
  328.5 5.8 collective-permute-start.3
  341.1 130.6 %all-reduce.14.cloned.1.call-start = ((), (), s32[]{:S(2)}) async-start(), calls=%async_computation.22 | async-start | bytes 7077888 | tf_op jit(solution)/shard_map/psum | solution.py:647
  394.9 0.7 copy-start.18
  394.9 6.2 copy-start.8
  394.9 6.2 copy-start.6
  394.9 227.0 %all-reduce.10.cloned.1.call-start = ((), (), s32[]{:S(2)}) async-start(), calls=%async_computation.17 | async-start | bytes 196608 | tf_op jit(solution)/shard_map/psum | solution.py:661
  395.6 5.5 collective-permute-start.4
  401.1 3.9 copy-start.9
  405.7 274.3 %all-reduce.12.cloned.1.call-start = ((), (), s32[]{:S(2)}) async-start(), calls=%async_computation.18 | async-start | bytes 3145728 | tf_op jit(solution)/shard_map/psum | solution.py:659
  407.0 334.4 %reduce-scatter.16.cloned.1.call-start = ((), (), s32[]{:S(2)}) async-start(), calls=%async_computation.20 | async-start | bytes 3932160
  414.9 1.9 copy-start
  414.9 389.0 %reduce-scatter.18.cloned.1.call-start = ((), (), s32[]{:S(2)}) async-start(), calls=%async_computation.21 | async-start | bytes 3932160
  416.8 1.7 copy-start.32
  418.5 4.1 copy-start.7
  422.6 1.7 copy-start.2
  422.6 2.1 copy-start.29
  424.7 4.7 copy-start.1
  424.7 4.7 copy-start.10
  471.6 33.2 %copy-start.5 = (bf16[4,384,384]{2,1,0:T(8,128)(2,1)S(1)}, bf16[4,384,384]{2,1,0:T(8,128)(2,1)}, u32[]{:S(2)}) copy-start(bf16[4,384,384]{2,1,0:T(8,128)(2,1)} %get-tuple-element.213) | copy-start | bytes 3538948
  504.9 37.1 %copy-start.16 = (f32[8,768]{1,0:T(8,128)S(1)}, f32[8,768]{1,0:T(8,128)}, u32[]{:S(2)}) copy-start(f32[8,768]{1,0:T(8,128)} %get-tuple-element.100) | copy-start | bytes 73732
  504.9 64.9 %copy-start.20 = (f32[8,256]{1,0:T(8,128)S(1)}, f32[8,256]{1,0:T(8,128)}, u32[]{:S(2)}) copy-start(f32[8,256]{1,0:T(8,128)} %get-tuple-element.103) | copy-start | bytes 24580
  535.7 281.5 %all-to-all-start.5 = ((bf16[384,4,384]{2,0,1:T(8,128)(2,1)}), bf16[384,4,384]{2,0,1:T(8,128)(2,1)}, u32[]{:S(2)}, u32[]{:S(2)}) async-start(bf16[384,4,384]{2,0,1:T(8,128)(2,1)} %get-tuple-element.214), calls=%async_computation.8 | async-start | bytes 2359296 | tf_op jit(solution)/shard_map/all_to_all | solution.py:656
Sparse Core Ops, SparseCore 0:
  43.7 35.1 all-gather.5
  81.0 36.0 all-gather.7
  118.7 38.8 all-gather.11
  159.0 63.3 all-gather.9
  275.6 41.8 reduce-scatter.13
  320.3 34.7 reduce-scatter.9
  357.9 34.5 reduce-scatter.11
  396.4 75.2 all-reduce.13
  475.6 51.6 all-reduce.9
  532.9 146.9 all-reduce.11
  682.3 59.1 reduce-scatter.15
  743.6 60.2 reduce-scatter.17

commit v2 on v1

--- a/solution.py
+++ b/solution.py
@@ -391,8 +391,567 @@
     return pl.BlockSpec((SPAN, cols), lambda i: (count - 1 - i, 0))
 
 
-def swap(values, axis):
-    return lax.ppermute(values, axis, [(0, 1), (1, 0)])
+MESH = pl.DeviceIdType.MESH
+SHARE = 4
+
+
+def lane_block(index, width):
+    return pl.ds(pl.multiple_of(index * width, 128), width)
+
+
+class Links:
+    def __init__(self, send, recv):
+        self.send, self.recv, self.used, self.all = send, recv, 0, []
+        dp = lax.axis_index("dp")
+        self.groups = lax.axis_size("dp") // SHARE
+        self.group = dp // SHARE
+        self.x = lax.rem(dp, SHARE) // 2
+        self.core = lax.rem(dp, 2)
+        self.y = lax.axis_index("row")
+        self.z = lax.axis_index("col")
+        self.cols = lax.axis_size("col")
+
+    def dp_of(self, group, x, core):
+        return group * SHARE + x * 2 + core
+
+    def mate(self):
+        return {"dp": self.dp_of(self.group, self.x, 1 - self.core)}
+
+    def across(self):
+        return {"dp": self.dp_of(self.group, 1 - self.x, self.core)}
+
+    def other_row(self):
+        return {"row": 1 - self.y}
+
+    def col_peer(self, off):
+        return lax.rem(self.z + off, self.cols)
+
+    def group_peer(self, off):
+        return {"dp": self.dp_of(lax.rem(self.group + off, self.groups), self.x, self.core)}
+
+    def meet(self, far_groups):
+        barrier = pltpu.get_barrier_semaphore()
+        peers = [self.mate(), self.across(), self.other_row()]
+        peers += [{"col": self.col_peer(off)} for off in range(1, self.cols)]
+        if far_groups:
+            peers += [self.group_peer(off) for off in range(1, self.groups)]
+        for peer in peers:
+            pl.semaphore_signal(barrier, inc=1, device_id=peer, device_id_type=MESH)
+        pl.semaphore_wait(barrier, len(peers))
+
+    def go(self, src, dst, peer):
+        at = self.used
+        self.used += 1
+        copy = pltpu.make_async_remote_copy(
+            src_ref=src, dst_ref=dst, send_sem=self.send.at[at], recv_sem=self.recv.at[at],
+            device_id=peer, device_id_type=MESH,
+        )
+        copy.start()
+        self.all.append(copy)
+        return copy
+
+    def finish(self):
+        for copy in self.all:
+            copy.wait_send()
+
+
+def wavefront(stages, items):
+    for turn in range(stages + len(items) - 1):
+        for s in reversed(range(stages)):
+            m = turn - s
+            if 0 <= m < len(items):
+                items[m](s)
+
+
+def fetch_kernel(
+    inner, gate, out, step, cot, par, halo,
+    wi, wg, wo, ws, cots, pars, halo_in,
+    send, recv, local,
+):
+    t = Links(send, recv)
+    t.meet(False)
+    x, y, z, core = t.x, t.y, t.z, t.core
+    part = inner.shape[0] // SHARE
+    block = inner.shape[1] // t.cols
+    own_rows = pl.ds(pl.multiple_of((x * 2 + core) * part, 16), part)
+    locals_ = []
+
+    def keep(src, dst):
+        copy = pltpu.make_async_copy(src, dst, local.at[len(locals_)])
+        copy.start()
+        locals_.append(copy)
+        return copy
+
+    small = [t.go(par, pars.at[y], t.other_row()), t.go(halo, halo_in, t.other_row())]
+    keep(par, pars.at[y])
+
+    def column_blocks(src, dst, width):
+        lanes = lane_block(y, width)
+        copies = []
+
+        def run(s):
+            if s == 0:
+                for off in range(1, t.cols):
+                    to = t.col_peer(off)
+                    copies.append(
+                        t.go(src.at[own_rows, lane_block(to, width)],
+                             dst.at[z, x, core, :, lanes], {"col": to})
+                    )
+                copies.append(keep(src.at[own_rows, lane_block(z, width)],
+                                   dst.at[z, x, core, :, lanes]))
+            elif s == 1:
+                for c in copies[:-1]:
+                    c.wait_recv()
+                copies[-1].wait()
+                here = dst.at[:, x, core, :, lanes]
+                copies.append(t.go(here, here, t.other_row()))
+            elif s == 2:
+                copies[-1].wait_recv()
+                here = dst.at[:, x, core]
+                copies.append(t.go(here, here, t.across()))
+            elif s == 3:
+                copies[-1].wait_recv()
+                here = dst.at[:, :, core]
+                copies.append(t.go(here, here, t.mate()))
+            else:
+                copies[-1].wait_recv()
+
+        return run
+
+    def row_blocks(src, dst, width):
+        copies = []
+
+        def rows_of(to):
+            return pl.ds(pl.multiple_of((to * SHARE + x * 2 + core) * part, 16), part)
+
+        def run(s):
+            if s == 0:
+                for off in range(1, t.cols):
+                    to = t.col_peer(off)
+                    copies.append(
+                        t.go(src.at[rows_of(to), :], dst.at[y, x, core, :, lane_block(z, width)],
+                             {"col": to})
+                    )
+                copies.append(keep(src.at[rows_of(z), :],
+                                   dst.at[y, x, core, :, lane_block(z, width)]))
+            elif s == 1:
+                for c in copies[:-1]:
+                    c.wait_recv()
+                copies[-1].wait()
+                here = dst.at[y, x, core]
+                copies.append(t.go(here, here, t.other_row()))
+            elif s == 2:
+                copies[-1].wait_recv()
+                here = dst.at[:, x, core]
+                copies.append(t.go(here, here, t.across()))
+            elif s == 3:
+                copies[-1].wait_recv()
+                here = dst.at[:, :, core]
+                copies.append(t.go(here, here, t.mate()))
+            else:
+                copies[-1].wait_recv()
+
+        return run
+
+    def cot_blocks(s):
+        if s == 0:
+            lanes = lane_block(z, cot.shape[1])
+            for off in range(1, t.cols):
+                small.append(t.go(cot, cots.at[:, lanes], {"col": t.col_peer(off)}))
+            keep(cot, cots.at[:, lanes])
+
+    wavefront(5, [
+        column_blocks(inner, wi, block), column_blocks(step, ws, step.shape[1] // t.cols),
+        column_blocks(gate, wg, block), row_blocks(out, wo, out.shape[1]), cot_blocks,
+    ])
+    for c in small:
+        c.wait_recv()
+    locals_[0].wait()
+    locals_[-1].wait()
+    t.finish()
+
+
+def fetch(inner, gate, out, step, cot, par, halo):
+    rows, all_cols = inner.shape
+    cols = lax.axis_size("col")
+    part, block = rows // SHARE, all_cols // cols
+    sds = jax.ShapeDtypeStruct
+    wide = sds((cols, 2, 2, part, 2 * block), bf16)
+    shapes = [
+        wide, wide, sds((2, 2, 2, out.shape[0] // cols // SHARE, cols * out.shape[1]), bf16),
+        sds((cols, 2, 2, part, 2 * (step.shape[1] // cols)), bf16),
+        sds((cot.shape[0], cols * cot.shape[1]), bf16), sds((2,) + par.shape, f32),
+        sds(halo.shape, bf16),
+    ]
+    got = pl.pallas_call(
+        fetch_kernel,
+        out_shape=shapes,
+        in_specs=[pl.BlockSpec(memory_space=pl.ANY)] * 7,
+        out_specs=[pl.BlockSpec(memory_space=pl.ANY)] * 7,
+        scratch_shapes=[
+            pltpu.SemaphoreType.DMA((40,)), pltpu.SemaphoreType.DMA((40,)),
+            pltpu.SemaphoreType.DMA((8,)),
+        ],
+        compiler_params=pltpu.CompilerParams(collective_id=1, has_side_effects=True),
+        name="fetch",
+    )(inner, gate, out, step, cot, par, halo)
+    wi, wg, wo, ws, cots, pars, halo_in = got
+    width = rows * cols
+    return (
+        wi.reshape(width, -1), wg.reshape(width, -1), wo.reshape(2 * block, -1),
+        ws.reshape(width, -1), cots, pars, halo_in,
+    )
+
+
+def col_sum_kernel(v, total, got, send, recv):
+    t = Links(send, recv)
+    barrier = pltpu.get_barrier_semaphore()
+    for off in range(1, t.cols):
+        pl.semaphore_signal(
+            barrier, inc=1, device_id={"col": t.col_peer(off)}, device_id_type=MESH
+        )
+    pl.semaphore_wait(barrier, t.cols - 1)
+    copies = [t.go(v, got.at[off - 1], {"col": t.col_peer(off)}) for off in range(1, t.cols)]
+    for c in copies:
+        c.wait_recv()
+    total[...] = v[...] + got[0] + got[1] + got[2]
+    t.finish()
+
+
+def col_sum(v):
+    cols = lax.axis_size("col")
+    return pl.pallas_call(
+        col_sum_kernel,
+        out_shape=jax.ShapeDtypeStruct(v.shape, v.dtype),
+        in_specs=[pl.BlockSpec(memory_space=pltpu.VMEM)],
+        out_specs=pl.BlockSpec(memory_space=pltpu.VMEM),
+        scratch_shapes=[
+            pltpu.VMEM((cols - 1,) + v.shape, v.dtype),
+            pltpu.SemaphoreType.DMA((cols - 1,)), pltpu.SemaphoreType.DMA((cols - 1,)),
+        ],
+        compiler_params=pltpu.CompilerParams(collective_id=2, has_side_effects=True),
+        name="colsum",
+    )(v)
+
+
+def add_into(target, source, count, index_target, index_source):
+    def body(i, carry):
+        a, b = index_target(i), index_source(i)
+        target[a] = (target[a].astype(f32) + source[b].astype(f32)).astype(target.dtype)
+        return carry
+
+    lax.fori_loop(0, count, body, 0)
+
+
+def tail_kernel(
+    part, ish, gi, gg, gz, go, gs, sm,
+    own_o, ish_o, oi, og, oz, oo, os, sm_o,
+    rpart, rish, i1, i2, i3, i4, g1, g2, g3, g4, z1, z2, z3, z4, o1, o2, o3, o4, s1, s2, s3, s4, s5,
+    msum, mgot, far_i, far_g, far_o, far_z, far_s, send, recv,
+):
+    t = Links(send, recv)
+    t.meet(True)
+    x, y, z, core = t.x, t.y, t.z, t.core
+    third = own_o.shape[1]
+    rows = own_o.shape[0]
+
+    sums = []
+    for off in range(1, t.cols):
+        to = t.col_peer(off)
+        sums.append(t.go(ish, rish.at[off - 1], {"col": to}))
+    parts = []
+
+    def part_item(s):
+        if s == 0:
+            for off in range(1, t.cols):
+                to = t.col_peer(off)
+                parts.append(t.go(part.at[:, lane_block(to, third)], rpart.at[off - 1], {"col": to}))
+
+    def matrix(g, a1, a2, a3, a4, far, o, by_col):
+        width = a4.shape[-1] if by_col else a4.shape[-1] // t.cols
+        copies = []
+        lead = g.shape[0]
+
+        def run(s):
+            if s == 0:
+                copies.append(t.go(g.at[:, :, 1 - core], a1, t.mate()))
+            elif s == 1:
+                copies[-1].wait_recv()
+
+                def body(i, c):
+                    for j in range(2):
+                        a1[i, j] = (a1[i, j].astype(f32) + g[i, j, core].astype(f32)).astype(bf16)
+                    return c
+
+                lax.fori_loop(0, lead, body, 0)
+                if by_col:
+                    copies.append(t.go(a1.at[:, :, :, lane_block(1 - y, width)], a2, t.other_row()))
+                else:
+                    copies.append(t.go(a1.at[1 - y], a2, t.other_row()))
+            elif s == 2:
+                copies[-1].wait_recv()
+                if by_col:
+                    def body(i, c):
+                        for j in range(2):
+                            mine = a1[i, j, :, lane_block(y, width)]
+                            a2[i, j] = (a2[i, j].astype(f32) + mine.astype(f32)).astype(bf16)
+                        return c
+
+                    lax.fori_loop(0, lead, body, 0)
+                    copies.append(t.go(a2.at[:, 1 - x], a3, t.across()))
+                else:
+                    for j in range(2):
+                        a2[j] = (a2[j].astype(f32) + a1[y, j].astype(f32)).astype(bf16)
+                    copies.append(t.go(a2.at[1 - x], a3, t.across()))
+            elif s == 3:
+                copies[-1].wait_recv()
+                if by_col:
+                    def body(i, c):
+                        a4[i] = (a3[i].astype(f32) + a2[i, x].astype(f32)).astype(bf16)
+                        return c
+
+                    lax.fori_loop(0, lead, body, 0)
+                else:
+                    a4[...] = (a3[...].astype(f32) + a2[x].astype(f32)).astype(bf16)
+                if t.groups > 1:
+                    more = [t.go(a4, far.at[off - 1], t.group_peer(off))
+                            for off in range(1, t.groups)]
+                    for c in more:
+                        c.wait()
+                    total = a4[...].astype(f32)
+                    for off in range(1, t.groups):
+                        total = total + far[off - 1].astype(f32)
+                    a4[...] = total.astype(bf16)
+                copies.clear()
+                for off in range(1, t.cols):
+                    to = t.col_peer(off)
+                    if by_col:
+                        copies.append(
+                            t.go(a4.at[to], o.at[x, core, :, lane_block(z, width)], {"col": to})
+                        )
+                    else:
+                        copies.append(
+                            t.go(a4.at[:, lane_block(to, width)], o.at[z, x, core], {"col": to})
+                        )
+                if by_col:
+                    o[x, core, :, lane_block(z, width)] = a4[z]
+                else:
+                    o[z, x, core] = a4[:, lane_block(z, width)]
+            elif s == 4:
+                for c in copies:
+                    c.wait_recv()
+                here = o.at[x, core] if by_col else o.at[:, x, core]
+                copies.append(t.go(here, here, t.across()))
+            elif s == 5:
+                copies[-1].wait_recv()
+                here = o.at[:, core] if by_col else o.at[:, :, core]
+                copies.append(t.go(here, here, t.mate()))
+            else:
+                copies[-1].wait_recv()
+
+        return run
+
+    state_copies = []
+
+    def states(s):
+        copies = state_copies
+        if s == 0:
+            copies.append(t.go(gs.at[:, :, :, 1 - core], s1, t.mate()))
+        elif s == 1:
+            copies[-1].wait_recv()
+
+            def body(i, c):
+                for j in range(2):
+                    for k in range(2):
+                        s1[i, j, k] = (
+                            s1[i, j, k].astype(f32) + gs[i, j, k, core].astype(f32)
+                        ).astype(bf16)
+                return c
+
+            lax.fori_loop(0, t.cols, body, 0)
+            copies.append(t.go(s1.at[:, 1 - y], s2, t.other_row()))
+        elif s == 2:
+            copies[-1].wait_recv()
+
+            def body(i, c):
+                for k in range(2):
+                    s2[i, k] = (s2[i, k].astype(f32) + s1[i, y, k].astype(f32)).astype(bf16)
+                return c
+
+            lax.fori_loop(0, t.cols, body, 0)
+            copies.append(t.go(s2.at[:, 1 - x], s3, t.across()))
+        elif s == 3:
+            copies[-1].wait_recv()
+
+            def body(i, c):
+                s4[i] = (s3[i].astype(f32) + s2[i, x].astype(f32)).astype(bf16)
+                return c
+
+            lax.fori_loop(0, t.cols, body, 0)
+            if t.groups > 1:
+                more = [t.go(s4, far_s.at[off - 1], t.group_peer(off))
+                        for off in range(1, t.groups)]
+                for c in more:
+                    c.wait()
+                total = s4[...].astype(f32)
+                for off in range(1, t.groups):
+                    total = total + far_s[off - 1].astype(f32)
+                s4[...] = total.astype(bf16)
+            copies.clear()
+            for off in range(1, t.cols):
+                to = t.col_peer(off)
+                copies.append(t.go(s4.at[to], s5.at[off - 1], {"col": to}))
+        elif s == 4:
+            for c in copies:
+                c.wait_recv()
+            total = s4[z].astype(f32)
+            for off in range(1, t.cols):
+                total = total + s5[off - 1].astype(f32)
+            os[z, y, x, core] = total.astype(bf16)
+            copies.clear()
+            here = os.at[z, y, x, core]
+            for off in range(1, t.cols):
+                copies.append(t.go(here, here, {"col": t.col_peer(off)}))
+        elif s == 5:
+            for c in copies:
+                c.wait_recv()
+            here = os.at[:, y, x, core]
+            copies.append(t.go(here, here, t.other_row()))
+        elif s == 6:
+            copies[-1].wait_recv()
+            here = os.at[:, :, x, core]
+            copies.append(t.go(here, here, t.across()))
+        elif s == 7:
+            copies[-1].wait_recv()
+            here = os.at[:, :, :, core]
+            copies.append(t.go(here, here, t.mate()))
+        else:
+            copies[-1].wait_recv()
+
+    few = []
+    tail_rows = sm.shape[0] * 3 // 8
+
+    def smalls(s):
+        if s == 0:
+            few.append(t.go(sm, mgot.at[0], t.mate()))
+        elif s == 1:
+            few[-1].wait_recv()
+            msum[0] = sm[...] + mgot[0]
+            few.append(t.go(msum.at[0], mgot.at[1], t.other_row()))
+        elif s == 2:
+            few[-1].wait_recv()
+            msum[1] = msum[0] + mgot[1]
+            few.append(t.go(msum.at[1], mgot.at[2], t.across()))
+        elif s == 3:
+            few[-1].wait_recv()
+            msum[2] = msum[1] + mgot[2]
+            if t.groups > 1:
+                more = [t.go(msum.at[2], mgot.at[5 + off], t.group_peer(off))
+                        for off in range(1, t.groups)]
+                for c in more:
+                    c.wait()
+                total = msum[2]
+                for off in range(1, t.groups):
+                    total = total + mgot[5 + off]
+                msum[2] = total
+            few.clear()
+            last = pl.ds(sm.shape[0] - tail_rows, tail_rows)
+            for off in range(1, t.cols):
+                few.append(t.go(msum.at[2, last], mgot.at[2 + off, last], {"col": t.col_peer(off)}))
+        elif s == 4:
+            for c in few:
+                c.wait_recv()
+            top = sm.shape[0] - tail_rows
+            sm_o[0:top] = msum[2, 0:top]
+            sm_o[top:] = msum[2, top:] + mgot[3, top:] + mgot[4, top:] + mgot[5, top:]
+
+    def late(item, limit):
+        return lambda s: item(s) if s <= limit else None
+
+    wavefront(9, [
+        late(matrix(go, o1, o2, o3, o4, far_o, oo, False), 6),
+        late(part_item, 0),
+        late(matrix(gi, i1, i2, i3, i4, far_i, oi, True), 6),
+        late(matrix(gz, z1, z2, z3, z4, far_z, oz, True), 6),
+        late(smalls, 4),
+        states,
+        late(matrix(gg, g1, g2, g3, g4, far_g, og, True), 6),
+    ])
+    for c in sums:
+        c.wait_recv()
+    ish_o[...] = ish[...] + rish[0] + rish[1] + rish[2]
+    for c in parts:
+        c.wait_recv()
+
+    def add_rows(i, c):
+        at = pl.ds(pl.multiple_of(i * 64, 64), 64)
+        total = part[at, lane_block(z, third)].astype(f32)
+        for j in range(t.cols - 1):
+            total = total + rpart[j, at].astype(f32)
+        own_o[at] = total
+        return c
+
+    lax.fori_loop(0, rows // 64, add_rows, 0)
+    t.finish()
+
+
+def tail(part, ish, gi, gg, gz, go, gs, sm):
+    cols = lax.axis_size("col")
+    groups = max(lax.axis_size("dp") // SHARE - 1, 1)
+    rows, width = part.shape
+    third = width // cols
+    own = gi.shape[1] // 2
+    q = third // SHARE
+    qo = own // SHARE
+    qs = width // (cols * 2 * SHARE)
+    zl = gz.shape[1] // 2
+    sds = jax.ShapeDtypeStruct
+    V = pltpu.VMEM
+
+    def col_scratch(w):
+        return [
+            V((cols, 2, q, 2 * w), bf16), V((cols, 2, q, w), bf16), V((cols, q, w), bf16),
+            V((cols, q, w), bf16),
+        ]
+
+    got = pl.pallas_call(
+        tail_kernel,
+        out_shape=[
+            sds((rows, third), f32), sds(ish.shape, f32),
+            sds((2, 2, q, cols * own), bf16), sds((2, 2, q, cols * own), bf16),
+            sds((2, 2, q, cols * zl), bf16), sds((cols, 2, 2, qo, third), bf16),
+            sds((cols, 2, 2, 2, qs, gs.shape[1]), bf16), sds(sm.shape, f32),
+        ],
+        in_specs=[pl.BlockSpec(memory_space=V)] * 8,
+        out_specs=[pl.BlockSpec(memory_space=V)] * 8,
+        scratch_shapes=[
+            V((cols - 1, rows, third), bf16), V((cols - 1,) + ish.shape, f32),
+        ] + col_scratch(own) + col_scratch(own) + col_scratch(zl) + [
+            V((2, 2, qo, width), bf16), V((2, qo, width), bf16), V((qo, width), bf16),
+            V((qo, width), bf16),
+            V((cols, 2, 2, qs, gs.shape[1]), bf16), V((cols, 2, qs, gs.shape[1]), bf16),
+            V((cols, qs, gs.shape[1]), bf16), V((cols, qs, gs.shape[1]), bf16),
+            V((cols - 1, qs, gs.shape[1]), bf16),
+            V((3,) + sm.shape, f32), V((6 + groups,) + sm.shape, f32),
+            V((groups, cols, q, own), bf16), V((groups, cols, q, own), bf16),
+            V((groups, qo, width), bf16),
+            V((groups, cols, q, zl), bf16), V((groups, cols, qs, gs.shape[1]), bf16),
+            pltpu.SemaphoreType.DMA((80,)), pltpu.SemaphoreType.DMA((80,)),
+        ],
+        compiler_params=pltpu.CompilerParams(
+            collective_id=3, has_side_effects=True, vmem_limit_bytes=56 * 1024 * 1024
+        ),
+        name="tail",
+    )(
+        part, ish, gi.reshape(cols, 2, 2, q, 2 * own), gg.reshape(cols, 2, 2, q, 2 * own),
+        gz.reshape(cols, 2, 2, q, 2 * zl), go.reshape(2, 2, 2, qo, width),
+        gs.reshape(cols, 2, 2, 2, qs, gs.shape[1]), sm,
+    )
+    own_o, ish_o, oi, og, oz, oo, os, sm_o = got
+    return (
+        own_o, ish_o, oi.reshape(third, -1), og.reshape(third, -1), oz.reshape(third, -1),
+        oo.reshape(cols * own, third), os.reshape(width, -1), sm_o,
+    )
 
 
 def per_device(
@@ -411,24 +970,6 @@
     inner_all = channels * cols
     col_width = width // cols
 
-    def fetch_columns(weight):
-        moved = lax.all_to_all(weight, "col", 1, 0, tiled=True)
-        return lax.all_gather(moved, "row", axis=1, tiled=True)
-
-    halo = lax.ppermute(tokens_in[-16:], "row", [(0, 1)])
-    w_inner = fetch_columns(proj_inner)
-    step_all = lax.all_gather(
-        lax.all_gather(proj_step, "col", axis=0, tiled=True), "row", axis=1, tiled=True
-    )
-    w_step = step_all.reshape(width, 2, cols, own_heads)
-    w_step = lax.dynamic_index_in_dim(w_step, col, 2, keepdims=False).reshape(width, 2 * own_heads)
-    w_step = jnp.pad(w_step, ((0, 0), (0, 128 - 2 * own_heads)))
-    w_gate = fetch_columns(proj_gate)
-    w_out = lax.all_gather(
-        lax.all_to_all(proj_out, "col", 0, 1, tiled=True), "row", axis=0, tiled=True
-    )
-    cot_all = lax.all_gather(cotangent, "col", axis=1, tiled=True)
-
     heads_own = jnp.stack([step_bias, decay_log, skip_gain])
     own = jnp.concatenate(
         [
@@ -440,7 +981,14 @@
         ],
         0,
     )
-    both = lax.all_gather(own, "row", axis=0)
+    pieces = jnp.pad(
+        proj_step.reshape(col_width, cols, own_heads), ((0, 0), (0, 0), (0, 128 - own_heads))
+    ).reshape(col_width, cols * 128)
+    w_inner, w_gate, w_out, w_step, cot_all, both, halo = fetch(
+        proj_inner, proj_gate, proj_out, pieces, cotangent, own, tokens_in[-16:]
+    )
+    w_step = jnp.concatenate([w_step[:, :own_heads], w_step[:, 128:128 + own_heads]], 1)
+    w_step = jnp.pad(w_step, ((0, 0), (0, 128 - 2 * own_heads)))
     par = jnp.concatenate([both[0], both[1]], 1)
     hp = jnp.concatenate(
         [both[i, 6, : 3 * own_heads].reshape(3, own_heads) for i in range(2)], 1
@@ -546,7 +1094,7 @@
         name="scan",
     )(x_low, wr, r, step, meta, docrow, fresh, state_in, head, par, gate, ggated)
 
-    sums = lax.psum(sums, "col")
+    sums = col_sum(sums)
 
     back3 = pl.BlockSpec((1, 128, channels), lambda i: (blocks - 1 - i, 0, 0))
     gated, g_gate, gy, dr, dsf, dsout, acc1 = pl.pallas_call(
@@ -628,44 +1176,18 @@
     inverse = lax.rsqrt(jnp.mean(wide * wide, -1, keepdims=True) + epsilon)
     input_share = jnp.sum(normed_grad * norm_gain * wide, -1)
     gain_share = jnp.sum(normed_grad * (wide * inverse), 0)
-    own_grad = lax.psum_scatter(
-        normed_grad.astype(bf16), "col", scatter_dimension=1, tiled=True
-    ).astype(f32)
-    input_total = lax.psum(input_share, "col")[:, None]
-    gain_cols = lax.dynamic_slice_in_dim(norm_gain, col * col_width, col_width, 0)
-    grad_input = inverse * (own_grad * gain_cols) - own_tokens * inverse**3 * (input_total / width)
-    grad_tokens = (grad_input + cotangent.astype(f32)).astype(bf16)
 
     def weight_grad(left, right):
         return lax.dot_general(
             left, right, (((0,), (0,)), ((), ())), preferred_element_type=f32
-        )
-
-    def reduce_columns(part):
-        part = part.reshape(width, 2, own_ch).astype(bf16)
-        part = lax.psum_scatter(part, "row", scatter_dimension=1)
-        part = lax.psum(part, "dp")
-        return lax.all_to_all(part, "col", 0, 1, tiled=True).astype(f32)
-
-    grad_gate = reduce_columns(weight_grad(normed, g_gate))
-    grad_inner = reduce_columns(weight_grad(normed, gx))
-    go = lax.psum_scatter(
-        grad_out_part.astype(bf16), "row", scatter_dimension=0, tiled=True
-    )
-    go = lax.psum(go, "dp")
-    grad_out = lax.all_to_all(go, "col", 1, 0, tiled=True).astype(f32)
-
-    g_rest = weight_grad(normed, jnp.concatenate([gs, gz], 1))
-    grad_states = lax.psum(g_rest[:, :256], ("dp", "row", "col"))
-    gz_part = g_rest[:, 256:256 + 2 * own_heads].reshape(width, 2, own_heads)
-    gz_own = lax.psum(gz_part, ("dp", "row"))
-    gz_all = lax.all_gather(gz_own, "col", axis=0)
-    gz_all = lax.dynamic_index_in_dim(gz_all, row, 2, keepdims=False)
-    gz_all = lax.dynamic_slice_in_dim(gz_all, col * col_width, col_width, 1)
-    grad_step = jnp.moveaxis(gz_all, 0, 1).reshape(col_width, cols * own_heads)
+        ).astype(bf16)
 
     def head_sum(values):
         return values.reshape(2 * own_heads, HEAD).sum(-1)
+
+    def lanes(values, multiple):
+        values = values.reshape(-1)
+        return jnp.pad(values, (0, multiple * 128 - values.shape[0])).reshape(multiple, 128)
 
     small = jnp.concatenate(
         [
@@ -677,15 +1199,42 @@
         ],
         1,
     )
-    small = lax.psum(small, ("dp", "row"))
+    few = jnp.concatenate(
+        [lanes(small, 40), lanes(jnp.concatenate([accs[0:5].reshape(-1), gain_share]), 24)], 0
+    )
+    gz_rows = jnp.concatenate(
+        [
+            jnp.pad(gz[:, i * own_heads:(i + 1) * own_heads], ((0, 0), (0, 128 - own_heads)))
+            for i in range(2)
+        ],
+        1,
+    )
+    own_grad, input_total, oi, og, oz, oo, os, few = tail(
+        normed_grad.astype(bf16), input_share.reshape(8, -1), weight_grad(normed, gx),
+        weight_grad(normed, g_gate), weight_grad(normed, gz_rows), grad_out_part.astype(bf16),
+        weight_grad(normed, gs), few,
+    )
+    input_total = input_total.reshape(tokens, 1)
+    gain_cols = lax.dynamic_slice_in_dim(norm_gain, col * col_width, col_width, 0)
+    grad_input = inverse * (own_grad * gain_cols) - own_tokens * inverse**3 * (input_total / width)
+    grad_tokens = (grad_input + cotangent.astype(f32)).astype(bf16)
+    grad_inner = oi.astype(f32)
+    grad_gate = og.astype(f32)
+    grad_out = oo.astype(f32)
+    grad_states = os.astype(f32)
+    grad_step = oz.reshape(col_width, cols, 128)[:, :, :own_heads].astype(f32)
+    grad_step = grad_step.reshape(col_width, cols * own_heads)
+    small = few[:40].reshape(-1)[: small.size].reshape(2, -1)
     small = lax.dynamic_index_in_dim(small, row, 0, keepdims=False)
     grad_conv_inner = small[: 4 * own_ch].reshape(4, own_ch)
     grad_conv_inner_bias = small[4 * own_ch:5 * own_ch]
     grad_gate_gain = small[5 * own_ch:6 * own_ch]
     rest = small[6 * own_ch:].reshape(3, own_heads)
-    accs = lax.psum(accs, ("dp", "row", "col"))
-    gain_all = lax.psum(gain_share, ("dp", "row", "col"))
-    grad_norm_gain = lax.dynamic_slice_in_dim(gain_all, col * col_width, col_width, 0)
+    summed = few[40:].reshape(-1)
+    accs = summed[: 5 * 256].reshape(5, 256)
+    grad_norm_gain = lax.dynamic_slice_in_dim(
+        summed, 5 * 256 + col * col_width, col_width, 0
+    )
 
     return (
         mixed_out,

time: 834 us -> 498 us (0.60)
  waiting for transfers between devices: 317 us -> 0.03 us
  blocking collectives: 291 us -> 0 us
  Pallas kernels: 60.8 us -> 337 us
  local copies, waits for them, and re-layouts: 58.9 us -> 43.6 us
  matrix products: 55.5 us -> 67.8 us
  other arithmetic: 13.9 us -> 22.4 us
    pallas_call x0 -> x3, Pallas kernels: none -> 276 us  [the longest x1 159 us: tail(): pl.pallas_call(tail_kernel, out_shape=[sds((rows, third), f32), sds(ish.s...]
    all_to_all x5 -> x0, blocking collectives: 160 us -> none  [the longest x2 65.5 us: fetch_columns(): moved = lax.all_to_all(weight, 'col', 1, 0, tiled=True)]
    unnamed x14 -> x2, waiting for transfers between devices: 119 us -> 0.02 us
    psum x4 -> x0, blocking collectives: 93.1 us -> none  [the longest x1 39.7 us: per_device(): gain_all = lax.psum(gain_share, ('dp', 'row', 'col'))]
    psum x3 -> x0, waiting for transfers between devices: 73.6 us -> none  [the longest x1 42.3 us: per_device(): grad_states = lax.psum(g_rest[:, :256], ('dp', 'row', 'col'))]
    all_gather x4 -> x0, waiting for transfers between devices: 50.5 us -> none  [the longest x1 50.5 us: per_device(): cot_all = lax.all_gather(cotangent, 'col', axis=1, tiled=True)]
    reduce_scatter x3 -> x0, waiting for transfers between devices: 46.6 us -> none  [the longest x2 46.6 us: reduce_columns(): part = lax.psum_scatter(part, 'row', scatter_dimension=1)]
    all_gather x4 -> x0, blocking collectives: 38.1 us -> none  [the longest x1 14 us: per_device(): gz_all = lax.all_gather(gz_own, 'col', axis=0)]
  transfers between devices with their start and end apart: 18 -> 5, of which waited for: 10 -> 0; matrix products, arithmetic and copies ran while one was open for 13% -> 20% of each run, Pallas kernels for 5% -> 37%
where the time goes in v2:
time: 498 us; the launch traced here: 492 us
  Pallas kernels  337 us (68%)
  matrix products  67.8 us (14%)
  local copies, waits for them, and re-layouts  43.6 us (9%)
  other arithmetic  22.4 us (4%)
  between operations  15 us (3%)
  starting transfers between devices  6.44 us (1%)
    pallas_call x1, Pallas kernels, tail(): pl.pallas_call(tail_kernel, out_shape=[sds((rows, third), f32), sds(ish.s...  159 us
    pallas_call x1, Pallas kernels, fetch(): pl.pallas_call(fetch_kernel, out_shape=shapes, in_specs=[pl.BlockSpec(mem...  92.7 us
    dot_general x5, matrix products, mm_nt(): lax.dot_general(a, b, (((1,), (1,)), ((), ())), preferred_element_type=f32)  30.9 us
    pallas_call x1, Pallas kernels, col_sum(): pl.pallas_call(col_sum_kernel, out_shape=jax.ShapeDtypeStruct(v.shape, v....  24.4 us
    pallas_call x1, Pallas kernels, per_device(): pl.pallas_call(back_kernel, grid=(blocks,), in_specs=[by_rows(channels, b...  22.6 us
    dot_general x4, matrix products, weight_grad(): lax.dot_general(left, right, (((0,), (0,)), ((), ())), preferred_element_...  20.4 us
    pallas_call x1, Pallas kernels, per_device(): pl.pallas_call(entry_kernel, grid=(blocks,), in_specs=[by_rows(width), wh...  15.8 us
    pallas_call x1, Pallas kernels, per_device(): pl.pallas_call(scan_kernel, grid=(blocks,), in_specs=[by_rows(channels),...  11.4 us
  transfers between devices with their start and end apart: 5, of which 0 were waited for; matrix products, arithmetic and copies ran while one was open for 20% of the time, Pallas kernels for 37%

profile of v2, /device:TPU:0, one launch (start us, length us, event | category | flops | bytes accessed | tf_op | source)
XLA Modules:
  0.0 491.9 jit_solution(3268460212982897722)
XLA Ops:
  7.2 0.7 reshape.248
  8.0 0.9 copy.94.step
  9.0 1.4 slice.201.halo
  10.4 0.7 pad_maximum_fusion.3
  11.2 0.7 broadcast_in_dim.31
  11.8 0.7 broadcast_in_dim.32
  12.5 1.3 concatenate.39.par
  13.8 92.7 %fetch.1 = (bf16[4,2,2,96,768]{4,3,2,1,0:T(8,128)(2,1)}, bf16[4,2,2,96,768]{4,3,2,1,0:T(8,128)(2,1)}, bf16[2,2,2,96,1536]{4,3,2,1,0:T(8,128)(2,1)}, bf16[4,2,2,9...) custom-call(bf16[384,1536]{1,0:T(8,128)(2,1)} %inner.1, ...), custom_call_target="tpu_custom_call" | custom-call | tf_op jit(solution)/shard_map/fetch/pallas_call | solution.py:586
  106.5 0.7 slice_reduce_fusion.6
  107.2 0.7 slice_bitcast_fusion.3
  108.9 0.8 convert_reduce_fusion
  109.8 0.7 pad_maximum_fusion.5
  110.9 1.0 copy.86.meta
  112.1 1.2 fusion.37
  114.0 0.9 pad.41.w_step
  117.4 15.8 %entry.1 = (bf16[1024,1536]{1,0:T(8,128)(2,1)}, bf16[1024,768]{1,0:T(8,128)(2,1)}, bf16[1024,256]{1,0:T(8,128)(2,1)}, bf16[1024,768]{1,0:T(8,128)(2,1)}, bf16[10...) custom-call(bf16[1024,1536]{1,0:T(8,128)(2,1)} %tok.1, ...), custom_call_target="tpu_custom_call" | custom-call | tf_op jit(solution)/shard_map/entry/pallas_call | solution.py:1040
  133.2 2.1 collective-permute-start
  136.9 7.0 %fusion.41.gate = f32[1024,768]{1,0:T(8,128)} fusion(bf16[1024,1536]{1,0:T(8,128)(2,1)} %get-tuple-element.97, bf16[1536,768]{1,0:T(8,128)(2,1)} %bitcast.158), kind=kOutput, calls=%fused_computation.122 | convolution fusion | flops 2415919104 | bytes 8650752 | tf_op jit(solution)/shard_map/dot_general | solution.py:20
  144.0 4.3 fusion.42.ggated
  150.1 1.4 stack.134.hmeta
  152.2 0.7 copy-done.9
  152.9 11.4 %scan.1 = (f32[1024,768]{1,0:T(8,128)}, f32[8,1024]{1,0:T(8,128)}, bf16[4,128,768]{2,1,0:T(8,128)(2,1)}) custom-call(bf16[1024,768]{1,0:T(8,128)(2,1)} %get-tuple-element.91.x, bf16[1024,256]{1,0:T(8,128)(2,1)} %get-tuple-element.92.wr, f32[1024,128]{1,0:T(8,128)} %get-tuple-element.93.r_ref, f32[1024,128]{1,0:T(8,128)} %get-tuple-element.94.step_ref, ...), custom_call_target="tpu_custom_call" | custom-call | tf_op jit(solution)/shard_map/scan/pallas_call | solution.py:1075
  164.4 24.4 %colsum.1.sums = f32[8,1024]{1,0:T(8,128)} custom-call(f32[8,1024]{1,0:T(8,128)} %get-tuple-element.102.v), custom_call_target="tpu_custom_call" | custom-call | tf_op jit(solution)/shard_map/colsum/pallas_call | solution.py:623
  188.8 11.0 %turn.1 = (bf16[1024,768]{1,0:T(8,128)(2,1)}, bf16[1024,768]{1,0:T(8,128)(2,1)}, bf16[1024,768]{1,0:T(8,128)(2,1)}, f32[1024,128]{1,0:T(8,128)}, f32[4,128,768]{...) custom-call(f32[1024,768]{1,0:T(8,128)} %get-tuple-element.101.y_ref, f32[1024,768]{1,0:T(8,128)} %fusion.41.gate, ...), custom_call_target="tpu_custom_call" | custom-call | tf_op jit(solution)/shard_map/turn/pallas_call | solution.py:1100
  199.8 5.5 %convolution_convert_fusion.1 = bf16[768,1536]{1,0:T(8,128)(2,1)} fusion(bf16[1024,768]{1,0:T(8,128)(2,1)} %get-tuple-element.103, bf16[1024,1536]{1,0:T(8,128)(2,1)S(1)} %copy-done.26), kind=kOutput, calls=%fused_computation.9 | convolution fusion | flops 2417098752 | bytes 7077888 | tf_op jit(solution)/shard_map/dot_general | solution.py:1129
  205.3 4.0 convolution_convert_fusion
  209.3 1.5 collective-permute-start.1
  210.8 1.4 slice_reduce_fusion
  212.2 1.4 reshape_squeeze.19
  213.6 1.3 reduce_sum.38
  214.9 1.3 reshape.265
  216.2 1.3 reshape_squeeze.17
  217.5 6.4 %convolution_convert_fusion.2 = bf16[1536,768]{1,0:T(8,128)(2,1)} fusion(bf16[1024,1536]{1,0:T(8,128)(2,1)} %get-tuple-element.97, bf16[1024,768]{1,0:T(8,128)(2,1)} %get-tuple-element.104), kind=kOutput, calls=%fused_computation.10 | convolution fusion | flops 2417098752 | bytes 7077888 | tf_op jit(solution)/shard_map/dot_general | solution.py:1181
  223.9 4.8 copy.95
  228.7 7.4 %fusion.43 = f32[1024,1536]{1,0:T(8,128)} fusion(bf16[1024,768]{1,0:T(8,128)(2,1)} %get-tuple-element.104, bf16[1536,768]{1,0:T(8,128)(2,1)} %bitcast.159), kind=kOutput, calls=%fused_computation.124 | convolution fusion | flops 2415919104 | bytes 10223616 | tf_op jit(solution)/shard_map/dot_general | solution.py:24
  236.1 0.8 copy-done.10
  236.9 22.6 %back.1 = (bf16[1024,768]{1,0:T(8,128)(2,1)}, bf16[1024,256]{1,0:T(8,128)(2,1)}, bf16[1024,128]{1,0:T(8,128)(2,1)}, f32[8,768]{1,0:T(8,128)}, f32[8,256]{1,0:T(8...) custom-call(bf16[1024,768]{1,0:T(8,128)(2,1)} %get-tuple-element.91.x, ...), custom_call_target="tpu_custom_call" | custom-call | tf_op jit(solution)/shard_map/back/pallas_call | solution.py:1133
  259.5 4.6 fusion.35
  264.2 0.8 slice.227
  265.0 0.7 slice_multiply_fusion
  265.7 0.7 slice_reduce_fusion.3
  266.8 1.3 collective-permute-start.3
  268.2 1.5 collective-permute-start.2
  269.8 3.9 convolution_convert_fusion.5
  273.7 1.3 add_dynamic-update-slice_fusion.1
  275.0 4.0 convolution_convert_fusion.4
  279.0 1.3 add_dynamic-update-slice_fusion
  280.3 7.6 %fusion.44 = f32[1024,1536]{1,0:T(8,128)} fusion(bf16[1024,768]{1,0:T(8,128)(2,1)} %add_dynamic-update-slice_fusion, bf16[1536,768]{1,0:T(8,128)(2,1)} %bitcast.121), kind=kOutput, calls=%fused_computation.125 | convolution fusion | flops 2415919104 | bytes 10223616 | tf_op jit(solution)/shard_map/dot_general | solution.py:24
  288.0 6.9 %fusion.3 = (f32[1536]{0:T(1024)S(1)}, f32[1024]{0:T(1024)}, bf16[1024,1536]{1,0:T(8,128)(2,1)}) fusion(bf16[1024,1536]{1,0:T(8,128)(2,1)S(1)} %copy-done, f32[1024]{0:T(1024)S(1)} %get-tuple-element.165, f32[1536]{0:T(1024)S(1)} %copy-done.12, f32[1024,1536]{1,0:T(8,128)S(1)} %bitcast.116, f32[1024,1536]{1,0:T(8,128)S(1)} %bitcast.119, ...), kind=kOutput, calls=%fused_computation.6 | convolution fusion | flops 822605312 | bytes 26497024 | tf_op jit(solution)/shard_map/dot_general | solution.py:24
  295.5 6.0 %convolution_convert_fusion.3 = bf16[1536,768]{1,0:T(8,128)(2,1)} fusion(bf16[1024,1536]{1,0:T(8,128)(2,1)} %get-tuple-element.97, bf16[1024,768]{1,0:T(8,128)(2,1)S(1)} %copy-done.24), kind=kOutput, calls=%fused_computation.11 | convolution fusion | flops 2417098752 | bytes 7077888 | tf_op jit(solution)/shard_map/dot_general | solution.py:1181
  301.5 158.9 %tail.1 = (f32[1024,384]{1,0:T(8,128)}, f32[8,128]{1,0:T(8,128)}, bf16[2,2,96,1536]{3,2,1,0:T(8,128)(2,1)}, bf16[2,2,96,1536]{3,2,1,0:T(8,128)(2,1)}, bf16[2,2,9...) custom-call(bf16[1024,1536]{1,0:T(8,128)(2,1)} %get-tuple-element.14, ...), custom_call_target="tpu_custom_call" | custom-call | tf_op jit(solution)/shard_map/tail/pallas_call | solution.py:917
  460.4 1.1 reshape_reshape.3
  461.5 0.9 copy.99
  462.4 1.4 reshape.291
  464.4 0.7 slice_bitcast_fusion
  466.5 0.8 slice_bitcast_fusion.1
  469.2 1.2 slice_bitcast_fusion.4
  470.4 0.7 multiply_bitcast_fusion
  471.1 2.4 bitcast_convert_fusion.3
  473.5 1.7 bitcast_convert_fusion
  475.2 1.8 bitcast_convert_fusion.1
  477.0 1.8 bitcast_convert_fusion.2
  478.7 2.3 copy.96
  481.0 3.6 fusion.8
  (138 shorter events, 14.1 us)
Async XLA Ops:
  7.2 471.6 %reduce-scatter.4.cloned.1.call-start = ((), (), s32[]{:S(2)}) async-start(), calls=%async_computation.1 | async-start | bytes 3932160
  13.8 94.1 %copy-start.18 = (s32[1,2048]{1,0:T(1,128)S(1)}, s32[1,2048]{1,0:T(1,128)}, u32[]{:S(2)}) copy-start(s32[1,2048]{1,0:T(1,128)} %param.22) | copy-start | bytes 24580
  108.0 6.9 %copy-start.12 = (f32[1536]{0:T(1024)S(1)}, f32[1536]{0:T(1024)}, u32[]{:S(2)}) copy-start(f32[1536]{0:T(1024)} %param.23) | copy-start | bytes 18436
  108.1 7.4 %copy-start.11 = (f32[1024]{0:T(1024)}, f32[1024]{0:T(1024)S(1)}, u32[]{:S(2)}) copy-start(f32[1024]{0:T(1024)S(1)} %get-tuple-element.146) | copy-start | bytes 12292
  109.8 6.4 %copy-start.20 = (f32[4,256]{1,0:T(4,128)S(1)}, f32[4,256]{1,0:T(4,128)}, u32[]{:S(2)}) copy-start(f32[4,256]{1,0:T(4,128)} %param.30) | copy-start | bytes 12292
  109.8 6.4 %copy-start.21 = (f32[256]{0:T(256)S(1)}, f32[256]{0:T(256)}, u32[]{:S(2)}) copy-start(f32[256]{0:T(256)} %param.31) | copy-start | bytes 3076
  114.0 19.2 %copy-start.2 = (bf16[1536,12]{1,0:T(8,128)(2,1)}, bf16[1536,12]{1,0:T(8,128)(2,1)S(1)}, u32[]{:S(2)}) copy-start(bf16[1536,12]{1,0:T(8,128)(2,1)S(1)} %copy.85) | copy-start | bytes 110596
  133.2 18.9 %collective-permute-start = (f32[128,768]{1,0:T(8,128)}, f32[128,768]{1,0:T(8,128)S(1)}, u32[]{:S(2)}, u32[]{:S(2)}) collective-permute-start(f32[128,768]{1,0:T(8,128)} %get-tuple-element.96), channel_id=1, source_target_pairs={{0,4},{1,5},{2,6},{3,7},{8,12},{9,13},{10,14},{11,15},{16,20},{17,... | collective-permute-start | bytes 1179656 | tf_op jit(solution)/shard_map/ppermute | solution.py:1071
  136.9 7.0 %copy-start.25 = (bf16[1024,1536]{1,0:T(8,128)(2,1)S(1)}, bf16[1024,1536]{1,0:T(8,128)(2,1)}, u32[]{:S(2)}) copy-start(bf16[1024,1536]{1,0:T(8,128)(2,1)} %get-tuple-element.99) | copy-start | bytes 9437188
  136.9 7.0 %copy-start.27 = (bf16[2,2,2,96,1536]{4,3,2,1,0:T(8,128)(2,1)S(1)}, bf16[2,2,2,96,1536]{4,3,2,1,0:T(8,128)(2,1)}, u32[]{:S(2)}) copy-start(bf16[2,2,2,96,1536]{4,3,2,1,0:T(8,128)(2,1)} %get-tuple-element.100) | copy-start | bytes 7077892
  144.0 7.5 %copy-start = (bf16[1024,1536]{1,0:T(8,128)(2,1)S(1)}, bf16[1024,1536]{1,0:T(8,128)(2,1)}, u32[]{:S(2)}) copy-start(bf16[1024,1536]{1,0:T(8,128)(2,1)} %tok.1) | copy-start | bytes 9437188
  152.2 0.7 copy-start.9
  188.8 11.0 %copy-start.26 = (bf16[1024,1536]{1,0:T(8,128)(2,1)S(1)}, bf16[1024,1536]{1,0:T(8,128)(2,1)}, u32[]{:S(2)}) copy-start(bf16[1024,1536]{1,0:T(8,128)(2,1)} %get-tuple-element.99) | copy-start | bytes 9437188
  199.7 5.5 %copy-start.28 = (bf16[2,2,2,96,1536]{4,3,2,1,0:T(8,128)(2,1)S(1)}, bf16[2,2,2,96,1536]{4,3,2,1,0:T(8,128)(2,1)}, u32[]{:S(2)}) copy-start(bf16[2,2,2,96,1536]{4,3,2,1,0:T(8,128)(2,1)} %get-tuple-element.100) | copy-start | bytes 7077892
  199.8 5.5 %copy-start.29 = (bf16[1024,768]{1,0:T(8,128)(2,1)S(1)}, bf16[1024,768]{1,0:T(8,128)(2,1)}, u32[]{:S(2)}) copy-start(bf16[1024,768]{1,0:T(8,128)(2,1)} %get-tuple-element.103) | copy-start | bytes 4718596
  209.3 26.8 %collective-permute-start.1 = (f32[128,768]{1,0:T(8,128)}, f32[128,768]{1,0:T(8,128)S(1)}, u32[]{:S(2)}, u32[]{:S(2)}) collective-permute-start(f32[128,768]{1,0:T(8,128)} %get-tuple-element.110), channel_id=1, source_target_pairs={{4,0},{5,1},{6,2},{7,3},{12,8},{13,9},{14,10},{15,11},{20,16},{21,... | collective-permute-start | bytes 1179656 | tf_op jit(solution)/shard_map/ppermute | solution.py:1124
  236.1 0.8 copy-start.10
  236.9 22.6 %copy-start.3 = (bf16[1536,12]{1,0:T(8,128)(2,1)S(1)}, bf16[1536,12]{1,0:T(8,128)(2,1)}, u32[]{:S(2)}) copy-start(bf16[1536,12]{1,0:T(8,128)(2,1)} %copy-done.2) | copy-start | bytes 110596
  259.5 4.7 copy-start.1
  259.5 7.1 %copy-start.14 = (f32[8,768]{1,0:T(8,128)S(1)}, f32[8,768]{1,0:T(8,128)}, u32[]{:S(2)}) copy-start(f32[8,768]{1,0:T(8,128)} %get-tuple-element.122) | copy-start | bytes 73732
  259.5 7.1 %copy-start.15 = (f32[2,384]{1,0:T(2,128)S(1)}, f32[2,384]{1,0:T(2,128)}, u32[]{:S(2)}) copy-start(f32[2,384]{1,0:T(2,128)} %reshape_squeeze.17) | copy-start | bytes 9220
  259.5 7.1 %copy-start.22 = (f32[2,6]{1,0:T(2,128)S(1)}, f32[2,6]{1,0:T(2,128)}, u32[]{:S(2)}) copy-start(f32[2,6]{1,0:T(2,128)} %reshape.265) | copy-start | bytes 148
  259.5 7.3 %copy-start.17 = (f32[8,256]{1,0:T(8,128)S(1)}, f32[8,256]{1,0:T(8,128)}, u32[]{:S(2)}) copy-start(f32[8,256]{1,0:T(8,128)} %get-tuple-element.121) | copy-start | bytes 24580
  259.5 8.6 %copy-start.13 = (f32[8,768]{1,0:T(8,128)S(1)}, f32[8,768]{1,0:T(8,128)}, u32[]{:S(2)}) copy-start(f32[8,768]{1,0:T(8,128)} %get-tuple-element.118) | copy-start | bytes 73732
  259.5 10.2 %copy-start.23 = (pred[128]{0:T(512)(128)(4,1)S(1)}, pred[128]{0:T(512)(128)(4,1)}, u32[]{:S(2)}) copy-start(pred[128]{0:T(512)(128)(4,1)} %constant.97.clone.1) | copy-start | bytes 388
  266.8 6.8 %collective-permute-start.3 = (bf16[8,256]{1,0:T(8,128)(2,1)S(1)}, bf16[8,256]{1,0:T(8,128)(2,1)S(1)}, u32[]{:S(2)}, u32[]{:S(2)}) collective-permute-start(bf16[8,256]{1,0:T(8,128)(2,1)S(1)} %convert.25), channel_id=1, source_target_pairs={{4,0},{5,1},{6,2},{7,3},{12,8},{13,9},{14,10},{15,11},{20,16},{21,... | collective-permute-start | bytes 12296 | tf_op jit(solution)/shard_map/ppermute | solution.py:1168
  268.2 10.8 %collective-permute-start.2 = (bf16[8,768]{1,0:T(8,128)(2,1)S(1)}, bf16[8,768]{1,0:T(8,128)(2,1)S(1)}, u32[]{:S(2)}, u32[]{:S(2)}) collective-permute-start(bf16[8,768]{1,0:T(8,128)(2,1)S(1)} %convert.26), channel_id=1, source_target_pairs={{4,0},{5,1},{6,2},{7,3},{12,8},{13,9},{14,10},{15,11},{20,16},{21,... | collective-permute-start | bytes 36872 | tf_op jit(solution)/shard_map/ppermute | solution.py:1168
  269.8 3.9 copy-start.19
  275.0 13.0 %slice-start = ((s8[6291456]{0:T(1024)(128)(4,1)}), s8[4194304]{0:T(1024)(128)(4,1)S(1)}, s32[]{:S(2)}) async-start(s8[6291456]{0:T(1024)(128)(4,1)} %bitcast.115), calls=%async_computation.2 | async-start | bytes 8388608
  275.0 13.0 %slice-start.2 = ((s8[6291456]{0:T(1024)(128)(4,1)}), s8[4194304]{0:T(1024)(128)(4,1)S(1)}, s32[]{:S(2)}) async-start(s8[6291456]{0:T(1024)(128)(4,1)} %bitcast.118), calls=%async_computation.4 | async-start | bytes 8388608
  280.3 7.6 %slice-start.1 = ((s8[6291456]{0:T(1024)(128)(4,1)}), s8[2097152]{0:T(1024)(128)(4,1)S(1)}, s32[]{:S(2)}) async-start(s8[6291456]{0:T(1024)(128)(4,1)} %bitcast.115), calls=%async_computation.3 | async-start | bytes 4194304
  280.3 7.6 %slice-start.3 = ((s8[6291456]{0:T(1024)(128)(4,1)}), s8[2097152]{0:T(1024)(128)(4,1)S(1)}, s32[]{:S(2)}) async-start(s8[6291456]{0:T(1024)(128)(4,1)} %bitcast.118), calls=%async_computation.5 | async-start | bytes 4194304
  280.3 7.6 %copy-start.4 = (bf16[1536,256]{1,0:T(8,128)(2,1)S(1)}, bf16[1536,256]{1,0:T(8,128)(2,1)}, u32[]{:S(2)}) copy-start(bf16[1536,256]{1,0:T(8,128)(2,1)} %w_states.1) | copy-start | bytes 2359300
  280.3 7.6 %copy-start.8 = (bf16[1024,256]{1,0:T(8,128)(2,1)S(1)}, bf16[1024,256]{1,0:T(8,128)(2,1)}, u32[]{:S(2)}) copy-start(bf16[1024,256]{1,0:T(8,128)(2,1)} %add_dynamic-update-slice_fusion.1) | copy-start | bytes 1572868
  288.0 7.5 %copy-start.24 = (bf16[1024,768]{1,0:T(8,128)(2,1)S(1)}, bf16[1024,768]{1,0:T(8,128)(2,1)}, u32[]{:S(2)}) copy-start(bf16[1024,768]{1,0:T(8,128)(2,1)} %add_dynamic-update-slice_fusion) | copy-start | bytes 4718596
  466.5 7.1 %copy-start.7 = (bf16[4,2,2,96,384]{4,3,2,1,0:T(8,128)(2,1)S(1)}, bf16[4,2,2,96,384]{4,3,2,1,0:T(8,128)(2,1)}, u32[]{:S(2)}) copy-start(bf16[4,2,2,96,384]{4,3,2,1,0:T(8,128)(2,1)} %get-tuple-element.133) | copy-start | bytes 3538948
  473.5 1.7 copy-start.6
  475.2 1.8 copy-start.5
  477.0 4.1 copy-start.16
Sparse Core Ops, SparseCore 0:
  228.8 61.7 reduce-scatter.3

commit v3 on v2

--- a/solution.py
+++ b/solution.py
@@ -80,179 +80,6 @@
     wide = tok.astype(f32)
     inverse = lax.rsqrt(jnp.mean(wide * wide, -1, keepdims=True) + epsilon)
     return (wide * inverse * gain).astype(bf16)
-
-
-def entry_kernel(
-    tok, halo, ngain, w_inner, w_states, w_step, par, spar, head, meta,
-    normed_o, pre_o, spre_o, sd_o, ssd_o, x_o, wr_o, step_o, r_o, sig_o, fresh_o, end_o,
-    hpre_o, hspre_o,
-    xbuf, sbuf, mem,
-):
-    at = pl.program_id(0)
-    channels = w_inner.shape[1]
-    gain = ngain[...]
-
-    @pl.when(at == 0)
-    def _():
-        hn = rms_rows(halo[...], gain)
-        hp = mm(hn, w_inner[...])[8:16]
-        hs = mm(hn, w_states[...])[8:16]
-        xbuf[0:8, :] = hp
-        sbuf[0:8, :] = hs
-        hpre_o[...] = hp
-        hspre_o[...] = hs
-        mem[...] = jnp.zeros_like(mem)
-
-    @pl.when(at > 0)
-    def _():
-        xbuf[0:8, :] = xbuf[SPAN:SPAN + 8, :]
-        sbuf[0:8, :] = sbuf[SPAN:SPAN + 8, :]
-
-    normed = rms_rows(tok[...], gain)
-    normed_o[...] = normed
-    x_pre = mm(normed, w_inner[...])
-    s_pre = mm(normed, w_states[...])
-    xbuf[8:SPAN + 8, :] = x_pre
-    sbuf[8:SPAN + 8, :] = s_pre
-    pre_o[...] = x_pre.astype(bf16)
-    spre_o[...] = s_pre.astype(bf16)
-
-    def conv_silu(buf, here, taps):
-        v = taps[4:5, :] + taps[0:1, :] * here
-        for k in range(1, 4):
-            v = v + meta[:, k:k + 1] * (taps[k:k + 1, :] * buf[8 - k:8 - k + SPAN, :])
-        sg = sigmoid(v)
-        return v * sg, sg * (1.0 + v * (1.0 - sg))
-
-    act, slope = conv_silu(xbuf, x_pre, par)
-    x_low = act.astype(bf16)
-    x_o[...] = x_low
-    sd_o[...] = slope.astype(bf16)
-    sact, sslope = conv_silu(sbuf, s_pre, spar)
-    wr = sact.astype(bf16)
-    wr_o[...] = wr
-    ssd_o[...] = sslope.astype(bf16)
-
-    raw = mm(normed, w_step[...]) + head[0:1, :]
-    step = jnp.maximum(raw, 0.0) + jnp.log1p(jnp.exp(-jnp.abs(raw)))
-    sig_o[...] = sigmoid(raw)
-    step_o[...] = step
-    r = split_mm(lower_ones(), step * head[1:2, :])
-    r_o[...] = r
-    last = r[SPAN - 1:SPAN, :]
-    to_end = jnp.exp2(jnp.minimum(last - r, 0.0)) * meta[:, 5:6]
-    spread = spread_matrix(channels)
-    coef = mm_split(to_end * step, spread)
-    w_t = jnp.transpose(wr[:, 0:128].astype(f32)).astype(bf16)
-    fresh = mm(w_t, (coef * x_low.astype(f32)).astype(bf16))
-    fresh_o[...] = fresh[None]
-    keep = mm_split(jnp.broadcast_to(jnp.exp2(last) * meta[0:1, 6:7], (8, 128)), spread)[0:1]
-    mem[...] = keep * mem[...] + fresh
-    end_o[...] = mem[...]
-
-
-def scan_kernel(
-    x, wr, r_ref, step_ref, meta, docrow, fresh, state_in, head, par, gate, ggated,
-    y_o, sums_o, sprev_o,
-    mem, ybuf,
-):
-    at = pl.program_id(0)
-    channels = x.shape[1]
-
-    @pl.when(at == 0)
-    def _():
-        mem[...] = state_in[...]
-
-    spread = spread_matrix(channels)
-    w_low = wr[:, 0:128]
-    r_low = wr[:, 128:256]
-    r = r_ref[...]
-    r_t = jnp.transpose(r)
-    rows = lax.broadcasted_iota(jnp.int32, (SPAN, SPAN), 0)
-    cols = lax.broadcasted_iota(jnp.int32, (SPAN, SPAN), 1)
-    allowed = (rows >= cols) & (meta[:, 0:1] == docrow[...])
-    scores = jnp.where(allowed, mm_nt(r_low, w_low), 0.0)
-    wide = x[...].astype(f32)
-    xd = (mm_split(step_ref[...], spread) * wide).astype(bf16)
-    sprev = mem[...].astype(bf16)
-    sprev_o[...] = sprev[None]
-    linked = jnp.exp2(r) * meta[:, 4:5]
-    carried = mm(r_low, sprev) * mm_split(linked, spread)
-    skip = mm_split(jnp.broadcast_to(head[2:3, :], (8, 128)), spread)[0:1]
-    ybuf[...] = carried + skip * wide
-    first = half_masks()
-    for pair in range(channels // 128):
-        lanes = slice(pair * 128, pair * 128 + 128)
-        xp = xd[:, lanes]
-        total = ybuf[:, lanes]
-        for half in range(2):
-            h = 2 * pair + half
-            decay = jnp.exp2(jnp.minimum(r[:, h:h + 1] - r_t[h:h + 1, :], 0.0))
-            mixing = (scores * decay).astype(bf16)
-            own = jnp.where(first if half == 0 else ~first, xp, jnp.zeros_like(xp))
-            total = total + mm(mixing, own)
-        ybuf[:, lanes] = total
-    last = r[SPAN - 1:SPAN, :]
-    keep = mm_split(jnp.broadcast_to(jnp.exp2(last) * meta[0:1, 6:7], (8, 128)), spread)[0:1]
-    mem[...] = keep * mem[...] + fresh[0]
-    y = ybuf[...]
-    y_o[...] = y
-    g = gate[...]
-    mixed = y * (g * sigmoid(g))
-    ones = jnp.ones((8, channels), bf16)
-    sq = sum(mm_nt(ones, part) for part in split(mixed * mixed, 2))
-    pr = sum(mm_nt(ones, part) for part in split(mixed * (par[5:6, :] * ggated[...]), 2))
-    row = lax.broadcasted_iota(jnp.int32, (8, SPAN), 0)
-    sums_o[...] = jnp.where(row == 0, sq, jnp.where(row == 1, pr, 0.0))
-
-
-def turn_kernel(
-    inner, y_ref, gate, ggated, sums, x, wr, r_ref, meta, head, par,
-    gated_o, ggate_o, gy_o, dr_o, dsf_o, dsout_o, acc_o,
-    dmem,
-):
-    at = pl.program_id(0)
-    channels = x.shape[1]
-
-    @pl.when(at == 0)
-    def _():
-        dmem[...] = jnp.zeros_like(dmem)
-        acc_o[...] = jnp.zeros_like(acc_o)
-
-    spread = spread_matrix(channels)
-    totals = jnp.transpose(sums[...])
-    scale = lax.rsqrt(totals[:, 0:1] / inner + epsilon)
-    cross = totals[:, 1:2] / inner
-    y = y_ref[...]
-    g = gate[...]
-    sg = sigmoid(g)
-    sl = g * sg
-    mixed = y * sl
-    gg = ggated[...]
-    gain = par[5:6, :]
-    normal = mixed * scale
-    gated_o[...] = (normal * gain).astype(bf16)
-    g_mixed = scale * (gain * gg - normal * (scale * cross))
-    ggate_o[...] = (g_mixed * y * (sg * (1.0 + g * (1.0 - sg)))).astype(bf16)
-    gy = (g_mixed * sl).astype(bf16)
-    gy_o[...] = gy
-    gyw = gy.astype(f32)
-    wide = x[...].astype(f32)
-    skip = mm_split(jnp.broadcast_to(head[2:3, :], (8, 128)), spread)[0:1]
-    dr_o[...] = mm_split(gyw * (y - skip * wide), gather_matrix(channels))
-    row = lax.broadcasted_iota(jnp.int32, (8, channels), 0)
-    ggain = jnp.sum(gg * normal, 0, keepdims=True)
-    gskip = jnp.sum(gyw * wide, 0, keepdims=True)
-    acc_o[...] += jnp.where(row == 0, ggain, jnp.where(row == 1, gskip, 0.0))
-    r = r_ref[...]
-    linked = mm_split(jnp.exp2(r) * meta[:, 4:5], spread)
-    r_t = jnp.transpose(wr[:, 128:256].astype(f32)).astype(bf16)
-    dfresh = mm(r_t, (linked * gyw).astype(bf16))
-    dsf_o[...] = dfresh[None]
-    last = r[SPAN - 1:SPAN, :]
-    keep = mm_split(jnp.broadcast_to(jnp.exp2(last) * meta[0:1, 6:7], (8, 128)), spread)[0:1]
-    dmem[...] = keep * dmem[...] + dfresh
-    dsout_o[...] = dmem[...]
 
 
 def back_kernel(
@@ -400,8 +227,9 @@
 
 
 class Links:
-    def __init__(self, send, recv):
-        self.send, self.recv, self.used, self.all = send, recv, 0, []
+    def __init__(self, send, recv, local=None):
+        self.send, self.recv, self.local = send, recv, local
+        self.used, self.kept, self.sent = 0, 0, []
         dp = lax.axis_index("dp")
         self.groups = lax.axis_size("dp") // SHARE
         self.group = dp // SHARE
@@ -439,20 +267,462 @@
             pl.semaphore_signal(barrier, inc=1, device_id=peer, device_id_type=MESH)
         pl.semaphore_wait(barrier, len(peers))
 
-    def go(self, src, dst, peer):
+    def make(self, src, dst, peer, when=None, track=True):
         at = self.used
         self.used += 1
         copy = pltpu.make_async_remote_copy(
             src_ref=src, dst_ref=dst, send_sem=self.send.at[at], recv_sem=self.recv.at[at],
             device_id=peer, device_id_type=MESH,
         )
+        if track:
+            self.sent.append((copy, when))
+        return copy
+
+    def go(self, src, dst, peer, track=True):
+        copy = self.make(src, dst, peer, track=track)
         copy.start()
-        self.all.append(copy)
         return copy
 
+    def keep(self, src, dst):
+        copy = pltpu.make_async_copy(src, dst, self.local.at[self.kept])
+        self.kept += 1
+        return copy
+
     def finish(self):
-        for copy in self.all:
-            copy.wait_send()
+        for copy, when in self.sent:
+            if when is None:
+                copy.wait_send()
+            else:
+                pl.when(when)(copy.wait_send)
+
+
+class Steps:
+    def __init__(self):
+        self.stages = []
+
+    def add(self, remote, local=()):
+        self.stages.append((remote, list(local)))
+
+    def run(self, s):
+        if 0 < s <= len(self.stages):
+            remote, local = self.stages[s - 1]
+            for c in remote:
+                c.wait_recv()
+            for c in local:
+                c.wait()
+        if s < len(self.stages):
+            remote, local = self.stages[s]
+            for c in remote + local:
+                c.start()
+
+
+def spread_steps(t, dst_row, dst_x, dst_core, steps):
+    steps.add([t.make(dst_row, dst_row, t.other_row())])
+    steps.add([t.make(dst_x, dst_x, t.across())])
+    steps.add([t.make(dst_core, dst_core, t.mate())])
+    return steps
+
+
+def column_steps(t, src, dst, width):
+    part = src.shape[0] // SHARE
+    x, y, z, core = t.x, t.y, t.z, t.core
+    rows = pl.ds(pl.multiple_of((x * 2 + core) * part, 16), part)
+    lanes = lane_block(y, width)
+    steps = Steps()
+    here = dst.at[z, x, core, :, lanes]
+    remote = []
+    for off in range(1, t.cols):
+        to = t.col_peer(off)
+        remote.append(t.make(src.at[rows, lane_block(to, width)], here, {"col": to}))
+    steps.add(remote, [t.keep(src.at[rows, lane_block(z, width)], here)])
+    return spread_steps(
+        t, dst.at[:, x, core, :, lanes], dst.at[:, x, core], dst.at[:, :, core], steps
+    )
+
+
+def row_steps(t, src, dst, width):
+    part = src.shape[0] // t.cols // SHARE
+    x, y, z, core = t.x, t.y, t.z, t.core
+
+    def rows(to):
+        return pl.ds(pl.multiple_of((to * SHARE + x * 2 + core) * part, 16), part)
+
+    steps = Steps()
+    here = dst.at[y, x, core, :, lane_block(z, width)]
+    remote = []
+    for off in range(1, t.cols):
+        to = t.col_peer(off)
+        remote.append(t.make(src.at[rows(to), :], here, {"col": to}))
+    steps.add(remote, [t.keep(src.at[rows(z), :], here)])
+    return spread_steps(t, dst.at[y, x, core], dst.at[:, x, core], dst.at[:, :, core], steps)
+
+
+class Relay:
+    def __init__(self, t, own, whole):
+        width = own.shape[1]
+        z, last = t.z, t.cols - 1
+        self.hops = []
+        for hop in range(1, t.cols):
+            pair = []
+            for side in (1, -1):
+                chunk = jnp.clip(z - side * (hop - 1), 0, last)
+                there = whole.at[:, lane_block(chunk, width)]
+                to = jnp.clip(z + side, 0, last)
+                if side == 1:
+                    sends = (z < last) & (z >= hop - 1)
+                    gets = z >= hop
+                else:
+                    sends = (z > 0) & (z <= last - hop + 1)
+                    gets = z <= last - hop
+                copy = t.make(own if hop == 1 else there, there, {"col": to}, sends)
+                pair.append((copy, sends, gets))
+            self.hops.append(pair)
+
+    def run(self, s):
+        if s > 0:
+            for copy, _, gets in self.hops[s - 1]:
+                pl.when(gets)(copy.wait_recv)
+        if s < len(self.hops):
+            for copy, sends, _ in self.hops[s]:
+                pl.when(sends)(copy.start)
+
+
+def front_kernel(
+    inner_total,
+    tok, ngain, w_states, meta, docrow, spar, inner, gate, out, step_w, cot, par_own, head_own, halo,
+    wi_o, wg_o, wo_o, ws_o, cots_o, par_o, head_o,
+    normed_o, pre_o, spre_o, sd_o, ssd_o, x_o, wr_o, step_o, r_o, sig_o, hpre_o, hspre_o, sprev_o,
+    gated_o, ggate_o, gy_o, dr_o, dsf_o, dsout_o, acc_o,
+    wi, wg, wo, ws2, ws, cots, par, head, head_in, halo_in,
+    normed_s, pre_s, spre_s, sd_s, ssd_s, x_s, wr_s, step_s, r_s, sig_s, hpre_s, hspre_s, sprev_s,
+    gated_s, ggate_s, gy_s, dr_s, dsf_s, acc_s,
+    fresh_s, y_s, gate_s, gg_s, sums_s, sums_in,
+    xbuf, sbuf, mem, mem_in,
+    send, recv, local,
+):
+    t = Links(send, recv, local)
+    t.meet(False)
+    x, y, z, core = t.x, t.y, t.z, t.core
+    blocks = tok.shape[0] // SPAN
+    channels = x_s.shape[1]
+    half = channels // 2
+    outputs = []
+
+    def write(src, dst):
+        copy = t.keep(src, dst)
+        copy.start()
+        outputs.append(copy)
+
+    few = [
+        t.go(par_own, par.at[:, lane_block(y, half)], t.other_row()),
+        t.go(head_own, head_in, t.other_row()),
+        t.go(halo, halo_in, t.other_row()),
+    ]
+    block = inner.shape[1] // t.cols
+    get_inner = column_steps(t, inner, wi, block)
+    get_step = column_steps(t, step_w, ws2, step_w.shape[1] // t.cols)
+    get_gate = column_steps(t, gate, wg, block)
+    get_out = row_steps(t, out, wo, out.shape[1])
+    get_cot = Relay(t, cot, cots)
+    own_cot = t.keep(cot, cots.at[:, lane_block(z, cot.shape[1])])
+    pass_state = t.make(mem, mem_in, t.other_row(), track=False)
+    pass_sums = [
+        t.make(sums_s, sums_in.at[off - 1], {"col": t.col_peer(off)}) for off in range(1, t.cols)
+    ]
+    get_inner.run(0)
+    get_step.run(0)
+    get_gate.run(0)
+    get_out.run(0)
+    get_cot.run(0)
+    own_cot.start()
+    par[:, lane_block(y, half)] = par_own[...]
+    for s in range(1, 5):
+        get_inner.run(s)
+        get_step.run(s)
+        if s > 1:
+            get_gate.run(s - 1)
+        if s > 2:
+            get_out.run(s - 2)
+    for c in few:
+        c.wait_recv()
+    head[...] = head_own[...] + head_in[...]
+    wide_in = normed_s.shape[1]
+    ws[...] = (
+        ws2[:, :, :, :, 0:128].reshape(wide_in, 128) + ws2[:, :, :, :, 128:256].reshape(wide_in, 128)
+    )
+    spread = spread_matrix(channels)
+    gain = ngain[...]
+
+    def w_of(ref):
+        return ref[...].reshape(-1, ref.shape[-1])
+
+    def rows_of(i):
+        return pl.ds(pl.multiple_of(i * SPAN, SPAN), SPAN)
+
+    hn = rms_rows(halo_in[...], gain)
+    hp = mm(hn, w_of(wi))[8:16]
+    hs = mm(hn, w_states[...])[8:16]
+    xbuf[0:8, :] = hp
+    sbuf[0:8, :] = hs
+    hpre_s[...] = hp
+    hspre_s[...] = hs
+    mem[...] = jnp.zeros_like(mem)
+
+    def entry(i, carry):
+        at = rows_of(i)
+
+        @pl.when(i > 0)
+        def _():
+            xbuf[0:8, :] = xbuf[SPAN:SPAN + 8, :]
+            sbuf[0:8, :] = sbuf[SPAN:SPAN + 8, :]
+
+        normed = rms_rows(tok[at, :], gain)
+        normed_s[at, :] = normed
+        x_pre = mm(normed, w_of(wi))
+        s_pre = mm(normed, w_states[...])
+        xbuf[8:SPAN + 8, :] = x_pre
+        sbuf[8:SPAN + 8, :] = s_pre
+        pre_s[at, :] = x_pre.astype(bf16)
+        spre_s[at, :] = s_pre.astype(bf16)
+        marks = meta[at, :]
+
+        def conv_silu(buf, here, taps):
+            v = taps[4:5, :] + taps[0:1, :] * here
+            for k in range(1, 4):
+                v = v + marks[:, k:k + 1] * (taps[k:k + 1, :] * buf[8 - k:8 - k + SPAN, :])
+            sg = sigmoid(v)
+            return v * sg, sg * (1.0 + v * (1.0 - sg))
+
+        act, slope = conv_silu(xbuf, x_pre, par)
+        x_low = act.astype(bf16)
+        x_s[at, :] = x_low
+        sd_s[at, :] = slope.astype(bf16)
+        sact, sslope = conv_silu(sbuf, s_pre, spar)
+        wr = sact.astype(bf16)
+        wr_s[at, :] = wr
+        ssd_s[at, :] = sslope.astype(bf16)
+
+        raw = mm(normed, ws[...]) + head[0:1, :]
+        step = jnp.maximum(raw, 0.0) + jnp.log1p(jnp.exp(-jnp.abs(raw)))
+        sig_s[at, :] = sigmoid(raw)
+        step_s[at, :] = step
+        r = split_mm(lower_ones(), step * head[1:2, :])
+        r_s[at, :] = r
+        last = r[SPAN - 1:SPAN, :]
+        to_end = jnp.exp2(jnp.minimum(last - r, 0.0)) * marks[:, 5:6]
+        coef = mm_split(to_end * step, spread)
+        w_t = jnp.transpose(wr[:, 0:128].astype(f32)).astype(bf16)
+        fresh = mm(w_t, (coef * x_low.astype(f32)).astype(bf16))
+        fresh_s[i] = fresh
+        mem[...] = keep_of(last, marks) * mem[...] + fresh
+
+        @pl.when(i == 0)
+        def _():
+            get_gate.run(4)
+            get_out.run(3)
+            get_cot.run(1)
+
+        @pl.when(i == 2)
+        def _():
+            get_out.run(4)
+
+        return carry
+
+    def keep_of(last, marks):
+        return mm_split(jnp.broadcast_to(jnp.exp2(last) * marks[0:1, 6:7], (8, 128)), spread)[0:1]
+
+    lax.fori_loop(0, blocks, entry, 0)
+    pass_state.start()
+    get_cot.run(2)
+    for src, dst in (
+        (normed_s, normed_o), (pre_s, pre_o), (spre_s, spre_o), (sd_s, sd_o), (ssd_s, ssd_o),
+        (x_s, x_o), (wr_s, wr_o), (step_s, step_o), (r_s, r_o), (sig_s, sig_o), (hpre_s, hpre_o),
+        (hspre_s, hspre_o), (wi, wi_o), (wg, wg_o), (wo, wo_o), (ws, ws_o), (par, par_o),
+        (head, head_o),
+    ):
+        write(src, dst)
+
+    def gate_block(i, carry):
+        at = rows_of(i)
+        gate_s[at, :] = mm(normed_s[at, :], w_of(wg))
+        return carry
+
+    lax.fori_loop(0, blocks, gate_block, 0)
+
+    pass_state.wait()
+    mem[...] = mem_in[...] * jnp.where(y == 1, 1.0, 0.0)
+    skip = mm_split(jnp.broadcast_to(head[2:3, :], (8, 128)), spread)[0:1]
+    first = half_masks()
+
+    def scan(i, carry):
+        at = rows_of(i)
+        marks = meta[at, :]
+        w_low = wr_s[at, 0:128]
+        r_low = wr_s[at, 128:256]
+        r = r_s[at, :]
+        r_t = jnp.transpose(r)
+        rows = lax.broadcasted_iota(jnp.int32, (SPAN, SPAN), 0)
+        cols = lax.broadcasted_iota(jnp.int32, (SPAN, SPAN), 1)
+        allowed = (rows >= cols) & (marks[:, 0:1] == docrow[:, at])
+        scores = jnp.where(allowed, mm_nt(r_low, w_low), 0.0)
+        wide = x_s[at, :].astype(f32)
+        xd = (mm_split(step_s[at, :], spread) * wide).astype(bf16)
+        sprev = mem[...].astype(bf16)
+        sprev_s[i] = sprev
+        linked = jnp.exp2(r) * marks[:, 4:5]
+        carried = mm(r_low, sprev) * mm_split(linked, spread)
+        y_s[at, :] = carried + skip * wide
+        for pair in range(channels // 128):
+            lanes = slice(pair * 128, pair * 128 + 128)
+            xp = xd[:, lanes]
+            total = y_s[at, lanes]
+            for part in range(2):
+                h = 2 * pair + part
+                decay = jnp.exp2(jnp.minimum(r[:, h:h + 1] - r_t[h:h + 1, :], 0.0))
+                mixing = (scores * decay).astype(bf16)
+                own = jnp.where(first if part == 0 else ~first, xp, jnp.zeros_like(xp))
+                total = total + mm(mixing, own)
+            y_s[at, lanes] = total
+        last = r[SPAN - 1:SPAN, :]
+        mem[...] = keep_of(last, marks) * mem[...] + fresh_s[i]
+        return carry
+
+    lax.fori_loop(0, blocks, scan, 0)
+    write(sprev_s, sprev_o)
+
+    get_cot.run(3)
+    own_cot.wait()
+    write(cots, cots_o)
+    ones = jnp.ones((8, channels), bf16)
+
+    def totals_of(i, carry):
+        at = rows_of(i)
+        gg = mm_nt(cots[at, :], w_of(wo))
+        gg_s[at, :] = gg
+        g = gate_s[at, :]
+        mixed = y_s[at, :] * (g * sigmoid(g))
+        sq = sum(mm_nt(ones, part) for part in split(mixed * mixed, 2))
+        pr = sum(mm_nt(ones, part) for part in split(mixed * (par[5:6, :] * gg), 2))
+        row = lax.broadcasted_iota(jnp.int32, (8, SPAN), 0)
+        sums_s[:, at] = jnp.where(row == 0, sq, jnp.where(row == 1, pr, 0.0))
+        return carry
+
+    lax.fori_loop(0, blocks, totals_of, 0)
+    for c in pass_sums:
+        c.start()
+    for c in pass_sums:
+        c.wait_recv()
+    mem[...] = jnp.zeros_like(mem)
+    acc_s[...] = jnp.zeros_like(acc_s)
+    gather = gather_matrix(channels)
+
+    def turn(back_i, carry):
+        i = blocks - 1 - back_i
+        at = rows_of(i)
+        marks = meta[at, :]
+        both = sums_s[:, at]
+        for off in range(1, t.cols):
+            both = both + sums_in[off - 1, :, at]
+        totals = jnp.transpose(both)
+        scale = lax.rsqrt(totals[:, 0:1] / inner_total + epsilon)
+        cross = totals[:, 1:2] / inner_total
+        yv = y_s[at, :]
+        g = gate_s[at, :]
+        sg = sigmoid(g)
+        sl = g * sg
+        gg = gg_s[at, :]
+        ngate = par[5:6, :]
+        normal = yv * sl * scale
+        gated_s[at, :] = (normal * ngate).astype(bf16)
+        g_mixed = scale * (ngate * gg - normal * (scale * cross))
+        ggate_s[at, :] = (g_mixed * yv * (sg * (1.0 + g * (1.0 - sg)))).astype(bf16)
+        gy = (g_mixed * sl).astype(bf16)
+        gy_s[at, :] = gy
+        gyw = gy.astype(f32)
+        wide = x_s[at, :].astype(f32)
+        dr_s[at, :] = mm_split(gyw * (yv - skip * wide), gather)
+        row = lax.broadcasted_iota(jnp.int32, (8, channels), 0)
+        ggain = jnp.sum(gg * normal, 0, keepdims=True)
+        gskip = jnp.sum(gyw * wide, 0, keepdims=True)
+        acc_s[...] += jnp.where(row == 0, ggain, jnp.where(row == 1, gskip, 0.0))
+        r = r_s[at, :]
+        linked = mm_split(jnp.exp2(r) * marks[:, 4:5], spread)
+        r_t = jnp.transpose(wr_s[at, 128:256].astype(f32)).astype(bf16)
+        dfresh = mm(r_t, (linked * gyw).astype(bf16))
+        dsf_s[i] = dfresh
+        mem[...] = keep_of(r[SPAN - 1:SPAN, :], marks) * mem[...] + dfresh
+        return carry
+
+    lax.fori_loop(0, blocks, turn, 0)
+    for src, dst in (
+        (gated_s, gated_o), (ggate_s, ggate_o), (gy_s, gy_o), (dr_s, dr_o), (dsf_s, dsf_o),
+        (mem, dsout_o), (acc_s, acc_o),
+    ):
+        write(src, dst)
+    for copy in outputs:
+        copy.wait()
+    t.finish()
+
+
+def front(inner_all, tok, ngain, w_states, meta, docrow, spar, inner, gate, out, step_w, cot, par_own,
+          head_own, halo):
+    tokens, width = tok.shape
+    blocks = tokens // SPAN
+    cols = lax.axis_size("col")
+    part, half = inner.shape[0] // SHARE, inner.shape[1] // cols
+    channels = 2 * half
+    sds = jax.ShapeDtypeStruct
+    V = pltpu.VMEM
+    weights = [
+        ((cols, 2, 2, part, channels), bf16), ((cols, 2, 2, part, channels), bf16),
+        ((2, 2, 2, half // SHARE, width), bf16),
+    ]
+    entry_shapes = [
+        ((tokens, width), bf16), ((tokens, channels), bf16), ((tokens, 256), bf16),
+        ((tokens, channels), bf16), ((tokens, 256), bf16), ((tokens, channels), bf16),
+        ((tokens, 256), bf16), ((tokens, 128), f32), ((tokens, 128), f32), ((tokens, 128), f32),
+        ((8, channels), f32), ((8, 256), f32), ((blocks, 128, channels), bf16),
+    ]
+    turn_shapes = [
+        ((tokens, channels), bf16), ((tokens, channels), bf16), ((tokens, channels), bf16),
+        ((tokens, 128), f32), ((blocks, 128, channels), f32),
+    ]
+    state = ((128, channels), f32)
+    acc = ((8, channels), f32)
+    outs = (
+        weights + [((width, 128), bf16), ((tokens, width), bf16), ((8, channels), f32), ((8, 128), f32)]
+        + entry_shapes + turn_shapes + [state, acc]
+    )
+    scratch = (
+        weights
+        + [((cols, 2, 2, part, 256), bf16), ((width, 128), bf16), ((tokens, width), bf16),
+           ((8, channels), f32), ((8, 128), f32), ((8, 128), f32), (halo.shape, bf16)]
+        + entry_shapes + turn_shapes + [acc]
+        + [((blocks, 128, channels), f32), ((tokens, channels), f32), ((tokens, channels), f32),
+           ((tokens, channels), f32), ((8, tokens), f32), ((cols - 1, 8, tokens), f32),
+           ((SPAN + 8, channels), f32), ((SPAN + 8, 256), f32), state, state]
+    )
+    vmem = pl.BlockSpec(memory_space=V)
+    hbm = pl.BlockSpec(memory_space=pl.ANY)
+    got = pl.pallas_call(
+        functools.partial(front_kernel, float(inner_all)),
+        out_shape=[sds(*o) for o in outs],
+        in_specs=[vmem] * 6 + [hbm] * 5 + [vmem, vmem, hbm],
+        out_specs=[hbm] * len(outs),
+        scratch_shapes=[V(*s) for s in scratch] + [
+            pltpu.SemaphoreType.DMA((48,)), pltpu.SemaphoreType.DMA((48,)),
+            pltpu.SemaphoreType.DMA((48,)),
+        ],
+        compiler_params=pltpu.CompilerParams(
+            collective_id=1, has_side_effects=True, vmem_limit_bytes=62 * 1024 * 1024
+        ),
+        name="front",
+    )(tok, ngain, w_states, meta, docrow, spar, inner, gate, out, step_w, cot, par_own, head_own, halo)
+    got = list(got)
+    got[0] = got[0].reshape(width, channels)
+    got[1] = got[1].reshape(width, channels)
+    got[2] = got[2].reshape(channels, width)
+    return got
 
 
 def wavefront(stages, items):
@@ -461,177 +731,6 @@
             m = turn - s
             if 0 <= m < len(items):
                 items[m](s)
-
-
-def fetch_kernel(
-    inner, gate, out, step, cot, par, halo,
-    wi, wg, wo, ws, cots, pars, halo_in,
-    send, recv, local,
-):
-    t = Links(send, recv)
-    t.meet(False)
-    x, y, z, core = t.x, t.y, t.z, t.core
-    part = inner.shape[0] // SHARE
-    block = inner.shape[1] // t.cols
-    own_rows = pl.ds(pl.multiple_of((x * 2 + core) * part, 16), part)
-    locals_ = []
-
-    def keep(src, dst):
-        copy = pltpu.make_async_copy(src, dst, local.at[len(locals_)])
-        copy.start()
-        locals_.append(copy)
-        return copy
-
-    small = [t.go(par, pars.at[y], t.other_row()), t.go(halo, halo_in, t.other_row())]
-    keep(par, pars.at[y])
-
-    def column_blocks(src, dst, width):
-        lanes = lane_block(y, width)
-        copies = []
-
-        def run(s):
-            if s == 0:
-                for off in range(1, t.cols):
-                    to = t.col_peer(off)
-                    copies.append(
-                        t.go(src.at[own_rows, lane_block(to, width)],
-                             dst.at[z, x, core, :, lanes], {"col": to})
-                    )
-                copies.append(keep(src.at[own_rows, lane_block(z, width)],
-                                   dst.at[z, x, core, :, lanes]))
-            elif s == 1:
-                for c in copies[:-1]:
-                    c.wait_recv()
-                copies[-1].wait()
-                here = dst.at[:, x, core, :, lanes]
-                copies.append(t.go(here, here, t.other_row()))
-            elif s == 2:
-                copies[-1].wait_recv()
-                here = dst.at[:, x, core]
-                copies.append(t.go(here, here, t.across()))
-            elif s == 3:
-                copies[-1].wait_recv()
-                here = dst.at[:, :, core]
-                copies.append(t.go(here, here, t.mate()))
-            else:
-                copies[-1].wait_recv()
-
-        return run
-
-    def row_blocks(src, dst, width):
-        copies = []
-
-        def rows_of(to):
-            return pl.ds(pl.multiple_of((to * SHARE + x * 2 + core) * part, 16), part)
-
-        def run(s):
-            if s == 0:
-                for off in range(1, t.cols):
-                    to = t.col_peer(off)
-                    copies.append(
-                        t.go(src.at[rows_of(to), :], dst.at[y, x, core, :, lane_block(z, width)],
-                             {"col": to})
-                    )
-                copies.append(keep(src.at[rows_of(z), :],
-                                   dst.at[y, x, core, :, lane_block(z, width)]))
-            elif s == 1:
-                for c in copies[:-1]:
-                    c.wait_recv()
-                copies[-1].wait()
-                here = dst.at[y, x, core]
-                copies.append(t.go(here, here, t.other_row()))
-            elif s == 2:
-                copies[-1].wait_recv()
-                here = dst.at[:, x, core]
-                copies.append(t.go(here, here, t.across()))
-            elif s == 3:
-                copies[-1].wait_recv()
-                here = dst.at[:, :, core]
-                copies.append(t.go(here, here, t.mate()))
-            else:
-                copies[-1].wait_recv()
-
-        return run
-
-    def cot_blocks(s):
-        if s == 0:
-            lanes = lane_block(z, cot.shape[1])
-            for off in range(1, t.cols):
-                small.append(t.go(cot, cots.at[:, lanes], {"col": t.col_peer(off)}))
-            keep(cot, cots.at[:, lanes])
-
-    wavefront(5, [
-        column_blocks(inner, wi, block), column_blocks(step, ws, step.shape[1] // t.cols),
-        column_blocks(gate, wg, block), row_blocks(out, wo, out.shape[1]), cot_blocks,
-    ])
-    for c in small:
-        c.wait_recv()
-    locals_[0].wait()
-    locals_[-1].wait()
-    t.finish()
-
-
-def fetch(inner, gate, out, step, cot, par, halo):
-    rows, all_cols = inner.shape
-    cols = lax.axis_size("col")
-    part, block = rows // SHARE, all_cols // cols
-    sds = jax.ShapeDtypeStruct
-    wide = sds((cols, 2, 2, part, 2 * block), bf16)
-    shapes = [
-        wide, wide, sds((2, 2, 2, out.shape[0] // cols // SHARE, cols * out.shape[1]), bf16),
-        sds((cols, 2, 2, part, 2 * (step.shape[1] // cols)), bf16),
-        sds((cot.shape[0], cols * cot.shape[1]), bf16), sds((2,) + par.shape, f32),
-        sds(halo.shape, bf16),
-    ]
-    got = pl.pallas_call(
-        fetch_kernel,
-        out_shape=shapes,
-        in_specs=[pl.BlockSpec(memory_space=pl.ANY)] * 7,
-        out_specs=[pl.BlockSpec(memory_space=pl.ANY)] * 7,
-        scratch_shapes=[
-            pltpu.SemaphoreType.DMA((40,)), pltpu.SemaphoreType.DMA((40,)),
-            pltpu.SemaphoreType.DMA((8,)),
-        ],
-        compiler_params=pltpu.CompilerParams(collective_id=1, has_side_effects=True),
-        name="fetch",
-    )(inner, gate, out, step, cot, par, halo)
-    wi, wg, wo, ws, cots, pars, halo_in = got
-    width = rows * cols
-    return (
-        wi.reshape(width, -1), wg.reshape(width, -1), wo.reshape(2 * block, -1),
-        ws.reshape(width, -1), cots, pars, halo_in,
-    )
-
-
-def col_sum_kernel(v, total, got, send, recv):
-    t = Links(send, recv)
-    barrier = pltpu.get_barrier_semaphore()
-    for off in range(1, t.cols):
-        pl.semaphore_signal(
-            barrier, inc=1, device_id={"col": t.col_peer(off)}, device_id_type=MESH
-        )
-    pl.semaphore_wait(barrier, t.cols - 1)
-    copies = [t.go(v, got.at[off - 1], {"col": t.col_peer(off)}) for off in range(1, t.cols)]
-    for c in copies:
-        c.wait_recv()
-    total[...] = v[...] + got[0] + got[1] + got[2]
-    t.finish()
-
-
-def col_sum(v):
-    cols = lax.axis_size("col")
-    return pl.pallas_call(
-        col_sum_kernel,
-        out_shape=jax.ShapeDtypeStruct(v.shape, v.dtype),
-        in_specs=[pl.BlockSpec(memory_space=pltpu.VMEM)],
-        out_specs=pl.BlockSpec(memory_space=pltpu.VMEM),
-        scratch_shapes=[
-            pltpu.VMEM((cols - 1,) + v.shape, v.dtype),
-            pltpu.SemaphoreType.DMA((cols - 1,)), pltpu.SemaphoreType.DMA((cols - 1,)),
-        ],
-        compiler_params=pltpu.CompilerParams(collective_id=2, has_side_effects=True),
-        name="colsum",
-    )(v)
 
 
 def add_into(target, source, count, index_target, index_source):
@@ -714,7 +813,7 @@
                 else:
                     a4[...] = (a3[...].astype(f32) + a2[x].astype(f32)).astype(bf16)
                 if t.groups > 1:
-                    more = [t.go(a4, far.at[off - 1], t.group_peer(off))
+                    more = [t.go(a4, far.at[off - 1], t.group_peer(off), False)
                             for off in range(1, t.groups)]
                     for c in more:
                         c.wait()
@@ -789,7 +888,7 @@
 
             lax.fori_loop(0, t.cols, body, 0)
             if t.groups > 1:
-                more = [t.go(s4, far_s.at[off - 1], t.group_peer(off))
+                more = [t.go(s4, far_s.at[off - 1], t.group_peer(off), False)
                         for off in range(1, t.groups)]
                 for c in more:
                     c.wait()
@@ -846,7 +945,7 @@
             few[-1].wait_recv()
             msum[2] = msum[1] + mgot[2]
             if t.groups > 1:
-                more = [t.go(msum.at[2], mgot.at[5 + off], t.group_peer(off))
+                more = [t.go(msum.at[2], mgot.at[5 + off], t.group_peer(off), False)
                         for off in range(1, t.groups)]
                 for c in more:
                     c.wait()
@@ -970,32 +1069,20 @@
     inner_all = channels * cols
     col_width = width // cols
 
-    heads_own = jnp.stack([step_bias, decay_log, skip_gain])
     own = jnp.concatenate(
-        [
-            conv_inner,
-            conv_inner_bias[None],
-            gate_gain[None],
-            jnp.pad(heads_own.reshape(1, -1), ((0, 0), (0, own_ch - 3 * own_heads))),
-            jnp.zeros((1, own_ch), f32),
-        ],
-        0,
-    )
-    pieces = jnp.pad(
-        proj_step.reshape(col_width, cols, own_heads), ((0, 0), (0, 0), (0, 128 - own_heads))
-    ).reshape(col_width, cols * 128)
-    w_inner, w_gate, w_out, w_step, cot_all, both, halo = fetch(
-        proj_inner, proj_gate, proj_out, pieces, cotangent, own, tokens_in[-16:]
-    )
-    w_step = jnp.concatenate([w_step[:, :own_heads], w_step[:, 128:128 + own_heads]], 1)
-    w_step = jnp.pad(w_step, ((0, 0), (0, 128 - 2 * own_heads)))
-    par = jnp.concatenate([both[0], both[1]], 1)
-    hp = jnp.concatenate(
-        [both[i, 6, : 3 * own_heads].reshape(3, own_heads) for i in range(2)], 1
-    )
-    rate = -jnp.exp(hp[1])
-    head = jnp.pad(
-        jnp.stack([hp[0], rate * LOG2E, hp[2], rate]), ((0, 4), (0, 128 - 2 * own_heads))
+        [conv_inner, conv_inner_bias[None], gate_gain[None], jnp.zeros((2, own_ch), f32)], 0
+    )
+
+    def at_row(values):
+        pad = [(0, 0)] * (values.ndim - 1)
+        low = jnp.pad(values, pad + [(0, 128 - own_heads)])
+        high = jnp.pad(values, pad + [(own_heads, 128 - 2 * own_heads)])
+        return jnp.where(row == 0, low, high)
+
+    pieces = at_row(proj_step.reshape(col_width, cols, own_heads)).reshape(col_width, cols * 128)
+    rate = -jnp.exp(decay_log)
+    head_own = jnp.pad(
+        at_row(jnp.stack([step_bias, rate * LOG2E, skip_gain, rate])), ((0, 4), (0, 0))
     )
     spar = jnp.concatenate([conv_states, conv_states_bias[None], jnp.zeros((3, 256), f32)], 0)
 
@@ -1035,91 +1122,15 @@
     docrow = here[None, :]
 
     sds = jax.ShapeDtypeStruct
+    back3 = pl.BlockSpec((1, 128, channels), lambda i: (blocks - 1 - i, 0, 0))
     (
-        normed, pre, spre, sd, ssd, x_low, wr, step, r, sig, fresh, end, hpre, hspre,
-    ) = pl.pallas_call(
-        entry_kernel,
-        grid=(blocks,),
-        in_specs=[
-            by_rows(width), whole((16, width)), whole((1, width)), whole((width, channels)),
-            whole((width, 256)), whole((width, 128)), whole((8, channels)), whole((8, 256)),
-            whole((8, 128)), by_rows(16),
-        ],
-        out_specs=[
-            by_rows(width), by_rows(channels), by_rows(256), by_rows(channels), by_rows(256),
-            by_rows(channels), by_rows(256), by_rows(128), by_rows(128), by_rows(128),
-            pl.BlockSpec((1, 128, channels), lambda i: (i, 0, 0)), whole((128, channels)),
-            whole((8, channels)), whole((8, 256)),
-        ],
-        out_shape=[
-            sds((tokens, width), bf16), sds((tokens, channels), bf16), sds((tokens, 256), bf16),
-            sds((tokens, channels), bf16), sds((tokens, 256), bf16),
-            sds((tokens, channels), bf16), sds((tokens, 256), bf16),
-            sds((tokens, 128), f32), sds((tokens, 128), f32), sds((tokens, 128), f32),
-            sds((blocks, 128, channels), f32), sds((128, channels), f32),
-            sds((8, channels), f32), sds((8, 256), f32),
-        ],
-        scratch_shapes=[
-            pltpu.VMEM((SPAN + 8, channels), f32),
-            pltpu.VMEM((SPAN + 8, 256), f32),
-            pltpu.VMEM((128, channels), f32),
-        ],
-        compiler_params=pltpu.CompilerParams(**PARAMS),
-        name="entry",
-    )(tokens_in, halo, norm_gain[None], w_inner, proj_states, w_step, par, spar, head, meta)
-
-    state_in = lax.ppermute(end, "row", [(0, 1)])
-    gate = mm(normed, w_gate)
-    ggated = mm_nt(cot_all, w_out)
-
-    y, sums, sprev = pl.pallas_call(
-        scan_kernel,
-        grid=(blocks,),
-        in_specs=[
-            by_rows(channels), by_rows(256), by_rows(128), by_rows(128), by_rows(16),
-            pl.BlockSpec((1, SPAN), lambda i: (0, i)),
-            pl.BlockSpec((1, 128, channels), lambda i: (i, 0, 0)), whole((128, channels)),
-            whole((8, 128)), whole((8, channels)), by_rows(channels), by_rows(channels),
-        ],
-        out_specs=[
-            by_rows(channels), pl.BlockSpec((8, SPAN), lambda i: (0, i)),
-            pl.BlockSpec((1, 128, channels), lambda i: (i, 0, 0)),
-        ],
-        out_shape=[
-            sds((tokens, channels), f32), sds((8, tokens), f32),
-            sds((blocks, 128, channels), bf16),
-        ],
-        scratch_shapes=[pltpu.VMEM((128, channels), f32), pltpu.VMEM((SPAN, channels), f32)],
-        compiler_params=pltpu.CompilerParams(**PARAMS),
-        name="scan",
-    )(x_low, wr, r, step, meta, docrow, fresh, state_in, head, par, gate, ggated)
-
-    sums = col_sum(sums)
-
-    back3 = pl.BlockSpec((1, 128, channels), lambda i: (blocks - 1 - i, 0, 0))
-    gated, g_gate, gy, dr, dsf, dsout, acc1 = pl.pallas_call(
-        functools.partial(turn_kernel, float(inner_all)),
-        grid=(blocks,),
-        in_specs=[
-            by_rows(channels, blocks), by_rows(channels, blocks), by_rows(channels, blocks),
-            pl.BlockSpec((8, SPAN), lambda i: (0, blocks - 1 - i)),
-            by_rows(channels, blocks), by_rows(256, blocks), by_rows(128, blocks),
-            by_rows(16, blocks), whole((8, 128)), whole((8, channels)),
-        ],
-        out_specs=[
-            by_rows(channels, blocks), by_rows(channels, blocks), by_rows(channels, blocks),
-            by_rows(128, blocks), back3, whole((128, channels)), whole((8, channels)),
-        ],
-        out_shape=[
-            sds((tokens, channels), bf16), sds((tokens, channels), bf16),
-            sds((tokens, channels), bf16), sds((tokens, 128), f32),
-            sds((blocks, 128, channels), f32), sds((128, channels), f32),
-            sds((8, channels), f32),
-        ],
-        scratch_shapes=[pltpu.VMEM((128, channels), f32)],
-        compiler_params=pltpu.CompilerParams(**PARAMS),
-        name="turn",
-    )(y, gate, ggated, sums, x_low, wr, r, meta, head, par)
+        w_inner, w_gate, w_out, w_step, cot_all, par, head,
+        normed, pre, spre, sd, ssd, x_low, wr, step, r, sig, hpre, hspre, sprev,
+        gated, g_gate, gy, dr, dsf, dsout, acc1,
+    ) = front(
+        inner_all, tokens_in, norm_gain[None], proj_states, meta, docrow, spar,
+        proj_inner, proj_gate, proj_out, pieces, cotangent, own, head_own, tokens_in[-16:],
+    )
 
     ds_in = lax.ppermute(dsout, "row", [(1, 0)])
     out_part = mm(gated, w_out).astype(bf16)

time: 498 us -> 437 us (0.88)
  Pallas kernels: 337 us -> 300 us
  matrix products: 67.8 us -> 50.4 us
    pallas_call x5 -> x1, Pallas kernels: 155 us -> 117 us  [front(): pl.pallas_call(functools.partial(front_kernel, float(inner_all)), out_sha...]
    dot_general x5 -> x4, matrix products: 30.9 us -> 23.8 us  [mm_nt(): lax.dot_general(a, b, (((1,), (1,)), ((), ())), preferred_element_type=f32)]
    dot_general x2 -> x1, matrix products: 11.1 us -> 4.74 us  [mm(): lax.dot_general(a, b, (((1,), (0,)), ((), ())), preferred_element_type=f32)]
    unnamed x79 -> x67, local copies, waits for them, and re-layouts: 10.2 us -> 7.14 us
  transfers between devices with their start and end apart: 5 -> 4, of which waited for: 0 -> 0; matrix products, arithmetic and copies ran while one was open for 20% -> 22% of each run, Pallas kernels for 37% -> 42%
where the time goes in v3:
time: 437 us; the launch traced here: 434 us
  Pallas kernels  300 us (69%)
  matrix products  50.4 us (12%)
  local copies, waits for them, and re-layouts  39.3 us (9%)
  other arithmetic  26.1 us (6%)
  between operations  14.4 us (3%)
    pallas_call x1, Pallas kernels, tail(): pl.pallas_call(tail_kernel, out_shape=[sds((rows, third), f32), sds(ish.s...  160 us
    pallas_call x1, Pallas kernels, front(): pl.pallas_call(functools.partial(front_kernel, float(inner_all)), out_sha...  117 us
    dot_general x4, matrix products, mm_nt(): lax.dot_general(a, b, (((1,), (1,)), ((), ())), preferred_element_type=f32)  23.8 us
    pallas_call x1, Pallas kernels, per_device(): pl.pallas_call(back_kernel, grid=(blocks,), in_specs=[by_rows(channels, b...  22.6 us
    dot_general x4, matrix products, weight_grad(): lax.dot_general(left, right, (((0,), (0,)), ((), ())), preferred_element_...  15.9 us
  transfers between devices with their start and end apart: 4, of which 0 were waited for; matrix products, arithmetic and copies ran while one was open for 22% of the time, Pallas kernels for 42%

profile of v3, /device:TPU:0, one launch (start us, length us, event | category | flops | bytes accessed | tf_op | source)
XLA Modules:
  0.0 434.0 jit_solution(10792519730739834864)
XLA Ops:
  7.4 0.7 multiply_bitcast_fusion.1
  8.1 0.7 broadcast_in_dim.36
  8.8 0.7 broadcast_in_dim.37
  9.5 0.7 pad_maximum_fusion.1
  10.8 1.3 broadcast_in_dim.31.ngain
  12.1 0.7 convert_element_type.122
  13.7 0.7 pad_maximum_fusion.2
  14.5 0.8 convert_reduce_fusion
  15.5 0.7 reshape.243
  16.2 1.4 slice.184.halo
  17.7 0.9 copy.85.step_w
  18.8 1.0 copy.79.meta
  19.8 0.7 maximum_maximum_fusion.1.spar
  20.5 0.7 maximum_maximum_fusion.par_own
  21.2 117.0 %front.1 = (bf16[4,2,2,96,768]{4,3,2,1,0:T(8,128)(2,1)}, bf16[4,2,2,96,768]{4,3,2,1,0:T(8,128)(2,1)}, bf16[2,2,2,96,1536]{4,3,2,1,0:T(8,128)(2,1)}, bf16[1536,12...) custom-call(bf16[1024,1536]{1,0:T(8,128)(2,1)} %tok.1, ...), custom_call_target="tpu_custom_call" | custom-call | tf_op jit(solution)/shard_map/front/pallas_call | solution.py:707
  138.2 1.5 collective-permute-start
  139.6 4.7 %convolution_convert_fusion = bf16[1024,1536]{1,0:T(8,128)(2,1)S(1)} fusion(bf16[1024,768]{1,0:T(8,128)(2,1)} %get-tuple-element.83, bf16[768,1536]{1,0:T(8,128)(2,1)} %bitcast.151), kind=kOutput, calls=%fused_computation.8 | convolution fusion | flops 2417491968 | bytes 7077888 | tf_op jit(solution)/shard_map/dot_general | solution.py:20
  144.4 2.9 copy.86
  147.3 1.5 dynamic_slice.18
  149.1 0.8 slice_reduce_fusion
  151.4 5.9 %convolution_convert_fusion.1 = bf16[768,1536]{1,0:T(8,128)(2,1)} fusion(bf16[1024,768]{1,0:T(8,128)(2,1)S(1)} %copy-done.24, bf16[1024,1536]{1,0:T(8,128)(2,1)} %get-tuple-element.113), kind=kOutput, calls=%fused_computation.9 | convolution fusion | flops 2417098752 | bytes 7077888 | tf_op jit(solution)/shard_map/dot_general | solution.py:1140
  157.3 4.0 convolution_convert_fusion.2
  161.3 4.6 %fusion.37 = f32[1024,1536]{1,0:T(8,128)} fusion(bf16[1024,768]{1,0:T(8,128)(2,1)S(1)} %copy-done.23, bf16[1536,768]{1,0:T(8,128)(2,1)S(1)} %bitcast.150), kind=kOutput, calls=%fused_computation.109 | convolution fusion | flops 2415919104 | bytes 10223616 | tf_op jit(solution)/shard_map/dot_general | solution.py:24
  167.1 1.4 stack.132.hmeta
  168.4 0.7 fusion
  169.7 0.7 copy-done.7
  170.5 22.6 %back.1 = (bf16[1024,768]{1,0:T(8,128)(2,1)}, bf16[1024,256]{1,0:T(8,128)(2,1)}, bf16[1024,128]{1,0:T(8,128)(2,1)}, f32[8,768]{1,0:T(8,128)}, f32[8,256]{1,0:T(8...) custom-call(bf16[1024,768]{1,0:T(8,128)(2,1)} %get-tuple-element.87.x, ...), custom_call_target="tpu_custom_call" | custom-call | tf_op jit(solution)/shard_map/back/pallas_call | solution.py:1144
  193.0 0.7 slice_multiply_fusion
  193.7 0.7 slice_reduce_fusion.3
  195.7 1.3 convert.25
  197.0 1.3 convert.26
  198.4 1.3 collective-permute-start.2
  199.6 0.8 reshape.254
  200.4 1.4 concatenate.36
  201.8 1.4 reshape.258
  203.2 1.5 collective-permute-start.1
  204.7 1.1 slice.191
  205.8 1.0 broadcast_select_fusion
  206.8 4.7 %fusion.39 = f32[1024,1536]{1,0:T(8,128)} fusion(bf16[1024,128]{1,0:T(8,128)(2,1)} %get-tuple-element.108, bf16[1536,128]{1,0:T(8,128)(2,1)S(1)} %copy-done.6), kind=kOutput, calls=%fused_computation.111 | convolution fusion | flops 402653184 | bytes 6946816 | tf_op jit(solution)/shard_map/dot_general | solution.py:24
  211.5 1.9 convolution_convert_fusion.5
  213.5 1.3 add_dynamic-update-slice_fusion.1
  214.8 4.0 convolution_convert_fusion.4
  218.9 1.3 add_dynamic-update-slice_fusion
  220.2 7.6 %fusion.38 = f32[1024,1536]{1,0:T(8,128)} fusion(bf16[1024,768]{1,0:T(8,128)(2,1)} %add_dynamic-update-slice_fusion, bf16[1536,768]{1,0:T(8,128)(2,1)} %bitcast.149), kind=kOutput, calls=%fused_computation.110 | convolution fusion | flops 2415919104 | bytes 10223616 | tf_op jit(solution)/shard_map/dot_general | solution.py:24
  227.9 7.0 %fusion.3 = (f32[1536]{0:T(1024)S(1)}, f32[1024]{0:T(1024)}, bf16[1024,1536]{1,0:T(8,128)(2,1)}) fusion(bf16[1024,1536]{1,0:T(8,128)(2,1)S(1)} %copy-done, f32[1024]{0:T(1024)S(1)} %copy-done.12, f32[1536]{0:T(1024)S(1)} %copy-done.11, f32[1024,1536]{1,0:T(8,128)S(1)} %bitcast.111, f32[1024,1536]{1,0:T(8,128)S(1)} %bitcast.114, f32[1024,1536]{1,0:T(8,128)} %fusion.38, ...), kind=kOutput, calls=%fused_computation.6 | convolution fusion | flops 822605312 | bytes 26497024 | tf_op jit(solution)/shard_map/dot_general | solution.py:24
  235.5 6.0 %convolution_convert_fusion.3 = bf16[1536,768]{1,0:T(8,128)(2,1)} fusion(bf16[1024,1536]{1,0:T(8,128)(2,1)} %get-tuple-element.112, bf16[1024,768]{1,0:T(8,128)(2,1)S(1)} %copy-done.19), kind=kOutput, calls=%fused_computation.11 | convolution fusion | flops 2417098752 | bytes 7077888 | tf_op jit(solution)/shard_map/dot_general | solution.py:1192
  241.4 160.0 %tail.1 = (f32[1024,384]{1,0:T(8,128)}, f32[8,128]{1,0:T(8,128)}, bf16[2,2,96,1536]{3,2,1,0:T(8,128)(2,1)}, bf16[2,2,96,1536]{3,2,1,0:T(8,128)(2,1)}, bf16[2,2,9...) custom-call(bf16[1024,1536]{1,0:T(8,128)(2,1)} %get-tuple-element.13, ...), custom_call_target="tpu_custom_call" | custom-call | tf_op jit(solution)/shard_map/tail/pallas_call | solution.py:1016
  401.4 0.7 slice.207
  402.7 0.7 slice_bitcast_fusion
  404.2 1.1 reshape_reshape.3
  405.3 0.9 copy.88
  406.1 1.4 reshape.283
  407.5 0.8 slice_bitcast_fusion.1
  408.3 0.7 dynamic_slice.19
  409.0 1.4 dynamic-slice_reduce_fusion.1
  410.3 1.4 dynamic-slice_bitcast_fusion
  411.7 1.2 slice_bitcast_fusion.2
  413.0 0.7 multiply_bitcast_fusion
  413.7 2.4 bitcast_convert_fusion.3
  416.0 1.8 bitcast_convert_fusion.2
  417.8 1.8 bitcast_convert_fusion.1
  419.6 1.7 bitcast_convert_fusion
  421.3 2.3 copy.87
  423.6 3.6 fusion.8
  (108 shorter events, 9.2 us)
Async XLA Ops:
  7.2 12.7 %copy-start.18 = (f32[256]{0:T(256)S(1)}, f32[256]{0:T(256)}, u32[]{:S(2)}) copy-start(f32[256]{0:T(256)} %param.31) | copy-start | bytes 3076
  7.2 12.7 %copy-start.17 = (f32[4,256]{1,0:T(4,128)S(1)}, f32[4,256]{1,0:T(4,128)}, u32[]{:S(2)}) copy-start(f32[4,256]{1,0:T(4,128)} %param.30) | copy-start | bytes 12292
  7.2 13.3 %copy-start.16 = (f32[4,384]{1,0:T(4,128)S(1)}, f32[4,384]{1,0:T(4,128)}, u32[]{:S(2)}) copy-start(f32[4,384]{1,0:T(4,128)} %param.28) | copy-start | bytes 18436
  7.2 414.1 %reduce-scatter.4.cloned.1.call-start = ((), (), s32[]{:S(2)}) async-start(), calls=%async_computation.1 | async-start | bytes 3932160
  13.5 7.7 %copy-start.8 = (f32[1024]{0:T(1024)}, f32[1024]{0:T(1024)S(1)}, u32[]{:S(2)}) copy-start(f32[1024]{0:T(1024)S(1)} %get-tuple-element.136) | copy-start | bytes 12292
  138.2 31.6 %collective-permute-start = (f32[128,768]{1,0:T(8,128)}, f32[128,768]{1,0:T(8,128)S(1)}, u32[]{:S(2)}, u32[]{:S(2)}) collective-permute-start(f32[128,768]{1,0:T(8,128)} %get-tuple-element.96), channel_id=1, source_target_pairs={{4,0},{5,1},{6,2},{7,3},{12,8},{13,9},{14,10},{15,11},{20,16},{21,... | collective-permute-start | bytes 1179656 | tf_op jit(solution)/shard_map/ppermute | solution.py:1135
  147.3 4.1 copy-start.24
  151.4 5.9 %copy-start.20 = (bf16[1024,1536]{1,0:T(8,128)(2,1)S(1)}, bf16[1024,1536]{1,0:T(8,128)(2,1)}, u32[]{:S(2)}) copy-start(bf16[1024,1536]{1,0:T(8,128)(2,1)} %get-tuple-element.112) | copy-start | bytes 9437188
  151.4 5.9 %copy-start.23 = (bf16[1024,768]{1,0:T(8,128)(2,1)S(1)}, bf16[1024,768]{1,0:T(8,128)(2,1)}, u32[]{:S(2)}) copy-start(bf16[1024,768]{1,0:T(8,128)(2,1)} %get-tuple-element.85) | copy-start | bytes 4718596
  157.3 4.0 copy-start.22
  161.3 7.1 %copy-start = (bf16[1024,1536]{1,0:T(8,128)(2,1)S(1)}, bf16[1024,1536]{1,0:T(8,128)(2,1)}, u32[]{:S(2)}) copy-start(bf16[1024,1536]{1,0:T(8,128)(2,1)} %tok.1) | copy-start | bytes 9437188
  169.7 0.7 copy-start.7
  170.5 36.3 %copy-start.6 = (bf16[1536,128]{1,0:T(8,128)(2,1)S(1)}, bf16[1536,128]{1,0:T(8,128)(2,1)}, u32[]{:S(2)}) copy-start(bf16[1536,128]{1,0:T(8,128)(2,1)} %get-tuple-element.109) | copy-start | bytes 1179652
  198.4 15.2 %collective-permute-start.2 = (bf16[8,256]{1,0:T(8,128)(2,1)}, bf16[8,256]{1,0:T(8,128)(2,1)}, u32[]{:S(2)}, u32[]{:S(2)}) collective-permute-start(bf16[8,256]{1,0:T(8,128)(2,1)} %convert.25), channel_id=1, source_target_pairs={{4,0},{5,1},{6,2},{7,3},{12,8},{13,9},{14,10},{15,11},{20,16},{21,... | collective-permute-start | bytes 12296 | tf_op jit(solution)/shard_map/ppermute | solution.py:1179
  203.2 15.6 %collective-permute-start.1 = (bf16[8,768]{1,0:T(8,128)(2,1)}, bf16[8,768]{1,0:T(8,128)(2,1)S(1)}, u32[]{:S(2)}, u32[]{:S(2)}) collective-permute-start(bf16[8,768]{1,0:T(8,128)(2,1)} %convert.26), channel_id=1, source_target_pairs={{4,0},{5,1},{6,2},{7,3},{12,8},{13,9},{14,10},{15,11},{20,16},{21,... | collective-permute-start | bytes 36872 | tf_op jit(solution)/shard_map/ppermute | solution.py:1179
  206.8 4.7 %copy-start.21 = (bf16[1024,1536]{1,0:T(8,128)(2,1)S(1)}, bf16[1024,1536]{1,0:T(8,128)(2,1)}, u32[]{:S(2)}) copy-start(bf16[1024,1536]{1,0:T(8,128)(2,1)} %get-tuple-element.112) | copy-start | bytes 9437188
  211.5 1.9 copy-start.9
  211.5 1.9 copy-start.15
  214.8 13.0 %slice-start = ((s8[6291456]{0:T(1024)(128)(4,1)}), s8[4194304]{0:T(1024)(128)(4,1)S(1)}, s32[]{:S(2)}) async-start(s8[6291456]{0:T(1024)(128)(4,1)} %bitcast.110), calls=%async_computation.2 | async-start | bytes 8388608
  214.8 13.0 %slice-start.2 = ((s8[6291456]{0:T(1024)(128)(4,1)}), s8[4194304]{0:T(1024)(128)(4,1)S(1)}, s32[]{:S(2)}) async-start(s8[6291456]{0:T(1024)(128)(4,1)} %bitcast.113), calls=%async_computation.4 | async-start | bytes 8388608
  220.2 7.6 %slice-start.1 = ((s8[6291456]{0:T(1024)(128)(4,1)}), s8[2097152]{0:T(1024)(128)(4,1)S(1)}, s32[]{:S(2)}) async-start(s8[6291456]{0:T(1024)(128)(4,1)} %bitcast.110), calls=%async_computation.3 | async-start | bytes 4194304
  220.2 7.6 %slice-start.3 = ((s8[6291456]{0:T(1024)(128)(4,1)}), s8[2097152]{0:T(1024)(128)(4,1)S(1)}, s32[]{:S(2)}) async-start(s8[6291456]{0:T(1024)(128)(4,1)} %bitcast.113), calls=%async_computation.5 | async-start | bytes 4194304
  220.2 7.6 %copy-start.1 = (bf16[1536,256]{1,0:T(8,128)(2,1)S(1)}, bf16[1536,256]{1,0:T(8,128)(2,1)}, u32[]{:S(2)}) copy-start(bf16[1536,256]{1,0:T(8,128)(2,1)} %w_states.1) | copy-start | bytes 2359300
  220.2 7.7 %copy-start.5 = (bf16[1024,256]{1,0:T(8,128)(2,1)S(1)}, bf16[1024,256]{1,0:T(8,128)(2,1)}, u32[]{:S(2)}) copy-start(bf16[1024,256]{1,0:T(8,128)(2,1)} %add_dynamic-update-slice_fusion.1) | copy-start | bytes 1572868
  220.2 7.7 %copy-start.11 = (f32[1536]{0:T(1024)S(1)}, f32[1536]{0:T(1024)}, u32[]{:S(2)}) copy-start(f32[1536]{0:T(1024)} %param.23) | copy-start | bytes 18436
  220.2 7.7 %copy-start.12 = (f32[1024]{0:T(1024)S(1)}, f32[1024]{0:T(1024)}, u32[]{:S(2)}) copy-start(f32[1024]{0:T(1024)} %get-tuple-element.151) | copy-start | bytes 12292
  227.9 7.6 %copy-start.19 = (bf16[1024,768]{1,0:T(8,128)(2,1)S(1)}, bf16[1024,768]{1,0:T(8,128)(2,1)}, u32[]{:S(2)}) copy-start(bf16[1024,768]{1,0:T(8,128)(2,1)} %add_dynamic-update-slice_fusion) | copy-start | bytes 4718596
  403.5 0.7 copy-start.10
  407.5 8.5 %copy-start.4 = (bf16[2,2,96,1536]{3,2,1,0:T(8,128)(2,1)S(1)}, bf16[2,2,96,1536]{3,2,1,0:T(8,128)(2,1)}, u32[]{:S(2)}) copy-start(bf16[2,2,96,1536]{3,2,1,0:T(8,128)(2,1)} %get-tuple-element.121) | copy-start | bytes 3538948
  416.0 1.8 copy-start.3
  417.8 1.8 copy-start.2
  419.6 4.0 copy-start.13
  419.6 4.0 copy-start.14
Sparse Core Ops, SparseCore 0:
  147.4 64.5 reduce-scatter.3

commit v4 on v3

v4 whole, which is shorter than its diff:
```python
import functools

import jax
import jax.numpy as jnp
from jax import lax
from jax.experimental import pallas as pl
from jax.experimental.pallas import tpu as pltpu
from jax.sharding import PartitionSpec as P

SPAN = 256
HEAD = 64
epsilon = 1e-05
LOG2E = 1.4426950408889634
f32 = jnp.float32
bf16 = jnp.bfloat16
ANY = pl.ANY


def mm(a, b):
    return lax.dot_general(a, b, (((1,), (0,)), ((), ())), preferred_element_type=f32)


def mm_nt(a, b):
    return lax.dot_general(a, b, (((1,), (1,)), ((), ())), preferred_element_type=f32)


def split(v, terms):
    parts = []
    for _ in range(terms):
        part = v.astype(bf16)
        parts.append(part)
        v = v - part.astype(f32)
    return parts


def mm_split(a, exact, terms=2):
    return sum(mm(part, exact) for part in split(a, terms))


def split_mm(exact, b, terms=3):
    return sum(mm(exact, part) for part in split(b, terms))


def spread_matrix(channels):
    heads = lax.broadcasted_iota(jnp.int32, (128, channels), 0)
    cols = lax.broadcasted_iota(jnp.int32, (128, channels), 1)
    low = heads * HEAD
    return jnp.where((cols >= low) & (cols < low + HEAD), 1.0, 0.0).astype(bf16)


def gather_matrix(channels):
    heads = lax.broadcasted_iota(jnp.int32, (channels, 128), 1)
    rows = lax.broadcasted_iota(jnp.int32, (channels, 128), 0)
    low = heads * HEAD
    return jnp.where((rows >= low) & (rows < low + HEAD), 1.0, 0.0).astype(bf16)


def lower_ones():
    rows = lax.broadcasted_iota(jnp.int32, (SPAN, SPAN), 0)
    cols = lax.broadcasted_iota(jnp.int32, (SPAN, SPAN), 1)
    return jnp.where(rows >= cols, 1.0, 0.0).astype(bf16)


def upper_ones():
    rows = lax.broadcasted_iota(jnp.int32, (SPAN, SPAN), 0)
    cols = lax.broadcasted_iota(jnp.int32, (SPAN, SPAN), 1)
    return jnp.where(rows <= cols, 1.0, 0.0).astype(bf16)


def sigmoid(v):
    return 1.0 / (1.0 + jnp.exp(-v))


def half_masks():
    lane = lax.broadcasted_iota(jnp.int32, (SPAN, 128), 1)
    return lane < HEAD


def rms_rows(tok, gain):
    wide = tok.astype(f32)
    inverse = lax.rsqrt(jnp.mean(wide * wide, -1, keepdims=True) + epsilon)
    return (wide * inverse * gain).astype(bf16)


MESH = pl.DeviceIdType.MESH
SHARE = 4


def lane_block(index, width):
    return pl.ds(pl.multiple_of(index * width, 128), width)


class Links:
    def __init__(self, send, recv, local=None):
        self.send, self.recv, self.local = send, recv, local
        self.used, self.kept, self.sent = 0, 0, []
        dp = lax.axis_index("dp")
        self.groups = lax.axis_size("dp") // SHARE
        self.group = dp // SHARE
        self.x = lax.rem(dp, SHARE) // 2
        self.core = lax.rem(dp, 2)
        self.y = lax.axis_index("row")
        self.z = lax.axis_index("col")
        self.cols = lax.axis_size("col")

    def dp_of(self, group, x, core):
        return group * SHARE + x * 2 + core

    def mate(self):
        return {"dp": self.dp_of(self.group, self.x, 1 - self.core)}

    def across(self):
        return {"dp": self.dp_of(self.group, 1 - self.x, self.core)}

    def other_row(self):
        return {"row": 1 - self.y}

    def col_peer(self, off):
        return lax.rem(self.z + off, self.cols)

    def group_peer(self, off):
        return {"dp": self.dp_of(lax.rem(self.group + off, self.groups), self.x, self.core)}

    def meet(self, far_groups):
        barrier = pltpu.get_barrier_semaphore()
        peers = [self.mate(), self.across(), self.other_row()]
        peers += [{"col": self.col_peer(off)} for off in range(1, self.cols)]
        if far_groups:
            peers += [self.group_peer(off) for off in range(1, self.groups)]
        for peer in peers:
            pl.semaphore_signal(barrier, inc=1, device_id=peer, device_id_type=MESH)
        pl.semaphore_wait(barrier, len(peers))

    def make(self, src, dst, peer, when=None, track=True):
        at = self.used
        self.used += 1
        copy = pltpu.make_async_remote_copy(
            src_ref=src, dst_ref=dst, send_sem=self.send.at[at], recv_sem=self.recv.at[at],
            device_id=peer, device_id_type=MESH,
        )
        if track:
            self.sent.append((copy, when))
        return copy

    def go(self, src, dst, peer, track=True):
        copy = self.make(src, dst, peer, track=track)
        copy.start()
        return copy

    def keep(self, src, dst):
        copy = pltpu.make_async_copy(src, dst, self.local.at[self.kept])
        self.kept += 1
        return copy

    def finish(self):
        for copy, when in self.sent:
            if when is None:
                copy.wait_send()
            else:
                pl.when(when)(copy.wait_send)


class Steps:
    def __init__(self):
        self.stages = []

    def add(self, remote, local=(), before=None):
        self.stages.append((remote, list(local), before))

    def run(self, s):
        if 0 < s <= len(self.stages):
            remote, local, _ = self.stages[s - 1]
            for c in remote:
                c.wait_recv()
            for c in local:
                c.wait()
        if s < len(self.stages):
            remote, local, before = self.stages[s]
            if before is not None:
                before()
            for c in remote + local:
                c.start()


def spread_steps(t, dst_row, dst_x, dst_core, steps):
    steps.add([t.make(dst_row, dst_row, t.other_row())])
    steps.add([t.make(dst_x, dst_x, t.across())])
    steps.add([t.make(dst_core, dst_core, t.mate())])
    return steps


def column_steps(t, src, dst, width):
    part = src.shape[0] // SHARE
    x, y, z, core = t.x, t.y, t.z, t.core
    rows = pl.ds(pl.multiple_of((x * 2 + core) * part, 16), part)
    lanes = lane_block(y, width)
    steps = Steps()
    here = dst.at[z, x, core, :, lanes]
    remote = []
    for off in range(1, t.cols):
        to = t.col_peer(off)
        remote.append(t.make(src.at[rows, lane_block(to, width)], here, {"col": to}))
    steps.add(remote, [t.keep(src.at[rows, lane_block(z, width)], here)])
    return spread_steps(
        t, dst.at[:, x, core, :, lanes], dst.at[:, x, core], dst.at[:, :, core], steps
    )


def row_steps(t, src, dst, width):
    part = src.shape[0] // t.cols // SHARE
    x, y, z, core = t.x, t.y, t.z, t.core

    def rows(to):
        return pl.ds(pl.multiple_of((to * SHARE + x * 2 + core) * part, 16), part)

    steps = Steps()
    here = dst.at[y, x, core, :, lane_block(z, width)]
    remote = []
    for off in range(1, t.cols):
        to = t.col_peer(off)
        remote.append(t.make(src.at[rows(to), :], here, {"col": to}))
    steps.add(remote, [t.keep(src.at[rows(z), :], here)])
    return spread_steps(t, dst.at[y, x, core], dst.at[:, x, core], dst.at[:, :, core], steps)


def gather_steps(t, own, whole):
    width = own.shape[1]
    z = t.z
    mate, far = z + 1 - 2 * lax.rem(z, 2), lax.rem(z + 2, 4)
    here, there = whole.at[:, lane_block(z, width)], whole.at[:, lane_block(far, width)]
    steps = Steps()
    cross = t.make(own, here, {"col": far})
    near = t.make(own, here, {"col": mate})
    steps.add([cross], [t.keep(own, here)])
    steps.add([near, t.make(there, there, {"col": mate})])
    return steps


def front_kernel(
    inner_total,
    tok, ngain, w_states, meta, docrow, spar, inner, gate, out, step_w, cot, par_own, head_own, halo,
    wi_o, wg_o, wo_o, ws_o, cots_o, par_o, head_o,
    normed_o, pre_o, spre_o, sd_o, ssd_o, x_o, wr_o, step_o, r_o, sig_o, hpre_o, hspre_o, sprev_o,
    gated_o, ggate_o, gy_o, dr_o, dsf_o, dsout_o, acc_o,
    wi, wg, wo, ws2, ws, cots, par, head, head_in, halo_in,
    normed_s, pre_s, spre_s, sd_s, ssd_s, x_s, wr_s, step_s, r_s, sig_s, hpre_s, hspre_s, sprev_s,
    gated_s, ggate_s, gy_s, dr_s, dsf_s, acc_s,
    fresh_s, y_s, gate_s, gg_s, sums_s, sums_in,
    xbuf, sbuf, mem, mem_in,
    send, recv, local,
):
    t = Links(send, recv, local)
    t.meet(False)
    x, y, z, core = t.x, t.y, t.z, t.core
    blocks = tok.shape[0] // SPAN
    channels = x_s.shape[1]
    half = channels // 2
    outputs = []

    def write(src, dst):
        copy = t.keep(src, dst)
        copy.start()
        outputs.append(copy)

    few = [
        t.go(par_own, par.at[:, lane_block(y, half)], t.other_row()),
        t.go(head_own, head_in, t.other_row()),
        t.go(halo, halo_in, t.other_row()),
    ]
    block = inner.shape[1] // t.cols
    get_inner = column_steps(t, inner, wi, block)
    get_step = column_steps(t, step_w, ws2, step_w.shape[1] // t.cols)
    get_gate = column_steps(t, gate, wg, block)
    get_out = row_steps(t, out, wo, out.shape[1])
    get_cot = gather_steps(t, cot, cots)
    pass_state = t.make(mem, mem_in, t.other_row(), track=False)
    pass_sums = [
        t.make(sums_s, sums_in.at[off - 1], {"col": t.col_peer(off)}) for off in range(1, t.cols)
    ]
    get_inner.run(0)
    get_step.run(0)
    get_gate.run(0)
    get_out.run(0)
    get_cot.run(0)
    par[:, lane_block(y, half)] = par_own[...]
    for s in range(1, 5):
        get_inner.run(s)
        get_step.run(s)
        if s > 1:
            get_gate.run(s - 1)
        if s > 2:
            get_out.run(s - 2)
    for c in few:
        c.wait_recv()
    head[...] = head_own[...] + head_in[...]
    wide_in = normed_s.shape[1]
    ws[...] = (
        ws2[:, :, :, :, 0:128].reshape(wide_in, 128) + ws2[:, :, :, :, 128:256].reshape(wide_in, 128)
    )
    spread = spread_matrix(channels)
    gain = ngain[...]

    def w_of(ref):
        return ref[...].reshape(-1, ref.shape[-1])

    def rows_of(i):
        return pl.ds(pl.multiple_of(i * SPAN, SPAN), SPAN)

    hn = rms_rows(halo_in[...], gain)
    hp = mm(hn, w_of(wi))[8:16]
    hs = mm(hn, w_states[...])[8:16]
    xbuf[0:8, :] = hp
    sbuf[0:8, :] = hs
    hpre_s[...] = hp
    hspre_s[...] = hs
    mem[...] = jnp.zeros_like(mem)

    def entry(i, carry):
        at = rows_of(i)

        @pl.when(i > 0)
        def _():
            xbuf[0:8, :] = xbuf[SPAN:SPAN + 8, :]
            sbuf[0:8, :] = sbuf[SPAN:SPAN + 8, :]

        wide_tok = tok[at, :].astype(f32)
        inverse = lax.rsqrt(jnp.mean(wide_tok * wide_tok, -1, keepdims=True) + epsilon)
        normed = (wide_tok * inverse * gain).astype(bf16)
        normed_s[at, :] = normed
        x_pre = mm(normed, w_of(wi))
        s_pre = mm(normed, w_states[...])
        xbuf[8:SPAN + 8, :] = x_pre
        sbuf[8:SPAN + 8, :] = s_pre
        pre_s[at, :] = x_pre.astype(bf16)
        spre_s[at, :] = s_pre.astype(bf16)
        marks = meta[at, :]

        def conv_silu(buf, here, taps):
            v = taps[4:5, :] + taps[0:1, :] * here
            for k in range(1, 4):
                v = v + marks[:, k:k + 1] * (taps[k:k + 1, :] * buf[8 - k:8 - k + SPAN, :])
            sg = sigmoid(v)
            return v * sg, sg * (1.0 + v * (1.0 - sg))

        act, slope = conv_silu(xbuf, x_pre, par)
        x_low = act.astype(bf16)
        x_s[at, :] = x_low
        sd_s[at, :] = slope.astype(bf16)
        sact, sslope = conv_silu(sbuf, s_pre, spar)
        wr = sact.astype(bf16)
        wr_s[at, :] = wr
        ssd_s[at, :] = sslope.astype(bf16)

        raw = mm(normed, ws[...]) + head[0:1, :]
        step = jnp.maximum(raw, 0.0) + jnp.log1p(jnp.exp(-jnp.abs(raw)))
        lane = lax.broadcasted_iota(jnp.int32, (SPAN, 128), 1)
        sig_s[at, :] = jnp.where(lane == 127, inverse, sigmoid(raw))
        step_s[at, :] = step
        r = split_mm(lower_ones(), step * head[1:2, :])
        r_s[at, :] = r
        last = r[SPAN - 1:SPAN, :]
        to_end = jnp.exp2(jnp.minimum(last - r, 0.0)) * marks[:, 5:6]
        coef = mm_split(to_end * step, spread)
        w_t = jnp.transpose(wr[:, 0:128].astype(f32)).astype(bf16)
        fresh = mm(w_t, (coef * x_low.astype(f32)).astype(bf16))
        fresh_s[i] = fresh
        mem[...] = keep_of(last, marks) * mem[...] + fresh

        @pl.when(i == 0)
        def _():
            get_gate.run(4)
            get_out.run(3)
            get_cot.run(1)

        @pl.when(i == 2)
        def _():
            get_out.run(4)

        return carry

    def keep_of(last, marks):
        return mm_split(jnp.broadcast_to(jnp.exp2(last) * marks[0:1, 6:7], (8, 128)), spread)[0:1]

    lax.fori_loop(0, blocks, entry, 0)
    pass_state.start()
    for src, dst in (
        (normed_s, normed_o), (pre_s, pre_o), (spre_s, spre_o), (sd_s, sd_o), (ssd_s, ssd_o),
        (x_s, x_o), (wr_s, wr_o), (step_s, step_o), (r_s, r_o), (sig_s, sig_o), (hpre_s, hpre_o),
        (hspre_s, hspre_o), (wi, wi_o), (wg, wg_o), (wo, wo_o), (ws, ws_o), (par, par_o),
        (head, head_o),
    ):
        write(src, dst)

    def gate_block(i, carry):
        at = rows_of(i)
        gate_s[at, :] = mm(normed_s[at, :], w_of(wg))
        return carry

    lax.fori_loop(0, blocks, gate_block, 0)

    pass_state.wait()
    mem[...] = mem_in[...] * jnp.where(y == 1, 1.0, 0.0)
    skip = mm_split(jnp.broadcast_to(head[2:3, :], (8, 128)), spread)[0:1]
    first = half_masks()

    def scan(i, carry):
        at = rows_of(i)
        marks = meta[at, :]
        w_low = wr_s[at, 0:128]
        r_low = wr_s[at, 128:256]
        r = r_s[at, :]
        r_t = jnp.transpose(r)
        rows = lax.broadcasted_iota(jnp.int32, (SPAN, SPAN), 0)
        cols = lax.broadcasted_iota(jnp.int32, (SPAN, SPAN), 1)
        allowed = (rows >= cols) & (marks[:, 0:1] == docrow[:, at])
        scores = jnp.where(allowed, mm_nt(r_low, w_low), 0.0)
        wide = x_s[at, :].astype(f32)
        xd = (mm_split(step_s[at, :], spread) * wide).astype(bf16)
        sprev = mem[...].astype(bf16)
        sprev_s[i] = sprev
        linked = jnp.exp2(r) * marks[:, 4:5]
        carried = mm(r_low, sprev) * mm_split(linked, spread)
        y_s[at, :] = carried + skip * wide
        for pair in range(channels // 128):
            lanes = slice(pair * 128, pair * 128 + 128)
            xp = xd[:, lanes]
            total = y_s[at, lanes]
            for part in range(2):
                h = 2 * pair + part
                decay = jnp.exp2(jnp.minimum(r[:, h:h + 1] - r_t[h:h + 1, :], 0.0))
                mixing = (scores * decay).astype(bf16)
                own = jnp.where(first if part == 0 else ~first, xp, jnp.zeros_like(xp))
                total = total + mm(mixing, own)
            y_s[at, lanes] = total
        last = r[SPAN - 1:SPAN, :]
        mem[...] = keep_of(last, marks) * mem[...] + fresh_s[i]
        return carry

    lax.fori_loop(0, blocks, scan, 0)
    write(sprev_s, sprev_o)

    get_cot.run(2)
    write(cots, cots_o)
    ones = jnp.ones((8, channels), bf16)

    def totals_of(i, carry):
        at = rows_of(i)
        gg = mm_nt(cots[at, :], w_of(wo))
        gg_s[at, :] = gg
        g = gate_s[at, :]
        mixed = y_s[at, :] * (g * sigmoid(g))
        sq = sum(mm_nt(ones, part) for part in split(mixed * mixed, 2))
        pr = sum(mm_nt(ones, part) for part in split(mixed * (par[5:6, :] * gg), 2))
        row = lax.broadcasted_iota(jnp.int32, (8, SPAN), 0)
        sums_s[:, at] = jnp.where(row == 0, sq, jnp.where(row == 1, pr, 0.0))
        return carry

    lax.fori_loop(0, blocks, totals_of, 0)
    for c in pass_sums:
        c.start()
    for c in pass_sums:
        c.wait_recv()
    mem[...] = jnp.zeros_like(mem)
    acc_s[...] = jnp.zeros_like(acc_s)
    gather = gather_matrix(channels)

    def turn(back_i, carry):
        i = blocks - 1 - back_i
        at = rows_of(i)
        marks = meta[at, :]
        both = sums_s[:, at]
        for off in range(1, t.cols):
            both = both + sums_in[off - 1, :, at]
        totals = jnp.transpose(both)
        scale = lax.rsqrt(totals[:, 0:1] / inner_total + epsilon)
        cross = totals[:, 1:2] / inner_total
        yv = y_s[at, :]
        g = gate_s[at, :]
        sg = sigmoid(g)
        sl = g * sg
        gg = gg_s[at, :]
        ngate = par[5:6, :]
        normal = yv * sl * scale
        gated_s[at, :] = (normal * ngate).astype(bf16)
        g_mixed = scale * (ngate * gg - normal * (scale * cross))
        ggate_s[at, :] = (g_mixed * yv * (sg * (1.0 + g * (1.0 - sg)))).astype(bf16)
        gy = (g_mixed * sl).astype(bf16)
        gy_s[at, :] = gy
        gyw = gy.astype(f32)
        wide = x_s[at, :].astype(f32)
        dr_s[at, :] = mm_split(gyw * (yv - skip * wide), gather)
        row = lax.broadcasted_iota(jnp.int32, (8, channels), 0)
        ggain = jnp.sum(gg * normal, 0, keepdims=True)
        gskip = jnp.sum(gyw * wide, 0, keepdims=True)
        acc_s[...] += jnp.where(row == 0, ggain, jnp.where(row == 1, gskip, 0.0))
        r = r_s[at, :]
        linked = mm_split(jnp.exp2(r) * marks[:, 4:5], spread)
        r_t = jnp.transpose(wr_s[at, 128:256].astype(f32)).astype(bf16)
        dfresh = mm(r_t, (linked * gyw).astype(bf16))
        dsf_s[i] = dfresh
        mem[...] = keep_of(r[SPAN - 1:SPAN, :], marks) * mem[...] + dfresh
        return carry

    lax.fori_loop(0, blocks, turn, 0)
    for src, dst in (
        (gated_s, gated_o), (ggate_s, ggate_o), (gy_s, gy_o), (dr_s, dr_o), (dsf_s, dsf_o),
        (mem, dsout_o), (acc_s, acc_o),
    ):
        write(src, dst)
    for copy in outputs:
        copy.wait()
    t.finish()


def front(inner_all, tok, ngain, w_states, meta, docrow, spar, inner, gate, out, step_w, cot, par_own,
          head_own, halo):
    tokens, width = tok.shape
    blocks = tokens // SPAN
    cols = lax.axis_size("col")
    part, half = inner.shape[0] // SHARE, inner.shape[1] // cols
    channels = 2 * half
    sds = jax.ShapeDtypeStruct
    V = pltpu.VMEM
    weights = [
        ((cols, 2, 2, part, channels), bf16), ((cols, 2, 2, part, channels), bf16),
        ((2, 2, 2, half // SHARE, width), bf16),
    ]
    entry_shapes = [
        ((tokens, width), bf16), ((tokens, channels), bf16), ((tokens, 256), bf16),
        ((tokens, channels), bf16), ((tokens, 256), bf16), ((tokens, channels), bf16),
        ((tokens, 256), bf16), ((tokens, 128), f32), ((tokens, 128), f32), ((tokens, 128), f32),
        ((8, channels), f32), ((8, 256), f32), ((blocks, 128, channels), bf16),
    ]
    turn_shapes = [
        ((tokens, channels), bf16), ((tokens, channels), bf16), ((tokens, channels), bf16),
        ((tokens, 128), f32), ((blocks, 128, channels), f32),
    ]
    state = ((128, channels), f32)
    acc = ((8, channels), f32)
    outs = (
        weights + [((width, 128), bf16), ((tokens, width), bf16), ((8, channels), f32), ((8, 128), f32)]
        + entry_shapes + turn_shapes + [state, acc]
    )
    scratch = (
        weights
        + [((cols, 2, 2, part, 256), bf16), ((width, 128), bf16), ((tokens, width), bf16),
           ((8, channels), f32), ((8, 128), f32), ((8, 128), f32), (halo.shape, bf16)]
        + entry_shapes + turn_shapes + [acc]
        + [((blocks, 128, channels), f32), ((tokens, channels), f32), ((tokens, channels), f32),
           ((tokens, channels), f32), ((8, tokens), f32), ((cols - 1, 8, tokens), f32),
           ((SPAN + 8, channels), f32), ((SPAN + 8, 256), f32), state, state]
    )
    vmem = pl.BlockSpec(memory_space=V)
    hbm = pl.BlockSpec(memory_space=pl.ANY)
    got = pl.pallas_call(
        functools.partial(front_kernel, float(inner_all)),
        out_shape=[sds(*o) for o in outs],
        in_specs=[vmem] * 6 + [hbm] * 5 + [vmem, vmem, hbm],
        out_specs=[hbm] * len(outs),
        scratch_shapes=[V(*s) for s in scratch] + [
            pltpu.SemaphoreType.DMA((48,)), pltpu.SemaphoreType.DMA((48,)),
            pltpu.SemaphoreType.DMA((48,)),
        ],
        compiler_params=pltpu.CompilerParams(
            collective_id=1, has_side_effects=True, vmem_limit_bytes=62 * 1024 * 1024
        ),
        name="front",
    )(tok, ngain, w_states, meta, docrow, spar, inner, gate, out, step_w, cot, par_own, head_own, halo)
    got = list(got)
    got[0] = got[0].reshape(width, channels)
    got[1] = got[1].reshape(width, channels)
    got[2] = got[2].reshape(channels, width)
    return got


def mm_tn(a, b):
    return lax.dot_general(a, b, (((0,), (0,)), ((), ())), preferred_element_type=f32)


def add_bf16(a, b):
    return (a.astype(f32) + b.astype(f32)).astype(bf16)


def sum_far_groups(t, own, got, spare):
    if t.groups == 1:
        return
    more = [t.go(own, got.at[off - 1], t.group_peer(off), False) for off in range(1, t.groups)]
    for c in more:
        c.wait()
    for off in range(1, t.groups):
        back = t.keep(got.at[off - 1], spare)
        back.start()
        back.wait()
        own[...] = add_bf16(own[...], spare[...])


def column_sums(t, g, a1, a2, a3, a4, far, o):
    x, y, z, core = t.x, t.y, t.z, t.core
    width = a4.shape[-1]
    steps = Steps()
    steps.add([t.make(g.at[:, :, 1 - core], a1, t.mate())])

    def add_core():
        def body(i, c):
            for j in range(2):
                a1[i, j] = add_bf16(a1[i, j], g[i, j, core])
            return c

        lax.fori_loop(0, t.cols, body, 0)

    steps.add([t.make(a1.at[:, :, :, lane_block(1 - y, width)], a2, t.other_row())], (), add_core)
    mine = lane_block(y, width)

    def add_row():
        def body(i, c):
            for j in range(2):
                a2[i, j] = add_bf16(a2[i, j], a1[i, j, :, mine])
            return c

        lax.fori_loop(0, t.cols, body, 0)

    steps.add([t.make(a2.at[:, 1 - x], a3, t.across())], (), add_row)

    def add_x():
        def body(i, c):
            a4[i] = add_bf16(a3[i], a2[i, x])
            return c

        lax.fori_loop(0, t.cols, body, 0)
        sum_far_groups(t, a4, far, a3)

    here = o.at[x, core, :, lane_block(z, width)]
    steps.add(
        [t.make(a4.at[t.col_peer(off)], here, {"col": t.col_peer(off)}) for off in range(1, t.cols)],
        [t.keep(a4.at[z], here)], add_x,
    )
    steps.add([t.make(o.at[x, core], o.at[x, core], t.across())])
    steps.add([t.make(o.at[:, core], o.at[:, core], t.mate())])
    return steps


def row_sums(t, g, a1, a2, a3, a4, far, o):
    x, y, z, core = t.x, t.y, t.z, t.core
    width = o.shape[-1]
    steps = Steps()
    steps.add([t.make(g.at[:, :, 1 - core], a1, t.mate())])

    def add_core():
        def body(i, c):
            for j in range(2):
                a1[i, j] = add_bf16(a1[i, j], g[i, j, core])
            return c

        lax.fori_loop(0, 2, body, 0)

    steps.add([t.make(a1.at[1 - y], a2, t.other_row())], (), add_core)

    def add_row():
        for j in range(2):
            a2[j] = add_bf16(a2[j], a1[y, j])

    steps.add([t.make(a2.at[1 - x], a3, t.across())], (), add_row)

    def add_x():
        a4[...] = add_bf16(a3[...], a2[x])
        sum_far_groups(t, a4, far, a3)

    here = o.at[z, x, core]
    steps.add(
        [t.make(a4.at[:, lane_block(t.col_peer(off), width)], here, {"col": t.col_peer(off)})
         for off in range(1, t.cols)],
        [t.keep(a4.at[:, lane_block(z, width)], here)], add_x,
    )
    steps.add([t.make(o.at[:, x, core], o.at[:, x, core], t.across())])
    steps.add([t.make(o.at[:, :, core], o.at[:, :, core], t.mate())])
    return steps


def full_sums(t, g, s1, s2, s3, s4, s5, far, o):
    x, y, z, core = t.x, t.y, t.z, t.core
    steps = Steps()
    steps.add([t.make(g.at[:, :, :, 1 - core], s1, t.mate())])

    def add_core():
        def body(i, c):
            for j in range(2):
                for k in range(2):
                    s1[i, j, k] = add_bf16(s1[i, j, k], g[i, j, k, core])
            return c

        lax.fori_loop(0, t.cols, body, 0)

    steps.add([t.make(s1.at[:, 1 - y], s2, t.other_row())], (), add_core)

    def add_row():
        def body(i, c):
            for k in range(2):
                s2[i, k] = add_bf16(s2[i, k], s1[i, y, k])
            return c

        lax.fori_loop(0, t.cols, body, 0)

    steps.add([t.make(s2.at[:, 1 - x], s3, t.across())], (), add_row)

    def add_x():
        def body(i, c):
            s4[i] = add_bf16(s3[i], s2[i, x])
            return c

        lax.fori_loop(0, t.cols, body, 0)
        sum_far_groups(t, s4, far, s3)

    steps.add(
        [t.make(s4.at[t.col_peer(off)], s5.at[off - 1], {"col": t.col_peer(off)})
         for off in range(1, t.cols)], (), add_x,
    )

    def add_cols():
        total = s4[z].astype(f32)
        for off in range(1, t.cols):
            total = total + s5[off - 1].astype(f32)
        s4[z] = total.astype(bf16)

    here = o.at[z, y, x, core]
    steps.add(
        [t.make(s4.at[z], here, {"col": t.col_peer(off)}) for off in range(1, t.cols)],
        [t.keep(s4.at[z], here)], add_cols,
    )
    here = o.at[:, y, x, core]
    steps.add([t.make(here, here, t.other_row())])
    here = o.at[:, :, x, core]
    steps.add([t.make(here, here, t.across())])
    here = o.at[:, :, :, core]
    steps.add([t.make(here, here, t.mate())])
    return steps


def small_sums(t, sm, msum, mgot, out, rest):
    steps = Steps()
    steps.add([t.make(sm, mgot.at[0], t.mate())])

    def add_core():
        msum[0] = sm[...] + mgot[0]

    steps.add([t.make(msum.at[0], mgot.at[1], t.other_row())], (), add_core)

    def add_row():
        msum[1] = msum[0] + mgot[1]

    steps.add([t.make(msum.at[1], mgot.at[2], t.across())], (), add_row)

    def add_x():
        msum[2] = msum[1] + mgot[2]
        if t.groups > 1:
            more = [t.go(msum.at[2], mgot.at[5 + off], t.group_peer(off), False)
                    for off in range(1, t.groups)]
            for c in more:
                c.wait()
            total = msum[2]
            for off in range(1, t.groups):
                total = total + mgot[5 + off]
            msum[2] = total

    last = pl.ds(rest, sm.shape[0] - rest)
    steps.add(
        [t.make(msum.at[2, last], mgot.at[2 + off, last], {"col": t.col_peer(off)})
         for off in range(1, t.cols)], (), add_x,
    )

    def done():
        out[0:rest] = msum[2, 0:rest]
        out[rest:] = msum[2, rest:] + mgot[3, rest:] + mgot[4, rest:] + mgot[5, rest:]

    steps.add([], (), done)
    return steps


class PairSum:
    def __init__(self, t, part, near, far_in, rows):
        z = t.z
        mate = z + 1 - 2 * lax.rem(z, 2)
        far = lax.rem(z + 2, 4)
        mate_far = lax.rem(mate + 2, 4)
        width = near.shape[-1]
        self.part, self.near, self.far_in, self.rows = part, near, far_in, rows
        self.own, self.far = lane_block(z, width), lane_block(far, width)
        to_mate = [
            t.make(part.at[rows, lane_block(mate_far, width)], near.at[1, rows], {"col": mate}),
            t.make(part.at[rows, lane_block(mate, width)], near.at[0, rows], {"col": mate}),
        ]
        self.first, self.second = to_mate
        self.across = t.make(near.at[1, rows], far_in.at[rows], {"col": far})

    def start(self):
        self.first.start()
        self.second.start()

    def forward(self):
        self.first.wait_recv()
        count = self.rows.size // 64

        def body(i, c):
            at = pl.ds(pl.multiple_of(self.rows.start + i * 64, 16), 64)
            self.near[1, at] = add_bf16(self.near[1, at], self.part[at, self.far])
            return c

        lax.fori_loop(0, count, body, 0)
        self.across.start()

    def arrive(self):
        self.second.wait_recv()
        self.across.wait_recv()

    def total(self, at):
        return (
            self.part[at, self.own].astype(f32) + self.near[0, at].astype(f32)
            + self.far_in[at].astype(f32)
        )


def rear_kernel(
    meta, hmeta, docrow, head, par, spar, hpre, hspre, acc1, ngain_cols,
    tok_h, w_states_h, dsout_h, wi_h, wg_h, wo_h, ws_h, cots_h, normed_h, pre_h, spre_h, sd_h, ssd_h,
    x_h, wr_h, step_h, r_h, sig_h, sprev_h, gated_h, ggate_h, gy_h, dr_h, dsf_h,
    mixed_o, gtok_o, oi, og, oz, oo, os, sm_o, far_i, far_g, far_z, far_o, far_s,
    tok, wst, dsout, wi, wg, wo, ws, cots, normed, pre, spre, sd, ssd,
    x_s, wr_s, step_s, r_s, sig_s, sprev_s, gated, ggate, gy_s, dr_s, dsf_s,
    cot_own, dmem, gs_s, gz_s, gbuf, hbuf, hx, hs, hx_in, hs_in, accx, accs, acch, gshare,
    out_part, out_near, out_far, g_near, g_far, ish, ish_in,
    gi, i1, i2, i3, i4, gg, g1, g2, g3, g4, gz, z1, z2, z3, z4, o1, o2, o3, o4,
    gs, s1, s2, s3, s4, s5, sm, msum, mgot,
    send, recv, local,
):
    t = Links(send, recv, local)
    x, y, z, core = t.x, t.y, t.z, t.core
    tokens, width = normed.shape
    channels = gated.shape[1]
    third = width // t.cols
    blocks = tokens // SPAN
    own_cols = lane_block(z, third)

    def load(src, dst):
        copy = t.keep(src, dst)
        copy.start()
        return copy

    load_out = [load(gated_h, gated), load(wo_h, wo), load(dsout_h, dsout)]
    load_grad = [load(cots_h, cots), load(cots_h.at[:, own_cols], cot_own)]
    load_gate = [load(normed_h, normed), load(ggate_h, ggate)]
    load_back = [
        load(a, b) for a, b in (
            (x_h, x_s), (wr_h, wr_s), (gy_h, gy_s), (r_h, r_s), (step_h, step_s), (sig_h, sig_s),
            (dr_h, dr_s), (sprev_h, sprev_s), (dsf_h, dsf_s), (pre_h, pre), (spre_h, spre),
            (sd_h, sd), (ssd_h, ssd),
        )
    ]
    load_norm = [load(wg_h, wg), load(wi_h, wi), load(ws_h, ws), load(w_states_h, wst),
                 load(tok_h.at[:, own_cols], tok)]

    go = wo
    gx_s = gated
    part = cots
    pass_state = t.make(dsout, dmem, t.other_row())
    halo_x = t.make(hx, hx_in, t.other_row())
    halo_s = t.make(hs, hs_in, t.other_row())
    out_sum = PairSum(t, out_part, out_near, out_far, pl.ds(0, tokens))
    norm_sums = [PairSum(t, part, g_near, g_far, pl.ds(b * SPAN, SPAN)) for b in range(blocks)]
    sum_out = row_sums(t, go, o1, o2, o3, o4, far_o, oo)
    sum_gate = column_sums(t, gg, g1, g2, g3, g4, far_g, og)
    sum_inner = column_sums(t, gi, i1, i2, i3, i4, far_i, oi)
    sum_step = column_sums(t, gz, z1, z2, z3, z4, far_z, oz)
    sum_states = full_sums(t, gs, s1, s2, s3, s4, s5, far_s, os)
    sum_small = small_sums(t, sm, msum, mgot, sm_o, 16)
    send_ish = [t.make(ish, ish_in.at[off - 1], {"col": t.col_peer(off)}) for off in range(1, t.cols)]
    t.meet(True)

    def rows_of(i):
        return pl.ds(pl.multiple_of(i * SPAN, SPAN), SPAN)

    def w_of(ref):
        return ref[...].reshape(-1, ref.shape[-1])

    for c in load_out:
        c.wait()
    pass_state.start()

    def project(i, carry):
        at = rows_of(i)
        out_part[at, :] = mm(gated[at, :], w_of(wo)).astype(bf16)
        return carry

    lax.fori_loop(0, blocks, project, 0)
    out_sum.start()
    for c in load_grad:
        c.wait()

    def grad_out(i, carry):
        rows = pl.ds(pl.multiple_of(i * (channels // 2), 128), channels // 2)
        for n in range(2):
            lanes = slice(n * width // 2, (n + 1) * width // 2)
            value = mm_tn(gated[:, rows], cots[:, lanes]).astype(bf16)
            go[i, :, :, :, lanes] = value.reshape(go.shape[1:4] + (width // 2,))
        return carry

    lax.fori_loop(0, 2, grad_out, 0)
    sum_out.run(0)
    for c in load_gate:
        c.wait()

    def weight_grad(right, target):
        def body(i, carry):
            rows = pl.ds(pl.multiple_of(i * third, 128), third)
            target[i] = mm_tn(normed[:, rows], right[...]).astype(bf16).reshape(target.shape[1:])
            return carry

        lax.fori_loop(0, t.cols, body, 0)

    weight_grad(ggate, gg)
    sum_gate.run(0)
    for c in load_back + load_norm:
        c.wait()
    pass_state.wait_recv()
    dmem[...] = dmem[...] * jnp.where(y == 0, 1.0, 0.0)
    accx[...] = jnp.zeros_like(accx)
    accs[...] = jnp.zeros_like(accs)
    acch[...] = jnp.zeros_like(acch)
    gshare[...] = jnp.zeros_like(gshare)
    gbuf[...] = jnp.zeros_like(gbuf)
    hbuf[...] = jnp.zeros_like(hbuf)
    spread = spread_matrix(channels)
    gather = gather_matrix(channels)
    first = half_masks()
    skip = mm_split(jnp.broadcast_to(head[2:3, :], (8, 128)), spread)[0:1]

    def normed_grad(i):
        at = rows_of(i)

        def body(c, column):
            lanes = pl.ds(pl.multiple_of(c * third, 128), third)
            total = (
                mm_nt(ggate[at, :], wg[lanes, :]) + mm_nt(gx_s[at, :], wi[lanes, :])
                + mm_nt(gz_s[at, :], ws[lanes, :]) + mm_nt(gs_s[at, :], wst[lanes, :])
            )
            part[at, lanes] = total.astype(bf16)
            weighed = total * normed[at, lanes].astype(f32)
            gshare[0:1, lanes] += jnp.sum(weighed, 0, keepdims=True)
            return column + jnp.sum(weighed, -1, keepdims=True)

        column = lax.fori_loop(0, t.cols, body, jnp.zeros((SPAN, 1), f32))
        ish[:, at] = jnp.transpose(jnp.broadcast_to(column, (SPAN, 128)))[0:8]

    def back(back_i, carry):
        i = blocks - 1 - back_i
        at = rows_of(i)

        @pl.when(back_i > 0)
        def _():
            gbuf[SPAN + 8:SPAN + 16, :] = gbuf[8:16, :]
            hbuf[SPAN + 8:SPAN + 16, :] = hbuf[8:16, :]

        marks = meta[at, :]
        w_low = wr_s[at, 0:128]
        r_low = wr_s[at, 128:256]
        r = r_s[at, :]
        r_t = jnp.transpose(r)
        step = step_s[at, :]
        last = r[SPAN - 1:SPAN, :]
        rows = lax.broadcasted_iota(jnp.int32, (SPAN, SPAN), 0)
        cols = lax.broadcasted_iota(jnp.int32, (SPAN, SPAN), 1)
        allowed = (rows <= cols) & (marks[:, 0:1] == docrow[:, at])
        scores = jnp.where(allowed, mm_nt(w_low, r_low), 0.0)
        ds = dmem[...]
        ds_low = ds.astype(bf16)
        step_parts = split(step, 2)
        te_parts = split(jnp.exp2(jnp.minimum(last - r, 0.0)) * marks[:, 5:6], 2)
        linked_parts = split(jnp.exp2(r) * marks[:, 4:5], 2)
        keep = mm_split(jnp.broadcast_to(jnp.exp2(last) * marks[0:1, 6:7], (8, 128)), spread)[0:1]
        final = jnp.where(back_i == blocks - 1, 1.0, 0.0)

        def conv_back(buf, lanes, gv, base, taps, acc, halo_pre, out, halo_out):
            buf[8:SPAN + 8, lanes] = gv
            cols_here = gv.shape[1]
            total = taps[0:1, lanes] * gv
            sums = [jnp.sum(gv * base, 0, keepdims=True)]
            halo = jnp.zeros((8, cols_here), f32)
            hsum = []
            for k in range(1, 4):
                moved = marks[:, 7 + k:8 + k] * buf[8 + k:8 + k + SPAN, lanes]
                total = total + taps[k:k + 1, lanes] * moved
                sums.append(jnp.sum(moved * base, 0, keepdims=True))
                hmoved = hmeta[:, 7 + k:8 + k] * buf[k:8 + k, lanes]
                halo = halo + taps[k:k + 1, lanes] * hmoved
                hsum.append(jnp.sum(hmoved * halo_pre[:, lanes], 0, keepdims=True))
            sums.append(jnp.sum(gv, 0, keepdims=True))
            out[at, lanes] = total.astype(bf16)
            halo_out[:, lanes] = halo
            rows8 = lax.broadcasted_iota(jnp.int32, (8, cols_here), 0)
            add = jnp.zeros((8, cols_here), f32)
            for n, s in enumerate(sums):
                if 1 <= n <= 3:
                    s = s + final * hsum[n - 1]
                add = add + jnp.where(rows8 == n, s, 0.0)
            acc[:, lanes] += add

        zero = jnp.zeros((SPAN, 128), f32)
        dscores = jnp.zeros((SPAN, SPAN), f32)
        g_write, g_read, dr_cols, dstep = zero, zero, zero, zero
        at_end = jnp.zeros((8, 128), f32)
        for pair in range(channels // 128):
            lanes = slice(pair * 128, pair * 128 + 128)
            to_lanes, to_heads = spread[:, lanes], gather[lanes, :]

            def widen(parts):
                return sum(mm(p, to_lanes) for p in parts)

            wide = x_s[at, lanes].astype(f32)
            step_wide = widen(step_parts)
            xp = (step_wide * wide).astype(bf16)
            xdw = xp.astype(f32)
            gp = gy_s[at, lanes]
            gyw = gp.astype(f32)
            ds_pair = ds_low[:, lanes]
            sprev = sprev_s[i, :, lanes]
            te = widen(te_parts)
            total = te * mm(w_low, ds_pair)
            ending = jnp.sum(xdw * total, 0, keepdims=True) + keep[:, lanes] * jnp.sum(
                sprev.astype(f32) * ds[:, lanes], 0, keepdims=True
            )
            at_end = at_end + mm_split(jnp.broadcast_to(ending, (8, 128)), to_heads, 3)
            for half in range(2):
                h = 2 * pair + half
                own = first if half == 0 else ~first
                decay = jnp.exp2(jnp.minimum(r_t[h:h + 1, :] - r[:, h:h + 1], 0.0))
                mixing = (scores * decay).astype(bf16)
                gown = jnp.where(own, gp, jnp.zeros_like(gp))
                total = total + mm(mixing, gown)
                dscores = dscores + mm_nt(xp, gown) * decay
            g_write = g_write + mm_nt((te * xdw).astype(bf16), ds_pair)
            g_read = g_read + mm_nt((widen(linked_parts) * gyw).astype(bf16), sprev)
            dr_cols = dr_cols + mm_split(xdw * total, to_heads)
            dstep = dstep + mm_split(wide * total, to_heads)
            g_x = step_wide * total + skip[:, lanes] * gyw
            conv_back(gbuf, lanes, g_x * sd[at, lanes].astype(f32), pre[at, lanes].astype(f32), par,
                      accx, hpre, gx_s, hx)
        dscores = jnp.where(allowed, dscores, 0.0)
        g_write = g_write + mm(dscores.astype(bf16), r_low)
        g_read = g_read + mm(jnp.transpose(dscores).astype(bf16), w_low)
        both = slice(0, 256)
        g_wr = jnp.concatenate([g_write, g_read], 1)
        conv_back(hbuf, both, g_wr * ssd[at, :].astype(f32), spre[at, :].astype(f32), spar, accs,
                  hspre, gs_s, hs)
        tail_row = lax.broadcasted_iota(jnp.int32, (SPAN, 128), 0) == SPAN - 1
        dr = dr_s[at, :] - dr_cols + jnp.where(tail_row, at_end[0:1], 0.0)
        da = split_mm(upper_ones(), dr)
        dstep = dstep + head[3:4, :] * da
        gzv = dstep * sig_s[at, :]
        gz_s[at, :] = gzv.astype(bf16)
        row = lax.broadcasted_iota(jnp.int32, (8, 128), 0)
        gbias = jnp.sum(gzv, 0, keepdims=True)
        grate = jnp.sum(da * step, 0, keepdims=True)
        acch[...] += jnp.where(row == 0, gbias, jnp.where(row == 1, grate, 0.0))
        dmem[...] = keep * ds + dsf_s[i]

        @pl.when(back_i > 0)
        def _():
            normed_grad(i)

        @pl.when(back_i == 0)
        def _():
            sum_out.run(1)
            sum_gate.run(1)

        @pl.when(back_i == 1)
        def _():
            norm_sums[2].start()
            sum_out.run(2)
            sum_gate.run(2)
            out_sum.forward()

        @pl.when(back_i == 2)
        def _():
            norm_sums[1].start()
            sum_out.run(3)
            sum_gate.run(3)
            norm_sums[2].forward()

        return carry

    lax.fori_loop(0, blocks, back, 0)
    halo_x.start()
    halo_s.start()
    norm_sums[0].start()
    sum_out.run(4)
    sum_gate.run(4)
    norm_sums[1].forward()
    halo_x.wait_recv()
    halo_s.wait_recv()
    use = jnp.where(y == 0, 1.0, 0.0)
    end = pl.ds(tokens - 16, 16)
    zeros = jnp.zeros((8, channels), f32)
    gx_s[end, :] = (
        gx_s[end, :].astype(f32) + jnp.concatenate([zeros, use * hx_in[...]], 0)
    ).astype(bf16)
    zeros = jnp.zeros((8, 256), f32)
    gs_s[end, :] = (
        gs_s[end, :].astype(f32) + jnp.concatenate([zeros, use * hs_in[...]], 0)
    ).astype(bf16)
    normed_grad(blocks - 1)
    norm_sums[3].start()
    for c in send_ish:
        c.start()
    weight_grad(gx_s, gi)
    sum_inner.run(0)
    norm_sums[0].forward()
    sum_out.run(5)
    sum_gate.run(5)

    def gz_body(i, carry):
        rows = pl.ds(pl.multiple_of(i * third, 128), third)
        value = mm_tn(normed[:, rows], gz_s[...]).astype(bf16)
        gz[i] = jnp.concatenate([value, value], 1).reshape(gz.shape[1:])
        return carry

    lax.fori_loop(0, t.cols, gz_body, 0)
    sum_step.run(0)
    sum_inner.run(1)

    def gs_body(i, carry):
        rows = pl.ds(pl.multiple_of(i * third, 128), third)
        gs[i] = mm_tn(normed[:, rows], gs_s[...]).astype(bf16).reshape(gs.shape[1:])
        return carry

    lax.fori_loop(0, t.cols, gs_body, 0)
    sum_states.run(0)
    sm[0:8, :] = accx[...]
    sm[8:16, :] = acc1[...]
    sm[16:24, 0:256] = accs[...]
    sm[10:12, 0:128] = acch[0:2, :]
    sm[16:24, 256:] = jnp.zeros((8, channels - 256), f32)
    sm[24:32, :] = gshare[:, 0:channels]
    sm[32:40, :] = gshare[:, channels:]
    sum_small.run(0)
    norm_sums[3].forward()
    sum_out.run(6)
    sum_gate.run(6)
    chain = [sum_inner, sum_step, sum_small, sum_states]
    at_stage = [2, 1, 1, 1]
    for _ in range(9):
        for n, item in enumerate(chain):
            if at_stage[n] <= len(item.stages):
                item.run(at_stage[n])
                at_stage[n] += 1

    out_sum.arrive()
    for c in send_ish:
        c.wait_recv()
    for n in norm_sums:
        n.arrive()

    def finish(i, carry):
        at = rows_of(i)
        own = tok[at, :].astype(f32)
        out_far[at, :] = (own + out_sum.total(at)).astype(bf16)
        both = ish[:, at]
        for off in range(1, t.cols):
            both = both + ish_in[off - 1, :, at]
        along = jnp.transpose(both)[:, 0:1] / width
        inverse = sig_s[at, 127:128]
        grad = inverse * (norm_sums[0].total(at) * ngain_cols[...] - own * (inverse * along))
        g_far[at, :] = (grad + cot_own[at, :].astype(f32)).astype(bf16)
        return carry

    lax.fori_loop(0, blocks, finish, 0)
    results = [load(out_far, mixed_o), load(g_far, gtok_o)]
    for c in results:
        c.wait()
    t.finish()


def rear(meta, hmeta, docrow, head, par, spar, hpre, hspre, acc1, ngain_cols, tok, w_states, dsout,
         weights, cots, normed, pre, spre, sd, ssd, x, wr, step, r, sig, sprev, gated, ggate, gy, dr, dsf):
    wi, wg, wo, ws = weights
    tokens, width = normed.shape
    channels = gated.shape[1]
    blocks = tokens // SPAN
    cols = lax.axis_size("col")
    groups = lax.axis_size("dp") // SHARE - 1
    third, own = width // cols, channels // 2
    q, qo, qs = third // SHARE, own // SHARE, width // (cols * 2 * SHARE)
    sds = jax.ShapeDtypeStruct
    V = pltpu.VMEM
    big = [tok, w_states, dsout, wi, wg, wo.reshape(2, 2, 2, qo, width), ws, cots, normed, pre, spre,
           sd, ssd, x, wr, step, r, sig, sprev, gated, ggate, gy, dr, dsf]
    scratch = [((tokens, third), bf16)] + [(b.shape, b.dtype) for b in big[1:]]

    def col_scratch(w):
        return [((cols, 2, 2, q, 2 * w), bf16), ((cols, 2, q, 2 * w), bf16), ((cols, 2, q, w), bf16),
                ((cols, q, w), bf16), ((cols, q, w), bf16)]

    scratch += [
        ((tokens, third), bf16), ((128, channels), f32),
        ((tokens, 256), bf16), ((tokens, 128), bf16),
        ((SPAN + 16, channels), f32), ((SPAN + 16, 256), f32), ((8, channels), f32), ((8, 256), f32),
        ((8, channels), f32), ((8, 256), f32), ((8, channels), f32), ((8, 256), f32), ((8, 128), f32),
        ((8, width), f32),
        ((tokens, width), bf16), ((2, tokens, third), bf16), ((tokens, third), bf16),
        ((2, tokens, third), bf16), ((tokens, third), bf16), ((8, tokens), f32),
        ((cols - 1, 8, tokens), f32),
    ]
    scratch += col_scratch(own) + col_scratch(own) + col_scratch(128)
    scratch += [
        ((2, 2, qo, width), bf16), ((2, qo, width), bf16), ((qo, width), bf16), ((qo, width), bf16),
        ((cols, 2, 2, 2, qs, 256), bf16), ((cols, 2, 2, qs, 256), bf16), ((cols, 2, qs, 256), bf16),
        ((cols, qs, 256), bf16), ((cols, qs, 256), bf16), ((cols - 1, qs, 256), bf16),
        ((40, channels), f32), ((3, 40, channels), f32), ((6 + groups, 40, channels), f32),
    ]
    if groups:
        far = [(groups, cols, q, own), (groups, cols, q, own), (groups, cols, q, 128),
               (groups, qo, width), (groups, cols, qs, 256)]
    else:
        far = [(16, 128)] * 5
    vmem = pl.BlockSpec(memory_space=V)
    hbm = pl.BlockSpec(memory_space=pl.ANY)
    small = [meta, hmeta, docrow, head, par, spar, hpre, hspre, acc1, ngain_cols]
    got = pl.pallas_call(
        rear_kernel,
        out_shape=[
            sds((tokens, third), bf16), sds((tokens, third), bf16),
            sds((2, 2, q, cols * own), bf16), sds((2, 2, q, cols * own), bf16),
            sds((2, 2, q, cols * 128), bf16), sds((cols, 2, 2, qo, third), bf16),
            sds((cols, 2, 2, 2, qs, 256), bf16), sds((40, channels), f32),
        ] + [sds(f, bf16) for f in far],
        in_specs=[vmem] * len(small) + [hbm] * len(big),
        out_specs=[hbm] * 7 + [vmem] + [hbm] * 5,
        scratch_shapes=[V(*s) for s in scratch] + [
            pltpu.SemaphoreType.DMA((100,)), pltpu.SemaphoreType.DMA((100,)),
            pltpu.SemaphoreType.DMA((48,)),
        ],
        compiler_params=pltpu.CompilerParams(
            collective_id=2, has_side_effects=True, vmem_limit_bytes=64 * 1024 * 1024
        ),
        name="rear",
    )(*small, *big)
    mixed, gtok, oi, og, oz, oo, os, sm = got[:8]
    return (
        mixed, gtok, oi.reshape(third, -1), og.reshape(third, -1), oz.reshape(third, -1),
        oo.reshape(cols * own, third), os.reshape(width, -1), sm,
    )


def per_device(
    tokens_in, segment_ids, norm_gain, proj_gate, proj_inner, proj_step, proj_states,
    conv_inner, conv_inner_bias, conv_states, conv_states_bias, step_bias, decay_log,
    skip_gain, gate_gain, proj_out, cotangent,
):
    tokens, width = tokens_in.shape
    blocks = tokens // SPAN
    row = lax.axis_index("row")
    col = lax.axis_index("col")
    cols = lax.axis_size("col")
    own_ch = conv_inner.shape[1]
    own_heads = step_bias.shape[0]
    channels = 2 * own_ch
    inner_all = channels * cols
    col_width = width // cols

    own = jnp.concatenate(
        [conv_inner, conv_inner_bias[None], gate_gain[None], jnp.zeros((2, own_ch), f32)], 0
    )

    def at_row(values):
        pad = [(0, 0)] * (values.ndim - 1)
        low = jnp.pad(values, pad + [(0, 128 - own_heads)])
        high = jnp.pad(values, pad + [(own_heads, 128 - 2 * own_heads)])
        return jnp.where(row == 0, low, high)

    pieces = at_row(proj_step.reshape(col_width, cols, own_heads)).reshape(col_width, cols * 128)
    rate = -jnp.exp(decay_log)
    head_own = jnp.pad(
        at_row(jnp.stack([step_bias, rate * LOG2E, skip_gain, rate])), ((0, 4), (0, 0))
    )
    spar = jnp.concatenate([conv_states, conv_states_bias[None], jnp.zeros((3, 256), f32)], 0)

    docs = jnp.pad(segment_ids[0].astype(f32), (8, 8), constant_values=-1.0)
    docs = lax.dynamic_slice_in_dim(docs, row * tokens, tokens + 16, 0)
    here = docs[8:8 + tokens]
    spans = here.reshape(blocks, SPAN)
    before = jnp.concatenate([docs[7:8], spans[:-1, -1]])
    after = spans[:, -1]

    def flat(cond):
        return jnp.broadcast_to(cond, (blocks, SPAN)).reshape(tokens)

    def forward_same(start, count):
        own_docs = docs[start:start + count]
        return [own_docs == docs[start + k:start + k + count] for k in range(1, 4)]

    meta = jnp.stack(
        [here]
        + [(here == docs[8 - k:8 - k + tokens]) for k in range(1, 4)]
        + [
            flat(spans == before[:, None]),
            flat(spans == after[:, None]),
            flat((before == after)[:, None]),
            jnp.zeros_like(here),
        ]
        + forward_same(8, tokens)
        + [jnp.zeros_like(here)] * 5,
        1,
    ).astype(f32)
    hmeta = jnp.stack(
        [jnp.zeros((8,), f32)] * 8
        + forward_same(0, 8)
        + [jnp.zeros((8,), f32)] * 5,
        1,
    ).astype(f32)
    docrow = here[None, :]

    sds = jax.ShapeDtypeStruct
    (
        w_inner, w_gate, w_out, w_step, cot_all, par, head,
        normed, pre, spre, sd, ssd, x_low, wr, step, r, sig, hpre, hspre, sprev,
        gated, g_gate, gy, dr, dsf, dsout, acc1,
    ) = front(
        inner_all, tokens_in, norm_gain[None], proj_states, meta, docrow, spar,
        proj_inner, proj_gate, proj_out, pieces, cotangent, own, head_own, tokens_in[-16:],
    )

    gain_cols = lax.dynamic_slice_in_dim(norm_gain, col * col_width, col_width, 0)
    mixed_out, grad_tokens, oi, og, oz, oo, os, few = rear(
        meta, hmeta, docrow, head, par, spar, hpre, hspre, acc1, gain_cols[None], tokens_in,
        proj_states, dsout, (w_inner, w_gate, w_out, w_step), cot_all, normed, pre, spre, sd, ssd,
        x_low, wr, step, r, sig, sprev, gated, g_gate, gy, dr, dsf,
    )
    grad_inner = oi.astype(f32)
    grad_gate = og.astype(f32)
    grad_out = oo.astype(f32)
    grad_states = os.astype(f32)
    oz = lax.dynamic_slice_in_dim(oz.reshape(col_width, cols, 128), row * own_heads, own_heads, 2)
    grad_step = oz.astype(f32).reshape(col_width, cols * own_heads)
    own_few = lax.dynamic_slice_in_dim(few, row * own_ch, own_ch, 1)

    def head_row(values):
        return lax.dynamic_slice_in_dim(values, row * own_heads, own_heads, 0)

    grad_conv_inner = own_few[0:4]
    grad_conv_inner_bias = own_few[4]
    grad_gate_gain = own_few[8]
    grad_skip = own_few[9].reshape(own_heads, HEAD).sum(-1)
    grad_step_bias = head_row(few[10, 0:128])
    grad_decay = head_row(few[11, 0:128]) * rate
    grad_norm_gain = few[24:40:8].reshape(-1)
    grad_norm_gain = lax.dynamic_slice_in_dim(
        grad_norm_gain, col * col_width, col_width, 0
    ) / gain_cols

    return (
        mixed_out,
        grad_tokens,
        grad_norm_gain,
        grad_gate,
        grad_inner,
        grad_step,
        grad_states,
        grad_conv_inner,
        grad_conv_inner_bias,
        few[16:20, 0:256],
        few[20, 0:256],
        grad_step_bias,
        grad_decay,
        grad_skip,
        grad_gate_gain,
        grad_out,
    )


def solution(mesh):
    in_specs = (
        P(("dp", "row"), None),
        P("dp", None),
        P(),
        P("col", "row"),
        P("col", "row"),
        P("col", "row"),
        P(),
        P(None, ("row", "col")),
        P(("row", "col")),
        P(),
        P(),
        P(("row", "col")),
        P(("row", "col")),
        P(("row", "col")),
        P(("row", "col")),
        P("row", "col"),
        P(("dp", "row"), "col"),
    )
    out_specs = (
        P(("dp", "row"), "col"),
        P(("dp", "row"), "col"),
        P("col"),
        P("col", "row"),
        P("col", "row"),
        P("col", "row"),
        P(),
        P(None, ("row", "col")),
        P(("row", "col")),
        P(),
        P(),
        P(("row", "col")),
        P(("row", "col")),
        P(("row", "col")),
        P(("row", "col")),
        P("row", "col"),
    )
    return jax.shard_map(
        per_device, mesh=mesh, in_specs=in_specs, out_specs=out_specs, check_vma=False
    )
```

time: 437 us -> 336 us (0.77)
  matrix products: 50.4 us -> 0 us
  local copies, waits for them, and re-layouts: 39.3 us -> 18.8 us
  between operations: 14.4 us -> 0.83 us
  other arithmetic: 26.1 us -> 15.5 us
    dot_general x10 -> x0, matrix products: 50.4 us -> none  [the longest x4 23.8 us: mm_nt(): lax.dot_general(a, b, (((1,), (1,)), ((), ())), preferred_element_type=f32)]
    pallas_call x2 -> x1, Pallas kernels: 183 us -> 171 us  [rear(): pl.pallas_call(rear_kernel, out_shape=[sds((tokens, third), bf16), sds((t...]
    pallas_call x1, Pallas kernels: 117 us -> 127 us  [front(): pl.pallas_call(functools.partial(front_kernel, float(inner_all)), out_sha...]
    reshape x11 -> x2, local copies, waits for them, and re-layouts: 7.05 us -> 0.65 us  [the longest x1 0.64 us: per_device(): grad_step = oz.astype(f32).reshape(col_width, cols * own_heads)]
    convert_element_type x2 -> x0, other arithmetic: 5.38 us -> none  [the longest x1 3.61 us: per_device(): grad_tokens = (grad_input + cotangent.astype(f32)).astype(bf16)]
    unnamed x67 -> x35, local copies, waits for them, and re-layouts: 7.14 us -> 2.3 us
  transfers between devices with their start and end apart: 4 -> 0, of which waited for: 0 -> 0; matrix products, arithmetic and copies ran while one was open for 22% -> 0% of each run, Pallas kernels for 42% -> 0%
where the time goes in v4:
time: 336 us; the launch traced here: 333 us
  Pallas kernels  298 us (89%)
  local copies, waits for them, and re-layouts  18.8 us (6%)
  other arithmetic  15.5 us (5%)
    pallas_call x1, Pallas kernels, rear(): pl.pallas_call(rear_kernel, out_shape=[sds((tokens, third), bf16), sds((t...  171 us
    pallas_call x1, Pallas kernels, front(): pl.pallas_call(functools.partial(front_kernel, float(inner_all)), out_sha...  127 us

profile of v4, /device:TPU:0, one launch (start us, length us, event | category | flops | bytes accessed | tf_op | source)
XLA Modules:
  0.0 333.4 jit_solution(13427262825062988391)
XLA Ops:
  0.6 0.0 copy-start.11
  0.7 0.0 copy-start.8
  0.7 0.0 copy-start.9
  0.7 0.0 copy-start.10
  0.7 0.0 copy-start.7
  0.7 0.0 copy-start.6
  0.7 0.7 convert_element_type.69
  1.4 0.1 fusion.6
  1.5 0.2 fusion.20
  1.7 0.6 pad_dynamic-slice_fusion.6
  2.3 0.8 convert_reduce_fusion
  3.1 0.1 broadcast_bitcast_fusion.1
  3.2 0.7 pad_maximum_fusion.1
  3.9 0.1 broadcast_bitcast_fusion.2
  4.0 0.1 fusion.7
  4.1 0.1 broadcast_bitcast_fusion
  4.2 0.1 stack.118
  4.3 1.0 copy.83.meta
  5.3 0.7 multiply_bitcast_fusion
  6.0 0.7 pad_maximum_fusion
  6.7 0.1 pad_select_fusion.1
  6.8 0.6 pad.29.head_own
  7.4 0.7 reshape.94
  8.1 0.9 copy.85.step_w
  9.1 0.1 pad.40.clone
  9.2 0.0 copy-done.11
  9.2 0.7 maximum_maximum_fusion.1.spar
  9.8 1.4 slice.87.halo
  11.3 0.1 pad.37.clone
  11.4 0.0 copy-done.7
  11.4 0.7 maximum_maximum_fusion.par_own
  12.0 0.0 copy-done.6
  12.0 0.6 broadcast_in_dim.33.ngain
  12.6 127.4 %front.1 = (bf16[4,2,2,96,768]{4,3,2,1,0:T(8,128)(2,1)}, bf16[4,2,2,96,768]{4,3,2,1,0:T(8,128)(2,1)}, bf16[2,2,2,96,1536]{4,3,2,1,0:T(8,128)(2,1)}, bf16[1536,12...) custom-call(bf16[1024,1536]{1,0:T(8,128)(2,1)} %tok_h.1, ...), custom_call_target="tpu_custom_call" | custom-call | tf_op jit(solution)/shard_map/front/pallas_call | solution.py:555
  140.0 0.1 fusion.17
  140.1 0.1 copy.78
  140.2 0.1 copy.79
  140.3 0.1 copy.80
  140.4 0.7 stack.127.hmeta
  141.0 0.1 dynamic_slice.26
  141.1 0.6 broadcast_in_dim.39.ngain_cols
  141.7 170.9 %rear.1 = (bf16[1024,384]{1,0:T(8,128)(2,1)}, bf16[1024,384]{1,0:T(8,128)(2,1)}, bf16[2,2,96,1536]{3,2,1,0:T(8,128)(2,1)}, bf16[2,2,96,1536]{3,2,1,0:T(8,128)(2,...) custom-call(f32[1024,16]{1,0:T(8,128)} %copy.83.meta, ...), custom_call_target="tpu_custom_call" | custom-call | tf_op jit(solution)/shard_map/rear/pallas_call | solution.py:1225
  312.6 4.6 %bitcast_convert_fusion.1 = (f32[384,1536]{1,0:T(8,128)}, f32[384,1536]{1,0:T(8,128)}) fusion(bf16[2,2,96,1536]{3,2,1,0:T(8,128)(2,1)} %get-tuple-element.82, bf16[2,2,96,1536]{3,2,1,0:T(8,128)(2,1)} %get-tuple-element.81), kind=kLoop, calls=%fused_computation.1 | loop fusion | flops 1179648 | bytes 7077888 | tf_op jit(solution)/shard_map/convert_element_type | solution.py:1335
  317.2 1.7 bitcast_convert_fusion
  318.9 1.3 bitcast_convert_fusion.3
  320.2 0.0 copy-done.4
  320.2 0.1 reshape_reshape.3
  320.3 0.0 copy-start.1
  320.3 0.3 constant_dynamic-slice_fusion.3
  320.6 0.3 copy.86
  320.8 0.6 reshape.116
  321.5 0.8 slice.88
  322.3 1.4 dynamic-slice_divide_fusion
  323.7 1.5 dynamic-slice_reduce_fusion
  325.1 0.1 reshape_squeeze.3
  325.2 0.6 reduce_sum.9
  325.8 1.3 constant_dynamic-slice_fusion
  327.1 0.8 fusion.19
  327.9 0.6 fusion.12
  328.5 0.6 fusion.14
  329.1 1.3 slice.91
  330.3 1.3 slice.92
  331.6 0.9 copy.92
  332.5 0.9 copy.93
  (30 shorter events, 0.1 us)
Async XLA Ops:
  0.6 8.5 %copy-start.11 = (f32[256]{0:T(256)S(1)}, f32[256]{0:T(256)}, u32[]{:S(2)}) copy-start(f32[256]{0:T(256)} %param.27) | copy-start | bytes 3076
  0.7 8.5 %copy-start.8 = (f32[4,256]{1,0:T(4,128)S(1)}, f32[4,256]{1,0:T(4,128)}, u32[]{:S(2)}) copy-start(f32[4,256]{1,0:T(4,128)} %param.26) | copy-start | bytes 12292
  0.7 10.6 %copy-start.9 = (f32[384]{0:T(512)S(1)}, f32[384]{0:T(512)}, u32[]{:S(2)}) copy-start(f32[384]{0:T(512)} %param.25) | copy-start | bytes 4612
  0.7 10.6 %copy-start.10 = (f32[384]{0:T(512)S(1)}, f32[384]{0:T(512)}, u32[]{:S(2)}) copy-start(f32[384]{0:T(512)} %param.31) | copy-start | bytes 4612
  0.7 10.7 %copy-start.7 = (f32[4,384]{1,0:T(4,128)S(1)}, f32[4,384]{1,0:T(4,128)}, u32[]{:S(2)}) copy-start(f32[4,384]{1,0:T(4,128)} %param.24) | copy-start | bytes 18436
  0.7 11.3 %copy-start.6 = (f32[1536]{0:T(1024)S(1)}, f32[1536]{0:T(1024)}, u32[]{:S(2)}) copy-start(f32[1536]{0:T(1024)} %param.19) | copy-start | bytes 18436
  1.5 11.1 %copy-start.5 = (f32[1024]{0:T(1024)}, f32[1024]{0:T(1024)S(1)}, u32[]{:S(2)}) copy-start(f32[1024]{0:T(1024)S(1)} %get-tuple-element.92) | copy-start | bytes 12292
  312.6 4.6 %copy-start = (bf16[4,2,2,96,384]{4,3,2,1,0:T(8,128)(2,1)S(1)}, bf16[4,2,2,96,384]{4,3,2,1,0:T(8,128)(2,1)}, u32[]{:S(2)}) copy-start(bf16[4,2,2,96,384]{4,3,2,1,0:T(8,128)(2,1)} %get-tuple-element.85) | copy-start | bytes 3538948
  317.2 1.7 copy-start.3
  318.9 1.3 copy-start.4
  320.2 8.3 %copy-start.12 = (f32[6]{0:T(128)S(1)}, f32[6]{0:T(128)}, u32[]{:S(2)}) copy-start(f32[6]{0:T(128)} %param.29) | copy-start | bytes 76
  320.2 11.4 %copy-start.2 = (bf16[1024,384]{1,0:T(8,128)(2,1)S(1)}, bf16[1024,384]{1,0:T(8,128)(2,1)}, u32[]{:S(2)}) copy-start(bf16[1024,384]{1,0:T(8,128)(2,1)} %get-tuple-element.127) | copy-start | bytes 2359300
  320.3 12.2 %copy-start.1 = (bf16[1024,384]{1,0:T(8,128)(2,1)S(1)}, bf16[1024,384]{1,0:T(8,128)(2,1)}, u32[]{:S(2)}) copy-start(bf16[1024,384]{1,0:T(8,128)(2,1)} %get-tuple-element.128) | copy-start | bytes 2359300

commit v5 on v4

v5 whole, which is shorter than its diff:
```python
import functools

import jax
import jax.numpy as jnp
from jax import lax
from jax.experimental import pallas as pl
from jax.experimental.pallas import tpu as pltpu
from jax.sharding import PartitionSpec as P

SPAN = 256
HEAD = 64
epsilon = 1e-05
LOG2E = 1.4426950408889634
f32 = jnp.float32
bf16 = jnp.bfloat16
ANY = pl.ANY


def mm(a, b):
    return lax.dot_general(a, b, (((1,), (0,)), ((), ())), preferred_element_type=f32)


def mm_nt(a, b):
    return lax.dot_general(a, b, (((1,), (1,)), ((), ())), preferred_element_type=f32)


def split(v, terms):
    parts = []
    for _ in range(terms):
        part = v.astype(bf16)
        parts.append(part)
        v = v - part.astype(f32)
    return parts


def mm_split(a, exact, terms=2):
    return sum(mm(part, exact) for part in split(a, terms))


def split_mm(exact, b, terms=3):
    return sum(mm(exact, part) for part in split(b, terms))


def spread_matrix(channels):
    heads = lax.broadcasted_iota(jnp.int32, (128, channels), 0)
    cols = lax.broadcasted_iota(jnp.int32, (128, channels), 1)
    low = heads * HEAD
    return jnp.where((cols >= low) & (cols < low + HEAD), 1.0, 0.0).astype(bf16)


def gather_matrix(channels):
    heads = lax.broadcasted_iota(jnp.int32, (channels, 128), 1)
    rows = lax.broadcasted_iota(jnp.int32, (channels, 128), 0)
    low = heads * HEAD
    return jnp.where((rows >= low) & (rows < low + HEAD), 1.0, 0.0).astype(bf16)


def lower_ones():
    rows = lax.broadcasted_iota(jnp.int32, (SPAN, SPAN), 0)
    cols = lax.broadcasted_iota(jnp.int32, (SPAN, SPAN), 1)
    return jnp.where(rows >= cols, 1.0, 0.0).astype(bf16)


def upper_ones():
    rows = lax.broadcasted_iota(jnp.int32, (SPAN, SPAN), 0)
    cols = lax.broadcasted_iota(jnp.int32, (SPAN, SPAN), 1)
    return jnp.where(rows <= cols, 1.0, 0.0).astype(bf16)


def sigmoid(v):
    return 1.0 / (1.0 + jnp.exp(-v))


def half_masks():
    lane = lax.broadcasted_iota(jnp.int32, (SPAN, 128), 1)
    return lane < HEAD


def rms_rows(tok, gain):
    wide = tok.astype(f32)
    inverse = lax.rsqrt(jnp.mean(wide * wide, -1, keepdims=True) + epsilon)
    return (wide * inverse * gain).astype(bf16)


MESH = pl.DeviceIdType.MESH
SHARE = 4


def lane_block(index, width):
    return pl.ds(pl.multiple_of(index * width, 128), width)


class Links:
    def __init__(self, send, recv, local=None):
        self.send, self.recv, self.local = send, recv, local
        self.used, self.kept, self.sent = 0, 0, []
        dp = lax.axis_index("dp")
        self.groups = lax.axis_size("dp") // SHARE
        self.group = dp // SHARE
        self.x = lax.rem(dp, SHARE) // 2
        self.core = lax.rem(dp, 2)
        self.y = lax.axis_index("row")
        self.z = lax.axis_index("col")
        self.cols = lax.axis_size("col")

    def dp_of(self, group, x, core):
        return group * SHARE + x * 2 + core

    def mate(self):
        return {"dp": self.dp_of(self.group, self.x, 1 - self.core)}

    def across(self):
        return {"dp": self.dp_of(self.group, 1 - self.x, self.core)}

    def other_row(self):
        return {"row": 1 - self.y}

    def col_peer(self, off):
        return lax.rem(self.z + off, self.cols)

    def group_peer(self, off):
        return {"dp": self.dp_of(lax.rem(self.group + off, self.groups), self.x, self.core)}

    def meet(self, far_groups):
        barrier = pltpu.get_barrier_semaphore()
        peers = [self.mate(), self.across(), self.other_row()]
        peers += [{"col": self.col_peer(off)} for off in range(1, self.cols)]
        if far_groups:
            peers += [self.group_peer(off) for off in range(1, self.groups)]
        for peer in peers:
            pl.semaphore_signal(barrier, inc=1, device_id=peer, device_id_type=MESH)
        pl.semaphore_wait(barrier, len(peers))

    def make(self, src, dst, peer, when=None, track=True):
        at = self.used
        self.used += 1
        copy = pltpu.make_async_remote_copy(
            src_ref=src, dst_ref=dst, send_sem=self.send.at[at], recv_sem=self.recv.at[at],
            device_id=peer, device_id_type=MESH,
        )
        if track:
            self.sent.append((copy, when))
        return copy

    def go(self, src, dst, peer, track=True):
        copy = self.make(src, dst, peer, track=track)
        copy.start()
        return copy

    def keep(self, src, dst):
        copy = pltpu.make_async_copy(src, dst, self.local.at[self.kept])
        self.kept += 1
        return copy

    def finish(self):
        for copy, when in self.sent:
            if when is None:
                copy.wait_send()
            else:
                pl.when(when)(copy.wait_send)


class Steps:
    def __init__(self):
        self.stages = []

    def add(self, remote, local=(), before=None):
        self.stages.append((remote, list(local), before))

    def drain(self, t):
        for remote, _, _ in self.stages:
            for c in remote:
                c.wait_send()
                t.sent = [(copy, when) for copy, when in t.sent if copy is not c]

    def run(self, s):
        if 0 < s <= len(self.stages):
            remote, local, _ = self.stages[s - 1]
            for c in remote:
                c.wait_recv()
            for c in local:
                c.wait()
        if s < len(self.stages):
            remote, local, before = self.stages[s]
            if before is not None:
                before()
            for c in remote + local:
                c.start()


def spread_steps(t, view, steps):
    x, y = t.x, t.y
    first, second = view(x, y, 0), view(x, y, 1)
    steps.add([t.make(first, first, t.other_row()), t.make(second, second, t.across())])
    first, second = view(x, None, 0), view(None, y, 1)
    steps.add([t.make(first, first, t.across()), t.make(second, second, t.other_row())])
    every = view(None, None, None)
    steps.add([t.make(every, every, t.mate())])
    return steps


def half_lines(part, half):
    return slice(None) if half is None else pl.ds(half * (part // 2), part // 2)


def column_steps(t, src, dst, width):
    part = src.shape[0] // SHARE
    x, y, z, core = t.x, t.y, t.z, t.core
    rows = pl.ds(pl.multiple_of((x * 2 + core) * part, 16), part)
    lanes = lane_block(y, width)
    steps = Steps()
    here = dst.at[z, x, core, :, lanes]
    remote = []
    for off in range(1, t.cols):
        to = t.col_peer(off)
        remote.append(t.make(src.at[rows, lane_block(to, width)], here, {"col": to}))
    steps.add(remote, [t.keep(src.at[rows, lane_block(z, width)], here)])

    def view(at_x, at_y, half):
        return dst.at[:, slice(None) if at_x is None else at_x, core, half_lines(part, half),
                      slice(None) if at_y is None else lanes]

    return spread_steps(t, view, steps)


def row_steps(t, src, dst, width):
    part = src.shape[0] // t.cols // SHARE
    x, y, z, core = t.x, t.y, t.z, t.core

    def rows(to):
        return pl.ds(pl.multiple_of((to * SHARE + x * 2 + core) * part, 16), part)

    steps = Steps()
    here = dst.at[y, x, core, :, lane_block(z, width)]
    remote = []
    for off in range(1, t.cols):
        to = t.col_peer(off)
        remote.append(t.make(src.at[rows(to), :], here, {"col": to}))
    steps.add(remote, [t.keep(src.at[rows(z), :], here)])

    def view(at_x, at_y, half):
        return dst.at[slice(None) if at_y is None else at_y, slice(None) if at_x is None else at_x,
                      core, half_lines(part, half), :]

    return spread_steps(t, view, steps)


def gather_steps(t, own, whole, rows):
    width = own.shape[1]
    z = t.z
    mate, far = z + 1 - 2 * lax.rem(z, 2), lax.rem(z + 2, 4)
    here, there = whole.at[rows, lane_block(z, width)], whole.at[rows, lane_block(far, width)]
    steps = Steps()
    cross = t.make(own.at[rows, :], here, {"col": far})
    near = t.make(own.at[rows, :], here, {"col": mate})
    steps.add([cross, near], [t.keep(own.at[rows, :], here)])
    steps.add([t.make(there, there, {"col": mate})])
    return steps


def mm_tn(a, b):
    return lax.dot_general(a, b, (((0,), (0,)), ((), ())), preferred_element_type=f32)


def add_bf16(a, b):
    return (a.astype(f32) + b.astype(f32)).astype(bf16)


class PairSum:
    def __init__(self, t, part, near, far_in, rows):
        z = t.z
        mate = z + 1 - 2 * lax.rem(z, 2)
        far = lax.rem(z + 2, 4)
        mate_far = lax.rem(mate + 2, 4)
        width = near.shape[-1]
        self.part, self.near, self.far_in, self.rows = part, near, far_in, rows
        self.own, self.far = lane_block(z, width), lane_block(far, width)
        to_mate = [
            t.make(part.at[rows, lane_block(mate_far, width)], near.at[1, rows], {"col": mate}),
            t.make(part.at[rows, lane_block(mate, width)], near.at[0, rows], {"col": mate}),
        ]
        self.first, self.second = to_mate
        self.across = t.make(near.at[1, rows], far_in.at[rows], {"col": far})

    def start(self):
        self.first.start()

    def forward(self):
        self.first.wait_recv()
        count = self.rows.size // 64

        def body(i, c):
            at = pl.ds(pl.multiple_of(self.rows.start + i * 64, 16), 64)
            self.near[1, at] = add_bf16(self.near[1, at], self.part[at, self.far])
            return c

        lax.fori_loop(0, count, body, 0)
        self.across.start()
        self.second.start()

    def arrive(self):
        self.second.wait_recv()
        self.across.wait_recv()

    def total(self, at):
        return (
            self.part[at, self.own].astype(f32) + self.near[0, at].astype(f32)
            + self.far_in[at].astype(f32)
        )


def sum_far_groups(t, own, got):
    if t.groups == 1:
        return
    more = [t.go(own, got.at[off - 1], t.group_peer(off), False) for off in range(1, t.groups)]
    for c in more:
        c.wait()

    def total(spare):
        for off in range(1, t.groups):
            back = t.keep(got.at[off - 1], spare)
            back.start()
            back.wait()
            own[...] = add_bf16(own[...], spare[...])

    pl.run_scoped(total, pltpu.VMEM(own.shape, own.dtype))


def column_sums(t, g, a1, yx, xy, yx2, xy2, a4, far):
    x, y, core = t.x, t.y, t.core
    width = a4.shape[-1]
    h = a4.shape[1] // 2
    mine, other = lane_block(y, width), lane_block(1 - y, width)
    top, low = pl.ds(0, h), pl.ds(h, h)
    steps = Steps()
    steps.add([t.make(g.at[:, :, 1 - core], a1, t.mate())])

    def add_core():
        def body(i, c):
            for j in range(2):
                a1[i, j] = add_bf16(a1[i, j], g[i, j, core])
            return c

        lax.fori_loop(0, t.cols, body, 0)

    steps.add([
        t.make(a1.at[:, :, top, other], yx, t.other_row()),
        t.make(a1.at[:, 1 - x, low, :], xy, t.across()),
    ], (), add_core)

    def add_first():
        def body(i, c):
            for j in range(2):
                yx[i, j] = add_bf16(yx[i, j], a1[i, j, top, mine])
            xy[i] = add_bf16(xy[i], a1[i, x, low, :])
            return c

        lax.fori_loop(0, t.cols, body, 0)

    steps.add([
        t.make(yx.at[:, 1 - x], yx2, t.across()),
        t.make(xy.at[:, :, other], xy2, t.other_row()),
    ], (), add_first)

    def add_second():
        def body(i, c):
            a4[i, top] = add_bf16(yx2[i], yx[i, x])
            a4[i, low] = add_bf16(xy2[i], xy[i, :, mine])
            return c

        lax.fori_loop(0, t.cols, body, 0)
        sum_far_groups(t, a4, far)

    steps.add([], (), add_second)
    return steps


def column_sum_shapes(cols, q, w):
    h = q // 2
    return [((cols, 2, q, 2 * w), bf16), ((cols, 2, h, w), bf16), ((cols, h, 2 * w), bf16),
            ((cols, h, w), bf16), ((cols, h, w), bf16), ((cols, q, w), bf16)]


def column_home(t, a4, o, steps):
    x, z, core = t.x, t.z, t.core
    here = o.at[x, core, :, lane_block(z, a4.shape[-1])]
    steps.add(
        [t.make(a4.at[t.col_peer(off)], here, {"col": t.col_peer(off)}) for off in range(1, t.cols)],
        [t.keep(a4.at[z], here)],
    )
    steps.add([t.make(o.at[x, core], o.at[x, core], t.across())])
    steps.add([t.make(o.at[:, core], o.at[:, core], t.mate())])
    return steps


def row_sums(t, g, a1, yx, xy, yx2, xy2, a4, far):
    x, y, core = t.x, t.y, t.core
    h = a4.shape[0] // 2
    top, low = pl.ds(0, h), pl.ds(h, h)
    steps = Steps()
    steps.add([t.make(g.at[:, :, 1 - core], a1, t.mate())])

    def add_core():
        def body(i, c):
            for j in range(2):
                a1[i, j] = add_bf16(a1[i, j], g[i, j, core])
            return c

        lax.fori_loop(0, 2, body, 0)

    steps.add([
        t.make(a1.at[1 - y, :, top], yx, t.other_row()),
        t.make(a1.at[:, 1 - x, low], xy, t.across()),
    ], (), add_core)

    def add_first():
        for j in range(2):
            yx[j] = add_bf16(yx[j], a1[y, j, top])
            xy[j] = add_bf16(xy[j], a1[j, x, low])

    steps.add([
        t.make(yx.at[1 - x], yx2, t.across()), t.make(xy.at[1 - y], xy2, t.other_row()),
    ], (), add_first)

    def add_second():
        a4[top] = add_bf16(yx2[...], yx[x])
        a4[low] = add_bf16(xy2[...], xy[y])
        sum_far_groups(t, a4, far)

    steps.add([], (), add_second)
    return steps


def row_sum_shapes(q, width):
    h = q // 2
    return [((2, 2, q, width), bf16), ((2, h, width), bf16), ((2, h, width), bf16),
            ((h, width), bf16), ((h, width), bf16), ((q, width), bf16)]


def row_home(t, a4, o, steps):
    x, z, core = t.x, t.z, t.core
    width = o.shape[-1]
    here = o.at[z, x, core]
    steps.add(
        [t.make(a4.at[:, lane_block(t.col_peer(off), width)], here, {"col": t.col_peer(off)})
         for off in range(1, t.cols)],
        [t.keep(a4.at[:, lane_block(z, width)], here)],
    )
    steps.add([t.make(o.at[:, x, core], o.at[:, x, core], t.across())])
    steps.add([t.make(o.at[:, :, core], o.at[:, :, core], t.mate())])
    return steps


def full_sums(t, g, s1, s2, s3, s4, s5, far, o):
    x, y, z, core = t.x, t.y, t.z, t.core
    steps = Steps()
    steps.add([t.make(g.at[:, :, :, 1 - core], s1, t.mate())])

    def add_core():
        def body(i, c):
            for j in range(2):
                for k in range(2):
                    s1[i, j, k] = add_bf16(s1[i, j, k], g[i, j, k, core])
            return c

        lax.fori_loop(0, t.cols, body, 0)

    steps.add([t.make(s1.at[:, 1 - y], s2, t.other_row())], (), add_core)

    def add_row():
        def body(i, c):
            for k in range(2):
                s2[i, k] = add_bf16(s2[i, k], s1[i, y, k])
            return c

        lax.fori_loop(0, t.cols, body, 0)

    steps.add([t.make(s2.at[:, 1 - x], s3, t.across())], (), add_row)

    def add_x():
        def body(i, c):
            s4[i] = add_bf16(s3[i], s2[i, x])
            return c

        lax.fori_loop(0, t.cols, body, 0)
        sum_far_groups(t, s4, far)

    steps.add(
        [t.make(s4.at[t.col_peer(off)], s5.at[off - 1], {"col": t.col_peer(off)})
         for off in range(1, t.cols)], (), add_x,
    )

    def add_cols():
        total = s4[z].astype(f32)
        for off in range(1, t.cols):
            total = total + s5[off - 1].astype(f32)
        s4[z] = total.astype(bf16)

    here = o.at[z, y, x, core]
    steps.add(
        [t.make(s4.at[z], here, {"col": t.col_peer(off)}) for off in range(1, t.cols)],
        [t.keep(s4.at[z], here)], add_cols,
    )
    here = o.at[:, y, x, core]
    steps.add([t.make(here, here, t.other_row())])
    here = o.at[:, :, x, core]
    steps.add([t.make(here, here, t.across())])
    here = o.at[:, :, :, core]
    steps.add([t.make(here, here, t.mate())])
    return steps


def small_sums(t, sm, msum, mgot, out, rest):
    steps = Steps()
    steps.add([t.make(sm, mgot.at[0], t.mate())])

    def add_core():
        msum[0] = sm[...] + mgot[0]

    steps.add([t.make(msum.at[0], mgot.at[1], t.other_row())], (), add_core)

    def add_row():
        msum[1] = msum[0] + mgot[1]

    steps.add([t.make(msum.at[1], mgot.at[2], t.across())], (), add_row)

    def add_x():
        msum[2] = msum[1] + mgot[2]
        if t.groups > 1:
            more = [t.go(msum.at[2], mgot.at[5 + off], t.group_peer(off), False)
                    for off in range(1, t.groups)]
            for c in more:
                c.wait()
            total = msum[2]
            for off in range(1, t.groups):
                total = total + mgot[5 + off]
            msum[2] = total

    last = pl.ds(rest, sm.shape[0] - rest)
    steps.add(
        [t.make(msum.at[2, last], mgot.at[2 + off, last], {"col": t.col_peer(off)})
         for off in range(1, t.cols)], (), add_x,
    )

    def done():
        out[0:rest] = msum[2, 0:rest]
        out[rest:] = msum[2, rest:] + mgot[3, rest:] + mgot[4, rest:] + mgot[5, rest:]

    steps.add([], (), done)
    return steps


def front_kernel(
    inner_total,
    ngain_v, w_states, segments, taps_inner, bias_inner, gain_gate, taps_states, bias_states, step_all,
    step_bias, decay_log, skip_gain,
    tok_h, inner, gate, out, cot,
    mixed_o, wi_o, wg_o, ws_o, normed_o, sig_o, gx_o, gs_o, gz_o, accx_o, accs_o, acch_o, acc_o,
    gg4_o, go4_o, ggate_o, far_g, far_o,
    wi, wg, wo, ws2, ws, step_w, cots, par, spar, head, head_own, head_in, halo_in, tok, tok_own,
    meta, hmeta, docrow, docs,
    normed_s, pre_s, spre_s, sd_s, ssd_s, x_s, wr_s, step_s, r_s, sig_s, hpre_s, hspre_s, sprev_s,
    gated_s, ggate_s, gy_s, dr_s, fresh_s, y_s, gate_s, gg_s, gs_s, gz_s,
    out_near, out_far, sums_s, sums_in, xbuf, sbuf, mem, pass_out, state_in, dstate_in, pass_back,
    hx, hs, hx_in, hs_in, accx, accs, acch, acc_s, gg, g1, g2, g3, g5, g6, g4, o1, o2, o3, o5, o6, o4,
    send, recv, local,
):
    t = Links(send, recv, local)
    x, y, z, core = t.x, t.y, t.z, t.core
    blocks = tok.shape[0] // SPAN
    channels = x_s.shape[1]
    half = channels // 2
    outputs = []

    def write(src, dst):
        copy = t.keep(src, dst)
        copy.start()
        outputs.append(copy)

    def load(src, dst):
        copy = t.keep(src, dst)
        copy.start()
        return copy

    loads = [load(tok_h, tok), load(tok_h.at[:, lane_block(z, cot.shape[1])], tok_own)]
    own_lanes = lane_block(y, half)
    few = [
        t.make(par.at[:, own_lanes], par.at[:, own_lanes], t.other_row()),
        t.make(head_own, head_in, t.other_row()),
        t.make(tok_h.at[pl.ds(tok.shape[0] - 16, 16), :], halo_in, t.other_row()),
    ]
    block = inner.shape[1] // t.cols
    get_inner = column_steps(t, inner, wi, block)
    get_step = column_steps(t, step_w, ws2, step_w.shape[1] // t.cols)
    get_gate = column_steps(t, gate, wg, block)
    get_out = row_steps(t, out, wo, out.shape[1])
    half_rows = tok.shape[0] // 2
    get_cot = [gather_steps(t, cot, cots, pl.ds(n * half_rows, half_rows)) for n in range(2)]
    pass_state = t.make(pass_out, state_in, t.other_row())
    pass_back_state = t.make(pass_back, dstate_in, t.other_row())
    halo_x = t.make(hx, hx_in, t.other_row())
    halo_s = t.make(hs, hs_in, t.other_row())
    out_part = tok
    sum_gate = column_sums(t, gg, g1, g2, g3, g5, g6, g4, far_g)
    go = wo
    sum_out = row_sums(t, go, o1, o2, o3, o5, o6, o4, far_o)
    out_sums = [PairSum(t, out_part, out_near, out_far, pl.ds(b * SPAN, SPAN)) for b in range(blocks)]
    pass_sums = [
        t.make(sums_s, sums_in.at[off - 1], {"col": t.col_peer(off)}) for off in range(1, t.cols)
    ]
    t.meet(True)
    get_inner.run(0)

    own_heads = step_bias.shape[0]
    lane8 = lax.broadcasted_iota(jnp.int32, (8, 128), 1)
    row8 = lax.broadcasted_iota(jnp.int32, (8, 128), 0)
    scalars = jnp.zeros((8, 128), f32)
    for j in range(own_heads):
        here = lane8 == y * own_heads + j
        scalars = scalars + jnp.where(here & (row8 == 0), step_bias[j], 0.0)
        scalars = scalars + jnp.where(here & ((row8 == 1) | (row8 == 3)), decay_log[j], 0.0)
        scalars = scalars + jnp.where(here & (row8 == 2), skip_gain[j], 0.0)
    own_lane = (lane8 >= y * own_heads) & (lane8 < (y + 1) * own_heads)
    rate = jnp.where(own_lane, -jnp.exp(scalars), 0.0)
    head_own[...] = jnp.where(row8 == 1, rate * LOG2E, jnp.where(row8 == 3, rate, scalars))
    par[:, own_lanes] = jnp.zeros((8, half), f32)
    par[0:4, own_lanes] = taps_inner[...]
    par[4:5, own_lanes] = bias_inner[...].reshape(1, half)
    par[5:6, own_lanes] = gain_gate[...].reshape(1, half)
    spar[...] = jnp.zeros_like(spar)
    spar[0:4, :] = taps_states[...]
    spar[4:5, :] = bias_states[...].reshape(1, 256)
    every = step_all.shape[1]
    src = lax.broadcasted_iota(jnp.int32, (every, t.cols * 128), 0)
    dst = lax.broadcasted_iota(jnp.int32, (every, t.cols * 128), 1)
    place = jnp.zeros((every, t.cols * 128), f32)
    for c in range(t.cols):
        low = c * 128 + y * own_heads - c * own_heads
        mine = (src >= c * own_heads) & (src < (c + 1) * own_heads)
        place = place + jnp.where(mine & (dst - src == low), 1.0, 0.0)
    step_w[...] = mm(step_all[...], place.astype(bf16)).astype(bf16)
    get_step.run(0)
    for c in few:
        c.start()

    length = tok.shape[0]
    docs[:, 0:128] = jnp.full((8, 128), -1.0, f32)
    docs[:, 128:128 + 2 * length] = jnp.broadcast_to(segments[...].astype(f32), (8, 2 * length))
    docs[:, 128 + 2 * length:] = jnp.full((8, 128), -1.0, f32)
    window = docs[:, pl.ds(pl.multiple_of(y * length, 128), length + 256)]
    span_w = length + 256
    docrow[...] = window[:, 128:128 + length]
    same_before = [(window == pltpu.roll(window, k, 1)).astype(f32) for k in range(1, 4)]
    same_after = [(window == pltpu.roll(window, span_w - k, 1)).astype(f32) for k in range(1, 4)]
    row16 = lax.broadcasted_iota(jnp.int32, (8, SPAN), 0)
    for i in range(blocks):
        at = slice(128 + i * SPAN, 128 + (i + 1) * SPAN)
        here = window[:, at]
        before = window[0:1, 127 + i * SPAN:128 + i * SPAN]
        last = window[0:1, 127 + (i + 1) * SPAN:128 + (i + 1) * SPAN]
        low = jnp.where(row16 == 0, here, 0.0)
        for k in range(1, 4):
            low = low + jnp.where(row16 == k, same_before[k - 1][:, at], 0.0)
        low = low + jnp.where((row16 == 4) & (here == before), 1.0, 0.0)
        low = low + jnp.where((row16 == 5) & (here == last), 1.0, 0.0)
        low = low + jnp.where((row16 == 6) & (before == last), 1.0, 0.0)
        high = jnp.zeros((8, SPAN), f32)
        for k in range(1, 4):
            high = high + jnp.where(row16 == k - 1, same_after[k - 1][:, at], 0.0)
        rows128 = jnp.concatenate([low, high, jnp.zeros((112, SPAN), f32)], 0)
        meta[i * SPAN:(i + 1) * SPAN, :] = jnp.transpose(rows128)
    row16 = lax.broadcasted_iota(jnp.int32, (8, 128), 0)
    high = jnp.zeros((8, 128), f32)
    for k in range(1, 4):
        high = high + jnp.where(row16 == k - 1, same_after[k - 1][:, 0:128], 0.0)
    rows128 = jnp.concatenate([jnp.zeros((8, 128), f32), high, jnp.zeros((112, 128), f32)], 0)
    hmeta[...] = jnp.transpose(rows128)[120:128]

    gain = ngain_v[...].reshape(1, -1)
    for c in loads:
        c.wait()

    def rows_of(i):
        return pl.ds(pl.multiple_of(i * SPAN, SPAN), SPAN)

    def conv_silu(buf, lanes, here, taps, marks):
        v = taps[4:5, lanes] + taps[0:1, lanes] * here
        for k in range(1, 4):
            v = v + marks[:, k:k + 1] * (taps[k:k + 1, lanes] * buf[8 - k:8 - k + SPAN, lanes])
        sg = sigmoid(v)
        return v * sg, sg * (1.0 + v * (1.0 - sg))

    for c in few:
        c.wait_recv()
    hn = rms_rows(halo_in[...], gain)
    h_states = mm(hn, w_states[...])[8:16]
    sbuf[0:8, :] = h_states
    hspre_s[...] = h_states

    def norm_block(i, carry):
        at = rows_of(i)

        @pl.when(i > 0)
        def _():
            sbuf[0:8, :] = sbuf[SPAN:SPAN + 8, :]

        wide_tok = tok[at, :].astype(f32)
        inverse = lax.rsqrt(jnp.mean(wide_tok * wide_tok, -1, keepdims=True) + epsilon)
        normed = (wide_tok * inverse * gain).astype(bf16)
        normed_s[at, :] = normed
        s_pre = mm(normed, w_states[...])
        sbuf[8:SPAN + 8, :] = s_pre
        spre_s[at, :] = s_pre.astype(bf16)
        sact, sslope = conv_silu(sbuf, slice(0, 256), s_pre, spar, meta[at, :])
        wr_s[at, :] = sact.astype(bf16)
        ssd_s[at, :] = sslope.astype(bf16)
        sig_s[at, :] = jnp.broadcast_to(inverse, (SPAN, 128))
        pl.when(i == 0)(lambda: (get_inner.run(1), get_step.run(1), get_gate.run(0)) and None)
        return carry

    lax.fori_loop(0, blocks, norm_block, 0)
    head[...] = head_own[...] + head_in[...]
    get_inner.run(2)
    get_step.run(2)
    get_out.run(0)
    get_cot[0].run(0)
    get_inner.run(3)
    get_step.run(3)
    get_gate.run(1)
    get_inner.run(4)
    get_step.run(4)
    wide_in = normed_s.shape[1]
    ws[...] = (
        ws2[:, :, :, :, 0:128].reshape(wide_in, 128) + ws2[:, :, :, :, 128:256].reshape(wide_in, 128)
    )
    spread = spread_matrix(channels)

    def w_of(ref):
        return ref[...].reshape(-1, ref.shape[-1])

    h_inner = mm(hn, w_of(wi))[8:16]
    xbuf[0:8, :] = h_inner
    hpre_s[...] = h_inner
    mem[...] = jnp.zeros_like(mem)

    def entry(i, carry):
        at = rows_of(i)

        @pl.when(i > 0)
        def _():
            xbuf[0:8, :] = xbuf[SPAN:SPAN + 8, :]

        normed = normed_s[at, :]
        x_pre = mm(normed, w_of(wi))
        xbuf[8:SPAN + 8, :] = x_pre
        pre_s[at, :] = x_pre.astype(bf16)
        marks = meta[at, :]
        wr = wr_s[at, :]
        for pair in range(channels // 128):
            lanes = slice(pair * 128, pair * 128 + 128)
            act, slope = conv_silu(xbuf, lanes, xbuf[8:SPAN + 8, lanes], par, marks)
            x_s[at, lanes] = act.astype(bf16)
            sd_s[at, lanes] = slope.astype(bf16)
        x_low = x_s[at, :]

        raw = mm(normed, ws[...]) + head[0:1, :]
        step = jnp.maximum(raw, 0.0) + jnp.log1p(jnp.exp(-jnp.abs(raw)))
        lane = lax.broadcasted_iota(jnp.int32, (SPAN, 128), 1)
        sig_s[at, :] = jnp.where(lane == 127, sig_s[at, :], sigmoid(raw))
        step_s[at, :] = step
        r = split_mm(lower_ones(), step * head[1:2, :])
        r_s[at, :] = r
        last = r[SPAN - 1:SPAN, :]
        to_end = jnp.exp2(jnp.minimum(last - r, 0.0)) * marks[:, 5:6]
        coef = mm_split(to_end * step, spread)
        w_t = jnp.transpose(wr[:, 0:128].astype(f32)).astype(bf16)
        fresh = mm(w_t, (coef * x_low.astype(f32)).astype(bf16))
        fresh_s[i] = fresh
        mem[...] = keep_of(last, marks) * mem[...] + fresh

        @pl.when(i == 0)
        def _():
            get_gate.run(2)
            get_out.run(1)

        @pl.when(i == 2)
        def _():
            get_gate.run(3)
            get_out.run(2)
            get_cot[0].run(1)
            get_cot[1].run(0)

        return carry

    def keep_of(last, marks):
        return mm_split(jnp.broadcast_to(jnp.exp2(last) * marks[0:1, 6:7], (8, 128)), spread)[0:1]

    lax.fori_loop(0, blocks, entry, 0)
    pass_out[...] = mem[...].astype(bf16)
    pass_state.start()
    get_gate.run(4)
    for src, dst in (
        (normed_s, normed_o), (sig_s, sig_o), (wi, wi_o), (wg, wg_o), (ws, ws_o),
    ):
        write(src, dst)

    def gate_block(i, carry):
        at = rows_of(i)
        gate_s[at, :] = mm(normed_s[at, :], w_of(wg))
        return carry

    lax.fori_loop(0, blocks, gate_block, 0)

    pass_state.wait_recv()
    mem[...] = state_in[...].astype(f32) * jnp.where(y == 1, 1.0, 0.0)
    get_out.run(3)
    skip = mm_split(jnp.broadcast_to(head[2:3, :], (8, 128)), spread)[0:1]
    first = half_masks()

    def scan(i, carry):
        at = rows_of(i)
        marks = meta[at, :]
        w_low = wr_s[at, 0:128]
        r_low = wr_s[at, 128:256]
        r = r_s[at, :]
        r_t = jnp.transpose(r)
        rows = lax.broadcasted_iota(jnp.int32, (SPAN, SPAN), 0)
        cols = lax.broadcasted_iota(jnp.int32, (SPAN, SPAN), 1)
        allowed = (rows >= cols) & (marks[:, 0:1] == docrow[0:1, at])
        scores = jnp.where(allowed, mm_nt(r_low, w_low), 0.0)
        wide = x_s[at, :].astype(f32)
        xd = (mm_split(step_s[at, :], spread) * wide).astype(bf16)
        sprev = mem[...].astype(bf16)
        sprev_s[i] = sprev
        linked = jnp.exp2(r) * marks[:, 4:5]
        carried = mm(r_low, sprev) * mm_split(linked, spread)
        y_s[at, :] = carried + skip * wide
        for pair in range(channels // 128):
            lanes = slice(pair * 128, pair * 128 + 128)
            xp = xd[:, lanes]
            total = y_s[at, lanes]
            for part in range(2):
                h = 2 * pair + part
                decay = jnp.exp2(jnp.minimum(r[:, h:h + 1] - r_t[h:h + 1, :], 0.0))
                mixing = (scores * decay).astype(bf16)
                own = jnp.where(first if part == 0 else ~first, xp, jnp.zeros_like(xp))
                total = total + mm(mixing, own)
            y_s[at, lanes] = total
        last = r[SPAN - 1:SPAN, :]
        mem[...] = keep_of(last, marks) * mem[...] + fresh_s[i]

        @pl.when(i == 2)
        def _():
            get_cot[1].run(1)

        return carry

    lax.fori_loop(0, blocks, scan, 0)
    get_out.run(4)

    def project(i, carry):
        at = rows_of(i)
        g = gate_s[at, :]
        mixed = y_s[at, :] * (g * sigmoid(g))
        out_part[at, :] = mm((mixed * par[5:6, :]).astype(bf16), w_of(wo)).astype(bf16)
        return carry

    lax.fori_loop(0, blocks, project, 0)
    get_cot[0].run(2)
    ones = jnp.ones((8, channels), bf16)

    def totals_of(i, carry):
        at = rows_of(i)
        gg = mm_nt(cots[at, :], w_of(wo))
        gg_s[at, :] = gg.astype(bf16)
        g = gate_s[at, :]
        mixed = y_s[at, :] * (g * sigmoid(g))
        sq = sum(mm_nt(ones, part) for part in split(mixed * mixed, 2))
        pr = sum(mm_nt(ones, part) for part in split(mixed * (par[5:6, :] * gg), 2))
        row = lax.broadcasted_iota(jnp.int32, (8, SPAN), 0)
        sums_s[:, at] = jnp.where(row == 0, sq, jnp.where(row == 1, pr, 0.0))
        return carry

    lax.fori_loop(0, blocks // 2, totals_of, 0)
    get_cot[1].run(2)
    for s in out_sums:
        s.start()
    lax.fori_loop(blocks // 2, blocks, totals_of, 0)
    for c in pass_sums:
        c.start()
    out_sums[0].forward()
    for c in pass_sums:
        c.wait_recv()
    mem[...] = jnp.zeros_like(mem)
    acc_s[...] = jnp.zeros_like(acc_s)
    gather = gather_matrix(channels)

    def scale_of(at):
        both = sums_s[:, at]
        for off in range(1, t.cols):
            both = both + sums_in[off - 1, :, at]
        totals = jnp.transpose(both)
        return lax.rsqrt(totals[:, 0:1] / inner_total + epsilon), totals[:, 1:2] / inner_total

    def turn(back_i, carry):
        i = blocks - 1 - back_i
        at = rows_of(i)
        marks = meta[at, :]
        scale, cross = scale_of(at)
        yv = y_s[at, :]
        g = gate_s[at, :]
        sg = sigmoid(g)
        sl = g * sg
        gg = gg_s[at, :].astype(f32)
        ngate = par[5:6, :]
        normal = yv * sl * scale
        gated_s[at, :] = (normal * ngate).astype(bf16)
        g_mixed = scale * (ngate * gg - normal * (scale * cross))
        ggate_s[at, :] = (g_mixed * yv * (sg * (1.0 + g * (1.0 - sg)))).astype(bf16)
        gy = (g_mixed * sl).astype(bf16)
        gy_s[at, :] = gy
        gyw = gy.astype(f32)
        wide = x_s[at, :].astype(f32)
        dr_s[at, :] = mm_split(gyw * (yv - skip * wide), gather)
        row = lax.broadcasted_iota(jnp.int32, (8, channels), 0)
        ggain = jnp.sum(gg * normal, 0, keepdims=True)
        gskip = jnp.sum(gyw * wide, 0, keepdims=True)
        acc_s[...] += jnp.where(row == 0, ggain, jnp.where(row == 1, gskip, 0.0))
        r = r_s[at, :]
        linked = mm_split(jnp.exp2(r) * marks[:, 4:5], spread)
        r_t = jnp.transpose(wr_s[at, 128:256].astype(f32)).astype(bf16)
        dfresh = mm(r_t, (linked * gyw).astype(bf16))
        fresh_s[i] = dfresh
        mem[...] = keep_of(r[SPAN - 1:SPAN, :], marks) * mem[...] + dfresh

        @pl.when(back_i == 2)
        def _():
            out_sums[1].forward()

        return carry

    lax.fori_loop(0, blocks, turn, 0)
    pass_back[...] = mem[...].astype(bf16)
    pass_back_state.start()
    out_sums[2].forward()

    def grad_out(i, carry):
        rows = pl.ds(pl.multiple_of(i * half, 128), half)
        for n in range(2):
            lanes = slice(n * wide_in // 2, (n + 1) * wide_in // 2)
            value = mm_tn(gated_s[:, rows], cots[:, lanes]).astype(bf16)
            go[i, :, :, :, lanes] = value.reshape(go.shape[1:4] + (wide_in // 2,))
        return carry

    get_out.drain(t)
    lax.fori_loop(0, 2, grad_out, 0)
    sum_out.run(0)

    def grad_gate(i, carry):
        rows = pl.ds(pl.multiple_of(i * (wide_in // t.cols), 128), wide_in // t.cols)
        gg[i] = mm_tn(normed_s[:, rows], ggate_s[...]).astype(bf16).reshape(gg.shape[1:])
        return carry

    lax.fori_loop(0, t.cols, grad_gate, 0)
    sum_gate.run(0)
    sum_out.run(1)
    write(ggate_s, ggate_o)
    accx[...] = jnp.zeros_like(accx)
    accs[...] = jnp.zeros_like(accs)
    acch[...] = jnp.zeros_like(acch)
    xbuf[...] = jnp.zeros_like(xbuf)
    sbuf[...] = jnp.zeros_like(sbuf)
    pass_back_state.wait_recv()
    mem[...] = dstate_in[...].astype(f32) * jnp.where(y == 0, 1.0, 0.0)
    gx_s = gg_s

    def back(back_i, carry):
        i = blocks - 1 - back_i
        at = rows_of(i)

        @pl.when(back_i > 0)
        def _():
            xbuf[SPAN + 8:SPAN + 16, :] = xbuf[8:16, :]
            sbuf[SPAN + 8:SPAN + 16, :] = sbuf[8:16, :]

        marks = meta[at, :]
        w_low = wr_s[at, 0:128]
        r_low = wr_s[at, 128:256]
        r = r_s[at, :]
        r_t = jnp.transpose(r)
        step = step_s[at, :]
        last = r[SPAN - 1:SPAN, :]
        rows = lax.broadcasted_iota(jnp.int32, (SPAN, SPAN), 0)
        cols = lax.broadcasted_iota(jnp.int32, (SPAN, SPAN), 1)
        allowed = (rows <= cols) & (marks[:, 0:1] == docrow[0:1, at])
        scores = jnp.where(allowed, mm_nt(w_low, r_low), 0.0)
        ds = mem[...]
        ds_low = ds.astype(bf16)
        step_parts = split(step, 2)
        te_parts = split(jnp.exp2(jnp.minimum(last - r, 0.0)) * marks[:, 5:6], 2)
        linked_parts = split(jnp.exp2(r) * marks[:, 4:5], 2)
        keep = mm_split(jnp.broadcast_to(jnp.exp2(last) * marks[0:1, 6:7], (8, 128)), spread)[0:1]
        final = jnp.where(back_i == blocks - 1, 1.0, 0.0)

        def conv_back(buf, lanes, gv, base, taps, acc, halo_pre, out, halo_out):
            buf[8:SPAN + 8, lanes] = gv
            cols_here = gv.shape[1]
            total = taps[0:1, lanes] * gv
            sums = [jnp.sum(gv * base, 0, keepdims=True)]
            halo = jnp.zeros((8, cols_here), f32)
            hsum = []
            for k in range(1, 4):
                moved = marks[:, 7 + k:8 + k] * buf[8 + k:8 + k + SPAN, lanes]
                total = total + taps[k:k + 1, lanes] * moved
                sums.append(jnp.sum(moved * base, 0, keepdims=True))
                hmoved = hmeta[:, 7 + k:8 + k] * buf[k:8 + k, lanes]
                halo = halo + taps[k:k + 1, lanes] * hmoved
                hsum.append(jnp.sum(hmoved * halo_pre[:, lanes], 0, keepdims=True))
            sums.append(jnp.sum(gv, 0, keepdims=True))
            out[at, lanes] = total.astype(bf16)
            halo_out[:, lanes] = halo
            rows8 = lax.broadcasted_iota(jnp.int32, (8, cols_here), 0)
            add = jnp.zeros((8, cols_here), f32)
            for n, s in enumerate(sums):
                if 1 <= n <= 3:
                    s = s + final * hsum[n - 1]
                add = add + jnp.where(rows8 == n, s, 0.0)
            acc[:, lanes] += add

        zero = jnp.zeros((SPAN, 128), f32)
        dscores = jnp.zeros((SPAN, SPAN), f32)
        g_write, g_read, dr_cols, dstep = zero, zero, zero, zero
        at_end = jnp.zeros((8, 128), f32)
        for pair in range(channels // 128):
            lanes = slice(pair * 128, pair * 128 + 128)
            to_lanes, to_heads = spread[:, lanes], gather[lanes, :]

            def widen(parts):
                return sum(mm(p, to_lanes) for p in parts)

            wide = x_s[at, lanes].astype(f32)
            step_wide = widen(step_parts)
            xp = (step_wide * wide).astype(bf16)
            xdw = xp.astype(f32)
            gp = gy_s[at, lanes]
            gyw = gp.astype(f32)
            ds_pair = ds_low[:, lanes]
            sprev = sprev_s[i, :, lanes]
            te = widen(te_parts)
            total = te * mm(w_low, ds_pair)
            ending = jnp.sum(xdw * total, 0, keepdims=True) + keep[:, lanes] * jnp.sum(
                sprev.astype(f32) * ds[:, lanes], 0, keepdims=True
            )
            at_end = at_end + mm_split(jnp.broadcast_to(ending, (8, 128)), to_heads, 3)
            for half in range(2):
                h = 2 * pair + half
                own = first if half == 0 else ~first
                decay = jnp.exp2(jnp.minimum(r_t[h:h + 1, :] - r[:, h:h + 1], 0.0))
                mixing = (scores * decay).astype(bf16)
                gown = jnp.where(own, gp, jnp.zeros_like(gp))
                total = total + mm(mixing, gown)
                dscores = dscores + mm_nt(xp, gown) * decay
            g_write = g_write + mm_nt((te * xdw).astype(bf16), ds_pair)
            g_read = g_read + mm_nt((widen(linked_parts) * gyw).astype(bf16), sprev)
            dr_cols = dr_cols + mm_split(xdw * total, to_heads)
            dstep = dstep + mm_split(wide * total, to_heads)
            g_x = step_wide * total + skip[:, lanes] * gyw
            conv_back(xbuf, lanes, g_x * sd_s[at, lanes].astype(f32), pre_s[at, lanes].astype(f32), par,
                      accx, hpre_s, gg_s, hx)
        dscores = jnp.where(allowed, dscores, 0.0)
        g_write = g_write + mm(dscores.astype(bf16), r_low)
        g_read = g_read + mm(jnp.transpose(dscores).astype(bf16), w_low)
        both = slice(0, 256)
        g_wr = jnp.concatenate([g_write, g_read], 1)
        conv_back(sbuf, both, g_wr * ssd_s[at, :].astype(f32), spre_s[at, :].astype(f32), spar, accs,
                  hspre_s, gs_s, hs)
        tail_row = lax.broadcasted_iota(jnp.int32, (SPAN, 128), 0) == SPAN - 1
        dr = dr_s[at, :] - dr_cols + jnp.where(tail_row, at_end[0:1], 0.0)
        da = split_mm(upper_ones(), dr)
        dstep = dstep + head[3:4, :] * da
        gzv = dstep * sig_s[at, :]
        gz_s[at, :] = gzv.astype(bf16)
        row = lax.broadcasted_iota(jnp.int32, (8, 128), 0)
        gbias = jnp.sum(gzv, 0, keepdims=True)
        grate = jnp.sum(da * step, 0, keepdims=True)
        acch[...] += jnp.where(row == 0, gbias, jnp.where(row == 1, grate, 0.0))
        mem[...] = keep * ds + fresh_s[i]

        @pl.when(back_i == 0)
        def _():
            out_sums[3].forward()
            sum_gate.run(1)

        @pl.when(back_i == 1)
        def _():
            sum_out.run(2)

        @pl.when(back_i == 2)
        def _():
            sum_gate.run(2)

        return carry

    lax.fori_loop(0, blocks, back, 0)
    halo_x.start()
    halo_s.start()
    write(gz_s, gz_o)
    write(accx, accx_o)
    write(accs, accs_o)
    write(acch, acch_o)
    write(acc_s, acc_o)
    sum_out.run(3)
    sum_gate.run(3)
    write(o4, go4_o)
    write(g4, gg4_o)
    halo_x.wait_recv()
    halo_s.wait_recv()
    use = jnp.where(y == 0, 1.0, 0.0)
    end = pl.ds(tok.shape[0] - 16, 16)
    zeros = jnp.zeros((8, channels), f32)
    gx_s[end, :] = (
        gx_s[end, :].astype(f32) + jnp.concatenate([zeros, use * hx_in[...]], 0)
    ).astype(bf16)
    zeros = jnp.zeros((8, 256), f32)
    gs_s[end, :] = (
        gs_s[end, :].astype(f32) + jnp.concatenate([zeros, use * hs_in[...]], 0)
    ).astype(bf16)
    write(gx_s, gx_o)
    write(gs_s, gs_o)

    for s in out_sums:
        s.arrive()

    def finish(i, carry):
        at = rows_of(i)
        scale = scale_of(at)[0]
        out_far[at, :] = (
            tok_own[at, :].astype(f32) + scale * out_sums[0].total(at)
        ).astype(bf16)
        return carry

    lax.fori_loop(0, blocks, finish, 0)
    write(out_far, mixed_o)
    for copy in outputs:
        copy.wait()
    t.finish()


def front(inner_all, ngain, w_states, segments, taps_inner, bias_inner, gain_gate, taps_states,
          bias_states, step_all, step_bias, decay_log, skip_gain, tok, inner, gate, out, cot):
    tokens, width = tok.shape
    blocks = tokens // SPAN
    cols = lax.axis_size("col")
    groups = lax.axis_size("dp") // SHARE - 1
    part, half = inner.shape[0] // SHARE, inner.shape[1] // cols
    channels = 2 * half
    third = width // cols
    q, qo = third // SHARE, half // SHARE
    sds = jax.ShapeDtypeStruct
    V = pltpu.VMEM
    wide = ((cols, 2, 2, part, channels), bf16)
    by_channel = ((tokens, channels), bf16)
    by_state = ((tokens, 256), bf16)
    by_head = ((tokens, 128), f32)
    acc, sacc, hacc = ((8, channels), f32), ((8, 256), f32), ((8, 128), f32)
    passed = ((128, channels), bf16)
    far = [(groups, cols, q, half), (groups, qo, width)] if groups else [(16, 128)] * 2
    outs = [
        ((tokens, third), bf16), wide, wide, ((width, 128), bf16), ((tokens, width), bf16), by_head,
        by_channel, by_state, ((tokens, 128), bf16), acc, sacc, hacc, acc,
        ((cols, q, half), bf16), ((qo, width), bf16), by_channel,
    ] + [(shape, bf16) for shape in far]
    scratch = [
        wide, wide, ((2, 2, 2, half // SHARE, width), bf16), ((cols, 2, 2, part, 256), bf16),
        ((width, 128), bf16), ((part * SHARE, cols * 128), bf16), ((tokens, width), bf16), acc, sacc,
        hacc, hacc, hacc, ((16, width), bf16), ((tokens, width), bf16), ((tokens, third), bf16),
        by_head, hacc, ((8, tokens), f32), ((8, 2 * tokens + 256), f32),
        ((tokens, width), bf16), by_channel, by_state, by_channel, by_state, by_channel, by_state,
        by_head, by_head, by_head, acc, sacc, ((blocks, 128, channels), bf16),
        by_channel, by_channel, by_channel, by_head, ((blocks, 128, channels), f32),
        ((tokens, channels), f32), ((tokens, channels), f32), by_channel, by_state,
        ((tokens, 128), bf16),
        ((2, tokens, third), bf16), ((tokens, third), bf16), ((8, tokens), f32),
        ((cols - 1, 8, tokens), f32), ((SPAN + 16, channels), f32), ((SPAN + 16, 256), f32),
        ((128, channels), f32), passed, passed, passed, passed,
        acc, sacc, acc, sacc, acc, sacc, hacc, acc,
        ((cols, 2, 2, q, channels), bf16),
    ] + column_sum_shapes(cols, q, half) + row_sum_shapes(qo, width)
    vmem = pl.BlockSpec(memory_space=V)
    hbm = pl.BlockSpec(memory_space=pl.ANY)
    smem = pl.BlockSpec(memory_space=pltpu.SMEM)
    got = pl.pallas_call(
        functools.partial(front_kernel, float(inner_all)),
        out_shape=[sds(*o) for o in outs],
        in_specs=[vmem] * 9 + [smem] * 3 + [hbm] * 5,
        out_specs=[hbm] * len(outs),
        scratch_shapes=[V(*s) for s in scratch] + [
            pltpu.SemaphoreType.DMA((72,)), pltpu.SemaphoreType.DMA((72,)),
            pltpu.SemaphoreType.DMA((40,)),
        ],
        compiler_params=pltpu.CompilerParams(
            collective_id=1, has_side_effects=True, vmem_limit_bytes=63 * 1024 * 1024
        ),
        name="front",
    )(ngain, w_states, segments, taps_inner, bias_inner, gain_gate, taps_states, bias_states, step_all,
      step_bias, decay_log, skip_gain, tok, inner, gate, out, cot)
    got = list(got[:16])
    got[1] = got[1].reshape(width, channels)
    got[2] = got[2].reshape(width, channels)
    return got


def rear_kernel(
    accx, accs, acch, acc1, ngain_v,
    tok_h, w_states_h, wi_h, wg_h, ws_h, cot_h, normed_h, sig_h, ggate_h, gx_h, gs_h, gz_h, g4_h, o4_h,
    gtok_o, oi, og, oz, oo, os, sm_o, far_i, far_z, far_s,
    tok, wst, wi, wg, ws, cot_own, normed, sig_s, ggate, gx_s, gs_s, gz_s, g4, o4,
    ngain, part, gshare, g_near, g_far, ish, ish_in,
    gi, i1, i2, i3, i5, i6, i4, gz, z1, z2, z3, z5, z6, z4,
    gs, s1, s2, s3, s4, s5, sm, msum, mgot,
    send, recv, local,
):
    t = Links(send, recv, local)
    x, y, z, core = t.x, t.y, t.z, t.core
    tokens, width = normed.shape
    channels = ggate.shape[1]
    third = width // t.cols
    blocks = tokens // SPAN
    own_cols = lane_block(z, third)

    def load(src, dst):
        copy = t.keep(src, dst)
        copy.start()
        return copy

    first = [load(g4_h, g4), load(o4_h, o4)]
    loads = [load(a, b) for a, b in (
        (ggate_h, ggate), (wg_h, wg), (gx_h, gx_s), (wi_h, wi), (gz_h, gz_s), (ws_h, ws), (gs_h, gs_s),
        (w_states_h, wst), (normed_h, normed),
    )]
    later = [load(a, b) for a, b in (
        (cot_h, cot_own), (sig_h, sig_s), (tok_h.at[:, own_cols], tok),
    )]
    norm_sums = [PairSum(t, part, g_near, g_far, pl.ds(b * SPAN, SPAN)) for b in range(blocks)]
    home_out = row_home(t, o4, oo, Steps())
    home_gate = column_home(t, g4, og, Steps())
    sum_inner = column_home(t, i4, oi, column_sums(t, gi, i1, i2, i3, i5, i6, i4, far_i))
    sum_step = column_home(t, z4, oz, column_sums(t, gz, z1, z2, z3, z5, z6, z4, far_z))
    sum_states = full_sums(t, gs, s1, s2, s3, s4, s5, far_s, os)
    sum_small = small_sums(t, sm, msum, mgot, sm_o, 16)
    send_ish = [t.make(ish, ish_in.at[off - 1], {"col": t.col_peer(off)}) for off in range(1, t.cols)]
    t.meet(True)

    def rows_of(i):
        return pl.ds(pl.multiple_of(i * SPAN, SPAN), SPAN)

    for c in first:
        c.wait()
    home_out.run(0)
    home_gate.run(0)
    gshare[...] = jnp.zeros_like(gshare)
    ngain[...] = jnp.broadcast_to(ngain_v[...].reshape(1, width), (8, width))
    for c in loads:
        c.wait()

    def normed_grad(i, carry):
        at = rows_of(i)

        def body(c, column):
            lanes = pl.ds(pl.multiple_of(c * third, 128), third)
            total = (
                mm_nt(ggate[at, :], wg[lanes, :]) + mm_nt(gx_s[at, :], wi[lanes, :])
                + mm_nt(gz_s[at, :], ws[lanes, :]) + mm_nt(gs_s[at, :], wst[lanes, :])
            )
            part[at, lanes] = total.astype(bf16)
            weighed = total * normed[at, lanes].astype(f32)
            gshare[0:1, lanes] += jnp.sum(weighed, 0, keepdims=True)
            return column + jnp.sum(weighed, -1, keepdims=True)

        column = lax.fori_loop(0, t.cols, body, jnp.zeros((SPAN, 1), f32))
        ish[:, at] = jnp.transpose(jnp.broadcast_to(column, (SPAN, 128)))[0:8]
        for b in range(blocks):
            pl.when(i == b)(norm_sums[b].start)
        return carry

    def weight_grad(right, target):
        def body(i, carry):
            rows = pl.ds(pl.multiple_of(i * third, 128), third)
            target[i] = mm_tn(normed[:, rows], right[...]).astype(bf16).reshape(target.shape[1:])
            return carry

        lax.fori_loop(0, t.cols, body, 0)

    def gz_body(i, carry):
        rows = pl.ds(pl.multiple_of(i * third, 128), third)
        value = mm_tn(normed[:, rows], gz_s[...]).astype(bf16)
        gz[i] = jnp.concatenate([value, value], 1).reshape(gz.shape[1:])
        return carry

    def gs_body(i, carry):
        rows = pl.ds(pl.multiple_of(i * third, 128), third)
        gs[i] = mm_tn(normed[:, rows], gs_s[...]).astype(bf16).reshape(gs.shape[1:])
        return carry

    lax.fori_loop(0, 1, normed_grad, 0)
    weight_grad(gx_s, gi)
    sum_inner.run(0)
    lax.fori_loop(1, blocks, normed_grad, 0)
    sum_inner.run(1)
    lax.fori_loop(0, t.cols, gs_body, 0)
    sum_states.run(0)
    lax.fori_loop(0, t.cols, gz_body, 0)
    sum_step.run(0)
    sm[0:8, :] = accx[...]
    sm[8:16, :] = acc1[...]
    sm[10:12, 0:128] = acch[0:2, :]
    sm[16:24, 0:256] = accs[...]
    sm[16:24, 256:] = jnp.zeros((8, channels - 256), f32)
    sm[24:32, :] = gshare[:, 0:channels]
    sm[32:40, :] = gshare[:, channels:]
    sum_small.run(0)
    for c in send_ish:
        c.start()
    norm_sums[0].forward()
    home_out.run(1)
    home_gate.run(1)
    norm_sums[1].forward()
    sum_states.run(1)
    sum_step.run(1)
    sum_small.run(1)
    norm_sums[2].forward()
    sum_inner.run(2)
    norm_sums[3].forward()
    sum_states.run(2)
    sum_step.run(2)
    sum_small.run(2)
    sum_inner.run(3)
    sum_inner.run(4)
    sum_states.run(3)
    sum_step.run(3)
    sum_step.run(4)
    sum_small.run(3)
    home_out.run(2)
    home_gate.run(2)
    sum_states.run(4)
    sum_small.run(4)
    sum_step.run(5)
    sum_inner.run(5)
    sum_states.run(5)
    sum_step.run(6)
    sum_states.run(6)
    sum_inner.run(6)
    sum_states.run(7)
    for c in later:
        c.wait()

    for c in send_ish:
        c.wait_recv()
    for n in norm_sums:
        n.arrive()

    def finish(i, carry):
        at = rows_of(i)
        own = tok[at, :].astype(f32)
        both = ish[:, at]
        for off in range(1, t.cols):
            both = both + ish_in[off - 1, :, at]
        along = jnp.transpose(both)[:, 0:1] / width
        inverse = sig_s[at, 127:128]
        grad = inverse * (norm_sums[0].total(at) * ngain[0:1, own_cols] - own * (inverse * along))
        g_far[at, :] = (grad + cot_own[at, :].astype(f32)).astype(bf16)
        return carry

    lax.fori_loop(0, blocks, finish, 0)
    last = load(g_far, gtok_o)
    home_out.run(3)
    home_gate.run(3)
    sum_step.run(7)
    sum_inner.run(7)
    sum_states.run(8)
    sum_small.run(5)
    last.wait()
    t.finish()


def rear(accx, accs, acch, acc1, ngain, tok, w_states, wi, wg, ws, cot, normed, sig, ggate, gx, gs, gz,
         g4, o4):
    tokens, width = normed.shape
    channels = ggate.shape[1]
    cols = lax.axis_size("col")
    groups = lax.axis_size("dp") // SHARE - 1
    third, own = width // cols, channels // 2
    q, qo, qs = third // SHARE, own // SHARE, width // (cols * 2 * SHARE)
    sds = jax.ShapeDtypeStruct
    V = pltpu.VMEM
    small = [accx, accs, acch, acc1, ngain]
    big = [tok, w_states, wi, wg, ws, cot, normed, sig, ggate, gx, gs, gz, g4, o4]
    scratch = [((tokens, third), bf16)] + [(b.shape, b.dtype) for b in big[1:]]

    scratch += [
        ((8, width), f32), ((tokens, width), bf16), ((8, width), f32),
        ((2, tokens, third), bf16), ((tokens, third), bf16), ((8, tokens), f32),
        ((cols - 1, 8, tokens), f32),
    ]
    scratch += [((cols, 2, 2, q, 2 * own), bf16)] + column_sum_shapes(cols, q, own)
    scratch += [((cols, 2, 2, q, 256), bf16)] + column_sum_shapes(cols, q, 128)
    scratch += [
        ((cols, 2, 2, 2, qs, 256), bf16), ((cols, 2, 2, qs, 256), bf16), ((cols, 2, qs, 256), bf16),
        ((cols, qs, 256), bf16), ((cols, qs, 256), bf16), ((cols - 1, qs, 256), bf16),
        ((40, channels), f32), ((3, 40, channels), f32), ((6 + groups, 40, channels), f32),
    ]
    if groups:
        far = [(groups, cols, q, own), (groups, cols, q, 128), (groups, cols, qs, 256)]
    else:
        far = [(16, 128)] * 3
    vmem = pl.BlockSpec(memory_space=V)
    hbm = pl.BlockSpec(memory_space=pl.ANY)
    got = pl.pallas_call(
        rear_kernel,
        out_shape=[
            sds((tokens, third), bf16),
            sds((2, 2, q, cols * own), bf16), sds((2, 2, q, cols * own), bf16),
            sds((2, 2, q, cols * 128), bf16), sds((cols, 2, 2, qo, third), bf16),
            sds((cols, 2, 2, 2, qs, 256), bf16), sds((40, channels), f32),
        ] + [sds(f, bf16) for f in far],
        in_specs=[vmem] * len(small) + [hbm] * len(big),
        out_specs=[hbm] * 6 + [vmem] + [hbm] * 3,
        scratch_shapes=[V(*s) for s in scratch] + [
            pltpu.SemaphoreType.DMA((100,)), pltpu.SemaphoreType.DMA((100,)),
            pltpu.SemaphoreType.DMA((48,)),
        ],
        compiler_params=pltpu.CompilerParams(
            collective_id=2, has_side_effects=True, vmem_limit_bytes=62 * 1024 * 1024
        ),
        name="rear",
    )(*small, *big)
    gtok, oi, og, oz, oo, os, sm = got[:7]
    return (
        gtok, oi.reshape(third, -1), og.reshape(third, -1), oz.reshape(third, -1),
        oo.reshape(cols * own, third), os.reshape(width, -1), sm,
    )


def unpack_kernel(
    oi, og, oz, oo, os, sm, ngain, decay_log,
    inner_o, gate_o, step_o, out_o, states_o, taps_o, bias_o, staps_o, sbias_o, step_bias_o, decay_o,
    skip_o, gain_o, norm_o,
    wide,
):
    y, z = lax.axis_index("row"), lax.axis_index("col")
    inner_o[...] = oi[...].astype(f32)
    gate_o[...] = og[...].astype(f32)
    out_o[...] = oo[...].astype(f32)
    states_o[...] = os[...].astype(f32)
    heads = decay_log.shape[0]
    lanes, steps = oz.shape[1], step_o.shape[1]
    src = lax.broadcasted_iota(jnp.int32, (lanes, steps), 0)
    dst = lax.broadcasted_iota(jnp.int32, (lanes, steps), 1)
    pick = jnp.zeros((lanes, steps), f32)
    for c in range(steps // heads):
        mine = (dst >= c * heads) & (dst < (c + 1) * heads)
        pick = pick + jnp.where(mine & (src - dst == c * 128 + y * heads - c * heads), 1.0, 0.0)
    step_o[...] = mm(oz[...], pick.astype(bf16))

    @pl.when(pl.program_id(0) == 0)
    def _():
        own_ch, third = taps_o.shape[1], norm_o.shape[0]
        own = lane_block(y, own_ch)
        taps_o[...] = sm[0:4, own]
        bias_o[...] = sm[4:5, own].reshape(own_ch)
        gain_o[...] = sm[8:9, own].reshape(own_ch)
        staps_o[...] = sm[16:20, 0:256]
        sbias_o[...] = sm[20:21, 0:256].reshape(256)
        skip = mm_split(sm[8:16, own], gather_matrix(own_ch), 3)
        skip_o[...] = skip[1:2, 0:heads].reshape(heads)

        def own_head(row):
            both = sm[row:row + 1, 0:128]
            return jnp.where(y == 0, both[:, 0:heads], both[:, heads:2 * heads])

        step_bias_o[...] = own_head(10).reshape(heads)
        rate = -jnp.exp(decay_log[...].reshape(1, heads))
        decay_o[...] = (own_head(11) * rate).reshape(heads)
        half = sm.shape[1]
        wide[0:8, 0:half] = sm[24:32, :]
        wide[0:8, half:] = sm[32:40, :]
        wide[8:16, :] = jnp.broadcast_to(ngain[...].reshape(1, 2 * half), (8, 2 * half))
        cols = lane_block(z, third)
        norm_o[...] = (wide[0:1, cols] / wide[8:9, cols]).reshape(third)


def unpack(oi, og, oz, oo, os, sm, ngain, decay_log, own_ch):
    sds = jax.ShapeDtypeStruct
    heads, parts = decay_log.shape[0], 4
    third, block = oi.shape

    def rows(shape):
        return pl.BlockSpec((shape[0] // parts, shape[1]), lambda i: (i, 0))

    def whole(shape):
        return pl.BlockSpec(shape, lambda i: (0,) * len(shape))

    steps = (third, block // own_ch * heads)
    small = [(4, own_ch), (own_ch,), (4, 256), (256,), (heads,), (heads,), (heads,), (own_ch,),
             (third,)]
    big = [oi.shape, og.shape, steps, oo.shape, os.shape]
    ins = [rows(v.shape) for v in (oi, og, oz, oo, os)]
    return pl.pallas_call(
        unpack_kernel,
        grid=(parts,),
        out_shape=[sds(s, f32) for s in big + small],
        in_specs=ins + [whole(sm.shape), whole(ngain.shape), whole(decay_log.shape)],
        out_specs=[rows(s) for s in big] + [whole(s) for s in small],
        scratch_shapes=[pltpu.VMEM((16, 2 * sm.shape[1]), f32)],
        compiler_params=pltpu.CompilerParams(vmem_limit_bytes=62 * 1024 * 1024),
        name="unpack",
    )(oi, og, oz, oo, os, sm, ngain, decay_log)


def per_device(
    tokens_in, segment_ids, norm_gain, proj_gate, proj_inner, proj_step, proj_states,
    conv_inner, conv_inner_bias, conv_states, conv_states_bias, step_bias, decay_log,
    skip_gain, gate_gain, proj_out, cotangent,
):
    inner_all = proj_gate.shape[1] * lax.axis_size("row")
    (
        mixed_out, w_inner, w_gate, w_step, normed, sig, gx, gs, gz, accx, accs, acch, acc1, g4, o4,
        g_gate,
    ) = front(
        inner_all, norm_gain, proj_states, segment_ids, conv_inner, conv_inner_bias, gate_gain,
        conv_states, conv_states_bias, proj_step, step_bias, decay_log, skip_gain,
        tokens_in, proj_inner, proj_gate, proj_out, cotangent,
    )
    grad_tokens, oi, og, oz, oo, os, sums = rear(
        accx, accs, acch, acc1, norm_gain, tokens_in, proj_states, w_inner, w_gate, w_step, cotangent,
        normed, sig, g_gate, gx, gs, gz, g4, o4,
    )
    (
        grad_inner, grad_gate, grad_step, grad_out, grad_states, grad_conv_inner,
        grad_conv_inner_bias, grad_conv_states, grad_conv_states_bias, grad_step_bias, grad_decay,
        grad_skip, grad_gate_gain, grad_norm_gain,
    ) = unpack(oi, og, oz, oo, os, sums, norm_gain, decay_log, conv_inner.shape[1])
    return (
        mixed_out, grad_tokens, grad_norm_gain, grad_gate, grad_inner, grad_step, grad_states,
        grad_conv_inner, grad_conv_inner_bias, grad_conv_states, grad_conv_states_bias,
        grad_step_bias, grad_decay, grad_skip, grad_gate_gain, grad_out,
    )


def solution(mesh):
    in_specs = (
        P(("dp", "row"), None),
        P("dp", None),
        P(),
        P("col", "row"),
        P("col", "row"),
        P("col", "row"),
        P(),
        P(None, ("row", "col")),
        P(("row", "col")),
        P(),
        P(),
        P(("row", "col")),
        P(("row", "col")),
        P(("row", "col")),
        P(("row", "col")),
        P("row", "col"),
        P(("dp", "row"), "col"),
    )
    out_specs = (
        P(("dp", "row"), "col"),
        P(("dp", "row"), "col"),
        P("col"),
        P("col", "row"),
        P("col", "row"),
        P("col", "row"),
        P(),
        P(None, ("row", "col")),
        P(("row", "col")),
        P(),
        P(),
        P(("row", "col")),
        P(("row", "col")),
        P(("row", "col")),
        P(("row", "col")),
        P("row", "col"),
    )
    return jax.shard_map(
        per_device, mesh=mesh, in_specs=in_specs, out_specs=out_specs, check_vma=False
    )
```

time: 336 us -> 267 us (0.79)
  Pallas kernels: 298 us -> 261 us
  other arithmetic: 15.5 us -> 0 us
  local copies, waits for them, and re-layouts: 18.8 us -> 4.96 us
    pallas_call x1 -> x2, Pallas kernels: 171 us -> 109 us  [the longest x1 102 us: rear(): pl.pallas_call(rear_kernel, out_shape=[sds((tokens, third), bf16), sds((2...]
    pallas_call x1, Pallas kernels: 127 us -> 152 us  [front(): pl.pallas_call(functools.partial(front_kernel, float(inner_all)), out_sha...]
    convert_element_type x5 -> x0, other arithmetic: 9.1 us -> none  [the longest x1 4.55 us: per_device(): grad_inner = oi.astype(f32)]
    slice x9 -> x0, local copies, waits for them, and re-layouts: 9.07 us -> none  [the longest x1 1.45 us: per_device(): grad_gate_gain = own_few[8]]
where the time goes in v5:
time: 267 us
  Pallas kernels  261 us (98%)
  local copies, waits for them, and re-layouts  4.96 us (2%)
    pallas_call x1, Pallas kernels, front(): pl.pallas_call(functools.partial(front_kernel, float(inner_all)), out_sha...  152 us
    pallas_call x1, Pallas kernels, rear(): pl.pallas_call(rear_kernel, out_shape=[sds((tokens, third), bf16), sds((2...  102 us
    pallas_call x1, Pallas kernels, unpack(): pl.pallas_call(unpack_kernel, grid=(parts,), out_shape=[sds(s, f32) for s...  7.27 us

profile of v5, /device:TPU:0, one launch (start us, length us, event | category | flops | bytes accessed | tf_op | source)
XLA Modules:
  0.0 266.8 jit_solution(15198735269890134166)
XLA Ops:
  0.6 1.5 copy.33.step_all
  2.1 152.1 %front.1 = (bf16[1024,384]{1,0:T(8,128)(2,1)}, bf16[4,2,2,96,768]{4,3,2,1,0:T(8,128)(2,1)}, bf16[4,2,2,96,768]{4,3,2,1,0:T(8,128)(2,1)}, bf16[1536,128]{1,0:T(8,...) custom-call(f32[1536]{0:T(1024)} %ngain.1, ...), custom_call_target="tpu_custom_call" | custom-call | tf_op jit(solution)/shard_map/front/pallas_call | solution.py:1192
  154.2 101.9 %rear.1 = (bf16[1024,384]{1,0:T(8,128)(2,1)}, bf16[2,2,96,1536]{3,2,1,0:T(8,128)(2,1)}, bf16[2,2,96,1536]{3,2,1,0:T(8,128)(2,1)}, bf16[2,2,96,512]{3,2,1,0:T(8,1...) custom-call(f32[8,768]{1,0:T(8,128)} %get-tuple-element.54.accx, ...), custom_call_target="tpu_custom_call" | custom-call | tf_op jit(solution)/shard_map/rear/pallas_call | solution.py:1418
  256.1 0.0 copy-start
  256.1 7.3 %unpack.1 = (f32[384,1536]{1,0:T(8,128)}, f32[384,1536]{1,0:T(8,128)}, f32[384,24]{1,0:T(8,128)}, f32[1536,384]{1,0:T(8,128)}, f32[1536,256]{1,0:T(8,128)}, /*in...) custom-call(bf16[384,1536]{1,0:T(8,128)(2,1)} %bitcast.9, ...), custom_call_target="tpu_custom_call" | custom-call | tf_op jit(solution)/shard_map/unpack/pallas_call | solution.py:1508
  263.3 0.0 copy-start.1
  263.4 1.7 copy.34
  265.1 0.0 copy-done
  265.1 0.9 copy.37
  266.0 0.0 copy-done.1
  266.0 0.9 copy.38
Async XLA Ops:
  256.1 9.0 %copy-start = (bf16[1024,384]{1,0:T(8,128)(2,1)S(1)}, bf16[1024,384]{1,0:T(8,128)(2,1)}, u32[]{:S(2)}) copy-start(bf16[1024,384]{1,0:T(8,128)(2,1)} %get-tuple-element.122) | copy-start | bytes 2359300
  263.3 2.6 copy-start.1

commit v6 on v5

--- a/solution.py
+++ b/solution.py
@@ -69,6 +69,16 @@
 
 def sigmoid(v):
     return 1.0 / (1.0 + jnp.exp(-v))
+
+
+def widen(first, values, pair):
+    return jnp.where(first, values[:, 2 * pair:2 * pair + 1], values[:, 2 * pair + 1:2 * pair + 2])
+
+
+def head_totals(values, to_heads):
+    high = values.astype(bf16)
+    low = (values - high.astype(f32)).astype(bf16)
+    return mm(jnp.concatenate([high, low], 1), jnp.concatenate([to_heads, to_heads], 0))
 
 
 def half_masks():
@@ -285,7 +295,7 @@
     def start(self):
         self.first.start()
 
-    def forward(self):
+    def forward(self, both=True):
         self.first.wait_recv()
         count = self.rows.size // 64
 
@@ -296,7 +306,8 @@
 
         lax.fori_loop(0, count, body, 0)
         self.across.start()
-        self.second.start()
+        if both:
+            self.second.start()
 
     def arrive(self):
         self.second.wait_recv()
@@ -563,6 +574,7 @@
     gated_s, ggate_s, gy_s, dr_s, fresh_s, y_s, gate_s, gg_s, gs_s, gz_s,
     out_near, out_far, sums_s, sums_in, xbuf, sbuf, mem, pass_out, state_in, dstate_in, pass_back,
     hx, hs, hx_in, hs_in, accx, accs, acch, acc_s, gg, g1, g2, g3, g5, g6, g4, o1, o2, o3, o5, o6, o4,
+    tile_a, tile_b, wide_tile,
     send, recv, local,
 ):
     t = Links(send, recv, local)
@@ -630,7 +642,7 @@
     spar[...] = jnp.zeros_like(spar)
     spar[0:4, :] = taps_states[...]
     spar[4:5, :] = bias_states[...].reshape(1, 256)
-    every = step_all.shape[1]
+    every = step_all.shape[0]
     src = lax.broadcasted_iota(jnp.int32, (every, t.cols * 128), 0)
     dst = lax.broadcasted_iota(jnp.int32, (every, t.cols * 128), 1)
     place = jnp.zeros((every, t.cols * 128), f32)
@@ -638,7 +650,7 @@
         low = c * 128 + y * own_heads - c * own_heads
         mine = (src >= c * own_heads) & (src < (c + 1) * own_heads)
         place = place + jnp.where(mine & (dst - src == low), 1.0, 0.0)
-    step_w[...] = mm(step_all[...], place.astype(bf16)).astype(bf16)
+    step_w[...] = mm_tn(step_all[...], place.astype(bf16)).astype(bf16)
     get_step.run(0)
     for c in few:
         c.start()
@@ -715,15 +727,21 @@
         wr_s[at, :] = sact.astype(bf16)
         ssd_s[at, :] = sslope.astype(bf16)
         sig_s[at, :] = jnp.broadcast_to(inverse, (SPAN, 128))
-        pl.when(i == 0)(lambda: (get_inner.run(1), get_step.run(1), get_gate.run(0)) and None)
+
+        @pl.when(i == 0)
+        def _():
+            get_inner.run(1)
+            get_step.run(1)
+            get_gate.run(0)
+            get_out.run(0)
+            get_cot[0].run(0)
+
         return carry
 
     lax.fori_loop(0, blocks, norm_block, 0)
     head[...] = head_own[...] + head_in[...]
     get_inner.run(2)
     get_step.run(2)
-    get_out.run(0)
-    get_cot[0].run(0)
     get_inner.run(3)
     get_step.run(3)
     get_gate.run(1)
@@ -738,6 +756,7 @@
     def w_of(ref):
         return ref[...].reshape(-1, ref.shape[-1])
 
+    first = half_masks()
     h_inner = mm(hn, w_of(wi))[8:16]
     xbuf[0:8, :] = h_inner
     hpre_s[...] = h_inner
@@ -761,7 +780,6 @@
             act, slope = conv_silu(xbuf, lanes, xbuf[8:SPAN + 8, lanes], par, marks)
             x_s[at, lanes] = act.astype(bf16)
             sd_s[at, lanes] = slope.astype(bf16)
-        x_low = x_s[at, :]
 
         raw = mm(normed, ws[...]) + head[0:1, :]
         step = jnp.maximum(raw, 0.0) + jnp.log1p(jnp.exp(-jnp.abs(raw)))
@@ -772,9 +790,12 @@
         r_s[at, :] = r
         last = r[SPAN - 1:SPAN, :]
         to_end = jnp.exp2(jnp.minimum(last - r, 0.0)) * marks[:, 5:6]
-        coef = mm_split(to_end * step, spread)
+        coef = to_end * step
+        for pair in range(channels // 128):
+            lanes = slice(pair * 128, pair * 128 + 128)
+            tile_a[:, lanes] = (widen(first, coef, pair) * x_s[at, lanes].astype(f32)).astype(bf16)
         w_t = jnp.transpose(wr[:, 0:128].astype(f32)).astype(bf16)
-        fresh = mm(w_t, (coef * x_low.astype(f32)).astype(bf16))
+        fresh = mm(w_t, tile_a[...])
         fresh_s[i] = fresh
         mem[...] = keep_of(last, marks) * mem[...] + fresh
 
@@ -815,7 +836,6 @@
     mem[...] = state_in[...].astype(f32) * jnp.where(y == 1, 1.0, 0.0)
     get_out.run(3)
     skip = mm_split(jnp.broadcast_to(head[2:3, :], (8, 128)), spread)[0:1]
-    first = half_masks()
 
     def scan(i, carry):
         at = rows_of(i)
@@ -828,17 +848,16 @@
         cols = lax.broadcasted_iota(jnp.int32, (SPAN, SPAN), 1)
         allowed = (rows >= cols) & (marks[:, 0:1] == docrow[0:1, at])
         scores = jnp.where(allowed, mm_nt(r_low, w_low), 0.0)
-        wide = x_s[at, :].astype(f32)
-        xd = (mm_split(step_s[at, :], spread) * wide).astype(bf16)
+        step = step_s[at, :]
         sprev = mem[...].astype(bf16)
         sprev_s[i] = sprev
         linked = jnp.exp2(r) * marks[:, 4:5]
-        carried = mm(r_low, sprev) * mm_split(linked, spread)
-        y_s[at, :] = carried + skip * wide
+        y_s[at, :] = mm(r_low, sprev)
         for pair in range(channels // 128):
             lanes = slice(pair * 128, pair * 128 + 128)
-            xp = xd[:, lanes]
-            total = y_s[at, lanes]
+            wide = x_s[at, lanes].astype(f32)
+            xp = (widen(first, step, pair) * wide).astype(bf16)
+            total = y_s[at, lanes] * widen(first, linked, pair) + skip[:, lanes] * wide
             for part in range(2):
                 h = 2 * pair + part
                 decay = jnp.exp2(jnp.minimum(r[:, h:h + 1] - r_t[h:h + 1, :], 0.0))
@@ -877,8 +896,10 @@
         mixed = y_s[at, :] * (g * sigmoid(g))
         sq = sum(mm_nt(ones, part) for part in split(mixed * mixed, 2))
         pr = sum(mm_nt(ones, part) for part in split(mixed * (par[5:6, :] * gg), 2))
-        row = lax.broadcasted_iota(jnp.int32, (8, SPAN), 0)
-        sums_s[:, at] = jnp.where(row == 0, sq, jnp.where(row == 1, pr, 0.0))
+        for n in range(2):
+            lanes = slice(n * 128, n * 128 + 128)
+            sums_s[pl.ds(2 * i + n, 1), :] = sq[0:1, lanes]
+            sums_s[pl.ds(2 * blocks + 2 * i + n, 1), :] = pr[0:1, lanes]
         return carry
 
     lax.fori_loop(0, blocks // 2, totals_of, 0)
@@ -888,17 +909,23 @@
     lax.fori_loop(blocks // 2, blocks, totals_of, 0)
     for c in pass_sums:
         c.start()
-    out_sums[0].forward()
     for c in pass_sums:
         c.wait_recv()
     mem[...] = jnp.zeros_like(mem)
     acc_s[...] = jnp.zeros_like(acc_s)
     gather = gather_matrix(channels)
 
-    def scale_of(at):
-        both = sums_s[:, at]
-        for off in range(1, t.cols):
-            both = both + sums_in[off - 1, :, at]
+    def scale_of(i):
+        columns = []
+        for base in (0, 2 * blocks):
+            rows = pl.ds(base + 2 * i, 2)
+            pair = sums_s[rows, :]
+            for off in range(1, t.cols):
+                pair = pair + sums_in[off - 1, rows, :]
+            columns.append(jnp.concatenate([pair[0:1], pair[1:2]], 1))
+        row = lax.broadcasted_iota(jnp.int32, (8, SPAN), 0)
+        both = jnp.where(row == 0, jnp.broadcast_to(columns[0], (8, SPAN)),
+                         jnp.broadcast_to(columns[1], (8, SPAN)))
         totals = jnp.transpose(both)
         return lax.rsqrt(totals[:, 0:1] / inner_total + epsilon), totals[:, 1:2] / inner_total
 
@@ -906,43 +933,44 @@
         i = blocks - 1 - back_i
         at = rows_of(i)
         marks = meta[at, :]
-        scale, cross = scale_of(at)
-        yv = y_s[at, :]
-        g = gate_s[at, :]
-        sg = sigmoid(g)
-        sl = g * sg
-        gg = gg_s[at, :].astype(f32)
-        ngate = par[5:6, :]
-        normal = yv * sl * scale
-        gated_s[at, :] = (normal * ngate).astype(bf16)
-        g_mixed = scale * (ngate * gg - normal * (scale * cross))
-        ggate_s[at, :] = (g_mixed * yv * (sg * (1.0 + g * (1.0 - sg)))).astype(bf16)
-        gy = (g_mixed * sl).astype(bf16)
-        gy_s[at, :] = gy
-        gyw = gy.astype(f32)
-        wide = x_s[at, :].astype(f32)
-        dr_s[at, :] = mm_split(gyw * (yv - skip * wide), gather)
-        row = lax.broadcasted_iota(jnp.int32, (8, channels), 0)
-        ggain = jnp.sum(gg * normal, 0, keepdims=True)
-        gskip = jnp.sum(gyw * wide, 0, keepdims=True)
-        acc_s[...] += jnp.where(row == 0, ggain, jnp.where(row == 1, gskip, 0.0))
+        scale, cross = scale_of(i)
         r = r_s[at, :]
-        linked = mm_split(jnp.exp2(r) * marks[:, 4:5], spread)
+        linked = jnp.exp2(r) * marks[:, 4:5]
+        row = lax.broadcasted_iota(jnp.int32, (8, 128), 0)
+        dr = jnp.zeros((SPAN, 128), f32)
+        for pair in range(channels // 128):
+            lanes = slice(pair * 128, pair * 128 + 128)
+            yv = y_s[at, lanes]
+            g = gate_s[at, lanes]
+            sg = sigmoid(g)
+            sl = g * sg
+            gg = gg_s[at, lanes].astype(f32)
+            ngate = par[5:6, lanes]
+            normal = yv * sl * scale
+            gated_s[at, lanes] = (normal * ngate).astype(bf16)
+            g_mixed = scale * (ngate * gg - normal * (scale * cross))
+            ggate_s[at, lanes] = (g_mixed * yv * (sg * (1.0 + g * (1.0 - sg)))).astype(bf16)
+            gy = (g_mixed * sl).astype(bf16)
+            gy_s[at, lanes] = gy
+            gyw = gy.astype(f32)
+            wide = x_s[at, lanes].astype(f32)
+            dr = dr + head_totals(gyw * (yv - skip[:, lanes] * wide), gather[lanes, :])
+            ggain = jnp.sum(gg * normal, 0, keepdims=True)
+            gskip = jnp.sum(gyw * wide, 0, keepdims=True)
+            acc_s[:, lanes] += jnp.where(row == 0, ggain, jnp.where(row == 1, gskip, 0.0))
+            tile_a[:, lanes] = (widen(first, linked, pair) * gyw).astype(bf16)
+        dr_s[at, :] = dr
         r_t = jnp.transpose(wr_s[at, 128:256].astype(f32)).astype(bf16)
-        dfresh = mm(r_t, (linked * gyw).astype(bf16))
+        dfresh = mm(r_t, tile_a[...])
         fresh_s[i] = dfresh
+        for b in range(blocks):
+            pl.when(back_i == b)(out_sums[b].forward)
         mem[...] = keep_of(r[SPAN - 1:SPAN, :], marks) * mem[...] + dfresh
-
-        @pl.when(back_i == 2)
-        def _():
-            out_sums[1].forward()
-
         return carry
 
     lax.fori_loop(0, blocks, turn, 0)
     pass_back[...] = mem[...].astype(bf16)
     pass_back_state.start()
-    out_sums[2].forward()
 
     def grad_out(i, carry):
         rows = pl.ds(pl.multiple_of(i * half, 128), half)
@@ -996,9 +1024,9 @@
         scores = jnp.where(allowed, mm_nt(w_low, r_low), 0.0)
         ds = mem[...]
         ds_low = ds.astype(bf16)
-        step_parts = split(step, 2)
-        te_parts = split(jnp.exp2(jnp.minimum(last - r, 0.0)) * marks[:, 5:6], 2)
-        linked_parts = split(jnp.exp2(r) * marks[:, 4:5], 2)
+        to_end = jnp.exp2(jnp.minimum(last - r, 0.0)) * marks[:, 5:6]
+        linked = jnp.exp2(r) * marks[:, 4:5]
+        wide_tile[...] = mm(w_low, ds_low)
         keep = mm_split(jnp.broadcast_to(jnp.exp2(last) * marks[0:1, 6:7], (8, 128)), spread)[0:1]
         final = jnp.where(back_i == blocks - 1, 1.0, 0.0)
 
@@ -1029,29 +1057,24 @@
 
         zero = jnp.zeros((SPAN, 128), f32)
         dscores = jnp.zeros((SPAN, SPAN), f32)
-        g_write, g_read, dr_cols, dstep = zero, zero, zero, zero
-        at_end = jnp.zeros((8, 128), f32)
+        dr_cols, dstep = zero, zero
+        endings = []
         for pair in range(channels // 128):
             lanes = slice(pair * 128, pair * 128 + 128)
-            to_lanes, to_heads = spread[:, lanes], gather[lanes, :]
-
-            def widen(parts):
-                return sum(mm(p, to_lanes) for p in parts)
-
+            to_heads = gather[lanes, :]
             wide = x_s[at, lanes].astype(f32)
-            step_wide = widen(step_parts)
+            step_wide = widen(first, step, pair)
             xp = (step_wide * wide).astype(bf16)
             xdw = xp.astype(f32)
             gp = gy_s[at, lanes]
             gyw = gp.astype(f32)
-            ds_pair = ds_low[:, lanes]
             sprev = sprev_s[i, :, lanes]
-            te = widen(te_parts)
-            total = te * mm(w_low, ds_pair)
+            te = widen(first, to_end, pair)
+            total = te * wide_tile[:, lanes]
             ending = jnp.sum(xdw * total, 0, keepdims=True) + keep[:, lanes] * jnp.sum(
                 sprev.astype(f32) * ds[:, lanes], 0, keepdims=True
             )
-            at_end = at_end + mm_split(jnp.broadcast_to(ending, (8, 128)), to_heads, 3)
+            endings.append(ending)
             for half in range(2):
                 h = 2 * pair + half
                 own = first if half == 0 else ~first
@@ -1060,16 +1083,18 @@
                 gown = jnp.where(own, gp, jnp.zeros_like(gp))
                 total = total + mm(mixing, gown)
                 dscores = dscores + mm_nt(xp, gown) * decay
-            g_write = g_write + mm_nt((te * xdw).astype(bf16), ds_pair)
-            g_read = g_read + mm_nt((widen(linked_parts) * gyw).astype(bf16), sprev)
-            dr_cols = dr_cols + mm_split(xdw * total, to_heads)
-            dstep = dstep + mm_split(wide * total, to_heads)
+            tile_a[:, lanes] = (te * xdw).astype(bf16)
+            tile_b[:, lanes] = (widen(first, linked, pair) * gyw).astype(bf16)
+            dr_cols = dr_cols + head_totals(xdw * total, to_heads)
+            dstep = dstep + head_totals(wide * total, to_heads)
             g_x = step_wide * total + skip[:, lanes] * gyw
             conv_back(xbuf, lanes, g_x * sd_s[at, lanes].astype(f32), pre_s[at, lanes].astype(f32), par,
                       accx, hpre_s, gg_s, hx)
+        ending = jnp.broadcast_to(jnp.concatenate(endings, 1), (8, channels))
+        at_end = mm_split(ending, gather, 3)
         dscores = jnp.where(allowed, dscores, 0.0)
-        g_write = g_write + mm(dscores.astype(bf16), r_low)
-        g_read = g_read + mm(jnp.transpose(dscores).astype(bf16), w_low)
+        g_write = mm(dscores.astype(bf16), r_low) + mm_nt(tile_a[...], ds_low)
+        g_read = mm(jnp.transpose(dscores).astype(bf16), w_low) + mm_nt(tile_b[...], sprev_s[i])
         both = slice(0, 256)
         g_wr = jnp.concatenate([g_write, g_read], 1)
         conv_back(sbuf, both, g_wr * ssd_s[at, :].astype(f32), spre_s[at, :].astype(f32), spar, accs,
@@ -1088,7 +1113,6 @@
 
         @pl.when(back_i == 0)
         def _():
-            out_sums[3].forward()
             sum_gate.run(1)
 
         @pl.when(back_i == 1)
@@ -1133,7 +1157,7 @@
 
     def finish(i, carry):
         at = rows_of(i)
-        scale = scale_of(at)[0]
+        scale = scale_of(i)[0]
         out_far[at, :] = (
             tok_own[at, :].astype(f32) + scale * out_sums[0].total(at)
         ).astype(bf16)
@@ -1180,12 +1204,14 @@
         by_channel, by_channel, by_channel, by_head, ((blocks, 128, channels), f32),
         ((tokens, channels), f32), ((tokens, channels), f32), by_channel, by_state,
         ((tokens, 128), bf16),
-        ((2, tokens, third), bf16), ((tokens, third), bf16), ((8, tokens), f32),
-        ((cols - 1, 8, tokens), f32), ((SPAN + 16, channels), f32), ((SPAN + 16, 256), f32),
+        ((2, tokens, third), bf16), ((tokens, third), bf16), ((tokens // 64, 128), f32),
+        ((cols - 1, tokens // 64, 128), f32), ((SPAN + 16, channels), f32), ((SPAN + 16, 256), f32),
         ((128, channels), f32), passed, passed, passed, passed,
         acc, sacc, acc, sacc, acc, sacc, hacc, acc,
         ((cols, 2, 2, q, channels), bf16),
-    ] + column_sum_shapes(cols, q, half) + row_sum_shapes(qo, width)
+    ] + column_sum_shapes(cols, q, half) + row_sum_shapes(qo, width) + [
+        ((SPAN, channels), bf16), ((SPAN, channels), bf16), ((SPAN, channels), f32),
+    ]
     vmem = pl.BlockSpec(memory_space=V)
     hbm = pl.BlockSpec(memory_space=pl.ANY)
     smem = pl.BlockSpec(memory_space=pltpu.SMEM)
@@ -1234,9 +1260,10 @@
         return copy
 
     first = [load(g4_h, g4), load(o4_h, o4)]
+    early = [load(normed_h, normed), load(gx_h, gx_s)]
     loads = [load(a, b) for a, b in (
-        (ggate_h, ggate), (wg_h, wg), (gx_h, gx_s), (wi_h, wi), (gz_h, gz_s), (ws_h, ws), (gs_h, gs_s),
-        (w_states_h, wst), (normed_h, normed),
+        (ggate_h, ggate), (wg_h, wg), (wi_h, wi), (ws_h, ws), (w_states_h, wst), (gs_h, gs_s),
+        (gz_h, gz_s),
     )]
     later = [load(a, b) for a, b in (
         (cot_h, cot_own), (sig_h, sig_s), (tok_h.at[:, own_cols], tok),
@@ -1247,7 +1274,7 @@
     sum_inner = column_home(t, i4, oi, column_sums(t, gi, i1, i2, i3, i5, i6, i4, far_i))
     sum_step = column_home(t, z4, oz, column_sums(t, gz, z1, z2, z3, z5, z6, z4, far_z))
     sum_states = full_sums(t, gs, s1, s2, s3, s4, s5, far_s, os)
-    sum_small = small_sums(t, sm, msum, mgot, sm_o, 16)
+    sum_small = small_sums(t, sm, msum, mgot, sm_o, 8)
     send_ish = [t.make(ish, ish_in.at[off - 1], {"col": t.col_peer(off)}) for off in range(1, t.cols)]
     t.meet(True)
 
@@ -1260,8 +1287,6 @@
     home_gate.run(0)
     gshare[...] = jnp.zeros_like(gshare)
     ngain[...] = jnp.broadcast_to(ngain_v[...].reshape(1, width), (8, width))
-    for c in loads:
-        c.wait()
 
     def normed_grad(i, carry):
         at = rows_of(i)
@@ -1278,7 +1303,9 @@
             return column + jnp.sum(weighed, -1, keepdims=True)
 
         column = lax.fori_loop(0, t.cols, body, jnp.zeros((SPAN, 1), f32))
-        ish[:, at] = jnp.transpose(jnp.broadcast_to(column, (SPAN, 128)))[0:8]
+        along = jnp.transpose(jnp.broadcast_to(column, (SPAN, 128)))
+        for n in range(2):
+            ish[pl.ds(2 * i + n, 1), :] = along[0:1, n * 128:n * 128 + 128]
         for b in range(blocks):
             pl.when(i == b)(norm_sums[b].start)
         return carry
@@ -1302,38 +1329,45 @@
         gs[i] = mm_tn(normed[:, rows], gs_s[...]).astype(bf16).reshape(gs.shape[1:])
         return carry
 
-    lax.fori_loop(0, 1, normed_grad, 0)
+    for c in early:
+        c.wait()
     weight_grad(gx_s, gi)
     sum_inner.run(0)
-    lax.fori_loop(1, blocks, normed_grad, 0)
+    for c in loads:
+        c.wait()
+    lax.fori_loop(0, 1, normed_grad, 0)
     sum_inner.run(1)
+    lax.fori_loop(1, 2, normed_grad, 0)
     lax.fori_loop(0, t.cols, gs_body, 0)
     sum_states.run(0)
     lax.fori_loop(0, t.cols, gz_body, 0)
     sum_step.run(0)
-    sm[0:8, :] = accx[...]
-    sm[8:16, :] = acc1[...]
-    sm[10:12, 0:128] = acch[0:2, :]
-    sm[16:24, 0:256] = accs[...]
-    sm[16:24, 256:] = jnp.zeros((8, channels - 256), f32)
-    sm[24:32, :] = gshare[:, 0:channels]
-    sm[32:40, :] = gshare[:, channels:]
+    lax.fori_loop(2, 3, normed_grad, 0)
+    norm_sums[0].forward()
+    lax.fori_loop(3, blocks, normed_grad, 0)
+    norm_sums[1].forward()
+    sm[...] = jnp.zeros_like(sm)
+    sm[0:5, :] = accx[0:5, :]
+    sm[5:7, :] = acc1[0:2, :]
+    for n in range(2):
+        sm[7:8, n * 128:n * 128 + 128] = acch[n:n + 1, :]
+        sm[8 + n:9 + n, :] = gshare[0:1, n * channels:(n + 1) * channels]
+    for n in range(5):
+        sm[10 + n // 3:11 + n // 3, n % 3 * 256:n % 3 * 256 + 256] = accs[n:n + 1, :]
     sum_small.run(0)
     for c in send_ish:
         c.start()
-    norm_sums[0].forward()
-    home_out.run(1)
-    home_gate.run(1)
-    norm_sums[1].forward()
     sum_states.run(1)
     sum_step.run(1)
     sum_small.run(1)
-    norm_sums[2].forward()
+    home_out.run(1)
+    home_gate.run(1)
     sum_inner.run(2)
-    norm_sums[3].forward()
     sum_states.run(2)
     sum_step.run(2)
     sum_small.run(2)
+    norm_sums[2].forward()
+    norm_sums[3].forward()
     sum_inner.run(3)
     sum_inner.run(4)
     sum_states.run(3)
@@ -1343,12 +1377,12 @@
     home_out.run(2)
     home_gate.run(2)
     sum_states.run(4)
-    sum_small.run(4)
-    sum_step.run(5)
     sum_inner.run(5)
     sum_states.run(5)
+    sum_step.run(5)
+    sum_small.run(4)
+    sum_states.run(6)
     sum_step.run(6)
-    sum_states.run(6)
     sum_inner.run(6)
     sum_states.run(7)
     for c in later:
@@ -1362,10 +1396,12 @@
     def finish(i, carry):
         at = rows_of(i)
         own = tok[at, :].astype(f32)
-        both = ish[:, at]
+        rows = pl.ds(2 * i, 2)
+        pair = ish[rows, :]
         for off in range(1, t.cols):
-            both = both + ish_in[off - 1, :, at]
-        along = jnp.transpose(both)[:, 0:1] / width
+            pair = pair + ish_in[off - 1, rows, :]
+        line = jnp.concatenate([pair[0:1], pair[1:2]], 1)
+        along = jnp.transpose(jnp.broadcast_to(line, (8, SPAN)))[:, 0:1] / width
         inverse = sig_s[at, 127:128]
         grad = inverse * (norm_sums[0].total(at) * ngain[0:1, own_cols] - own * (inverse * along))
         g_far[at, :] = (grad + cot_own[at, :].astype(f32)).astype(bf16)
@@ -1399,15 +1435,15 @@
 
     scratch += [
         ((8, width), f32), ((tokens, width), bf16), ((8, width), f32),
-        ((2, tokens, third), bf16), ((tokens, third), bf16), ((8, tokens), f32),
-        ((cols - 1, 8, tokens), f32),
+        ((2, tokens, third), bf16), ((tokens, third), bf16), ((tokens // 128, 128), f32),
+        ((cols - 1, tokens // 128, 128), f32),
     ]
     scratch += [((cols, 2, 2, q, 2 * own), bf16)] + column_sum_shapes(cols, q, own)
     scratch += [((cols, 2, 2, q, 256), bf16)] + column_sum_shapes(cols, q, 128)
     scratch += [
         ((cols, 2, 2, 2, qs, 256), bf16), ((cols, 2, 2, qs, 256), bf16), ((cols, 2, qs, 256), bf16),
         ((cols, qs, 256), bf16), ((cols, qs, 256), bf16), ((cols - 1, qs, 256), bf16),
-        ((40, channels), f32), ((3, 40, channels), f32), ((6 + groups, 40, channels), f32),
+        ((16, channels), f32), ((3, 16, channels), f32), ((6 + groups, 16, channels), f32),
     ]
     if groups:
         far = [(groups, cols, q, own), (groups, cols, q, 128), (groups, cols, qs, 256)]
@@ -1421,7 +1457,7 @@
             sds((tokens, third), bf16),
             sds((2, 2, q, cols * own), bf16), sds((2, 2, q, cols * own), bf16),
             sds((2, 2, q, cols * 128), bf16), sds((cols, 2, 2, qo, third), bf16),
-            sds((cols, 2, 2, 2, qs, 256), bf16), sds((40, channels), f32),
+            sds((cols, 2, 2, 2, qs, 256), bf16), sds((16, channels), f32),
         ] + [sds(f, bf16) for f in far],
         in_specs=[vmem] * len(small) + [hbm] * len(big),
         out_specs=[hbm] * 6 + [vmem] + [hbm] * 3,
@@ -1453,37 +1489,39 @@
     out_o[...] = oo[...].astype(f32)
     states_o[...] = os[...].astype(f32)
     heads = decay_log.shape[0]
-    lanes, steps = oz.shape[1], step_o.shape[1]
-    src = lax.broadcasted_iota(jnp.int32, (lanes, steps), 0)
-    dst = lax.broadcasted_iota(jnp.int32, (lanes, steps), 1)
-    pick = jnp.zeros((lanes, steps), f32)
-    for c in range(steps // heads):
-        mine = (dst >= c * heads) & (dst < (c + 1) * heads)
-        pick = pick + jnp.where(mine & (src - dst == c * 128 + y * heads - c * heads), 1.0, 0.0)
-    step_o[...] = mm(oz[...], pick.astype(bf16))
 
     @pl.when(pl.program_id(0) == 0)
     def _():
         own_ch, third = taps_o.shape[1], norm_o.shape[0]
+        steps, lanes = step_o.shape[0], oz.shape[1]
+        dst = lax.broadcasted_iota(jnp.int32, (steps, lanes), 0)
+        src = lax.broadcasted_iota(jnp.int32, (steps, lanes), 1)
+        pick = jnp.zeros((steps, lanes), f32)
+        for c in range(steps // heads):
+            mine = (dst >= c * heads) & (dst < (c + 1) * heads)
+            place = src - dst == c * 128 + y * heads - c * heads
+            pick = pick + jnp.where(mine & place, 1.0, 0.0)
+        step_o[...] = mm_nt(pick.astype(bf16), oz[...])
         own = lane_block(y, own_ch)
         taps_o[...] = sm[0:4, own]
         bias_o[...] = sm[4:5, own].reshape(own_ch)
-        gain_o[...] = sm[8:9, own].reshape(own_ch)
-        staps_o[...] = sm[16:20, 0:256]
-        sbias_o[...] = sm[20:21, 0:256].reshape(256)
-        skip = mm_split(sm[8:16, own], gather_matrix(own_ch), 3)
-        skip_o[...] = skip[1:2, 0:heads].reshape(heads)
-
-        def own_head(row):
-            both = sm[row:row + 1, 0:128]
+        gain_o[...] = sm[5:6, own].reshape(own_ch)
+        for n in range(4):
+            staps_o[n:n + 1, :] = sm[10 + n // 3:11 + n // 3, n % 3 * 256:n % 3 * 256 + 256]
+        sbias_o[...] = sm[11:12, 256:512].reshape(256)
+        skip = mm_split(sm[0:8, own], gather_matrix(own_ch), 3)
+        skip_o[...] = skip[6:7, 0:heads].reshape(heads)
+
+        def own_head(n):
+            both = sm[7:8, n * 128:n * 128 + 128]
             return jnp.where(y == 0, both[:, 0:heads], both[:, heads:2 * heads])
 
-        step_bias_o[...] = own_head(10).reshape(heads)
+        step_bias_o[...] = own_head(0).reshape(heads)
         rate = -jnp.exp(decay_log[...].reshape(1, heads))
-        decay_o[...] = (own_head(11) * rate).reshape(heads)
+        decay_o[...] = (own_head(1) * rate).reshape(heads)
         half = sm.shape[1]
-        wide[0:8, 0:half] = sm[24:32, :]
-        wide[0:8, half:] = sm[32:40, :]
+        wide[0:1, 0:half] = sm[8:9, :]
+        wide[0:1, half:] = sm[9:10, :]
         wide[8:16, :] = jnp.broadcast_to(ngain[...].reshape(1, 2 * half), (8, 2 * half))
         cols = lane_block(z, third)
         norm_o[...] = (wide[0:1, cols] / wide[8:9, cols]).reshape(third)
@@ -1500,17 +1538,17 @@
     def whole(shape):
         return pl.BlockSpec(shape, lambda i: (0,) * len(shape))
 
-    steps = (third, block // own_ch * heads)
+    steps = (block // own_ch * heads, third)
     small = [(4, own_ch), (own_ch,), (4, 256), (256,), (heads,), (heads,), (heads,), (own_ch,),
              (third,)]
     big = [oi.shape, og.shape, steps, oo.shape, os.shape]
-    ins = [rows(v.shape) for v in (oi, og, oz, oo, os)]
+    ins = [rows(oi.shape), rows(og.shape), whole(oz.shape), rows(oo.shape), rows(os.shape)]
     return pl.pallas_call(
         unpack_kernel,
         grid=(parts,),
         out_shape=[sds(s, f32) for s in big + small],
         in_specs=ins + [whole(sm.shape), whole(ngain.shape), whole(decay_log.shape)],
-        out_specs=[rows(s) for s in big] + [whole(s) for s in small],
+        out_specs=[whole(s) if s == steps else rows(s) for s in big] + [whole(s) for s in small],
         scratch_shapes=[pltpu.VMEM((16, 2 * sm.shape[1]), f32)],
         compiler_params=pltpu.CompilerParams(vmem_limit_bytes=62 * 1024 * 1024),
         name="unpack",
@@ -1528,7 +1566,7 @@
         g_gate,
     ) = front(
         inner_all, norm_gain, proj_states, segment_ids, conv_inner, conv_inner_bias, gate_gain,
-        conv_states, conv_states_bias, proj_step, step_bias, decay_log, skip_gain,
+        conv_states, conv_states_bias, proj_step.T, step_bias, decay_log, skip_gain,
         tokens_in, proj_inner, proj_gate, proj_out, cotangent,
     )
     grad_tokens, oi, og, oz, oo, os, sums = rear(
@@ -1541,7 +1579,7 @@
         grad_skip, grad_gate_gain, grad_norm_gain,
     ) = unpack(oi, og, oz, oo, os, sums, norm_gain, decay_log, conv_inner.shape[1])
     return (
-        mixed_out, grad_tokens, grad_norm_gain, grad_gate, grad_inner, grad_step, grad_states,
+        mixed_out, grad_tokens, grad_norm_gain, grad_gate, grad_inner, grad_step.T, grad_states,
         grad_conv_inner, grad_conv_inner_bias, grad_conv_states, grad_conv_states_bias,
         grad_step_bias, grad_decay, grad_skip, grad_gate_gain, grad_out,
     )

time: 267 us -> 246 us (0.921)
  Pallas kernels: 261 us -> 242 us
  local copies, waits for them, and re-layouts: 4.96 us -> 2.28 us
    pallas_call x1, Pallas kernels: 102 us -> 91.7 us  [rear(): pl.pallas_call(rear_kernel, out_shape=[sds((tokens, third), bf16), sds((2...]
    pallas_call x1, Pallas kernels: 152 us -> 144 us  [front(): pl.pallas_call(functools.partial(front_kernel, float(inner_all)), out_sha...]
    unnamed x8 -> x6, local copies, waits for them, and re-layouts: 4.96 us -> 2.28 us
where the time goes in v6:
time: 246 us; the launch traced here: 245 us
  Pallas kernels  242 us (98%)
    pallas_call x1, Pallas kernels, front(): pl.pallas_call(functools.partial(front_kernel, float(inner_all)), out_sha...  144 us
    pallas_call x1, Pallas kernels, rear(): pl.pallas_call(rear_kernel, out_shape=[sds((tokens, third), bf16), sds((2...  91.7 us
    pallas_call x1, Pallas kernels, unpack(): pl.pallas_call(unpack_kernel, grid=(parts,), out_shape=[sds(s, f32) for s...  6.66 us

profile of v6, /device:TPU:0, one launch (start us, length us, event | category | flops | bytes accessed | tf_op | source)
XLA Modules:
  0.0 245.3 jit_solution(14191173660435954250)
XLA Ops:
  0.7 144.0 %front.1 = (bf16[1024,384]{1,0:T(8,128)(2,1)}, bf16[4,2,2,96,768]{4,3,2,1,0:T(8,128)(2,1)}, bf16[4,2,2,96,768]{4,3,2,1,0:T(8,128)(2,1)}, bf16[1536,128]{1,0:T(8,...) custom-call(f32[1536]{0:T(1024)} %ngain.1, ...), custom_call_target="tpu_custom_call" | custom-call | tf_op jit(solution)/shard_map/front/pallas_call | solution.py:1218
  144.7 91.7 %rear.1 = (bf16[1024,384]{1,0:T(8,128)(2,1)}, bf16[2,2,96,1536]{3,2,1,0:T(8,128)(2,1)}, bf16[2,2,96,1536]{3,2,1,0:T(8,128)(2,1)}, bf16[2,2,96,512]{3,2,1,0:T(8,1...) custom-call(f32[8,768]{1,0:T(8,128)} %get-tuple-element.54.accx, ...), custom_call_target="tpu_custom_call" | custom-call | tf_op jit(solution)/shard_map/rear/pallas_call | solution.py:1454
  236.4 0.0 copy-start
  236.4 6.7 %unpack.1 = (f32[384,1536]{1,0:T(8,128)}, f32[384,1536]{1,0:T(8,128)}, f32[24,384]{1,0:T(8,128)}, f32[1536,384]{1,0:T(8,128)}, f32[1536,256]{1,0:T(8,128)}, /*in...) custom-call(bf16[384,1536]{1,0:T(8,128)(2,1)} %bitcast.11, ...), custom_call_target="tpu_custom_call" | custom-call | tf_op jit(solution)/shard_map/unpack/pallas_call | solution.py:1546
  243.0 0.0 copy-start.1
  243.0 0.0 copy-done
  243.1 0.9 copy.35
  243.9 0.5 copy-done.1
  244.5 0.9 copy.36
Async XLA Ops:
  236.4 6.7 %copy-start = (bf16[1024,384]{1,0:T(8,128)(2,1)S(1)}, bf16[1024,384]{1,0:T(8,128)(2,1)}, u32[]{:S(2)}) copy-start(bf16[1024,384]{1,0:T(8,128)(2,1)} %get-tuple-element.106) | copy-start | bytes 2359300
  243.0 1.4 copy-start.1

commit v7 on v6

--- a/solution.py
+++ b/solution.py
@@ -695,10 +695,13 @@
     def rows_of(i):
         return pl.ds(pl.multiple_of(i * SPAN, SPAN), SPAN)
 
+    def over_lanes(column):
+        return jnp.broadcast_to(column, (SPAN, 128))
+
     def conv_silu(buf, lanes, here, taps, marks):
         v = taps[4:5, lanes] + taps[0:1, lanes] * here
         for k in range(1, 4):
-            v = v + marks[:, k:k + 1] * (taps[k:k + 1, lanes] * buf[8 - k:8 - k + SPAN, lanes])
+            v = v + marks[k - 1] * (taps[k:k + 1, lanes] * buf[8 - k:8 - k + SPAN, lanes])
         sg = sigmoid(v)
         return v * sg, sg * (1.0 + v * (1.0 - sg))
 
@@ -723,9 +726,11 @@
         s_pre = mm(normed, w_states[...])
         sbuf[8:SPAN + 8, :] = s_pre
         spre_s[at, :] = s_pre.astype(bf16)
-        sact, sslope = conv_silu(sbuf, slice(0, 256), s_pre, spar, meta[at, :])
-        wr_s[at, :] = sact.astype(bf16)
-        ssd_s[at, :] = sslope.astype(bf16)
+        earlier = [over_lanes(meta[at, k:k + 1]) for k in range(1, 4)]
+        for lanes in (slice(0, 128), slice(128, 256)):
+            sact, sslope = conv_silu(sbuf, lanes, sbuf[8:SPAN + 8, lanes], spar, earlier)
+            wr_s[at, lanes] = sact.astype(bf16)
+            ssd_s[at, lanes] = sslope.astype(bf16)
         sig_s[at, :] = jnp.broadcast_to(inverse, (SPAN, 128))
 
         @pl.when(i == 0)
@@ -775,9 +780,10 @@
         pre_s[at, :] = x_pre.astype(bf16)
         marks = meta[at, :]
         wr = wr_s[at, :]
+        earlier = [over_lanes(marks[:, k:k + 1]) for k in range(1, 4)]
         for pair in range(channels // 128):
             lanes = slice(pair * 128, pair * 128 + 128)
-            act, slope = conv_silu(xbuf, lanes, xbuf[8:SPAN + 8, lanes], par, marks)
+            act, slope = conv_silu(xbuf, lanes, xbuf[8:SPAN + 8, lanes], par, earlier)
             x_s[at, lanes] = act.astype(bf16)
             sd_s[at, lanes] = slope.astype(bf16)
 
@@ -803,13 +809,13 @@
         def _():
             get_gate.run(2)
             get_out.run(1)
+            get_cot[1].run(0)
 
         @pl.when(i == 2)
         def _():
             get_gate.run(3)
             get_out.run(2)
             get_cot[0].run(1)
-            get_cot[1].run(0)
 
         return carry
 
@@ -868,7 +874,7 @@
         last = r[SPAN - 1:SPAN, :]
         mem[...] = keep_of(last, marks) * mem[...] + fresh_s[i]
 
-        @pl.when(i == 2)
+        @pl.when(i == 3)
         def _():
             get_cot[1].run(1)
 
@@ -885,6 +891,8 @@
         return carry
 
     lax.fori_loop(0, blocks, project, 0)
+    for s in out_sums:
+        s.start()
     get_cot[0].run(2)
     ones = jnp.ones((8, channels), bf16)
 
@@ -904,8 +912,6 @@
 
     lax.fori_loop(0, blocks // 2, totals_of, 0)
     get_cot[1].run(2)
-    for s in out_sums:
-        s.start()
     lax.fori_loop(blocks // 2, blocks, totals_of, 0)
     for c in pass_sums:
         c.start()
@@ -1027,6 +1033,7 @@
         to_end = jnp.exp2(jnp.minimum(last - r, 0.0)) * marks[:, 5:6]
         linked = jnp.exp2(r) * marks[:, 4:5]
         wide_tile[...] = mm(w_low, ds_low)
+        after = [over_lanes(marks[:, 7 + k:8 + k]) for k in range(1, 4)]
         keep = mm_split(jnp.broadcast_to(jnp.exp2(last) * marks[0:1, 6:7], (8, 128)), spread)[0:1]
         final = jnp.where(back_i == blocks - 1, 1.0, 0.0)
 
@@ -1038,7 +1045,7 @@
             halo = jnp.zeros((8, cols_here), f32)
             hsum = []
             for k in range(1, 4):
-                moved = marks[:, 7 + k:8 + k] * buf[8 + k:8 + k + SPAN, lanes]
+                moved = after[k - 1] * buf[8 + k:8 + k + SPAN, lanes]
                 total = total + taps[k:k + 1, lanes] * moved
                 sums.append(jnp.sum(moved * base, 0, keepdims=True))
                 hmoved = hmeta[:, 7 + k:8 + k] * buf[k:8 + k, lanes]
@@ -1095,10 +1102,9 @@
         dscores = jnp.where(allowed, dscores, 0.0)
         g_write = mm(dscores.astype(bf16), r_low) + mm_nt(tile_a[...], ds_low)
         g_read = mm(jnp.transpose(dscores).astype(bf16), w_low) + mm_nt(tile_b[...], sprev_s[i])
-        both = slice(0, 256)
-        g_wr = jnp.concatenate([g_write, g_read], 1)
-        conv_back(sbuf, both, g_wr * ssd_s[at, :].astype(f32), spre_s[at, :].astype(f32), spar, accs,
-                  hspre_s, gs_s, hs)
+        for lanes, grad in ((slice(0, 128), g_write), (slice(128, 256), g_read)):
+            conv_back(sbuf, lanes, grad * ssd_s[at, lanes].astype(f32), spre_s[at, lanes].astype(f32),
+                      spar, accs, hspre_s, gs_s, hs)
         tail_row = lax.broadcasted_iota(jnp.int32, (SPAN, 128), 0) == SPAN - 1
         dr = dr_s[at, :] - dr_cols + jnp.where(tail_row, at_end[0:1], 0.0)
         da = split_mm(upper_ones(), dr)
@@ -1152,18 +1158,12 @@
     write(gx_s, gx_o)
     write(gs_s, gs_o)
 
-    for s in out_sums:
-        s.arrive()
-
-    def finish(i, carry):
-        at = rows_of(i)
-        scale = scale_of(i)[0]
+    for b in range(blocks):
+        out_sums[b].arrive()
+        at = slice(b * SPAN, (b + 1) * SPAN)
         out_far[at, :] = (
-            tok_own[at, :].astype(f32) + scale * out_sums[0].total(at)
+            tok_own[at, :].astype(f32) + scale_of(b)[0] * out_sums[b].total(at)
         ).astype(bf16)
-        return carry
-
-    lax.fori_loop(0, blocks, finish, 0)
     write(out_far, mixed_o)
     for copy in outputs:
         copy.wait()
@@ -1329,23 +1329,24 @@
         gs[i] = mm_tn(normed[:, rows], gs_s[...]).astype(bf16).reshape(gs.shape[1:])
         return carry
 
-    for c in early:
+    for c in early + loads:
         c.wait()
+    lax.fori_loop(0, 1, normed_grad, 0)
     weight_grad(gx_s, gi)
     sum_inner.run(0)
-    for c in loads:
-        c.wait()
-    lax.fori_loop(0, 1, normed_grad, 0)
-    sum_inner.run(1)
-    lax.fori_loop(1, 2, normed_grad, 0)
     lax.fori_loop(0, t.cols, gs_body, 0)
     sum_states.run(0)
+    lax.fori_loop(1, 2, normed_grad, 0)
+    sum_inner.run(1)
     lax.fori_loop(0, t.cols, gz_body, 0)
     sum_step.run(0)
+    sum_states.run(1)
     lax.fori_loop(2, 3, normed_grad, 0)
-    norm_sums[0].forward()
+    sum_step.run(1)
+    norm_sums[0].forward(False)
+    sum_inner.run(2)
+    sum_states.run(2)
     lax.fori_loop(3, blocks, normed_grad, 0)
-    norm_sums[1].forward()
     sm[...] = jnp.zeros_like(sm)
     sm[0:5, :] = accx[0:5, :]
     sm[5:7, :] = acc1[0:2, :]
@@ -1357,57 +1358,51 @@
     sum_small.run(0)
     for c in send_ish:
         c.start()
-    sum_states.run(1)
-    sum_step.run(1)
+    norm_sums[1].forward(False)
+    sum_states.run(3)
+    sum_step.run(2)
+    sum_inner.run(3)
+    sum_inner.run(4)
+    norm_sums[2].forward(False)
+    norm_sums[3].forward(False)
     sum_small.run(1)
     home_out.run(1)
     home_gate.run(1)
-    sum_inner.run(2)
-    sum_states.run(2)
-    sum_step.run(2)
-    sum_small.run(2)
-    norm_sums[2].forward()
-    norm_sums[3].forward()
-    sum_inner.run(3)
-    sum_inner.run(4)
-    sum_states.run(3)
     sum_step.run(3)
     sum_step.run(4)
-    sum_small.run(3)
+    sum_states.run(4)
+    sum_small.run(2)
+    sum_inner.run(5)
+    for n in norm_sums:
+        n.second.start()
+    sum_states.run(5)
     home_out.run(2)
     home_gate.run(2)
-    sum_states.run(4)
-    sum_inner.run(5)
-    sum_states.run(5)
+    sum_small.run(3)
+    sum_states.run(6)
     sum_step.run(5)
     sum_small.run(4)
-    sum_states.run(6)
-    sum_step.run(6)
     sum_inner.run(6)
     sum_states.run(7)
+    sum_step.run(6)
     for c in later:
         c.wait()
 
     for c in send_ish:
         c.wait_recv()
-    for n in norm_sums:
-        n.arrive()
-
-    def finish(i, carry):
-        at = rows_of(i)
+    for b in range(blocks):
+        norm_sums[b].arrive()
+        at = slice(b * SPAN, (b + 1) * SPAN)
         own = tok[at, :].astype(f32)
-        rows = pl.ds(2 * i, 2)
+        rows = slice(2 * b, 2 * b + 2)
         pair = ish[rows, :]
         for off in range(1, t.cols):
             pair = pair + ish_in[off - 1, rows, :]
         line = jnp.concatenate([pair[0:1], pair[1:2]], 1)
         along = jnp.transpose(jnp.broadcast_to(line, (8, SPAN)))[:, 0:1] / width
         inverse = sig_s[at, 127:128]
-        grad = inverse * (norm_sums[0].total(at) * ngain[0:1, own_cols] - own * (inverse * along))
+        grad = inverse * (norm_sums[b].total(at) * ngain[0:1, own_cols] - own * (inverse * along))
         g_far[at, :] = (grad + cot_own[at, :].astype(f32)).astype(bf16)
-        return carry
-
-    lax.fori_loop(0, blocks, finish, 0)
     last = load(g_far, gtok_o)
     home_out.run(3)
     home_gate.run(3)

time: 246 us -> 237 us (0.963)
  Pallas kernels: 242 us -> 234 us
    pallas_call x1, Pallas kernels: 91.7 us -> 87.6 us  [rear(): pl.pallas_call(rear_kernel, out_shape=[sds((tokens, third), bf16), sds((2...]
    pallas_call x1, Pallas kernels: 144 us -> 140 us  [front(): pl.pallas_call(functools.partial(front_kernel, float(inner_all)), out_sha...]
where the time goes in v7:
time: 237 us
  Pallas kernels  234 us (99%)
    pallas_call x1, Pallas kernels, front(): pl.pallas_call(functools.partial(front_kernel, float(inner_all)), out_sha...  140 us
    pallas_call x1, Pallas kernels, rear(): pl.pallas_call(rear_kernel, out_shape=[sds((tokens, third), bf16), sds((2...  87.6 us
    pallas_call x1, Pallas kernels, unpack(): pl.pallas_call(unpack_kernel, grid=(parts,), out_shape=[sds(s, f32) for s...  6.66 us

profile of v7, /device:TPU:0, one launch (start us, length us, event | category | flops | bytes accessed | tf_op | source)
XLA Modules:
  0.0 237.1 jit_solution(10763823267020207333)
XLA Ops:
  0.7 139.9 %front.1 = (bf16[1024,384]{1,0:T(8,128)(2,1)}, bf16[4,2,2,96,768]{4,3,2,1,0:T(8,128)(2,1)}, bf16[4,2,2,96,768]{4,3,2,1,0:T(8,128)(2,1)}, bf16[1536,128]{1,0:T(8,...) custom-call(f32[1536]{0:T(1024)} %ngain.1, ...), custom_call_target="tpu_custom_call" | custom-call | tf_op jit(solution)/shard_map/front/pallas_call | solution.py:1218
  140.6 87.6 %rear.1 = (bf16[1024,384]{1,0:T(8,128)(2,1)}, bf16[2,2,96,1536]{3,2,1,0:T(8,128)(2,1)}, bf16[2,2,96,1536]{3,2,1,0:T(8,128)(2,1)}, bf16[2,2,96,512]{3,2,1,0:T(8,1...) custom-call(f32[8,768]{1,0:T(8,128)} %get-tuple-element.54.accx, ...), custom_call_target="tpu_custom_call" | custom-call | tf_op jit(solution)/shard_map/rear/pallas_call | solution.py:1449
  228.1 0.0 copy-start
  228.2 6.7 %unpack.1 = (f32[384,1536]{1,0:T(8,128)}, f32[384,1536]{1,0:T(8,128)}, f32[24,384]{1,0:T(8,128)}, f32[1536,384]{1,0:T(8,128)}, f32[1536,256]{1,0:T(8,128)}, /*in...) custom-call(bf16[384,1536]{1,0:T(8,128)(2,1)} %bitcast.11, ...), custom_call_target="tpu_custom_call" | custom-call | tf_op jit(solution)/shard_map/unpack/pallas_call | solution.py:1541
  234.8 0.0 copy-start.1
  234.8 0.0 copy-done
  234.8 0.9 copy.35
  235.7 0.5 copy-done.1
  236.2 0.9 copy.36
Async XLA Ops:
  228.1 6.7 %copy-start = (bf16[1024,384]{1,0:T(8,128)(2,1)S(1)}, bf16[1024,384]{1,0:T(8,128)(2,1)}, u32[]{:S(2)}) copy-start(bf16[1024,384]{1,0:T(8,128)(2,1)} %get-tuple-element.106) | copy-start | bytes 2359300
  234.8 1.4 copy-start.1

commit v8 on v7

--- a/solution.py
+++ b/solution.py
@@ -1473,8 +1473,8 @@
 
 
 def unpack_kernel(
-    oi, og, oz, oo, os, sm, ngain, decay_log,
-    inner_o, gate_o, step_o, out_o, states_o, taps_o, bias_o, staps_o, sbias_o, step_bias_o, decay_o,
+    oi, og, oz, oo, os, mixed, gtok, sm, ngain, decay_log,
+    inner_o, gate_o, step_o, out_o, states_o, mixed_o, gtok_o, taps_o, bias_o, staps_o, sbias_o, step_bias_o, decay_o,
     skip_o, gain_o, norm_o,
     wide,
 ):
@@ -1483,6 +1483,8 @@
     gate_o[...] = og[...].astype(f32)
     out_o[...] = oo[...].astype(f32)
     states_o[...] = os[...].astype(f32)
+    mixed_o[...] = mixed[...]
+    gtok_o[...] = gtok[...]
     heads = decay_log.shape[0]
 
     @pl.when(pl.program_id(0) == 0)
@@ -1522,7 +1524,7 @@
         norm_o[...] = (wide[0:1, cols] / wide[8:9, cols]).reshape(third)
 
 
-def unpack(oi, og, oz, oo, os, sm, ngain, decay_log, own_ch):
+def unpack(oi, og, oz, oo, os, mixed, gtok, sm, ngain, decay_log, own_ch):
     sds = jax.ShapeDtypeStruct
     heads, parts = decay_log.shape[0], 4
     third, block = oi.shape
@@ -1537,17 +1539,20 @@
     small = [(4, own_ch), (own_ch,), (4, 256), (256,), (heads,), (heads,), (heads,), (own_ch,),
              (third,)]
     big = [oi.shape, og.shape, steps, oo.shape, os.shape]
-    ins = [rows(oi.shape), rows(og.shape), whole(oz.shape), rows(oo.shape), rows(os.shape)]
+    ins = [rows(oi.shape), rows(og.shape), whole(oz.shape), rows(oo.shape), rows(os.shape), rows(mixed.shape),
+           rows(gtok.shape)]
     return pl.pallas_call(
         unpack_kernel,
         grid=(parts,),
-        out_shape=[sds(s, f32) for s in big + small],
+        out_shape=[sds(s, f32) for s in big] + [sds(v.shape, v.dtype) for v in (mixed, gtok)]
+        + [sds(s, f32) for s in small],
         in_specs=ins + [whole(sm.shape), whole(ngain.shape), whole(decay_log.shape)],
-        out_specs=[whole(s) if s == steps else rows(s) for s in big] + [whole(s) for s in small],
+        out_specs=[whole(s) if s == steps else rows(s) for s in big]
+        + [rows(mixed.shape), rows(gtok.shape)] + [whole(s) for s in small],
         scratch_shapes=[pltpu.VMEM((16, 2 * sm.shape[1]), f32)],
         compiler_params=pltpu.CompilerParams(vmem_limit_bytes=62 * 1024 * 1024),
         name="unpack",
-    )(oi, og, oz, oo, os, sm, ngain, decay_log)
+    )(oi, og, oz, oo, os, mixed, gtok, sm, ngain, decay_log)
 
 
 def per_device(
@@ -1569,10 +1574,12 @@
         normed, sig, g_gate, gx, gs, gz, g4, o4,
     )
     (
-        grad_inner, grad_gate, grad_step, grad_out, grad_states, grad_conv_inner,
+        grad_inner, grad_gate, grad_step, grad_out, grad_states, mixed_out, grad_tokens, grad_conv_inner,
         grad_conv_inner_bias, grad_conv_states, grad_conv_states_bias, grad_step_bias, grad_decay,
         grad_skip, grad_gate_gain, grad_norm_gain,
-    ) = unpack(oi, og, oz, oo, os, sums, norm_gain, decay_log, conv_inner.shape[1])
+    ) = unpack(
+        oi, og, oz, oo, os, mixed_out, grad_tokens, sums, norm_gain, decay_log, conv_inner.shape[1]
+    )
     return (
         mixed_out, grad_tokens, grad_norm_gain, grad_gate, grad_inner, grad_step.T, grad_states,
         grad_conv_inner, grad_conv_inner_bias, grad_conv_states, grad_conv_states_bias,

time: 237 us -> 236 us (level)
  no operation moved by 1% of the time
where the time goes in v8:
time: 236 us
  Pallas kernels  235 us (100%)
    pallas_call x1, Pallas kernels, front(): pl.pallas_call(functools.partial(front_kernel, float(inner_all)), out_sha...  140 us
    pallas_call x1, Pallas kernels, rear(): pl.pallas_call(rear_kernel, out_shape=[sds((tokens, third), bf16), sds((2...  87.6 us
    pallas_call x1, Pallas kernels, unpack(): pl.pallas_call(unpack_kernel, grid=(parts,), out_shape=[sds(s, f32) for s...  7.54 us

profile of v8, /device:TPU:0, one launch (start us, length us, event | category | flops | bytes accessed | tf_op | source)
XLA Modules:
  0.0 235.9 jit_solution(540888494080786018)
XLA Ops:
  0.7 139.9 %front.1 = (bf16[1024,384]{1,0:T(8,128)(2,1)}, bf16[4,2,2,96,768]{4,3,2,1,0:T(8,128)(2,1)}, bf16[4,2,2,96,768]{4,3,2,1,0:T(8,128)(2,1)}, bf16[1536,128]{1,0:T(8,...) custom-call(f32[1536]{0:T(1024)} %ngain.1, ...), custom_call_target="tpu_custom_call" | custom-call | tf_op jit(solution)/shard_map/front/pallas_call | solution.py:1218
  140.6 87.6 %rear.1 = (bf16[1024,384]{1,0:T(8,128)(2,1)}, bf16[2,2,96,1536]{3,2,1,0:T(8,128)(2,1)}, bf16[2,2,96,1536]{3,2,1,0:T(8,128)(2,1)}, bf16[2,2,96,512]{3,2,1,0:T(8,1...) custom-call(f32[8,768]{1,0:T(8,128)} %get-tuple-element.55.accx, ...), custom_call_target="tpu_custom_call" | custom-call | tf_op jit(solution)/shard_map/rear/pallas_call | solution.py:1449
  228.2 7.5 %unpack.1 = (f32[384,1536]{1,0:T(8,128)}, f32[384,1536]{1,0:T(8,128)}, f32[24,384]{1,0:T(8,128)}, f32[1536,384]{1,0:T(8,128)}, f32[1536,256]{1,0:T(8,128)}, /*in...) custom-call(bf16[384,1536]{1,0:T(8,128)(2,1)} %bitcast.11, ...), custom_call_target="tpu_custom_call" | custom-call | tf_op jit(solution)/shard_map/unpack/pallas_call | solution.py:1544
